TPU v7x, 128 devices: a whole 4x4x4 slice. The times are simulated.
128 devices in a mesh: visit: 32 (over y, x, core), patch: 4 (over z).
Axes of the slice: x: 4, y: 4, z: 4, core: 2. Of those that a mesh axis runs over, the one named last changes fastest.
Arguments:
- images: bfloat16 [32, 16, 512, 512], P('visit', 'patch'), may hold values from -6 to 6
- variances: bfloat16 [32, 16, 512, 512], P('visit', 'patch'), may hold values from 0.25 to 4
- kernels: bfloat16 [32, 2, 3, 31], P('visit'), may hold values from -1 to 1
- coefficients: bfloat16 [32, 16, 3, 3], P('visit', 'patch'), may hold values from -3 to 3
- intersections: int32 [32, 16, 2], P('visit', 'patch'), may hold values from 0 to 3, all different within a row; in each aligned block of 4 rows (0 to 3, 4 to 7, ..., all dimensions but the last counted through in order) at most 2 rows name the same one
- offsets: int32 [32, 16, 2, 2], P('visit', 'patch'), may hold values from 0 to 1024
Outputs:
- coadd: float32 [4, 1536, 1536], P('patch', 'visit')
- weight_map: float32 [4, 1536, 1536], P('patch', 'visit')
Inputs may be any that keep to these rules, and one draw needn't show every extreme that they name: `intersections`: the two patches named for a tile differ. Among the 4 tiles that one device holds (aligned blocks of 4 CCDs of one visit) at most 2 name the same patch, a bound that some block reaches of them. `offsets`: every tile lies wholly inside each patch it intersects.
All inputs are finite; a program needn't handle non-finite values.
Results may differ from a plain program's by a relative error of at most 0.0065.
Values may be sent and summed in bfloat16 or wider, within the bound.
No kernel may reach another device: no remote copies, remote signals or barrier semaphores. Data moves between devices by JAX's collectives and lax.ppermute only.
A program may use at most 128 MiB of HBM per device.

v0:
```python
import jax
import jax.numpy as jnp
from jax import lax
from jax.sharding import PartitionSpec as P

TAPS = 31
BASES = 3
PATCH_PIX = 1536


def band_table(taps, length):
    rowpos = jnp.arange(length, dtype=jnp.int32)[:, None]
    colpos = jnp.arange(length, dtype=jnp.int32)[None, :]
    spread = rowpos - colpos + TAPS // 2
    table = jnp.zeros((length, length), jnp.float32)
    for offset in range(TAPS):
        table = table + jnp.where(
            spread == offset, taps[offset].astype(jnp.float32), jnp.float32(0.0)
        )
    return table.astype(jnp.bfloat16)


def match_image(image, coeffs, downs, acrosses):
    length = image.shape[0]
    coords = (jnp.arange(length, dtype=jnp.float32) - (length - 1) / 2.0) / (length / 2.0)
    total = jnp.zeros((length, length), jnp.float32)
    for basis in range(BASES):
        middle = jnp.dot(image, acrosses[basis], preferred_element_type=jnp.float32).astype(
            jnp.bfloat16
        )
        smoothed = lax.dot_general(
            downs[basis], middle, (((0,), (0,)), ((), ())), preferred_element_type=jnp.float32
        )
        factor = coeffs[basis].astype(jnp.float32)
        surface = factor[0] + factor[1] * coords[None, :] + factor[2] * coords[:, None]
        total = total + surface * smoothed
    return total.astype(jnp.bfloat16)


def body(images, variances, kernels, coefficients, intersections, offsets):
    owners = lax.axis_size("patch")
    tiles = images.shape[1]
    length = images.shape[2]
    capacity = max(2, 2 * tiles // owners)
    slots = owners * capacity
    downs = [band_table(kernels[0, 0, basis], length) for basis in range(BASES)]
    acrosses = [band_table(kernels[0, 1, basis], length) for basis in range(BASES)]
    owner_ids = intersections[0].reshape(-1)
    entries = owner_ids.shape[0]
    onehot = (owner_ids[:, None] == jnp.arange(owners, dtype=jnp.int32)[None, :]).astype(jnp.int32)
    slot_rank = jnp.sum((jnp.cumsum(onehot, 0) - onehot) * onehot, 1)
    chosen = (
        (owner_ids[None, None, :] == jnp.arange(owners, dtype=jnp.int32)[:, None, None])
        & (slot_rank[None, None, :] == jnp.arange(capacity, dtype=jnp.int32)[None, :, None])
    ).astype(jnp.int32)
    corners = offsets[0].reshape(entries, 2)
    placed = jnp.sum(chosen[:, :, :, None] * corners[None, None, :, :], 2)
    frames = jnp.concatenate([placed, jnp.sum(chosen, 2)[:, :, None]], 2)
    tile_pick = jnp.sum(chosen.reshape(owners, capacity, tiles, 2), 3).astype(jnp.bfloat16)
    got_frames = lax.all_to_all(frames, "patch", split_axis=0, concat_axis=0, tiled=True).reshape(
        slots, 3
    )

    def route(stack):
        return jnp.einsum(
            "ost,tij->osij", tile_pick, stack, preferred_element_type=jnp.float32
        ).astype(jnp.bfloat16)

    owner_side = True
    coeff_slots = jnp.einsum(
        "ost,tbk->osbk", tile_pick, coefficients[0], preferred_element_type=jnp.float32
    ).astype(jnp.bfloat16)
    got_images, got_vars, got_coeffs = (
        lax.all_to_all(route(images[0]), "patch", split_axis=0, concat_axis=0, tiled=True),
        lax.all_to_all(route(variances[0]), "patch", split_axis=0, concat_axis=0, tiled=True),
        lax.all_to_all(coeff_slots, "patch", split_axis=0, concat_axis=0, tiled=True),
    )
    got_images = got_images.reshape(slots, length, length)
    got_vars = got_vars.reshape(slots, length, length)
    got_coeffs = got_coeffs.reshape(slots, BASES, 3)

    def accumulate(slot, canvas):

        def add_slot(state):
            numer, denom = state
            matched = match_image(got_images[slot], got_coeffs[slot], downs, acrosses).astype(
                jnp.float32
            )
            weight = 1.0 / got_vars[slot].astype(jnp.float32)
            start = (got_frames[slot, 0], got_frames[slot, 1])
            region = lax.dynamic_slice(numer, start, (length, length))
            numer = lax.dynamic_update_slice(numer, region + weight * matched, start)
            region = lax.dynamic_slice(denom, start, (length, length))
            denom = lax.dynamic_update_slice(denom, region + weight, start)
            return (numer, denom)

        return lax.cond(got_frames[slot, 2] > 0, add_slot, lambda state: state, canvas)

    zeros = jnp.zeros((PATCH_PIX, PATCH_PIX), jnp.float32)
    numer, denom = lax.fori_loop(0, slots, accumulate, (zeros, zeros))
    numer_rows, denom_rows = (
        lax.psum_scatter(numer, "visit", scatter_dimension=0, tiled=True),
        lax.psum_scatter(denom, "visit", scatter_dimension=0, tiled=True),
    )
    coadd = numer_rows / (denom_rows + 1.0)
    return (coadd[None], denom_rows[None])


def solution(mesh):
    return jax.shard_map(
        body,
        mesh=mesh,
        in_specs=(
            P("visit", "patch", None, None),
            P("visit", "patch", None, None),
            P("visit", None, None, None),
            P("visit", "patch", None, None),
            P("visit", "patch", None),
            P("visit", "patch", None, None),
        ),
        out_specs=(P("patch", "visit", None), P("patch", "visit", None)),
        check_vma=False,
    )
```

profile of v0, /device:TPU:1, one launch (start us, length us, event | category | flops | bytes accessed | tf_op | source)
XLA Modules:
  0.0 753.4 jit_solution(12593522639158011971)
XLA Ops:
  10.1 5.9 all-to-all-start
  195.0 6.5 copy.101
  201.5 22.5 %all-to-all-done.3 = bf16[4,2,512,512]{3,2,1,0:T(8,128)(2,1)} async-done(((bf16[4,2,512,512]{3,2,1,0:T(8,128)(2,1)}), bf16[4,2,512,512]{3,2,1,0:T(8,128)(2,1)}, u32[]{:S(2)}, u32[]{:S(2)}) %all-to-all-start.3) | async-done | bytes 4194336 | tf_op jit(solution)/shard_map/all_to_all | solution.py:74
  233.7 303.5 %while.15 = (s32[]{:T(128)}, f32[1536,1536]{0,1:T(8,128)}, f32[1536,1536]{0,1:T(8,128)}, s32[8,3]{0,1:T(4,128)S(1)}, bf16[8,512,512]{1,2,0:T(8,128)(2,1)}, /*ind...) while((s32[]{:T(128)}, f32[1536,1536]{0,1:T(8,128)}, ...), condition=%wide.region_8.9_spmd, body=%wide.region_5.8_spmd.sunk | while | flops 1615862784 | bytes 18377424 | solution.py:100
  234.9 36.7 %conditional.2 = ((f32[1536,1536]{0,1:T(8,128)}, f32[1536,1536]{0,1:T(8,128)})) conditional(s32[]{:T(128)} %bitcast.463, (f32[1536,1536]{0,1:T(8,128)}, f32[1536,1536]{0,1:T(8,128)}) %tuple.235, (s32[]{:T(128)}, s32[8,3]{0,1:T(4,128)S(1)}, f32[1536,1536]{0,1:T(8,128)}, bf16[8,512,512]{1,2,0:T(8,128)(2,1)}, bf16[8,3,3]{0,2,1:T(4,128)(2,1)S(1)}, ...), branch_computations={%region_6.6_spmd, %region_7.7_spmd} | conditional | flops 1615862784 | bytes 18377148 | solution.py:97
  256.4 7.6 %dynamic_update_slice.5 = f32[1536,1536]{0,1:T(8,128)} dynamic-update-slice(f32[1536,1536]{0,1:T(8,128)} %get-tuple-element.245, f32[512,512]{0,1:T(8,128)S(1)} %bitcast_add_fusion, s32[]{:T(128)S(6)} %select_n.395, s32[]{:T(128)S(6)} %select_n.396) | dynamic-update-slice | bytes 2097156 | tf_op jit(solution)/shard_map/while/body/eval_jaxpr/cond/branch_1_fun/dynamic_update_slice | solution.py:94
  264.0 7.6 %dynamic_update_slice.4 = f32[1536,1536]{0,1:T(8,128)} dynamic-update-slice(f32[1536,1536]{0,1:T(8,128)} %get-tuple-element.233, f32[512,512]{0,1:T(8,128)S(1)} %fusion.8, s32[]{:T(128)S(6)} %select_n.395, s32[]{:T(128)S(6)} %select_n.396) | dynamic-update-slice | bytes 2097156 | tf_op jit(solution)/shard_map/while/body/eval_jaxpr/cond/branch_1_fun/dynamic_update_slice | solution.py:92
  272.8 36.7 %conditional.2 = ((f32[1536,1536]{0,1:T(8,128)}, f32[1536,1536]{0,1:T(8,128)})) conditional(s32[]{:T(128)} %bitcast.463, (f32[1536,1536]{0,1:T(8,128)}, f32[1536,1536]{0,1:T(8,128)}) %tuple.235, (s32[]{:T(128)}, s32[8,3]{0,1:T(4,128)S(1)}, f32[1536,1536]{0,1:T(8,128)}, bf16[8,512,512]{1,2,0:T(8,128)(2,1)}, bf16[8,3,3]{0,2,1:T(4,128)(2,1)S(1)}, ...), branch_computations={%region_6.6_spmd, %region_7.7_spmd} | conditional | flops 1615862784 | bytes 18377148 | solution.py:97
  294.3 7.6 %dynamic_update_slice.5 = f32[1536,1536]{0,1:T(8,128)} dynamic-update-slice(f32[1536,1536]{0,1:T(8,128)} %get-tuple-element.245, f32[512,512]{0,1:T(8,128)S(1)} %bitcast_add_fusion, s32[]{:T(128)S(6)} %select_n.395, s32[]{:T(128)S(6)} %select_n.396) | dynamic-update-slice | bytes 2097156 | tf_op jit(solution)/shard_map/while/body/eval_jaxpr/cond/branch_1_fun/dynamic_update_slice | solution.py:94
  301.9 7.6 %dynamic_update_slice.4 = f32[1536,1536]{0,1:T(8,128)} dynamic-update-slice(f32[1536,1536]{0,1:T(8,128)} %get-tuple-element.233, f32[512,512]{0,1:T(8,128)S(1)} %fusion.8, s32[]{:T(128)S(6)} %select_n.395, s32[]{:T(128)S(6)} %select_n.396) | dynamic-update-slice | bytes 2097156 | tf_op jit(solution)/shard_map/while/body/eval_jaxpr/cond/branch_1_fun/dynamic_update_slice | solution.py:92
  310.7 36.7 %conditional.2 = ((f32[1536,1536]{0,1:T(8,128)}, f32[1536,1536]{0,1:T(8,128)})) conditional(s32[]{:T(128)} %bitcast.463, (f32[1536,1536]{0,1:T(8,128)}, f32[1536,1536]{0,1:T(8,128)}) %tuple.235, (s32[]{:T(128)}, s32[8,3]{0,1:T(4,128)S(1)}, f32[1536,1536]{0,1:T(8,128)}, bf16[8,512,512]{1,2,0:T(8,128)(2,1)}, bf16[8,3,3]{0,2,1:T(4,128)(2,1)S(1)}, ...), branch_computations={%region_6.6_spmd, %region_7.7_spmd} | conditional | flops 1615862784 | bytes 18377148 | solution.py:97
  332.2 7.6 %dynamic_update_slice.5 = f32[1536,1536]{0,1:T(8,128)} dynamic-update-slice(f32[1536,1536]{0,1:T(8,128)} %get-tuple-element.245, f32[512,512]{0,1:T(8,128)S(1)} %bitcast_add_fusion, s32[]{:T(128)S(6)} %select_n.395, s32[]{:T(128)S(6)} %select_n.396) | dynamic-update-slice | bytes 2097156 | tf_op jit(solution)/shard_map/while/body/eval_jaxpr/cond/branch_1_fun/dynamic_update_slice | solution.py:94
  339.8 7.6 %dynamic_update_slice.4 = f32[1536,1536]{0,1:T(8,128)} dynamic-update-slice(f32[1536,1536]{0,1:T(8,128)} %get-tuple-element.233, f32[512,512]{0,1:T(8,128)S(1)} %fusion.8, s32[]{:T(128)S(6)} %select_n.395, s32[]{:T(128)S(6)} %select_n.396) | dynamic-update-slice | bytes 2097156 | tf_op jit(solution)/shard_map/while/body/eval_jaxpr/cond/branch_1_fun/dynamic_update_slice | solution.py:92
  348.7 36.7 %conditional.2 = ((f32[1536,1536]{0,1:T(8,128)}, f32[1536,1536]{0,1:T(8,128)})) conditional(s32[]{:T(128)} %bitcast.463, (f32[1536,1536]{0,1:T(8,128)}, f32[1536,1536]{0,1:T(8,128)}) %tuple.235, (s32[]{:T(128)}, s32[8,3]{0,1:T(4,128)S(1)}, f32[1536,1536]{0,1:T(8,128)}, bf16[8,512,512]{1,2,0:T(8,128)(2,1)}, bf16[8,3,3]{0,2,1:T(4,128)(2,1)S(1)}, ...), branch_computations={%region_6.6_spmd, %region_7.7_spmd} | conditional | flops 1615862784 | bytes 18377148 | solution.py:97
  370.2 7.6 %dynamic_update_slice.5 = f32[1536,1536]{0,1:T(8,128)} dynamic-update-slice(f32[1536,1536]{0,1:T(8,128)} %get-tuple-element.245, f32[512,512]{0,1:T(8,128)S(1)} %bitcast_add_fusion, s32[]{:T(128)S(6)} %select_n.395, s32[]{:T(128)S(6)} %select_n.396) | dynamic-update-slice | bytes 2097156 | tf_op jit(solution)/shard_map/while/body/eval_jaxpr/cond/branch_1_fun/dynamic_update_slice | solution.py:94
  377.8 7.6 %dynamic_update_slice.4 = f32[1536,1536]{0,1:T(8,128)} dynamic-update-slice(f32[1536,1536]{0,1:T(8,128)} %get-tuple-element.233, f32[512,512]{0,1:T(8,128)S(1)} %fusion.8, s32[]{:T(128)S(6)} %select_n.395, s32[]{:T(128)S(6)} %select_n.396) | dynamic-update-slice | bytes 2097156 | tf_op jit(solution)/shard_map/while/body/eval_jaxpr/cond/branch_1_fun/dynamic_update_slice | solution.py:92
  386.6 36.7 %conditional.2 = ((f32[1536,1536]{0,1:T(8,128)}, f32[1536,1536]{0,1:T(8,128)})) conditional(s32[]{:T(128)} %bitcast.463, (f32[1536,1536]{0,1:T(8,128)}, f32[1536,1536]{0,1:T(8,128)}) %tuple.235, (s32[]{:T(128)}, s32[8,3]{0,1:T(4,128)S(1)}, f32[1536,1536]{0,1:T(8,128)}, bf16[8,512,512]{1,2,0:T(8,128)(2,1)}, bf16[8,3,3]{0,2,1:T(4,128)(2,1)S(1)}, ...), branch_computations={%region_6.6_spmd, %region_7.7_spmd} | conditional | flops 1615862784 | bytes 18377148 | solution.py:97
  408.0 7.6 %dynamic_update_slice.5 = f32[1536,1536]{0,1:T(8,128)} dynamic-update-slice(f32[1536,1536]{0,1:T(8,128)} %get-tuple-element.245, f32[512,512]{0,1:T(8,128)S(1)} %bitcast_add_fusion, s32[]{:T(128)S(6)} %select_n.395, s32[]{:T(128)S(6)} %select_n.396) | dynamic-update-slice | bytes 2097156 | tf_op jit(solution)/shard_map/while/body/eval_jaxpr/cond/branch_1_fun/dynamic_update_slice | solution.py:94
  415.6 7.6 %dynamic_update_slice.4 = f32[1536,1536]{0,1:T(8,128)} dynamic-update-slice(f32[1536,1536]{0,1:T(8,128)} %get-tuple-element.233, f32[512,512]{0,1:T(8,128)S(1)} %fusion.8, s32[]{:T(128)S(6)} %select_n.395, s32[]{:T(128)S(6)} %select_n.396) | dynamic-update-slice | bytes 2097156 | tf_op jit(solution)/shard_map/while/body/eval_jaxpr/cond/branch_1_fun/dynamic_update_slice | solution.py:92
  424.5 37.2 %conditional.2 = ((f32[1536,1536]{0,1:T(8,128)}, f32[1536,1536]{0,1:T(8,128)})) conditional(s32[]{:T(128)} %bitcast.463, (f32[1536,1536]{0,1:T(8,128)}, f32[1536,1536]{0,1:T(8,128)}) %tuple.235, (s32[]{:T(128)}, s32[8,3]{0,1:T(4,128)S(1)}, f32[1536,1536]{0,1:T(8,128)}, bf16[8,512,512]{1,2,0:T(8,128)(2,1)}, bf16[8,3,3]{0,2,1:T(4,128)(2,1)S(1)}, ...), branch_computations={%region_6.6_spmd, %region_7.7_spmd} | conditional | flops 1615862784 | bytes 18377148 | solution.py:97
  446.0 7.9 %dynamic_update_slice.5 = f32[1536,1536]{0,1:T(8,128)} dynamic-update-slice(f32[1536,1536]{0,1:T(8,128)} %get-tuple-element.245, f32[512,512]{0,1:T(8,128)S(1)} %bitcast_add_fusion, s32[]{:T(128)S(6)} %select_n.395, s32[]{:T(128)S(6)} %select_n.396) | dynamic-update-slice | bytes 2097156 | tf_op jit(solution)/shard_map/while/body/eval_jaxpr/cond/branch_1_fun/dynamic_update_slice | solution.py:94
  453.8 7.8 %dynamic_update_slice.4 = f32[1536,1536]{0,1:T(8,128)} dynamic-update-slice(f32[1536,1536]{0,1:T(8,128)} %get-tuple-element.233, f32[512,512]{0,1:T(8,128)S(1)} %fusion.8, s32[]{:T(128)S(6)} %select_n.395, s32[]{:T(128)S(6)} %select_n.396) | dynamic-update-slice | bytes 2097156 | tf_op jit(solution)/shard_map/while/body/eval_jaxpr/cond/branch_1_fun/dynamic_update_slice | solution.py:92
  462.9 37.3 %conditional.2 = ((f32[1536,1536]{0,1:T(8,128)}, f32[1536,1536]{0,1:T(8,128)})) conditional(s32[]{:T(128)} %bitcast.463, (f32[1536,1536]{0,1:T(8,128)}, f32[1536,1536]{0,1:T(8,128)}) %tuple.235, (s32[]{:T(128)}, s32[8,3]{0,1:T(4,128)S(1)}, f32[1536,1536]{0,1:T(8,128)}, bf16[8,512,512]{1,2,0:T(8,128)(2,1)}, bf16[8,3,3]{0,2,1:T(4,128)(2,1)S(1)}, ...), branch_computations={%region_6.6_spmd, %region_7.7_spmd} | conditional | flops 1615862784 | bytes 18377148 | solution.py:97
  484.4 7.9 %dynamic_update_slice.5 = f32[1536,1536]{0,1:T(8,128)} dynamic-update-slice(f32[1536,1536]{0,1:T(8,128)} %get-tuple-element.245, f32[512,512]{0,1:T(8,128)S(1)} %bitcast_add_fusion, s32[]{:T(128)S(6)} %select_n.395, s32[]{:T(128)S(6)} %select_n.396) | dynamic-update-slice | bytes 2097156 | tf_op jit(solution)/shard_map/while/body/eval_jaxpr/cond/branch_1_fun/dynamic_update_slice | solution.py:94
  492.3 7.8 %dynamic_update_slice.4 = f32[1536,1536]{0,1:T(8,128)} dynamic-update-slice(f32[1536,1536]{0,1:T(8,128)} %get-tuple-element.233, f32[512,512]{0,1:T(8,128)S(1)} %fusion.8, s32[]{:T(128)S(6)} %select_n.395, s32[]{:T(128)S(6)} %select_n.396) | dynamic-update-slice | bytes 2097156 | tf_op jit(solution)/shard_map/while/body/eval_jaxpr/cond/branch_1_fun/dynamic_update_slice | solution.py:92
  501.4 35.7 %conditional.2 = ((f32[1536,1536]{0,1:T(8,128)}, f32[1536,1536]{0,1:T(8,128)})) conditional(s32[]{:T(128)} %bitcast.463, (f32[1536,1536]{0,1:T(8,128)}, f32[1536,1536]{0,1:T(8,128)}) %tuple.235, (s32[]{:T(128)}, s32[8,3]{0,1:T(4,128)S(1)}, f32[1536,1536]{0,1:T(8,128)}, bf16[8,512,512]{1,2,0:T(8,128)(2,1)}, bf16[8,3,3]{0,2,1:T(4,128)(2,1)S(1)}, ...), branch_computations={%region_6.6_spmd, %region_7.7_spmd} | conditional | flops 1615862784 | bytes 18377148 | solution.py:97
  522.9 7.2 dynamic_update_slice.5
  530.0 7.1 dynamic_update_slice.4
  537.1 9.6 %copy.104 = f32[1536,1536]{1,0:T(8,128)} copy(f32[1536,1536]{0,1:T(8,128)} %get-tuple-element.267) | data formatting | bytes 18874368 | tf_op jit(solution)/shard_map/while | solution.py:100
  546.9 9.6 %copy.103 = f32[1536,1536]{1,0:T(8,128)} copy(f32[1536,1536]{0,1:T(8,128)} %get-tuple-element.266) | data formatting | bytes 18874368 | tf_op jit(solution)/shard_map/while | solution.py:100
  556.5 89.2 %reduce-scatter.5.cloned.1.call-done = f32[48,1536]{1,0:T(8,128)} async-done(((f32[1536,1536]{1,0:T(8,128)}), f32[48,1536]{1,0:T(8,128)}) %reduce-scatter.5.cloned.1.call-update) | async-done | bytes 294928 | tf_op jit(solution)/shard_map/reduce_scatter | solution.py:103
  645.7 99.0 %reduce-scatter.3.cloned.1.call-done = f32[48,1536]{1,0:T(8,128)} async-done(((f32[1536,1536]{1,0:T(8,128)}), f32[48,1536]{1,0:T(8,128)}) %reduce-scatter.3.cloned.1.call-update) | async-done | bytes 294928 | tf_op jit(solution)/shard_map/reduce_scatter | solution.py:102
  (178 shorter events, 193.4 us)
Async XLA Ops:
  7.2 9.7 %copy-start = (bf16[1,4,3,3]{3,1,2,0:T(4,128)(2,1)S(1)}, bf16[1,4,3,3]{3,1,2,0:T(4,128)(2,1)}, u32[]{:S(2)}) copy-start(bf16[1,4,3,3]{3,1,2,0:T(4,128)(2,1)} %param.13) | copy-start | bytes 220
  10.1 10.0 %all-to-all-start = ((s32[4,2,3]{2,1,0:T(2,128)}), s32[4,2,3]{2,1,0:T(2,128)S(1)}, u32[]{:S(2)}, u32[]{:S(2)}) async-start(s32[4,2,3]{2,1,0:T(2,128)} %copy.91), calls=%async_computation | async-start | bytes 8192 | tf_op jit(solution)/shard_map/all_to_all | solution.py:60
  20.1 10.2 %all-to-all-start.2 = ((bf16[4,2,3,3]{3,1,2,0:T(2,128)(2,1)}), bf16[4,2,3,3]{3,1,2,0:T(2,128)(2,1)S(1)}, u32[]{:S(2)}, u32[]{:S(2)}) async-start(bf16[4,2,3,3]{3,1,2,0:T(2,128)(2,1)} %copy.96), calls=%async_computation.2 | async-start | bytes 12288 | tf_op jit(solution)/shard_map/all_to_all | solution.py:76
  30.3 5.2 copy-start.2
  30.3 129.2 %copy-start.3 = (bf16[1,4,512,512]{3,2,1,0:T(8,128)(2,1)S(1)}, bf16[1,4,512,512]{3,2,1,0:T(8,128)(2,1)}, u32[]{:S(2)}) copy-start(bf16[1,4,512,512]{3,2,1,0:T(8,128)(2,1)} %param.10) | copy-start | bytes 6291460
  30.3 142.0 %all-to-all-start.1 = ((bf16[4,2,512,512]{3,2,1,0:T(8,128)(2,1)}), bf16[4,2,512,512]{3,2,1,0:T(8,128)(2,1)}, u32[]{:S(2)}, u32[]{:S(2)}) async-start(bf16[4,2,512,512]{3,2,1,0:T(8,128)(2,1)} %copy.94), calls=%async_computation.1 | async-start | bytes 8388608 | tf_op jit(solution)/shard_map/all_to_all | solution.py:75
  172.3 51.6 %all-to-all-start.3 = ((bf16[4,2,512,512]{3,2,1,0:T(8,128)(2,1)}), bf16[4,2,512,512]{3,2,1,0:T(8,128)(2,1)}, u32[]{:S(2)}, u32[]{:S(2)}) async-start(bf16[4,2,512,512]{3,2,1,0:T(8,128)(2,1)} %copy.99), calls=%async_computation.3 | async-start | bytes 8388608 | tf_op jit(solution)/shard_map/all_to_all | solution.py:74
  177.2 468.5 %reduce-scatter.5.cloned.1.call-start = ((), (), s32[]{:S(2)}) async-start(), calls=%async_computation.7 | async-start | bytes 9732096 | tf_op jit(solution)/shard_map/reduce_scatter | solution.py:103
  546.8 197.9 %reduce-scatter.3.cloned.1.call-start = ((), (), s32[]{:S(2)}) async-start(), calls=%async_computation.6 | async-start | bytes 9732096 | tf_op jit(solution)/shard_map/reduce_scatter | solution.py:102
  556.4 190.1 %copy-start.1 = (bf16[1,4,3,3]{3,1,2,0:T(4,128)(2,1)S(1)}, bf16[1,4,3,3]{3,1,2,0:T(4,128)(2,1)}, u32[]{:S(2)}) copy-start(bf16[1,4,3,3]{3,1,2,0:T(4,128)(2,1)} %param.13) | copy-start | bytes 220
Sparse Core Ops, SparseCore 0:
  546.9 98.7 reduce-scatter.4
  649.9 94.7 reduce-scatter.2
where the time goes:
time: 762 us; the launch traced here: 753 us
  waiting for transfers between devices  213 us (28%)
  local copies, waits for them, and re-layouts  189 us (25%)
  between operations  130 us (17%)
  matrix products  73 us (10%)
  loops' own time  65.8 us (9%)
  other arithmetic  63.2 us (8%)
  starting transfers between devices  19.4 us (3%)
    reduce_scatter x1, waiting for transfers between devices, body(): lax.psum_scatter(numer, 'visit', scatter_dimension=0, tiled=True)  99 us
    reduce_scatter x1, waiting for transfers between devices, body(): lax.psum_scatter(denom, 'visit', scatter_dimension=0, tiled=True)  89.2 us
    dot_general x24, matrix products, match_image(): lax.dot_general(downs[basis], middle, (((0,), (0,)), ((), ())), preferred...  66.1 us
    dynamic_update_slice x8, local copies, waits for them, and re-layouts, add_slot(): denom = lax.dynamic_update_slice(denom, region + weight, start)  60.9 us
    dynamic_update_slice x8, local copies, waits for them, and re-layouts, add_slot(): numer = lax.dynamic_update_slice(numer, region + weight * matched, start)  60.7 us
    another operation x8, loops' own time, accumulate(): lax.cond(got_frames[slot, 2] > 0, add_slot, lambda state: state, canvas)  60.6 us
    while x5, local copies, waits for them, and re-layouts, body(): numer, denom = lax.fori_loop(0, slots, accumulate, (zeros, zeros))  25.9 us
    convert_element_type x6, other arithmetic, band_table(): return table.astype(jnp.bfloat16)  24.6 us
  transfers between devices with their start and end apart: 6, of which 4 were waited for; matrix products, arithmetic and copies ran while one was open for 8% of the time, Pallas kernels for 0%

commit v1 on v0

v1 whole, which is shorter than its diff:
```python
import functools

import jax
import jax.numpy as jnp
from jax import lax
from jax.experimental import pallas as pl
from jax.experimental.pallas import tpu as pltpu
from jax.sharding import PartitionSpec as P

TAPS = 31
BASES = 3
TILE = 512
PATCH_PIX = 1536
HALF = PATCH_PIX // 2
STRIP = 48
LANES = 128
ROWS = 8
SLAB = 384
BF16 = jnp.bfloat16
F32 = jnp.float32
BOTH = ("visit", "patch")


def visit_of(y, x, c):
    return (y * 4 + x) * 2 + c


def chips():
    return [(y, x) for y in range(4) for x in range(4)]


def across_x(value, step):
    pairs = [
        (visit_of(y, x, c), visit_of(y, (x + step) % 4, c)) for y, x in chips() for c in range(2)
    ]
    return lax.ppermute(value, "visit", pairs)


def across_y(value, step):
    pairs = [
        (visit_of(y, x, c), visit_of((y + step) % 4, x, c)) for y, x in chips() for c in range(2)
    ]
    return lax.ppermute(value, "visit", pairs)


def across_z(value, step):
    return lax.ppermute(value, "patch", [(z, (z + step) % 4) for z in range(4)])


def across_core(value):
    pairs = [(visit_of(y, x, c), visit_of(y, x, 1 - c)) for y, x in chips() for c in range(2)]
    return lax.ppermute(value, "visit", pairs)


def core_to_core(value, source, target, step):
    pairs = [
        (visit_of(y, x, source) * 4 + z, visit_of(y, x, target) * 4 + (z + step) % 4)
        for y, x in chips()
        for z in range(4)
    ]
    return lax.ppermute(value, BOTH, pairs)


def slot_of(info, entry):
    patch = info[0, entry]
    rank = jnp.int32(0)
    for other in range(8):
        rank += jnp.where((other < entry) & (info[0, other] == patch), 1, 0)
    return lax.rem(patch - info[0, 27] + 4, 4), jnp.minimum(rank, 1)


def weights_kernel(info, variance, plus, minus, held, sems):
    tile = pl.program_id(0)
    held[tile] = (1.0 / variance[0].astype(F32)).astype(BF16)

    def each(index, act):
        for which in range(2):
            towards, rank = slot_of(info, 2 * index + which)
            for wanted, target in ((1, plus), (3, minus)):

                @pl.when(towards == wanted)
                def _():
                    act(pltpu.make_async_copy(held.at[index], target.at[rank], sems.at[index, which]))

    each(tile, lambda copy: copy.start())

    @pl.when(tile == 3)
    def _():
        for index in range(4):
            each(index, lambda copy: copy.wait())


def send_weights(info, variances):
    out = jax.ShapeDtypeStruct((2, TILE, TILE), BF16)
    return pl.pallas_call(
        weights_kernel,
        grid=(4,),
        in_specs=[
            pl.BlockSpec(memory_space=pltpu.SMEM),
            pl.BlockSpec((1, TILE, TILE), lambda t: (t, 0, 0)),
        ],
        out_specs=[pl.BlockSpec(memory_space=pl.ANY)] * 2,
        out_shape=[out, out],
        scratch_shapes=[pltpu.VMEM((4, TILE, TILE), BF16), pltpu.SemaphoreType.DMA((4, 2))],
        compiler_params=pltpu.CompilerParams(vmem_limit_bytes=16 << 20),
        cost_estimate=pl.CostEstimate(flops=4 << 20, bytes_accessed=6 << 20, transcendentals=0),
    )(info, variances)


def match_kernel(
    info, coeffs, bands, image, variance, plus, minus, swap, stay, across, down, numer, weight, sems, wsems
):
    tile = pl.program_id(0)
    core = info[0, 26]

    @pl.when(tile == 0)
    def _():
        for basis in range(2 * BASES):
            row = jnp.broadcast_to(bands[basis : basis + 1, :], (LANES, 3 * LANES))
            band = pltpu.roll(row, 0, axis=1, stride=1, stride_axis=0).astype(BF16)
            table = across if basis < BASES else down
            for block in range(TILE // LANES):
                rows = slice(block * LANES, (block + 1) * LANES)
                table[basis % BASES, rows, :] = jnp.zeros((LANES, TILE), BF16)
                first = (block - 1) * LANES
                low, high = max(first, 0), min(first + 3 * LANES, TILE)
                table[basis % BASES, rows, low:high] = band[:, low - first : high - first]

    rows = lax.broadcasted_iota(jnp.int32, (TILE, 1), 0).astype(F32)
    columns = lax.broadcasted_iota(jnp.int32, (1, TILE), 1).astype(F32)
    rows = (rows - (TILE - 1) / 2.0) / (TILE / 2.0)
    columns = (columns - (TILE - 1) / 2.0) / (TILE / 2.0)
    total = jnp.zeros((TILE, TILE), F32)
    for basis in range(BASES):
        middle = jnp.dot(image[0], across[basis], preferred_element_type=F32).astype(BF16)
        smoothed = jnp.dot(down[basis], middle, preferred_element_type=F32)
        c0, c1, c2 = (coeffs[tile, 3 * basis + k] for k in range(3))
        total += ((c0 + c1 * columns) + c2 * rows) * smoothed
    inverse = 1.0 / variance[0].astype(F32)
    numer[tile] = (inverse * total).astype(BF16)
    weight[tile] = inverse.astype(BF16)

    def each(index, act):
        for which in range(2):
            towards, rank = slot_of(info, 2 * index + which)
            for wanted, target in ((1, plus), (3, minus)):

                @pl.when(towards == wanted)
                def _():
                    act(pltpu.make_async_copy(numer.at[index], target.at[rank], sems.at[index, which]))

            even = lax.rem(towards, 2) == 0
            place = lax.div(towards, 2)
            for own_core, (held, sent) in enumerate(((stay, swap), (swap, stay))):

                @pl.when(even & (core == own_core))
                def _():
                    act(pltpu.make_async_copy(numer.at[index], held.at[place, rank], sems.at[index, which]))
                    act(pltpu.make_async_copy(weight.at[index], sent.at[place, rank], wsems.at[index, which]))

    each(tile, lambda copy: copy.start())

    @pl.when(tile == 3)
    def _():
        for index in range(4):
            each(index, lambda copy: copy.wait())


def match_tiles(info, coeffs, bands, images, variances):
    pair = jax.ShapeDtypeStruct((2, TILE, TILE), BF16)
    quad = jax.ShapeDtypeStruct((2, 2, TILE, TILE), BF16)
    return pl.pallas_call(
        match_kernel,
        grid=(4,),
        in_specs=[
            pl.BlockSpec(memory_space=pltpu.SMEM),
            pl.BlockSpec(memory_space=pltpu.SMEM),
            pl.BlockSpec((8, 3 * LANES), lambda t: (0, 0)),
            pl.BlockSpec((1, TILE, TILE), lambda t: (t, 0, 0)),
            pl.BlockSpec((1, TILE, TILE), lambda t: (t, 0, 0)),
        ],
        out_specs=[pl.BlockSpec(memory_space=pl.ANY)] * 4,
        out_shape=[pair, pair, quad, quad],
        scratch_shapes=[
            pltpu.VMEM((BASES, TILE, TILE), BF16),
            pltpu.VMEM((BASES, TILE, TILE), BF16),
            pltpu.VMEM((4, TILE, TILE), BF16),
            pltpu.VMEM((4, TILE, TILE), BF16),
            pltpu.SemaphoreType.DMA((4, 2)),
            pltpu.SemaphoreType.DMA((4, 2)),
        ],
        compiler_params=pltpu.CompilerParams(vmem_limit_bytes=40 << 20),
        cost_estimate=pl.CostEstimate(flops=6 << 30, bytes_accessed=10 << 20, transcendentals=0),
    )(info, coeffs, bands, images, variances)


def frame_kernel(far, sources, table, *refs):
    stacks, refs = refs[: 2 if sources == 2 else 10], refs[2 if sources == 2 else 10 :]
    outs, (frame, held, packed, sems, out_sems) = refs[:8], refs[8:]
    y, x, core, z = (table[0, 24 + k] for k in range(4))
    patch = lax.rem(z + 2 * far, 4)

    def load(number):
        source, slot = number // 2, number % 2
        target, sem = held.at[number], sems.at[number]
        if source < 2:
            pltpu.make_async_copy(stacks[source].at[far, slot], target, sem).start()
            return
        for own_core in range(2):

            @pl.when(core == own_core)
            def _():
                stack = stacks[2 + 4 * own_core + source - 2]
                pltpu.make_async_copy(stack.at[slot], target, sem).start()

    for number in range(2 * sources):
        load(number)
    frame[...] = jnp.zeros_like(frame)
    apart = lax.broadcasted_iota(jnp.int32, (2 * LANES, LANES), 1) - lax.broadcasted_iota(
        jnp.int32, (2 * LANES, LANES), 0
    )

    inner = lax.broadcasted_iota(jnp.int32, (TILE // ROWS + 1, ROWS, LANES), 1)
    nothing = jnp.zeros((1, ROWS, LANES), F32)

    def add(number, carry):
        source, slot = lax.div(number, 2), lax.rem(number, 2)
        entry = jnp.int32(0)
        for k in range(8):
            named = table[source, k] == patch
            entry = jnp.where(named & ((slot == 1) | (entry == 0)), k + 1, entry)
        entry = jnp.maximum(entry - 1, 0)
        top, left = table[source, 8 + 2 * entry], table[source, 9 + 2 * entry]
        first = jnp.minimum(lax.div(left, LANES) * LANES, PATCH_PIX - TILE - LANES)
        group, lead = lax.div(top, ROWS), lax.rem(top, ROWS)
        shift = jnp.where(apart == left - first - LANES, F32(1.0), F32(0.0)).astype(BF16)
        pltpu.make_async_copy(stacks[0].at[far, 0], held.at[number], sems.at[number]).wait()
        for block in range(5):
            low, high = max(block - 1, 0) * LANES, min(block + 1, 4) * LANES
            moved = jnp.dot(
                held[number, :, low:high],
                shift[LANES * (block == 0) : 2 * LANES - LANES * (block == 4)],
                preferred_element_type=F32,
            )
            turned = pltpu.roll(moved.reshape(TILE // ROWS, ROWS, LANES), lead, axis=1)
            lower = jnp.concatenate([turned, nothing], axis=0)
            upper = jnp.concatenate([nothing, turned], axis=0)
            where = (
                pl.ds(group, TILE // ROWS + 1),
                slice(None),
                pl.ds(pl.multiple_of(first + block * LANES, LANES), LANES),
            )
            frame[where] += jnp.where(inner >= lead, lower, upper)
        return carry

    lax.fori_loop(0, 2 * sources, add, 0)

    copies = []
    for out in range(8):
        for part in range(4):
            dx, dy = (out, part) if out < 4 else (part, out - 4)
            for dc in range(2):
                row = (
                    2 * 4 * STRIP * lax.rem(y + dy, 4) + 2 * STRIP * lax.rem(x + dx, 4) + STRIP * lax.rem(core + dc, 2)
                )
                strip = frame[pl.ds(lax.div(row, ROWS), STRIP // ROWS), :, (out // 4) * HALF : (out // 4 + 1) * HALF]
                at = (2 * part + dc) * STRIP
                packed[out, at : at + STRIP, :] = strip.reshape(STRIP, HALF).astype(BF16)
        copies.append(pltpu.make_async_copy(packed.at[out], outs[out], out_sems.at[out]))
        copies[-1].start()
    for copy in copies:
        copy.wait()


def build_frame(far, sources, table, stacks):
    out = jax.ShapeDtypeStruct((SLAB, HALF), BF16)
    return pl.pallas_call(
        functools.partial(frame_kernel, far, sources),
        in_specs=[pl.BlockSpec(memory_space=pltpu.SMEM)] + [pl.BlockSpec(memory_space=pl.ANY)] * len(stacks),
        out_specs=[pl.BlockSpec(memory_space=pl.ANY)] * 8,
        out_shape=[out] * 8,
        scratch_shapes=[
            pltpu.VMEM((PATCH_PIX // ROWS + 1, ROWS, PATCH_PIX), F32),
            pltpu.VMEM((2 * sources, TILE, TILE), BF16),
            pltpu.VMEM((8, SLAB, HALF), BF16),
            pltpu.SemaphoreType.DMA((2 * sources,)),
            pltpu.SemaphoreType.DMA((8,)),
        ],
        compiler_params=pltpu.CompilerParams(vmem_limit_bytes=40 << 20),
        cost_estimate=pl.CostEstimate(flops=sources << 30, bytes_accessed=(5 + sources) << 20, transcendentals=0),
    )(table, *stacks)


def sum_kernel(count, *refs):
    for half in range(2):
        total = refs[half * count][...].astype(F32)
        for other in range(1, count):
            total += refs[half * count + other][...].astype(F32)
        for part in range(4):
            refs[2 * count + 4 * half + part][...] = total[part * 2 * STRIP : (part + 1) * 2 * STRIP].astype(BF16)


def sum_slabs(first, second):
    count = len(first)
    out = jax.ShapeDtypeStruct((2 * STRIP, HALF), BF16)
    return pl.pallas_call(
        functools.partial(sum_kernel, count),
        out_shape=[out] * 8,
        compiler_params=pltpu.CompilerParams(vmem_limit_bytes=40 << 20),
        cost_estimate=pl.CostEstimate(flops=6 << 20, bytes_accessed=(count + 1) << 20, transcendentals=0),
    )(*first, *second)


def spread(pieces, send):
    return [pieces[0]] + [send(pieces[step], step) for step in (1, 3, 2)]


def body(images, variances, kernels, coefficients, intersections, offsets):
    visit, z = lax.axis_index("visit"), lax.axis_index("patch")
    place = jnp.stack([visit // 8, (visit // 2) % 4, visit % 2, z]).astype(jnp.int32)
    info = jnp.concatenate([intersections.reshape(8), offsets.reshape(16), place, jnp.zeros((100,), jnp.int32)])
    info = info.reshape(1, LANES)

    weight_plus, weight_minus = send_weights(info, variances[0])
    weights = [
        core_to_core(buffer, source, 1, step)
        for source in range(2)
        for buffer, step in ((weight_plus, 1), (weight_minus, 3))
    ]
    chip = jnp.concatenate([info, across_core(info)])
    table = jnp.concatenate([chip, across_z(chip, 1), across_z(chip, 3)])

    taps = kernels[0].astype(F32)
    bands = jnp.concatenate([taps[1, :, ::-1], taps[0], jnp.zeros((2, TAPS), F32)])
    bands = jnp.pad(bands, ((0, 0), (LANES - TAPS // 2, 2 * LANES - TAPS + TAPS // 2)))
    coeffs = coefficients[0].astype(F32).reshape(4, 9)
    numer_plus, numer_minus, swap, stay = match_tiles(info, coeffs, bands, images[0], variances[0])
    swapped = across_core(swap)
    numers = [
        core_to_core(buffer, source, 0, step)
        for source in range(2)
        for buffer, step in ((numer_plus, 1), (numer_minus, 3))
    ]

    opposite = build_frame(1, 2, chip, [stay, swapped])
    first = spread(opposite[:4], across_x)
    second = spread(opposite[4:], across_y)
    passed = []
    for slabs in (first, second):
        total = sum(slab.astype(F32) for slab in slabs).astype(BF16)
        passed.append(across_z(total, 2))

    stacks = [stay, swapped, numers[0], numers[2], numers[1], numers[3], weights[2], weights[0], weights[3], weights[1]]
    own = build_frame(0, 6, table, stacks)
    first = spread(own[:4], across_x) + [passed[0]]
    second = spread(own[4:], across_y) + [passed[1]]
    pieces = sum_slabs(first, second)
    left = sum(piece.astype(F32) for piece in spread(pieces[:4], across_y))
    right = sum(piece.astype(F32) for piece in spread(pieces[4:], across_x))
    rows = jnp.concatenate([left, right], axis=1)
    keep, other = rows[:STRIP], across_core(rows[STRIP:])
    core = visit % 2
    numer = jnp.where(core == 0, keep, other)
    weight = jnp.where(core == 0, other, keep)
    return (numer / (weight + 1.0))[None], weight[None]


def solution(mesh):
    return jax.shard_map(
        body,
        mesh=mesh,
        in_specs=(
            P("visit", "patch", None, None),
            P("visit", "patch", None, None),
            P("visit", None, None, None),
            P("visit", "patch", None, None),
            P("visit", "patch", None),
            P("visit", "patch", None, None),
        ),
        out_specs=(P("patch", "visit", None), P("patch", "visit", None)),
        check_vma=False,
    )
```

time: 762 us -> 174 us (0.23); the launches traced: 753 us -> 174 us
  local copies, waits for them, and re-layouts: 189 us -> 10.3 us
  waiting for transfers between devices: 213 us -> 76.6 us
  between operations: 130 us -> 0.92 us
  matrix products: 73 us -> 0 us
  loops' own time: 65.8 us -> 0 us
  other arithmetic: 63.2 us -> 2.37 us
  starting transfers between devices: 19.4 us -> 56.3 us
  Pallas kernels: 0 us -> 27.8 us
    reduce_scatter x2 -> x0, waiting for transfers between devices: 188 us -> none  [the longest x1 99 us: body(): lax.psum_scatter(numer, 'visit', scatter_dimension=0, tiled=True)]
    dynamic_update_slice x16 -> x0, local copies, waits for them, and re-layouts: 122 us -> none  [the longest x8 60.9 us: add_slot(): denom = lax.dynamic_update_slice(denom, region + weight, start)]
    ppermute x0 -> x33, waiting for transfers between devices: none -> 76.6 us  [the longest x4 23.2 us: across_z(): return lax.ppermute(value, 'patch', [(z, (z + step) % 4) for z in range(4)])]
    dot_general x27 -> x0, matrix products: 73 us -> none  [the longest x24 66.1 us: match_image(): lax.dot_general(downs[basis], middle, (((0,), (0,)), ((), ())), preferred...]
    another operation x9 -> x0, loops' own time: 65.8 us -> none  [the longest x8 60.6 us: accumulate(): lax.cond(got_frames[slot, 2] > 0, add_slot, lambda state: state, canvas)]
    ppermute x0 -> x33, starting transfers between devices: none -> 56.3 us  [the longest x3 15.2 us: across_core(): return lax.ppermute(value, 'visit', pairs)]
    add x32 -> x2, other arithmetic: 30 us -> 0.14 us  [the longest x1 0.07 us: body(): left = sum((piece.astype(F32) for piece in spread(pieces[:4], across_y)))]
    pallas_call x0 -> x5, Pallas kernels: none -> 27.8 us  [the longest x2 15.1 us: build_frame(): pl.pallas_call(functools.partial(frame_kernel, far, sources), in_specs=[p...]
  transfers between devices with their start and end apart: 6 -> 33, of which waited for: 4 -> 14; matrix products, arithmetic and copies ran while one was open for 8% -> 0% of each run, Pallas kernels for 0% -> 10%
where the time goes in v1:
time: 174 us
  waiting for transfers between devices  76.6 us (44%)
  starting transfers between devices  56.3 us (32%)
  Pallas kernels  27.8 us (16%)
  local copies, waits for them, and re-layouts  10.3 us (6%)
  other arithmetic  2.37 us (1%)
    ppermute x4, waiting for transfers between devices, across_z(): return lax.ppermute(value, 'patch', [(z, (z + step) % 4) for z in range(4)])  23.2 us
    ppermute x8, waiting for transfers between devices, core_to_core(): return lax.ppermute(value, BOTH, pairs)  20.2 us
    ppermute x9, waiting for transfers between devices, across_y(): return lax.ppermute(value, 'visit', pairs)  18.1 us
    ppermute x3, starting transfers between devices, across_core(): return lax.ppermute(value, 'visit', pairs)  15.2 us
    ppermute x8, starting transfers between devices, core_to_core(): return lax.ppermute(value, BOTH, pairs)  15.1 us
    pallas_call x2, Pallas kernels, build_frame(): pl.pallas_call(functools.partial(frame_kernel, far, sources), in_specs=[p...  15.1 us
    ppermute x9, starting transfers between devices, across_x(): return lax.ppermute(value, 'visit', pairs)  14.6 us
    ppermute x9, waiting for transfers between devices, across_x(): return lax.ppermute(value, 'visit', pairs)  13 us
  transfers between devices with their start and end apart: 33, of which 14 were waited for; matrix products, arithmetic and copies ran while one was open for 0% of the time, Pallas kernels for 10%

profile of v1, /device:TPU:1, one launch (start us, length us, event | category | flops | bytes accessed | tf_op | source)
XLA Modules:
  0.0 174.2 jit_solution(17809015017059645930)
XLA Ops:
  5.0 1.6 copy-done
  6.5 1.6 copy-done.1
  8.1 10.3 %shard_map.77 = (bf16[2,512,512]{2,1,0:T(8,128)(2,1)S(1)}, bf16[2,512,512]{2,1,0:T(8,128)(2,1)S(1)}, bf16[2,2,512,512]{3,2,1,0:T(8,128)(2,1)S(1)}, bf16[2,2,512,512]{3,2,1,0:T(8,128)(2,1)S(1)}) custom-call(s32[1,128]{1,0:T(1,128)S(1)} %bitcast.21, f32[4,9]{1,0:T(4,128)S(1)} %reshape.24.coeffs, f32[8,384]{1,0:T(8,128)S(1)} %pad.4.bands, ...), custom_call_target="tpu_custom_call" | custom-call | flops 6442450944 | bytes 10485760 | tf_op jit(solution)/shard_map/pallas_call | solution.py:172
  19.9 1.4 collective-permute-start.3
  21.3 1.6 shard_map.78
  24.2 3.6 %collective-permute-start.8 = (bf16[2,512,512]{2,1,0:T(8,128)(2,1)S(1)}, bf16[2,512,512]{2,1,0:T(8,128)(2,1)S(1)}, u32[]{:S(2)}, u32[]{:S(2)}) collective-permute-start(bf16[2,512,512]{2,1,0:T(8,128)(2,1)S(1)} %get-tuple-element.36), channel_id=1, source_target_pairs={{4,5},{5,6},{6,7},{7,4},{12,13},{13,14},{14,15},{15,12},{20,21},{2... | collective-permute-start | bytes 3145736 | tf_op jit(solution)/shard_map/ppermute | solution.py:61
  29.1 3.3 %collective-permute-start = (s32[1,128]{1,0:T(1,128)S(1)}, s32[1,128]{1,0:T(1,128)S(1)}, u32[]{:S(2)}, u32[]{:S(2)}) collective-permute-start(s32[1,128]{1,0:T(1,128)S(1)} %bitcast.23), channel_id=1, source_target_pairs={{0,4},{4,0},{8,12},{12,8},{16,20},{20,16},{24,28},{28,24},{32,36},... | collective-permute-start | bytes 1544 | tf_op jit(solution)/shard_map/ppermute | solution.py:52
  33.3 1.5 collective-permute-start.2
  35.8 15.9 %collective-permute-done.1 = s32[2,128]{1,0:T(2,128)S(1)} collective-permute-done((s32[2,128]{1,0:T(2,128)S(1)}, s32[2,128]{1,0:T(2,128)S(1)}, u32[]{:S(2)}, u32[]{:S(2)}) %collective-permute-start.1) | collective-permute-done | bytes 1056 | tf_op jit(solution)/shard_map/ppermute | solution.py:47
  51.7 4.4 %collective-permute-start.10 = (bf16[2,512,512]{2,1,0:T(8,128)(2,1)S(1)}, bf16[2,512,512]{2,1,0:T(8,128)(2,1)S(1)}, u32[]{:S(2)}, u32[]{:S(2)}) collective-permute-start(bf16[2,512,512]{2,1,0:T(8,128)(2,1)S(1)} %get-tuple-element.37), channel_id=1, source_target_pairs={{4,7},{5,4},{6,5},{7,6},{12,15},{13,12},{14,13},{15,14},{20,23},{2... | collective-permute-start | bytes 3145736 | tf_op jit(solution)/shard_map/ppermute | solution.py:61
  56.1 1.4 collective-permute-start.5
  58.2 1.8 %collective-permute-start.7 = (bf16[2,512,512]{2,1,0:T(8,128)(2,1)S(1)}, bf16[2,512,512]{2,1,0:T(8,128)(2,1)S(1)}, u32[]{:S(2)}, u32[]{:S(2)}) collective-permute-start(bf16[2,512,512]{2,1,0:T(8,128)(2,1)S(1)} %get-tuple-element.35), channel_id=1, source_target_pairs={{4,3},{5,0},{6,1},{7,2},{12,11},{13,8},{14,9},{15,10},{20,19},{21,... | collective-permute-start | bytes 3145736 | tf_op jit(solution)/shard_map/ppermute | solution.py:61
  60.7 5.1 %shard_map.80 = (bf16[384,768]{1,0:T(8,128)(2,1)S(1)}, bf16[384,768]{1,0:T(8,128)(2,1)S(1)}, bf16[384,768]{1,0:T(8,128)(2,1)S(1)}, bf16[384,768]{1,0:T(8,128)(2,...) custom-call(s32[2,128]{1,0:T(2,128)S(1)} %pad_add_fusion.1.table, ...), custom_call_target="tpu_custom_call" | custom-call | flops 2147483648 | bytes 7340032 | tf_op jit(solution)/shard_map/pallas_call | solution.py:277
  65.8 7.4 %collective-permute-done.10.refs_8_ = bf16[2,512,512]{2,1,0:T(8,128)(2,1)S(1)} collective-permute-done((bf16[2,512,512]{2,1,0:T(8,128)(2,1)S(1)}, bf16[2,512,512]{2,1,0:T(8,128)(2,1)S(1)}, u32[]{:S(2)}, u32[]{:S(2)}) %collective-permute-start.10) | collective-permute-done | bytes 1048608 | tf_op jit(solution)/shard_map/ppermute | solution.py:61
  74.5 4.9 %collective-permute-done.5.refs_3_ = bf16[2,512,512]{2,1,0:T(8,128)(2,1)S(1)} collective-permute-done((bf16[2,512,512]{2,1,0:T(8,128)(2,1)S(1)}, bf16[2,512,512]{2,1,0:T(8,128)(2,1)S(1)}, u32[]{:S(2)}, u32[]{:S(2)}) %collective-permute-start.5) | collective-permute-done | bytes 1048608 | tf_op jit(solution)/shard_map/ppermute | solution.py:61
  79.4 2.5 %collective-permute-start.16 = (bf16[384,768]{1,0:T(8,128)(2,1)}, bf16[384,768]{1,0:T(8,128)(2,1)S(1)}, u32[]{:S(2)}, u32[]{:S(2)}) collective-permute-start(bf16[384,768]{1,0:T(8,128)(2,1)} %get-tuple-element.44), channel_id=1, source_target_pairs={{0,24},{4,28},{8,0},{12,4},{16,8},{20,12},{24,16},{28,20},{32,56},... | collective-permute-start | bytes 1769480 | tf_op jit(solution)/shard_map/ppermute | solution.py:36
  82.4 7.9 %collective-permute-done.7.refs_5_ = bf16[2,512,512]{2,1,0:T(8,128)(2,1)S(1)} collective-permute-done((bf16[2,512,512]{2,1,0:T(8,128)(2,1)S(1)}, bf16[2,512,512]{2,1,0:T(8,128)(2,1)S(1)}, u32[]{:S(2)}, u32[]{:S(2)}) %collective-permute-start.7) | collective-permute-done | bytes 1048608 | tf_op jit(solution)/shard_map/ppermute | solution.py:61
  92.6 1.5 collective-permute-start.23
  94.0 1.6 collective-permute-start.24
  96.9 10.0 %shard_map.79 = (bf16[384,768]{1,0:T(8,128)(2,1)S(1)}, bf16[384,768]{1,0:T(8,128)(2,1)S(1)}, bf16[384,768]{1,0:T(8,128)(2,1)S(1)}, bf16[384,768]{1,0:T(8,128)(2,...) custom-call(s32[6,128]{1,0:T(8,128)S(1)} %pad_add_fusion.table, ...), custom_call_target="tpu_custom_call" | custom-call | flops 6442450944 | bytes 11534336 | tf_op jit(solution)/shard_map/pallas_call | solution.py:277
  108.2 1.5 collective-permute-start.13
  109.7 1.6 collective-permute-start.14
  111.9 9.3 %collective-permute-done.24 = bf16[384,768]{1,0:T(8,128)(2,1)S(1)} collective-permute-done((bf16[384,768]{1,0:T(8,128)(2,1)S(1)}, bf16[384,768]{1,0:T(8,128)(2,1)S(1)}, u32[]{:S(2)}, u32[]{:S(2)}) %collective-permute-start.24) | collective-permute-done | bytes 589856 | tf_op jit(solution)/shard_map/ppermute | solution.py:43
  122.4 1.5 collective-permute-start.21
  123.9 10.6 %collective-permute-done.14.refs_3_ = bf16[384,768]{1,0:T(8,128)(2,1)S(1)} collective-permute-done((bf16[384,768]{1,0:T(8,128)(2,1)S(1)}, bf16[384,768]{1,0:T(8,128)(2,1)S(1)}, u32[]{:S(2)}, u32[]{:S(2)}) %collective-permute-start.14) | collective-permute-done | bytes 589856 | tf_op jit(solution)/shard_map/ppermute | solution.py:36
  134.5 8.7 %collective-permute-done.21.refs_8_ = bf16[384,768]{1,0:T(8,128)(2,1)S(1)} collective-permute-done((bf16[384,768]{1,0:T(8,128)(2,1)S(1)}, bf16[384,768]{1,0:T(8,128)(2,1)S(1)}, u32[]{:S(2)}, u32[]{:S(2)}) %collective-permute-start.21) | collective-permute-done | bytes 589856 | tf_op jit(solution)/shard_map/ppermute | solution.py:43
  143.2 6.2 %collective-permute-done.25.refs_9_ = bf16[384,768]{1,0:T(8,128)(2,1)S(1)} collective-permute-done((bf16[384,768]{1,0:T(8,128)(2,1)S(1)}, bf16[384,768]{1,0:T(8,128)(2,1)S(1)}, u32[]{:S(2)}, u32[]{:S(2)}) %collective-permute-start.25) | collective-permute-done | bytes 589856 | tf_op jit(solution)/shard_map/ppermute | solution.py:47
  150.2 2.7 %collective-permute-start.27 = (bf16[96,768]{1,0:T(8,128)(2,1)S(1)}, bf16[96,768]{1,0:T(8,128)(2,1)S(1)}, u32[]{:S(2)}, u32[]{:S(2)}) collective-permute-start(bf16[96,768]{1,0:T(8,128)(2,1)S(1)} %get-tuple-element.56), channel_id=1, source_target_pairs={{0,96},{4,100},{8,104},{12,108},{16,112},{20,116},{24,120},{28,124... | collective-permute-start | bytes 442376 | tf_op jit(solution)/shard_map/ppermute | solution.py:43
  152.9 2.6 %collective-permute-start.29 = (bf16[96,768]{1,0:T(8,128)(2,1)S(1)}, bf16[96,768]{1,0:T(8,128)(2,1)S(1)}, u32[]{:S(2)}, u32[]{:S(2)}) collective-permute-start(bf16[96,768]{1,0:T(8,128)(2,1)S(1)} %get-tuple-element.59), channel_id=1, source_target_pairs={{0,8},{4,12},{8,16},{12,20},{16,24},{20,28},{24,0},{28,4},{32,40},... | collective-permute-start | bytes 442376 | tf_op jit(solution)/shard_map/ppermute | solution.py:36
  155.7 3.4 %collective-permute-start.31 = (bf16[96,768]{1,0:T(8,128)(2,1)S(1)}, bf16[96,768]{1,0:T(8,128)(2,1)S(1)}, u32[]{:S(2)}, u32[]{:S(2)}) collective-permute-start(bf16[96,768]{1,0:T(8,128)(2,1)S(1)} %get-tuple-element.61), channel_id=1, source_target_pairs={{0,16},{4,20},{8,24},{12,28},{16,0},{20,4},{24,8},{28,12},{32,48},... | collective-permute-start | bytes 442376 | tf_op jit(solution)/shard_map/ppermute | solution.py:36
  159.4 2.2 %collective-permute-done.31 = bf16[96,768]{1,0:T(8,128)(2,1)S(1)} collective-permute-done((bf16[96,768]{1,0:T(8,128)(2,1)S(1)}, bf16[96,768]{1,0:T(8,128)(2,1)S(1)}, u32[]{:S(2)}, u32[]{:S(2)}) %collective-permute-start.31) | collective-permute-done | bytes 147488 | tf_op jit(solution)/shard_map/ppermute | solution.py:36
  161.7 10.4 %collective-permute-start.32 = (f32[48,1536]{1,0:T(8,128)S(1)}, f32[48,1536]{1,0:T(8,128)S(1)}, u32[]{:S(2)}, u32[]{:S(2)}) collective-permute-start(f32[48,1536]{1,0:T(8,128)S(1)} %pad_maximum_fusion), channel_id=1, source_target_pairs={{0,4},{4,0},{8,12},{12,8},{16,20},{20,16},{24,28},{28,24},{32,36},... | collective-permute-start | bytes 884744 | tf_op jit(solution)/shard_map/ppermute | solution.py:52
  (79 shorter events, 23.6 us)
Async XLA Ops:
  19.9 40.1 %collective-permute-start.3 = (bf16[2,2,512,512]{3,2,1,0:T(8,128)(2,1)S(1)}, bf16[2,2,512,512]{3,2,1,0:T(8,128)(2,1)S(1)}, u32[]{:S(2)}, u32[]{:S(2)}) collective-permute-start(bf16[2,2,512,512]{3,2,1,0:T(8,128)(2,1)S(1)} %get-tuple-element.33), channel_id=1, source_target_pairs={{0,4},{4,0},{8,12},{12,8},{16,20},{20,16},{24,28},{28,24},{32,36},... | collective-permute-start | bytes 6291464 | tf_op jit(solution)/shard_map/ppermute | solution.py:52
  22.9 33.2 %collective-permute-start.9 = (bf16[2,512,512]{2,1,0:T(8,128)(2,1)S(1)}, bf16[2,512,512]{2,1,0:T(8,128)(2,1)S(1)}, u32[]{:S(2)}, u32[]{:S(2)}) collective-permute-start(bf16[2,512,512]{2,1,0:T(8,128)(2,1)S(1)} %get-tuple-element.36), channel_id=1, source_target_pairs={{0,5},{1,6},{2,7},{3,4},{8,13},{9,14},{10,15},{11,12},{16,21},{17,... | collective-permute-start | bytes 3145736 | tf_op jit(solution)/shard_map/ppermute | solution.py:61
  24.2 33.3 %collective-permute-start.8 = (bf16[2,512,512]{2,1,0:T(8,128)(2,1)S(1)}, bf16[2,512,512]{2,1,0:T(8,128)(2,1)S(1)}, u32[]{:S(2)}, u32[]{:S(2)}) collective-permute-start(bf16[2,512,512]{2,1,0:T(8,128)(2,1)S(1)} %get-tuple-element.36), channel_id=1, source_target_pairs={{4,5},{5,6},{6,7},{7,4},{12,13},{13,14},{14,15},{15,12},{20,21},{2... | collective-permute-start | bytes 3145736 | tf_op jit(solution)/shard_map/ppermute | solution.py:61
  27.8 30.4 %collective-permute-start.11 = (bf16[2,512,512]{2,1,0:T(8,128)(2,1)S(1)}, bf16[2,512,512]{2,1,0:T(8,128)(2,1)S(1)}, u32[]{:S(2)}, u32[]{:S(2)}) collective-permute-start(bf16[2,512,512]{2,1,0:T(8,128)(2,1)S(1)} %get-tuple-element.37), channel_id=1, source_target_pairs={{0,7},{1,4},{2,5},{3,6},{8,15},{9,12},{10,13},{11,14},{16,23},{17,... | collective-permute-start | bytes 3145736 | tf_op jit(solution)/shard_map/ppermute | solution.py:61
  29.1 4.1 %collective-permute-start = (s32[1,128]{1,0:T(1,128)S(1)}, s32[1,128]{1,0:T(1,128)S(1)}, u32[]{:S(2)}, u32[]{:S(2)}) collective-permute-start(s32[1,128]{1,0:T(1,128)S(1)} %bitcast.23), channel_id=1, source_target_pairs={{0,4},{4,0},{8,12},{12,8},{16,20},{20,16},{24,28},{28,24},{32,36},... | collective-permute-start | bytes 1544 | tf_op jit(solution)/shard_map/ppermute | solution.py:52
  35.8 15.9 %collective-permute-start.1 = (s32[2,128]{1,0:T(2,128)S(1)}, s32[2,128]{1,0:T(2,128)S(1)}, u32[]{:S(2)}, u32[]{:S(2)}) collective-permute-start(s32[2,128]{1,0:T(2,128)S(1)} %pad_add_fusion.1.table), channel_id=1, source_target_pairs={{0,1},{1,2},{2,3},{3,0},{4,5},{5,6},{6,7},{7,4},{8,9},{9,10},{10,1... | collective-permute-start | bytes 3080 | tf_op jit(solution)/shard_map/ppermute | solution.py:47
  51.7 21.5 %collective-permute-start.10 = (bf16[2,512,512]{2,1,0:T(8,128)(2,1)S(1)}, bf16[2,512,512]{2,1,0:T(8,128)(2,1)S(1)}, u32[]{:S(2)}, u32[]{:S(2)}) collective-permute-start(bf16[2,512,512]{2,1,0:T(8,128)(2,1)S(1)} %get-tuple-element.37), channel_id=1, source_target_pairs={{4,7},{5,4},{6,5},{7,6},{12,15},{13,12},{14,13},{15,14},{20,23},{2... | collective-permute-start | bytes 3145736 | tf_op jit(solution)/shard_map/ppermute | solution.py:61
  56.1 23.3 %collective-permute-start.5 = (bf16[2,512,512]{2,1,0:T(8,128)(2,1)S(1)}, bf16[2,512,512]{2,1,0:T(8,128)(2,1)S(1)}, u32[]{:S(2)}, u32[]{:S(2)}) collective-permute-start(bf16[2,512,512]{2,1,0:T(8,128)(2,1)S(1)} %get-tuple-element.34), channel_id=1, source_target_pairs={{4,1},{5,2},{6,3},{7,0},{12,9},{13,10},{14,11},{15,8},{20,17},{21,... | collective-permute-start | bytes 3145736 | tf_op jit(solution)/shard_map/ppermute | solution.py:61
  57.5 24.4 %collective-permute-start.4 = (bf16[2,512,512]{2,1,0:T(8,128)(2,1)S(1)}, bf16[2,512,512]{2,1,0:T(8,128)(2,1)S(1)}, u32[]{:S(2)}, u32[]{:S(2)}) collective-permute-start(bf16[2,512,512]{2,1,0:T(8,128)(2,1)S(1)} %get-tuple-element.34), channel_id=1, source_target_pairs={{0,1},{1,2},{2,3},{3,0},{8,9},{9,10},{10,11},{11,8},{16,17},{17,18... | collective-permute-start | bytes 3145736 | tf_op jit(solution)/shard_map/ppermute | solution.py:61
  58.2 32.1 %collective-permute-start.7 = (bf16[2,512,512]{2,1,0:T(8,128)(2,1)S(1)}, bf16[2,512,512]{2,1,0:T(8,128)(2,1)S(1)}, u32[]{:S(2)}, u32[]{:S(2)}) collective-permute-start(bf16[2,512,512]{2,1,0:T(8,128)(2,1)S(1)} %get-tuple-element.35), channel_id=1, source_target_pairs={{4,3},{5,0},{6,1},{7,2},{12,11},{13,8},{14,9},{15,10},{20,19},{21,... | collective-permute-start | bytes 3145736 | tf_op jit(solution)/shard_map/ppermute | solution.py:61
  60.0 32.6 %collective-permute-start.6 = (bf16[2,512,512]{2,1,0:T(8,128)(2,1)S(1)}, bf16[2,512,512]{2,1,0:T(8,128)(2,1)S(1)}, u32[]{:S(2)}, u32[]{:S(2)}) collective-permute-start(bf16[2,512,512]{2,1,0:T(8,128)(2,1)S(1)} %get-tuple-element.35), channel_id=1, source_target_pairs={{0,3},{1,0},{2,1},{3,2},{8,11},{9,8},{10,9},{11,10},{16,19},{17,16... | collective-permute-start | bytes 3145736 | tf_op jit(solution)/shard_map/ppermute | solution.py:61
  73.2 20.8 %collective-permute-start.15 = (bf16[384,768]{1,0:T(8,128)(2,1)S(1)}, bf16[384,768]{1,0:T(8,128)(2,1)S(1)}, u32[]{:S(2)}, u32[]{:S(2)}) collective-permute-start(bf16[384,768]{1,0:T(8,128)(2,1)S(1)} %get-tuple-element.43), channel_id=1, source_target_pairs={{0,8},{4,12},{8,16},{12,20},{16,24},{20,28},{24,0},{28,4},{32,40},... | collective-permute-start | bytes 1769480 | tf_op jit(solution)/shard_map/ppermute | solution.py:36
  79.4 27.5 %collective-permute-start.16 = (bf16[384,768]{1,0:T(8,128)(2,1)}, bf16[384,768]{1,0:T(8,128)(2,1)S(1)}, u32[]{:S(2)}, u32[]{:S(2)}) collective-permute-start(bf16[384,768]{1,0:T(8,128)(2,1)} %get-tuple-element.44), channel_id=1, source_target_pairs={{0,24},{4,28},{8,0},{12,4},{16,8},{20,12},{24,16},{28,20},{32,56},... | collective-permute-start | bytes 1769480 | tf_op jit(solution)/shard_map/ppermute | solution.py:36
  81.9 26.3 %collective-permute-start.17 = (bf16[384,768]{1,0:T(8,128)(2,1)S(1)}, bf16[384,768]{1,0:T(8,128)(2,1)S(1)}, u32[]{:S(2)}, u32[]{:S(2)}) collective-permute-start(bf16[384,768]{1,0:T(8,128)(2,1)S(1)} %get-tuple-element.45), channel_id=1, source_target_pairs={{0,16},{4,20},{8,24},{12,28},{16,0},{20,4},{24,8},{28,12},{32,48},... | collective-permute-start | bytes 1769480 | tf_op jit(solution)/shard_map/ppermute | solution.py:36
  91.3 18.4 %collective-permute-start.22 = (bf16[384,768]{1,0:T(8,128)(2,1)S(1)}, bf16[384,768]{1,0:T(8,128)(2,1)S(1)}, u32[]{:S(2)}, u32[]{:S(2)}) collective-permute-start(bf16[384,768]{1,0:T(8,128)(2,1)S(1)} %get-tuple-element.51), channel_id=1, source_target_pairs={{0,32},{4,36},{8,40},{12,44},{16,48},{20,52},{24,56},{28,60},{32,6... | collective-permute-start | bytes 1769480 | tf_op jit(solution)/shard_map/ppermute | solution.py:43
  92.6 19.0 %collective-permute-start.23 = (bf16[384,768]{1,0:T(8,128)(2,1)S(1)}, bf16[384,768]{1,0:T(8,128)(2,1)S(1)}, u32[]{:S(2)}, u32[]{:S(2)}) collective-permute-start(bf16[384,768]{1,0:T(8,128)(2,1)S(1)} %get-tuple-element.52), channel_id=1, source_target_pairs={{0,96},{4,100},{8,104},{12,108},{16,112},{20,116},{24,120},{28,124... | collective-permute-start | bytes 1769480 | tf_op jit(solution)/shard_map/ppermute | solution.py:43
  94.0 27.2 %collective-permute-start.24 = (bf16[384,768]{1,0:T(8,128)(2,1)S(1)}, bf16[384,768]{1,0:T(8,128)(2,1)S(1)}, u32[]{:S(2)}, u32[]{:S(2)}) collective-permute-start(bf16[384,768]{1,0:T(8,128)(2,1)S(1)} %get-tuple-element.53), channel_id=1, source_target_pairs={{0,64},{4,68},{8,72},{12,76},{16,80},{20,84},{24,88},{28,92},{32,9... | collective-permute-start | bytes 1769480 | tf_op jit(solution)/shard_map/ppermute | solution.py:43
  106.9 15.5 %collective-permute-start.12 = (bf16[384,768]{1,0:T(8,128)(2,1)S(1)}, bf16[384,768]{1,0:T(8,128)(2,1)S(1)}, u32[]{:S(2)}, u32[]{:S(2)}) collective-permute-start(bf16[384,768]{1,0:T(8,128)(2,1)S(1)} %get-tuple-element.39), channel_id=1, source_target_pairs={{0,8},{4,12},{8,16},{12,20},{16,24},{20,28},{24,0},{28,4},{32,40},... | collective-permute-start | bytes 1769480 | tf_op jit(solution)/shard_map/ppermute | solution.py:36
  108.2 15.7 %collective-permute-start.13 = (bf16[384,768]{1,0:T(8,128)(2,1)S(1)}, bf16[384,768]{1,0:T(8,128)(2,1)S(1)}, u32[]{:S(2)}, u32[]{:S(2)}) collective-permute-start(bf16[384,768]{1,0:T(8,128)(2,1)S(1)} %get-tuple-element.40), channel_id=1, source_target_pairs={{0,24},{4,28},{8,0},{12,4},{16,8},{20,12},{24,16},{28,20},{32,56},... | collective-permute-start | bytes 1769480 | tf_op jit(solution)/shard_map/ppermute | solution.py:36
  109.7 24.8 %collective-permute-start.14 = (bf16[384,768]{1,0:T(8,128)(2,1)S(1)}, bf16[384,768]{1,0:T(8,128)(2,1)S(1)}, u32[]{:S(2)}, u32[]{:S(2)}) collective-permute-start(bf16[384,768]{1,0:T(8,128)(2,1)S(1)} %get-tuple-element.41), channel_id=1, source_target_pairs={{0,16},{4,20},{8,24},{12,28},{16,0},{20,4},{24,8},{28,12},{32,48},... | collective-permute-start | bytes 1769480 | tf_op jit(solution)/shard_map/ppermute | solution.py:36
  111.5 22.9 %collective-permute-start.19 = (bf16[384,768]{1,0:T(8,128)(2,1)S(1)}, bf16[384,768]{1,0:T(8,128)(2,1)S(1)}, u32[]{:S(2)}, u32[]{:S(2)}) collective-permute-start(bf16[384,768]{1,0:T(8,128)(2,1)S(1)} %get-tuple-element.47), channel_id=1, source_target_pairs={{0,32},{4,36},{8,40},{12,44},{16,48},{20,52},{24,56},{28,60},{32,6... | collective-permute-start | bytes 1769480 | tf_op jit(solution)/shard_map/ppermute | solution.py:43
  121.2 13.3 %collective-permute-start.20 = (bf16[384,768]{1,0:T(8,128)(2,1)S(1)}, bf16[384,768]{1,0:T(8,128)(2,1)S(1)}, u32[]{:S(2)}, u32[]{:S(2)}) collective-permute-start(bf16[384,768]{1,0:T(8,128)(2,1)S(1)} %get-tuple-element.48), channel_id=1, source_target_pairs={{0,96},{4,100},{8,104},{12,108},{16,112},{20,116},{24,120},{28,124... | collective-permute-start | bytes 1769480 | tf_op jit(solution)/shard_map/ppermute | solution.py:43
  122.4 20.7 %collective-permute-start.21 = (bf16[384,768]{1,0:T(8,128)(2,1)S(1)}, bf16[384,768]{1,0:T(8,128)(2,1)S(1)}, u32[]{:S(2)}, u32[]{:S(2)}) collective-permute-start(bf16[384,768]{1,0:T(8,128)(2,1)S(1)} %get-tuple-element.49), channel_id=1, source_target_pairs={{0,64},{4,68},{8,72},{12,76},{16,80},{20,84},{24,88},{28,92},{32,9... | collective-permute-start | bytes 1769480 | tf_op jit(solution)/shard_map/ppermute | solution.py:43
  123.9 19.3 %collective-permute-start.18 = (bf16[384,768]{1,0:T(8,128)(2,1)S(1)}, bf16[384,768]{1,0:T(8,128)(2,1)S(1)}, u32[]{:S(2)}, u32[]{:S(2)}) collective-permute-start(bf16[384,768]{1,0:T(8,128)(2,1)S(1)} %add_convert_fusion.1), channel_id=1, source_target_pairs={{0,2},{1,3},{2,0},{3,1},{4,6},{5,7},{6,4},{7,5},{8,10},{9,11},{10,... | collective-permute-start | bytes 1769480 | tf_op jit(solution)/shard_map/ppermute | solution.py:47
  134.5 14.9 %collective-permute-start.25 = (bf16[384,768]{1,0:T(8,128)(2,1)S(1)}, bf16[384,768]{1,0:T(8,128)(2,1)S(1)}, u32[]{:S(2)}, u32[]{:S(2)}) collective-permute-start(bf16[384,768]{1,0:T(8,128)(2,1)S(1)} %add_convert_fusion), channel_id=1, source_target_pairs={{0,2},{1,3},{2,0},{3,1},{4,6},{5,7},{6,4},{7,5},{8,10},{9,11},{10,... | collective-permute-start | bytes 1769480 | tf_op jit(solution)/shard_map/ppermute | solution.py:47
  150.1 5.6 %collective-permute-start.26 = (bf16[96,768]{1,0:T(8,128)(2,1)S(1)}, bf16[96,768]{1,0:T(8,128)(2,1)S(1)}, u32[]{:S(2)}, u32[]{:S(2)}) collective-permute-start(bf16[96,768]{1,0:T(8,128)(2,1)S(1)} %get-tuple-element.55), channel_id=1, source_target_pairs={{0,32},{4,36},{8,40},{12,44},{16,48},{20,52},{24,56},{28,60},{32,6... | collective-permute-start | bytes 442376 | tf_op jit(solution)/shard_map/ppermute | solution.py:43
  150.2 8.9 %collective-permute-start.27 = (bf16[96,768]{1,0:T(8,128)(2,1)S(1)}, bf16[96,768]{1,0:T(8,128)(2,1)S(1)}, u32[]{:S(2)}, u32[]{:S(2)}) collective-permute-start(bf16[96,768]{1,0:T(8,128)(2,1)S(1)} %get-tuple-element.56), channel_id=1, source_target_pairs={{0,96},{4,100},{8,104},{12,108},{16,112},{20,116},{24,120},{28,124... | collective-permute-start | bytes 442376 | tf_op jit(solution)/shard_map/ppermute | solution.py:43
  152.9 6.2 %collective-permute-start.28 = (bf16[96,768]{1,0:T(8,128)(2,1)S(1)}, bf16[96,768]{1,0:T(8,128)(2,1)S(1)}, u32[]{:S(2)}, u32[]{:S(2)}) collective-permute-start(bf16[96,768]{1,0:T(8,128)(2,1)S(1)} %get-tuple-element.57), channel_id=1, source_target_pairs={{0,64},{4,68},{8,72},{12,76},{16,80},{20,84},{24,88},{28,92},{32,9... | collective-permute-start | bytes 442376 | tf_op jit(solution)/shard_map/ppermute | solution.py:43
  152.9 6.3 %collective-permute-start.29 = (bf16[96,768]{1,0:T(8,128)(2,1)S(1)}, bf16[96,768]{1,0:T(8,128)(2,1)S(1)}, u32[]{:S(2)}, u32[]{:S(2)}) collective-permute-start(bf16[96,768]{1,0:T(8,128)(2,1)S(1)} %get-tuple-element.59), channel_id=1, source_target_pairs={{0,8},{4,12},{8,16},{12,20},{16,24},{20,28},{24,0},{28,4},{32,40},... | collective-permute-start | bytes 442376 | tf_op jit(solution)/shard_map/ppermute | solution.py:36
  155.4 4.0 %collective-permute-start.30 = (bf16[96,768]{1,0:T(8,128)(2,1)S(1)}, bf16[96,768]{1,0:T(8,128)(2,1)S(1)}, u32[]{:S(2)}, u32[]{:S(2)}) collective-permute-start(bf16[96,768]{1,0:T(8,128)(2,1)S(1)} %get-tuple-element.60), channel_id=1, source_target_pairs={{0,24},{4,28},{8,0},{12,4},{16,8},{20,12},{24,16},{28,20},{32,56},... | collective-permute-start | bytes 442376 | tf_op jit(solution)/shard_map/ppermute | solution.py:36
  155.7 5.9 %collective-permute-start.31 = (bf16[96,768]{1,0:T(8,128)(2,1)S(1)}, bf16[96,768]{1,0:T(8,128)(2,1)S(1)}, u32[]{:S(2)}, u32[]{:S(2)}) collective-permute-start(bf16[96,768]{1,0:T(8,128)(2,1)S(1)} %get-tuple-element.61), channel_id=1, source_target_pairs={{0,16},{4,20},{8,24},{12,28},{16,0},{20,4},{24,8},{28,12},{32,48},... | collective-permute-start | bytes 442376 | tf_op jit(solution)/shard_map/ppermute | solution.py:36
  161.7 11.6 %collective-permute-start.32 = (f32[48,1536]{1,0:T(8,128)S(1)}, f32[48,1536]{1,0:T(8,128)S(1)}, u32[]{:S(2)}, u32[]{:S(2)}) collective-permute-start(f32[48,1536]{1,0:T(8,128)S(1)} %pad_maximum_fusion), channel_id=1, source_target_pairs={{0,4},{4,0},{8,12},{12,8},{16,20},{20,16},{24,28},{28,24},{32,36},... | collective-permute-start | bytes 884744 | tf_op jit(solution)/shard_map/ppermute | solution.py:52
  (8 other events, 56.0 us)

commit v2 on v1

v2 whole, which is shorter than its diff:
```python
import functools

import jax
import jax.numpy as jnp
from jax import lax
from jax.experimental import pallas as pl
from jax.experimental.pallas import tpu as pltpu
from jax.sharding import PartitionSpec as P

TAPS = 31
BASES = 3
TILE = 512
PATCH_PIX = 1536
STRIP = 48
LANES = 128
ROWS = 8
SLAB = 384
BF16 = jnp.bfloat16
F32 = jnp.float32


def visit_of(y, x, c):
    return (y * 4 + x) * 2 + c


def chips():
    return [(y, x) for y in range(4) for x in range(4)]


def turn(value, step, second):
    pairs = []
    for y, x in chips():
        for c in range(2):
            along_y = (c == 1) != second
            target = visit_of((y + step) % 4, x, c) if along_y else visit_of(y, (x + step) % 4, c)
            pairs.append((visit_of(y, x, c), target))
    return lax.ppermute(value, "visit", pairs)


def across_z(value, step):
    return lax.ppermute(value, "patch", [(z, (z + step) % 4) for z in range(4)])


def across_core(value):
    pairs = [(visit_of(y, x, c), visit_of(y, x, 1 - c)) for y, x in chips() for c in range(2)]
    return lax.ppermute(value, "visit", pairs)


def across_both(value, step):
    pairs = [
        (visit_of(y, x, c) * 4 + z, visit_of(y, x, 1 - c) * 4 + (z + step) % 4)
        for y, x in chips()
        for c in range(2)
        for z in range(4)
    ]
    return lax.ppermute(value, ("visit", "patch"), pairs)


def info_kernel(patches, corners, info):
    for entry in range(8):
        tile, which = entry // 2, entry % 2
        info[0, entry] = patches[which, tile]
        info[0, 8 + 2 * entry] = corners[which, 0, tile]
        info[0, 9 + 2 * entry] = corners[which, 1, tile]


def pack_info(patches, corners):
    return pl.pallas_call(
        info_kernel,
        in_specs=[pl.BlockSpec(memory_space=pltpu.SMEM)] * 2,
        out_specs=pl.BlockSpec(memory_space=pltpu.SMEM),
        out_shape=jax.ShapeDtypeStruct((1, LANES), jnp.int32),
    )(patches, corners)


def match_kernel(
    place, patches, taps, coeffs, image, variance, stays, plus, minus, swaps, swap_plus, swap_minus,
    across, down, lanes, factors, numer, weight, sems, wsems,
):
    tile = pl.program_id(0)
    core, z = place[0, 2], place[0, 3]

    @pl.when(tile == 0)
    def _():
        lanes[...] = jnp.zeros_like(lanes)
        for basis in range(BASES):
            factors[basis, 0:4, 0:3] = coeffs[basis].astype(F32)
            for axis in range(2):
                lanes[2 * basis + axis : 2 * basis + axis + 1, 0:TAPS] = taps[basis, axis : axis + 1, :].astype(F32)
        for basis in range(BASES):
            for axis in range(2):
                row = jnp.broadcast_to(lanes[2 * basis + axis : 2 * basis + axis + 1, :], (LANES, 3 * LANES))
                band = pltpu.roll(row, LANES - TAPS // 2, axis=1, stride=1, stride_axis=0)
                if axis == 1:
                    band = band.T
                band = band.astype(BF16)
                table = across if axis == 1 else down
                table[basis] = jnp.zeros((TILE, TILE), BF16)
                for block in range(TILE // LANES):
                    first = (block - 1) * LANES
                    low, high = max(first, 0), min(first + 3 * LANES, TILE)
                    span = slice(block * LANES, (block + 1) * LANES)
                    if axis == 1:
                        table[basis, low:high, span] = band[low - first : high - first, :]
                    else:
                        table[basis, span, low:high] = band[:, low - first : high - first]

    rows = lax.broadcasted_iota(jnp.int32, (TILE, 1), 0).astype(F32)
    columns = lax.broadcasted_iota(jnp.int32, (1, TILE), 1).astype(F32)
    rows = (rows - (TILE - 1) / 2.0) / (TILE / 2.0)
    columns = (columns - (TILE - 1) / 2.0) / (TILE / 2.0)
    total = jnp.zeros((TILE, TILE), F32)
    for basis in range(BASES):
        middle = jnp.dot(image[0], across[basis], preferred_element_type=F32).astype(BF16)
        smoothed = jnp.dot(down[basis], middle, preferred_element_type=F32)
        c0, c1, c2 = (factors[basis, pl.ds(tile, 1), k : k + 1] for k in range(3))
        total += ((c0 + c1 * columns) + c2 * rows) * smoothed
    inverse = 1.0 / variance[0].astype(F32)
    numer[tile] = (inverse * total).astype(BF16)
    weight[tile] = inverse.astype(BF16)

    def each(index, act):
        for which in range(2):
            patch = patches[which, index]
            rank = jnp.int32(0)
            for other in range(8):
                before = (2 * index + which > other) & (patches[other % 2, other // 2] == patch)
                rank += jnp.where(before, 1, 0)
            rank = jnp.minimum(rank, 1)
            towards = lax.rem(patch - z + 4, 4)
            held, sent = numer.at[index], weight.at[index]
            sem, wsem = sems.at[index, which], wsems.at[index, which]
            for wanted, keep, give in (
                (0, stays.at[0], swaps.at[0]),
                (1, plus, swap_plus),
                (2, stays.at[1], swaps.at[1]),
                (3, minus, swap_minus),
            ):
                for own_core in range(2):

                    @pl.when((towards == wanted) & (core == own_core))
                    def _():
                        act(pltpu.make_async_copy(held, (give if own_core else keep).at[rank], sem))
                        act(pltpu.make_async_copy(sent, (keep if own_core else give).at[rank], wsem))

    each(tile, lambda copy: copy.start())

    @pl.when(tile == 3)
    def _():
        for index in range(4):
            each(index, lambda copy: copy.wait())


def match_tiles(place, patches, taps, coeffs, images, variances):
    pair = jax.ShapeDtypeStruct((2, TILE, TILE), BF16)
    quad = jax.ShapeDtypeStruct((2, 2, TILE, TILE), BF16)
    return pl.pallas_call(
        match_kernel,
        grid=(4,),
        in_specs=[
            pl.BlockSpec(memory_space=pltpu.SMEM),
            pl.BlockSpec(memory_space=pltpu.SMEM),
            pl.BlockSpec((BASES, 2, TAPS), lambda t: (0, 0, 0)),
            pl.BlockSpec((BASES, 4, 3), lambda t: (0, 0, 0)),
            pl.BlockSpec((1, TILE, TILE), lambda t: (t, 0, 0)),
            pl.BlockSpec((1, TILE, TILE), lambda t: (t, 0, 0)),
        ],
        out_specs=[pl.BlockSpec(memory_space=pl.ANY)] * 6,
        out_shape=[quad, pair, pair, quad, pair, pair],
        scratch_shapes=[
            pltpu.VMEM((BASES, TILE, TILE), BF16),
            pltpu.VMEM((BASES, TILE, TILE), BF16),
            pltpu.VMEM((8, 3 * LANES), F32),
            pltpu.VMEM((BASES, 8, LANES), F32),
            pltpu.VMEM((4, TILE, TILE), BF16),
            pltpu.VMEM((4, TILE, TILE), BF16),
            pltpu.SemaphoreType.DMA((4, 2)),
            pltpu.SemaphoreType.DMA((4, 2)),
        ],
        compiler_params=pltpu.CompilerParams(vmem_limit_bytes=40 << 20),
        cost_estimate=pl.CostEstimate(flops=6 << 30, bytes_accessed=12 << 20, transcendentals=0),
    )(place, patches, taps, coeffs, images, variances)


def frame_kernel(far, sources, place, mine, other, *refs):
    stacks, outs, (frame, held, packed, sems, out_sems) = refs[:sources], refs[sources : sources + 4], refs[sources + 4 :]
    y, x, core, z = (place[0, k] for k in range(4))
    patch = lax.rem(z + 2 * far, 4)

    for number in range(2 * sources):
        source, slot = number // 2, number % 2
        stack = stacks[source].at[far, slot] if source < 2 else stacks[source].at[slot]
        pltpu.make_async_copy(stack, held.at[number], sems.at[number]).start()
    frame[...] = jnp.zeros_like(frame)
    apart = lax.broadcasted_iota(jnp.int32, (2 * LANES, LANES), 1) - lax.broadcasted_iota(
        jnp.int32, (2 * LANES, LANES), 0
    )
    inner = lax.broadcasted_iota(jnp.int32, (TILE // ROWS + 1, ROWS, LANES), 1)
    nothing = jnp.zeros((1, ROWS, LANES), F32)

    def add(number, carry):
        source, slot = lax.div(number, 2), lax.rem(number, 2)
        sibling = lax.rem(source, 2) == 1
        from_z = lax.rem(z + jnp.where(source < 2, 4, jnp.where(source < 4, 3, 5)), 4)

        def look(k):
            return jnp.where(sibling, other[from_z, k], mine[from_z, k])

        entry = jnp.int32(0)
        for k in range(8):
            named = look(k) == patch
            entry = jnp.where(named & ((slot == 1) | (entry == 0)), k + 1, entry)
        entry = jnp.maximum(entry - 1, 0)
        top, left = look(8 + 2 * entry), look(9 + 2 * entry)
        first = jnp.minimum(lax.div(left, LANES) * LANES, PATCH_PIX - TILE - LANES)
        group, lead = lax.div(top, ROWS), lax.rem(top, ROWS)
        shift = jnp.where(apart == left - first - LANES, F32(1.0), F32(0.0)).astype(BF16)
        pltpu.make_async_copy(stacks[0].at[far, 0], held.at[number], sems.at[number]).wait()
        for block in range(5):
            low, high = max(block - 1, 0) * LANES, min(block + 1, 4) * LANES
            moved = jnp.dot(
                held[number, :, low:high],
                shift[LANES * (block == 0) : 2 * LANES - LANES * (block == 4)],
                preferred_element_type=F32,
            )
            turned = pltpu.roll(moved.reshape(TILE // ROWS, ROWS, LANES), lead, axis=1)
            lower = jnp.concatenate([turned, nothing], axis=0)
            upper = jnp.concatenate([nothing, turned], axis=0)
            where = (
                pl.ds(group, TILE // ROWS + 1),
                slice(None),
                pl.ds(pl.multiple_of(first + block * LANES, LANES), LANES),
            )
            frame[where] += jnp.where(inner >= lead, lower, upper)
        return carry

    lax.fori_loop(0, 2 * sources, add, 0)

    copies = []
    for out in range(4):
        for part in range(4):
            dx, dy = jnp.where(core == 0, out, part), jnp.where(core == 0, part, out)
            for dc in range(2):
                row = 8 * STRIP * lax.rem(y + dy, 4) + 2 * STRIP * lax.rem(x + dx, 4) + STRIP * lax.rem(core + dc, 2)
                strip = frame[pl.ds(lax.div(row, ROWS), STRIP // ROWS)]
                at = (2 * part + dc) * STRIP
                packed[out, at : at + STRIP, :] = strip.reshape(STRIP, PATCH_PIX).astype(BF16)
        copies.append(pltpu.make_async_copy(packed.at[out], outs[out], out_sems.at[out]))
        copies[-1].start()
    for copy in copies:
        copy.wait()


def build_frame(far, place, mine, other, stacks):
    sources = len(stacks)
    out = jax.ShapeDtypeStruct((SLAB, PATCH_PIX), BF16)
    return pl.pallas_call(
        functools.partial(frame_kernel, far, sources),
        in_specs=[pl.BlockSpec(memory_space=pltpu.SMEM)] * 3 + [pl.BlockSpec(memory_space=pl.ANY)] * sources,
        out_specs=[pl.BlockSpec(memory_space=pl.ANY)] * 4,
        out_shape=[out] * 4,
        scratch_shapes=[
            pltpu.VMEM((PATCH_PIX // ROWS + 1, ROWS, PATCH_PIX), F32),
            pltpu.VMEM((2 * sources, TILE, TILE), BF16),
            pltpu.VMEM((4, SLAB, PATCH_PIX), BF16),
            pltpu.SemaphoreType.DMA((2 * sources,)),
            pltpu.SemaphoreType.DMA((4,)),
        ],
        compiler_params=pltpu.CompilerParams(vmem_limit_bytes=40 << 20),
        cost_estimate=pl.CostEstimate(flops=sources << 30, bytes_accessed=(5 + sources) << 20, transcendentals=0),
    )(place, mine, other, *stacks)


def sum_kernel(count, *refs):
    for part in range(4):
        rows = slice(part * 2 * STRIP, (part + 1) * 2 * STRIP)
        total = refs[0][rows].astype(F32)
        for ref in refs[1:count]:
            total += ref[rows].astype(F32)
        refs[count + part][...] = total.astype(BF16)


def sum_slabs(slabs):
    count = len(slabs)
    out = jax.ShapeDtypeStruct((2 * STRIP, PATCH_PIX), BF16)
    return pl.pallas_call(
        functools.partial(sum_kernel, count),
        out_shape=[out] * 4,
        compiler_params=pltpu.CompilerParams(vmem_limit_bytes=40 << 20),
        cost_estimate=pl.CostEstimate(flops=3 << 20, bytes_accessed=(count + 1) << 20, transcendentals=0),
    )(*slabs)


def spread(pieces, second):
    return [pieces[0]] + [turn(pieces[step], step, second) for step in (1, 3, 2)]


def add_up(pieces):
    return sum(piece.astype(F32) for piece in pieces)


def body(images, variances, kernels, coefficients, intersections, offsets):
    visit, z = lax.axis_index("visit"), lax.axis_index("patch")
    core = lax.rem(visit, 2)
    place = jnp.stack([lax.div(visit, 8), lax.rem(lax.div(visit, 2), 4), core, z]).astype(jnp.int32).reshape(1, 4)
    patches = jnp.transpose(intersections[0])
    mine = lax.all_gather(pack_info(patches, jnp.transpose(offsets[0], (1, 2, 0))), "patch", axis=0, tiled=True)

    stays, plus, minus, swaps, swap_plus, swap_minus = match_tiles(
        place,
        patches,
        jnp.transpose(kernels[0], (1, 0, 2)),
        jnp.transpose(coefficients[0], (1, 0, 2)),
        images[0],
        variances[0],
    )
    swapped = across_core(swaps)
    other = across_core(mine)
    arrived = [across_z(plus, 1), across_both(swap_plus, 1), across_z(minus, 3), across_both(swap_minus, 3)]

    opposite = build_frame(1, place, mine, other, [stays, swapped])
    passed = across_z(add_up(spread(opposite, False)).astype(BF16), 2)
    own = build_frame(0, place, mine, other, [stays, swapped] + arrived)
    pieces = sum_slabs(spread(own, False) + [passed])
    rows = add_up(spread(pieces, True))
    keep, got = rows[:STRIP], across_core(rows[STRIP:])
    numer = jnp.where(core == 0, keep, got)
    weight = jnp.where(core == 0, got, keep)
    return (numer / (weight + 1.0))[None], weight[None]


def solution(mesh):
    return jax.shard_map(
        body,
        mesh=mesh,
        in_specs=(
            P("visit", "patch", None, None),
            P("visit", "patch", None, None),
            P("visit", None, None, None),
            P("visit", "patch", None, None),
            P("visit", "patch", None),
            P("visit", "patch", None, None),
        ),
        out_specs=(P("patch", "visit", None), P("patch", "visit", None)),
        check_vma=False,
    )
```

time: 174 us -> 183 us (1.052)
  blocking collectives: 0 us -> 47.5 us
  starting transfers between devices: 56.3 us -> 22.8 us
  waiting for transfers between devices: 76.6 us -> 71.7 us
    all_gather x0 -> x1, blocking collectives: none -> 47.5 us  [body(): lax.all_gather(pack_info(patches, jnp.transpose(offsets[0], (1, 2, 0))),...]
    ppermute x26 -> x11, starting transfers between devices: 39.7 us -> 16.7 us  [the longest x9 14.6 us: turn(): return lax.ppermute(value, 'visit', pairs)]
    ppermute x3, starting transfers between devices: 15.2 us -> 4.21 us  [across_core(): return lax.ppermute(value, 'visit', pairs)]
    ppermute x4 -> x3, waiting for transfers between devices: 23.2 us -> 15.1 us  [across_z(): return lax.ppermute(value, 'patch', [(z, (z + step) % 4) for z in range(4)])]
    ppermute x26 -> x11, waiting for transfers between devices: 51.3 us -> 54.7 us  [the longest x9 32.1 us: turn(): return lax.ppermute(value, 'visit', pairs)]
    unnamed x18 -> x20, local copies, waits for them, and re-layouts: 8.3 us -> 10.2 us
  transfers between devices with their start and end apart: 33 -> 17, of which waited for: 14 -> 11; matrix products, arithmetic and copies ran while one was open for 0% -> 0% of each run, Pallas kernels for 10% -> 9%
where the time goes in v2:
time: 183 us
  waiting for transfers between devices  71.7 us (39%)
  blocking collectives  47.5 us (26%)
  Pallas kernels  28.2 us (15%)
  starting transfers between devices  22.8 us (12%)
  local copies, waits for them, and re-layouts  10.2 us (6%)
    all_gather x1, blocking collectives, body(): lax.all_gather(pack_info(patches, jnp.transpose(offsets[0], (1, 2, 0))),...  47.5 us
    ppermute x9, waiting for transfers between devices, turn(): return lax.ppermute(value, 'visit', pairs)  32.1 us
    ppermute x2, waiting for transfers between devices, across_both(): return lax.ppermute(value, ('visit', 'patch'), pairs)  22.6 us
    ppermute x3, waiting for transfers between devices, across_z(): return lax.ppermute(value, 'patch', [(z, (z + step) % 4) for z in range(4)])  15.1 us
    pallas_call x2, Pallas kernels, build_frame(): pl.pallas_call(functools.partial(frame_kernel, far, sources), in_specs=[p...  15 us
    ppermute x9, starting transfers between devices, turn(): return lax.ppermute(value, 'visit', pairs)  14.6 us
    pallas_call x1, Pallas kernels, match_tiles(): pl.pallas_call(match_kernel, grid=(4,), in_specs=[pl.BlockSpec(memory_spa...  11.2 us
    unnamed x20, local copies, waits for them, and re-layouts  10.2 us
  transfers between devices with their start and end apart: 17, of which 11 were waited for; matrix products, arithmetic and copies ran while one was open for 0% of the time, Pallas kernels for 9%

profile of v2, /device:TPU:1, one launch (start us, length us, event | category | flops | bytes accessed | tf_op | source)
XLA Modules:
  0.0 182.9 jit_solution(15920704371725631598)
XLA Ops:
  1.4 1.6 copy-done.1
  3.0 1.6 copy-done.2
  6.0 11.2 %shard_map.78 = (bf16[2,2,512,512]{3,2,1,0:T(8,128)(2,1)S(1)}, bf16[2,512,512]{2,1,0:T(8,128)(2,1)}, bf16[2,512,512]{2,1,0:T(8,128)(2,1)S(1)}, bf16[2,2,512,512]...) custom-call(s32[1,4]{1,0:T(1,128)S(1)} %add_bitcast_fusion.place, ...), custom_call_target="tpu_custom_call" | custom-call | flops 6442450944 | bytes 12582912 | tf_op jit(solution)/shard_map/pallas_call | solution.py:157
  19.2 1.3 copy-done.7
  20.5 1.6 collective-permute-start.1
  22.1 1.7 collective-permute-start.2
  23.9 1.7 collective-permute-start.3
  25.5 1.2 shard_map.77
  26.8 47.5 %all-gather = s32[4,1,128]{2,1,0:T(1,128)S(1)} all-gather(s32[1,1,128]{2,1,0:T(1,128)} %bitcast.35), channel_id=1, replica_groups=mesh['visit'=32,'patch'=4] {'patch'}, dimensions={0}, use_global_device_ids=true | all-gather | bytes 2560 | tf_op jit(solution)/shard_map/all_gather | solution.py:307
  74.3 1.5 collective-permute-start
  77.1 1.6 copy-done.8
  78.7 5.2 %shard_map.80 = (bf16[384,1536]{1,0:T(8,128)(2,1)S(1)}, bf16[384,1536]{1,0:T(8,128)(2,1)S(1)}, bf16[384,1536]{1,0:T(8,128)(2,1)S(1)}, bf16[384,1536]{1,0:T(8,128)(2,1)S(1)}) custom-call(s32[1,4]{1,0:T(1,128)S(1)} %add_bitcast_fusion.place, s32[4,128]{1,0:T(4,128)S(1)} %bitcast.27, s32[4,128]{1,0:T(4,128)S(1)} %collective-permute-done.other, ...), custom_call_target="tpu_custom_call" | custom-call | flops 2147483648 | bytes 7340032 | tf_op jit(solution)/shard_map/pallas_call | solution.py:257
  83.8 1.4 collective-permute-start.9
  85.2 1.6 collective-permute-start.10
  86.8 1.4 collective-permute-start.11
  88.3 12.6 %collective-permute-done.4.refs_4_ = bf16[2,512,512]{2,1,0:T(8,128)(2,1)S(1)} collective-permute-done((bf16[2,512,512]{2,1,0:T(8,128)(2,1)}, bf16[2,512,512]{2,1,0:T(8,128)(2,1)S(1)}, u32[]{:S(2)}, u32[]{:S(2)}) %collective-permute-start.4) | collective-permute-done | bytes 1048608 | tf_op jit(solution)/shard_map/ppermute | solution.py:41
  100.9 22.6 %collective-permute-done.5.refs_5_ = bf16[2,512,512]{2,1,0:T(8,128)(2,1)S(1)} collective-permute-done((bf16[2,512,512]{2,1,0:T(8,128)(2,1)}, bf16[2,512,512]{2,1,0:T(8,128)(2,1)S(1)}, u32[]{:S(2)}, u32[]{:S(2)}) %collective-permute-start.5) | collective-permute-done | bytes 1048608 | tf_op jit(solution)/shard_map/ppermute | solution.py:56
  123.4 9.8 %shard_map.79 = (bf16[384,1536]{1,0:T(8,128)(2,1)S(1)}, bf16[384,1536]{1,0:T(8,128)(2,1)S(1)}, bf16[384,1536]{1,0:T(8,128)(2,1)S(1)}, bf16[384,1536]{1,0:T(8,128)(2,1)S(1)}) custom-call(s32[1,4]{1,0:T(1,128)S(1)} %add_bitcast_fusion.place, s32[4,128]{1,0:T(4,128)S(1)} %bitcast.28, s32[4,128]{1,0:T(4,128)S(1)} %collective-permute-done.other, ...), custom_call_target="tpu_custom_call" | custom-call | flops 6442450944 | bytes 11534336 | tf_op jit(solution)/shard_map/pallas_call | solution.py:257
  133.3 1.4 collective-permute-start.6
  134.7 1.5 collective-permute-start.7
  136.2 1.6 collective-permute-start.8
  138.5 11.5 %collective-permute-done.6.refs_1_ = bf16[384,1536]{1,0:T(8,128)(2,1)S(1)} collective-permute-done((bf16[384,1536]{1,0:T(8,128)(2,1)S(1)}, bf16[384,1536]{1,0:T(8,128)(2,1)S(1)}, u32[]{:S(2)}, u32[]{:S(2)}) %collective-permute-start.6) | collective-permute-done | bytes 1179680 | tf_op jit(solution)/shard_map/ppermute | solution.py:37
  150.0 12.0 %collective-permute-done.7.refs_2_ = bf16[384,1536]{1,0:T(8,128)(2,1)S(1)} collective-permute-done((bf16[384,1536]{1,0:T(8,128)(2,1)S(1)}, bf16[384,1536]{1,0:T(8,128)(2,1)S(1)}, u32[]{:S(2)}, u32[]{:S(2)}) %collective-permute-start.7) | collective-permute-done | bytes 1179680 | tf_op jit(solution)/shard_map/ppermute | solution.py:37
  162.0 1.8 %collective-permute-done.8.refs_3_ = bf16[384,1536]{1,0:T(8,128)(2,1)S(1)} collective-permute-done((bf16[384,1536]{1,0:T(8,128)(2,1)S(1)}, bf16[384,1536]{1,0:T(8,128)(2,1)S(1)}, u32[]{:S(2)}, u32[]{:S(2)}) %collective-permute-start.8) | collective-permute-done | bytes 1179680 | tf_op jit(solution)/shard_map/ppermute | solution.py:37
  163.8 2.5 %collective-permute-done.12.refs_4_ = bf16[384,1536]{1,0:T(8,128)(2,1)S(1)} collective-permute-done((bf16[384,1536]{1,0:T(8,128)(2,1)S(1)}, bf16[384,1536]{1,0:T(8,128)(2,1)S(1)}, u32[]{:S(2)}, u32[]{:S(2)}) %collective-permute-start.12) | collective-permute-done | bytes 1179680 | tf_op jit(solution)/shard_map/ppermute | solution.py:41
  167.1 2.4 %collective-permute-start.13 = (bf16[96,1536]{1,0:T(8,128)(2,1)S(1)}, bf16[96,1536]{1,0:T(8,128)(2,1)S(1)}, u32[]{:S(2)}, u32[]{:S(2)}) collective-permute-start(bf16[96,1536]{1,0:T(8,128)(2,1)S(1)} %get-tuple-element.35), channel_id=1, source_target_pairs={{0,32},{4,12},{8,40},{12,20},{16,48},{20,28},{24,56},{28,4},{32,64... | collective-permute-start | bytes 884744 | tf_op jit(solution)/shard_map/ppermute | solution.py:37
  169.5 1.5 collective-permute-start.14
  170.9 1.9 %collective-permute-start.15 = (bf16[96,1536]{1,0:T(8,128)(2,1)S(1)}, bf16[96,1536]{1,0:T(8,128)(2,1)S(1)}, u32[]{:S(2)}, u32[]{:S(2)}) collective-permute-start(bf16[96,1536]{1,0:T(8,128)(2,1)S(1)} %get-tuple-element.37), channel_id=1, source_target_pairs={{0,64},{4,20},{8,72},{12,28},{16,80},{20,4},{24,88},{28,12},{32,96... | collective-permute-start | bytes 884744 | tf_op jit(solution)/shard_map/ppermute | solution.py:37
  172.8 2.5 %collective-permute-done.13 = bf16[96,1536]{1,0:T(8,128)(2,1)S(1)} collective-permute-done((bf16[96,1536]{1,0:T(8,128)(2,1)S(1)}, bf16[96,1536]{1,0:T(8,128)(2,1)S(1)}, u32[]{:S(2)}, u32[]{:S(2)}) %collective-permute-start.13) | collective-permute-done | bytes 294944 | tf_op jit(solution)/shard_map/ppermute | solution.py:37
  175.4 4.2 %collective-permute-done.15 = bf16[96,1536]{1,0:T(8,128)(2,1)S(1)} collective-permute-done((bf16[96,1536]{1,0:T(8,128)(2,1)S(1)}, bf16[96,1536]{1,0:T(8,128)(2,1)S(1)}, u32[]{:S(2)}, u32[]{:S(2)}) %collective-permute-start.15) | collective-permute-done | bytes 294944 | tf_op jit(solution)/shard_map/ppermute | solution.py:37
  179.8 1.1 collective-permute-start.16
  180.8 1.2 collective-permute-done.16
  (33 shorter events, 7.9 us)
Async XLA Ops:
  0.7 0.7 copy-start
  1.4 1.6 copy-start.1
  3.0 1.6 copy-start.2
  4.6 0.7 copy-start.5
  5.3 0.7 copy-start.6
  17.2 1.0 copy-start.3
  18.2 1.0 copy-start.4
  19.2 1.3 copy-start.7
  20.5 56.5 %collective-permute-start.1 = (bf16[2,2,512,512]{3,2,1,0:T(8,128)(2,1)}, bf16[2,2,512,512]{3,2,1,0:T(8,128)(2,1)S(1)}, u32[]{:S(2)}, u32[]{:S(2)}) collective-permute-start(bf16[2,2,512,512]{3,2,1,0:T(8,128)(2,1)} %get-tuple-element.21), channel_id=1, source_target_pairs={{0,4},{4,0},{8,12},{12,8},{16,20},{20,16},{24,28},{28,24},{32,36},... | collective-permute-start | bytes 6291464 | tf_op jit(solution)/shard_map/ppermute | solution.py:46
  22.1 63.0 %collective-permute-start.2 = (bf16[2,512,512]{2,1,0:T(8,128)(2,1)}, bf16[2,512,512]{2,1,0:T(8,128)(2,1)S(1)}, u32[]{:S(2)}, u32[]{:S(2)}) collective-permute-start(bf16[2,512,512]{2,1,0:T(8,128)(2,1)} %get-tuple-element.22), channel_id=1, source_target_pairs={{0,1},{1,2},{2,3},{3,0},{4,5},{5,6},{6,7},{7,4},{8,9},{9,10},{10,1... | collective-permute-start | bytes 3145736 | tf_op jit(solution)/shard_map/ppermute | solution.py:41
  23.9 63.0 %collective-permute-start.3 = (bf16[2,512,512]{2,1,0:T(8,128)(2,1)}, bf16[2,512,512]{2,1,0:T(8,128)(2,1)}, u32[]{:S(2)}, u32[]{:S(2)}) collective-permute-start(bf16[2,512,512]{2,1,0:T(8,128)(2,1)} %get-tuple-element.23), channel_id=1, source_target_pairs={{0,5},{1,6},{2,7},{3,4},{4,1},{5,2},{6,3},{7,0},{8,13},{9,14},{10,... | collective-permute-start | bytes 3145736 | tf_op jit(solution)/shard_map/ppermute | solution.py:56
  74.3 2.4 %collective-permute-start = (s32[4,128]{1,0:T(4,128)S(1)}, s32[4,128]{1,0:T(4,128)S(1)}, u32[]{:S(2)}, u32[]{:S(2)}) collective-permute-start(s32[4,128]{1,0:T(4,128)S(1)} %bitcast.26), channel_id=1, source_target_pairs={{0,4},{4,0},{8,12},{12,8},{16,20},{20,16},{24,28},{28,24},{32,36},... | collective-permute-start | bytes 6152 | tf_op jit(solution)/shard_map/ppermute | solution.py:46
  75.9 25.0 %collective-permute-start.4 = (bf16[2,512,512]{2,1,0:T(8,128)(2,1)}, bf16[2,512,512]{2,1,0:T(8,128)(2,1)S(1)}, u32[]{:S(2)}, u32[]{:S(2)}) collective-permute-start(bf16[2,512,512]{2,1,0:T(8,128)(2,1)} %copy-done.4), channel_id=1, source_target_pairs={{0,3},{1,0},{2,1},{3,2},{4,7},{5,4},{6,5},{7,6},{8,11},{9,8},{10,9... | collective-permute-start | bytes 3145736 | tf_op jit(solution)/shard_map/ppermute | solution.py:41
  76.7 46.7 %collective-permute-start.5 = (bf16[2,512,512]{2,1,0:T(8,128)(2,1)}, bf16[2,512,512]{2,1,0:T(8,128)(2,1)S(1)}, u32[]{:S(2)}, u32[]{:S(2)}) collective-permute-start(bf16[2,512,512]{2,1,0:T(8,128)(2,1)} %copy-done.3), channel_id=1, source_target_pairs={{0,7},{1,4},{2,5},{3,6},{4,3},{5,0},{6,1},{7,2},{8,15},{9,12},{10,... | collective-permute-start | bytes 3145736 | tf_op jit(solution)/shard_map/ppermute | solution.py:56
  77.1 1.6 copy-start.8
  78.7 44.8 %copy-start.9 = (bf16[2,2,512,512]{3,2,1,0:T(8,128)(2,1)S(1)}, bf16[2,2,512,512]{3,2,1,0:T(8,128)(2,1)}, u32[]{:S(2)}) copy-start(bf16[2,2,512,512]{3,2,1,0:T(8,128)(2,1)} %copy-done.7) | copy-start | bytes 6291460
  83.8 52.4 %collective-permute-start.9 = (bf16[384,1536]{1,0:T(8,128)(2,1)S(1)}, bf16[384,1536]{1,0:T(8,128)(2,1)S(1)}, u32[]{:S(2)}, u32[]{:S(2)}) collective-permute-start(bf16[384,1536]{1,0:T(8,128)(2,1)S(1)} %get-tuple-element.31), channel_id=1, source_target_pairs={{0,8},{4,36},{8,16},{12,44},{16,24},{20,52},{24,0},{28,60},{32,40}... | collective-permute-start | bytes 3538952 | tf_op jit(solution)/shard_map/ppermute | solution.py:37
  85.2 52.6 %collective-permute-start.10 = (bf16[384,1536]{1,0:T(8,128)(2,1)S(1)}, bf16[384,1536]{1,0:T(8,128)(2,1)S(1)}, u32[]{:S(2)}, u32[]{:S(2)}) collective-permute-start(bf16[384,1536]{1,0:T(8,128)(2,1)S(1)} %get-tuple-element.32), channel_id=1, source_target_pairs={{0,24},{4,100},{8,0},{12,108},{16,8},{20,116},{24,16},{28,124},{32... | collective-permute-start | bytes 3538952 | tf_op jit(solution)/shard_map/ppermute | solution.py:37
  86.8 50.9 %collective-permute-start.11 = (bf16[384,1536]{1,0:T(8,128)(2,1)S(1)}, bf16[384,1536]{1,0:T(8,128)(2,1)S(1)}, u32[]{:S(2)}, u32[]{:S(2)}) collective-permute-start(bf16[384,1536]{1,0:T(8,128)(2,1)S(1)} %get-tuple-element.33), channel_id=1, source_target_pairs={{0,16},{4,68},{8,24},{12,76},{16,0},{20,84},{24,8},{28,92},{32,48}... | collective-permute-start | bytes 3538952 | tf_op jit(solution)/shard_map/ppermute | solution.py:37
  133.3 16.7 %collective-permute-start.6 = (bf16[384,1536]{1,0:T(8,128)(2,1)S(1)}, bf16[384,1536]{1,0:T(8,128)(2,1)S(1)}, u32[]{:S(2)}, u32[]{:S(2)}) collective-permute-start(bf16[384,1536]{1,0:T(8,128)(2,1)S(1)} %get-tuple-element.27), channel_id=1, source_target_pairs={{0,8},{4,36},{8,16},{12,44},{16,24},{20,52},{24,0},{28,60},{32,40}... | collective-permute-start | bytes 3538952 | tf_op jit(solution)/shard_map/ppermute | solution.py:37
  134.7 27.3 %collective-permute-start.7 = (bf16[384,1536]{1,0:T(8,128)(2,1)S(1)}, bf16[384,1536]{1,0:T(8,128)(2,1)S(1)}, u32[]{:S(2)}, u32[]{:S(2)}) collective-permute-start(bf16[384,1536]{1,0:T(8,128)(2,1)S(1)} %get-tuple-element.28), channel_id=1, source_target_pairs={{0,24},{4,100},{8,0},{12,108},{16,8},{20,116},{24,16},{28,124},{32... | collective-permute-start | bytes 3538952 | tf_op jit(solution)/shard_map/ppermute | solution.py:37
  136.2 27.6 %collective-permute-start.8 = (bf16[384,1536]{1,0:T(8,128)(2,1)S(1)}, bf16[384,1536]{1,0:T(8,128)(2,1)S(1)}, u32[]{:S(2)}, u32[]{:S(2)}) collective-permute-start(bf16[384,1536]{1,0:T(8,128)(2,1)S(1)} %get-tuple-element.29), channel_id=1, source_target_pairs={{0,16},{4,68},{8,24},{12,76},{16,0},{20,84},{24,8},{28,92},{32,48}... | collective-permute-start | bytes 3538952 | tf_op jit(solution)/shard_map/ppermute | solution.py:37
  138.4 28.0 %collective-permute-start.12 = (bf16[384,1536]{1,0:T(8,128)(2,1)S(1)}, bf16[384,1536]{1,0:T(8,128)(2,1)S(1)}, u32[]{:S(2)}, u32[]{:S(2)}) collective-permute-start(bf16[384,1536]{1,0:T(8,128)(2,1)S(1)} %add_convert_fusion), channel_id=1, source_target_pairs={{0,2},{1,3},{2,0},{3,1},{4,6},{5,7},{6,4},{7,5},{8,10},{9,11},{10,... | collective-permute-start | bytes 3538952 | tf_op jit(solution)/shard_map/ppermute | solution.py:41
  167.1 8.2 %collective-permute-start.13 = (bf16[96,1536]{1,0:T(8,128)(2,1)S(1)}, bf16[96,1536]{1,0:T(8,128)(2,1)S(1)}, u32[]{:S(2)}, u32[]{:S(2)}) collective-permute-start(bf16[96,1536]{1,0:T(8,128)(2,1)S(1)} %get-tuple-element.35), channel_id=1, source_target_pairs={{0,32},{4,12},{8,40},{12,20},{16,48},{20,28},{24,56},{28,4},{32,64... | collective-permute-start | bytes 884744 | tf_op jit(solution)/shard_map/ppermute | solution.py:37
  169.5 5.9 %collective-permute-start.14 = (bf16[96,1536]{1,0:T(8,128)(2,1)S(1)}, bf16[96,1536]{1,0:T(8,128)(2,1)S(1)}, u32[]{:S(2)}, u32[]{:S(2)}) collective-permute-start(bf16[96,1536]{1,0:T(8,128)(2,1)S(1)} %get-tuple-element.36), channel_id=1, source_target_pairs={{0,96},{4,28},{8,104},{12,4},{16,112},{20,12},{24,120},{28,20},{32... | collective-permute-start | bytes 884744 | tf_op jit(solution)/shard_map/ppermute | solution.py:37
  170.9 8.7 %collective-permute-start.15 = (bf16[96,1536]{1,0:T(8,128)(2,1)S(1)}, bf16[96,1536]{1,0:T(8,128)(2,1)S(1)}, u32[]{:S(2)}, u32[]{:S(2)}) collective-permute-start(bf16[96,1536]{1,0:T(8,128)(2,1)S(1)} %get-tuple-element.37), channel_id=1, source_target_pairs={{0,64},{4,20},{8,72},{12,28},{16,80},{20,4},{24,88},{28,12},{32,96... | collective-permute-start | bytes 884744 | tf_op jit(solution)/shard_map/ppermute | solution.py:37
  179.8 2.3 %collective-permute-start.16 = (f32[48,1536]{1,0:T(8,128)S(1)}, f32[48,1536]{1,0:T(8,128)S(1)}, u32[]{:S(2)}, u32[]{:S(2)}) collective-permute-start(f32[48,1536]{1,0:T(8,128)S(1)} %slice.9), channel_id=1, source_target_pairs={{0,4},{4,0},{8,12},{12,8},{16,20},{20,16},{24,28},{28,24},{32,36},... | collective-permute-start | bytes 884744 | tf_op jit(solution)/shard_map/ppermute | solution.py:46

commit v3 on v2

--- a/solution.py
+++ b/solution.py
@@ -56,32 +56,34 @@
     return lax.ppermute(value, ("visit", "patch"), pairs)
 
 
-def info_kernel(patches, corners, info):
-    for entry in range(8):
-        tile, which = entry // 2, entry % 2
-        info[0, entry] = patches[which, tile]
-        info[0, 8 + 2 * entry] = corners[which, 0, tile]
-        info[0, 9 + 2 * entry] = corners[which, 1, tile]
-
-
-def pack_info(patches, corners):
-    return pl.pallas_call(
-        info_kernel,
-        in_specs=[pl.BlockSpec(memory_space=pltpu.SMEM)] * 2,
-        out_specs=pl.BlockSpec(memory_space=pltpu.SMEM),
-        out_shape=jax.ShapeDtypeStruct((1, LANES), jnp.int32),
-    )(patches, corners)
+def position():
+    visit = lax.axis_index("visit")
+    return lax.div(visit, 8), lax.rem(lax.div(visit, 2), 4), lax.rem(visit, 2), lax.axis_index("patch")
+
+
+def lane_values(shape, pairs, default):
+    lane = lax.broadcasted_iota(jnp.int32, shape, len(shape) - 1)
+    out = jnp.full(shape, default, F32)
+    for where, value in pairs:
+        out = jnp.where(lane == where, value, out)
+    return out
 
 
 def match_kernel(
-    place, patches, taps, coeffs, image, variance, stays, plus, minus, swaps, swap_plus, swap_minus,
-    across, down, lanes, factors, numer, weight, sems, wsems,
+    patches_in, corners_in, taps_in, coeffs_in, image, variance, stays, plus, minus, swaps, swap_plus, swap_minus,
+    patches, corners, taps, coeffs, across, down, lanes, factors, numer, weight, in_sems, sems, wsems,
 ):
     tile = pl.program_id(0)
-    core, z = place[0, 2], place[0, 3]
+    _, _, core, z = position()
 
     @pl.when(tile == 0)
     def _():
+        small = [(patches_in, patches), (corners_in, corners), (taps_in, taps), (coeffs_in, coeffs)]
+        copies = [pltpu.make_async_copy(a, b, in_sems.at[k]) for k, (a, b) in enumerate(small)]
+        for copy in copies:
+            copy.start()
+        for copy in copies:
+            copy.wait()
         lanes[...] = jnp.zeros_like(lanes)
         for basis in range(BASES):
             factors[basis, 0:4, 0:3] = coeffs[basis].astype(F32)
@@ -116,8 +118,20 @@
         c0, c1, c2 = (factors[basis, pl.ds(tile, 1), k : k + 1] for k in range(3))
         total += ((c0 + c1 * columns) + c2 * rows) * smoothed
     inverse = 1.0 / variance[0].astype(F32)
-    numer[tile] = (inverse * total).astype(BF16)
-    weight[tile] = inverse.astype(BF16)
+    numer[tile, 0:TILE] = (inverse * total).astype(BF16)
+    weight[tile, 0:TILE] = inverse.astype(BF16)
+    named, tops, lefts = [], [], []
+    for which in range(2):
+        patch = patches[which, tile].astype(F32)
+        named += [(8 * which, patch), (8 * which + 1, patch)]
+        for axis, parts in enumerate((tops, lefts)):
+            corner = corners[which, axis, tile]
+            fine = lax.rem(corner, 32)
+            parts += [(8 * which, (corner - fine).astype(F32)), (8 * which + 1, fine.astype(F32))]
+    for held in (numer, weight):
+        for part, pairs in enumerate((named, tops, lefts)):
+            note = lane_values((16, LANES), pairs, -1.0 if part == 0 else 0.0)
+            held[tile, TILE : TILE + 16, part * LANES : (part + 1) * LANES] = note.astype(BF16)
 
     def each(index, act):
         for which in range(2):
@@ -151,41 +165,46 @@
             each(index, lambda copy: copy.wait())
 
 
-def match_tiles(place, patches, taps, coeffs, images, variances):
-    pair = jax.ShapeDtypeStruct((2, TILE, TILE), BF16)
-    quad = jax.ShapeDtypeStruct((2, 2, TILE, TILE), BF16)
+def match_tiles(patches, corners, taps, coeffs, images, variances):
+    pair = jax.ShapeDtypeStruct((2, TILE + 16, TILE), BF16)
+    quad = jax.ShapeDtypeStruct((2, 2, TILE + 16, TILE), BF16)
     return pl.pallas_call(
         match_kernel,
         grid=(4,),
         in_specs=[
-            pl.BlockSpec(memory_space=pltpu.SMEM),
-            pl.BlockSpec(memory_space=pltpu.SMEM),
-            pl.BlockSpec((BASES, 2, TAPS), lambda t: (0, 0, 0)),
-            pl.BlockSpec((BASES, 4, 3), lambda t: (0, 0, 0)),
+            pl.BlockSpec(memory_space=pl.ANY),
+            pl.BlockSpec(memory_space=pl.ANY),
+            pl.BlockSpec(memory_space=pl.ANY),
+            pl.BlockSpec(memory_space=pl.ANY),
             pl.BlockSpec((1, TILE, TILE), lambda t: (t, 0, 0)),
             pl.BlockSpec((1, TILE, TILE), lambda t: (t, 0, 0)),
         ],
         out_specs=[pl.BlockSpec(memory_space=pl.ANY)] * 6,
         out_shape=[quad, pair, pair, quad, pair, pair],
         scratch_shapes=[
+            pltpu.SMEM((2, 4), jnp.int32),
+            pltpu.SMEM((2, 2, 4), jnp.int32),
+            pltpu.VMEM((BASES, 2, TAPS), BF16),
+            pltpu.VMEM((BASES, 4, 3), BF16),
             pltpu.VMEM((BASES, TILE, TILE), BF16),
             pltpu.VMEM((BASES, TILE, TILE), BF16),
             pltpu.VMEM((8, 3 * LANES), F32),
             pltpu.VMEM((BASES, 8, LANES), F32),
-            pltpu.VMEM((4, TILE, TILE), BF16),
-            pltpu.VMEM((4, TILE, TILE), BF16),
+            pltpu.VMEM((4, TILE + 16, TILE), BF16),
+            pltpu.VMEM((4, TILE + 16, TILE), BF16),
+            pltpu.SemaphoreType.DMA((4,)),
             pltpu.SemaphoreType.DMA((4, 2)),
             pltpu.SemaphoreType.DMA((4, 2)),
         ],
         compiler_params=pltpu.CompilerParams(vmem_limit_bytes=40 << 20),
         cost_estimate=pl.CostEstimate(flops=6 << 30, bytes_accessed=12 << 20, transcendentals=0),
-    )(place, patches, taps, coeffs, images, variances)
-
-
-def frame_kernel(far, sources, place, mine, other, *refs):
+    )(patches, corners, taps, coeffs, images, variances)
+
+
+def frame_kernel(far, sources, *refs):
     stacks, outs, (frame, held, packed, sems, out_sems) = refs[:sources], refs[sources : sources + 4], refs[sources + 4 :]
-    y, x, core, z = (place[0, k] for k in range(4))
-    patch = lax.rem(z + 2 * far, 4)
+    y, x, core, z = position()
+    patch = lax.rem(z + 2 * far, 4).astype(F32)
 
     for number in range(2 * sources):
         source, slot = number // 2, number % 2
@@ -199,27 +218,19 @@
     nothing = jnp.zeros((1, ROWS, LANES), F32)
 
     def add(number, carry):
-        source, slot = lax.div(number, 2), lax.rem(number, 2)
-        sibling = lax.rem(source, 2) == 1
-        from_z = lax.rem(z + jnp.where(source < 2, 4, jnp.where(source < 4, 3, 5)), 4)
-
-        def look(k):
-            return jnp.where(sibling, other[from_z, k], mine[from_z, k])
-
-        entry = jnp.int32(0)
-        for k in range(8):
-            named = look(k) == patch
-            entry = jnp.where(named & ((slot == 1) | (entry == 0)), k + 1, entry)
-        entry = jnp.maximum(entry - 1, 0)
-        top, left = look(8 + 2 * entry), look(9 + 2 * entry)
+        pltpu.make_async_copy(stacks[0].at[far, 0], held.at[number], sems.at[number]).wait()
+        named, tops, lefts = (
+            held[number, TILE : TILE + 16, part * LANES : (part + 1) * LANES].astype(F32)[0:1] for part in range(3)
+        )
+        top = jnp.sum(jnp.where(named == patch, tops, 0.0)).astype(jnp.int32)
+        left = jnp.sum(jnp.where(named == patch, lefts, 0.0)).astype(jnp.int32)
         first = jnp.minimum(lax.div(left, LANES) * LANES, PATCH_PIX - TILE - LANES)
         group, lead = lax.div(top, ROWS), lax.rem(top, ROWS)
         shift = jnp.where(apart == left - first - LANES, F32(1.0), F32(0.0)).astype(BF16)
-        pltpu.make_async_copy(stacks[0].at[far, 0], held.at[number], sems.at[number]).wait()
         for block in range(5):
             low, high = max(block - 1, 0) * LANES, min(block + 1, 4) * LANES
             moved = jnp.dot(
-                held[number, :, low:high],
+                held[number, 0:TILE, low:high],
                 shift[LANES * (block == 0) : 2 * LANES - LANES * (block == 4)],
                 preferred_element_type=F32,
             )
@@ -251,24 +262,24 @@
         copy.wait()
 
 
-def build_frame(far, place, mine, other, stacks):
+def build_frame(far, stacks):
     sources = len(stacks)
     out = jax.ShapeDtypeStruct((SLAB, PATCH_PIX), BF16)
     return pl.pallas_call(
         functools.partial(frame_kernel, far, sources),
-        in_specs=[pl.BlockSpec(memory_space=pltpu.SMEM)] * 3 + [pl.BlockSpec(memory_space=pl.ANY)] * sources,
+        in_specs=[pl.BlockSpec(memory_space=pl.ANY)] * sources,
         out_specs=[pl.BlockSpec(memory_space=pl.ANY)] * 4,
         out_shape=[out] * 4,
         scratch_shapes=[
             pltpu.VMEM((PATCH_PIX // ROWS + 1, ROWS, PATCH_PIX), F32),
-            pltpu.VMEM((2 * sources, TILE, TILE), BF16),
+            pltpu.VMEM((2 * sources, TILE + 16, TILE), BF16),
             pltpu.VMEM((4, SLAB, PATCH_PIX), BF16),
             pltpu.SemaphoreType.DMA((2 * sources,)),
             pltpu.SemaphoreType.DMA((4,)),
         ],
         compiler_params=pltpu.CompilerParams(vmem_limit_bytes=40 << 20),
         cost_estimate=pl.CostEstimate(flops=sources << 30, bytes_accessed=(5 + sources) << 20, transcendentals=0),
-    )(place, mine, other, *stacks)
+    )(*stacks)
 
 
 def sum_kernel(count, *refs):
@@ -300,27 +311,21 @@
 
 
 def body(images, variances, kernels, coefficients, intersections, offsets):
-    visit, z = lax.axis_index("visit"), lax.axis_index("patch")
-    core = lax.rem(visit, 2)
-    place = jnp.stack([lax.div(visit, 8), lax.rem(lax.div(visit, 2), 4), core, z]).astype(jnp.int32).reshape(1, 4)
-    patches = jnp.transpose(intersections[0])
-    mine = lax.all_gather(pack_info(patches, jnp.transpose(offsets[0], (1, 2, 0))), "patch", axis=0, tiled=True)
-
+    core = lax.rem(lax.axis_index("visit"), 2)
     stays, plus, minus, swaps, swap_plus, swap_minus = match_tiles(
-        place,
-        patches,
+        jnp.transpose(intersections[0]),
+        jnp.transpose(offsets[0], (1, 2, 0)),
         jnp.transpose(kernels[0], (1, 0, 2)),
         jnp.transpose(coefficients[0], (1, 0, 2)),
         images[0],
         variances[0],
     )
     swapped = across_core(swaps)
-    other = across_core(mine)
     arrived = [across_z(plus, 1), across_both(swap_plus, 1), across_z(minus, 3), across_both(swap_minus, 3)]
 
-    opposite = build_frame(1, place, mine, other, [stays, swapped])
+    opposite = build_frame(1, [stays, swapped])
     passed = across_z(add_up(spread(opposite, False)).astype(BF16), 2)
-    own = build_frame(0, place, mine, other, [stays, swapped] + arrived)
+    own = build_frame(0, [stays, swapped] + arrived)
     pieces = sum_slabs(spread(own, False) + [passed])
     rows = add_up(spread(pieces, True))
     keep, got = rows[:STRIP], across_core(rows[STRIP:])

time: 183 us -> 134 us (0.73)
  blocking collectives: 47.5 us -> 0 us
  starting transfers between devices: 22.8 us -> 27.6 us
  local copies, waits for them, and re-layouts: 10.2 us -> 5.92 us
  waiting for transfers between devices: 71.7 us -> 69 us
    all_gather x1 -> x0, blocking collectives: 47.5 us -> none  [body(): lax.all_gather(pack_info(patches, jnp.transpose(offsets[0], (1, 2, 0))),...]
    unnamed x20 -> x12, local copies, waits for them, and re-layouts: 10.2 us -> 5.9 us
    ppermute x3, waiting for transfers between devices: 15.1 us -> 17.9 us  [across_z(): return lax.ppermute(value, 'patch', [(z, (z + step) % 4) for z in range(4)])]
    ppermute x9, waiting for transfers between devices: 32.1 us -> 29.5 us  [turn(): return lax.ppermute(value, 'visit', pairs)]
    ppermute x3, starting transfers between devices: 1.94 us -> 4.4 us  [across_z(): return lax.ppermute(value, 'patch', [(z, (z + step) % 4) for z in range(4)])]
    ppermute x2, waiting for transfers between devices: 22.6 us -> 20.4 us  [across_both(): return lax.ppermute(value, ('visit', 'patch'), pairs)]
    ppermute x3 -> x2, starting transfers between devices: 4.21 us -> 3.67 us  [across_core(): return lax.ppermute(value, 'visit', pairs)]
  transfers between devices with their start and end apart: 17 -> 16, of which waited for: 11 -> 9; matrix products, arithmetic and copies ran while one was open for 0% -> 2% of each run, Pallas kernels for 9% -> 12%
where the time goes in v3:
time: 134 us
  waiting for transfers between devices  69 us (51%)
  Pallas kernels  27.6 us (21%)
  starting transfers between devices  27.6 us (21%)
  local copies, waits for them, and re-layouts  5.92 us (4%)
  other arithmetic  3.2 us (2%)
    ppermute x9, waiting for transfers between devices, turn(): return lax.ppermute(value, 'visit', pairs)  29.5 us
    ppermute x2, waiting for transfers between devices, across_both(): return lax.ppermute(value, ('visit', 'patch'), pairs)  20.4 us
    ppermute x3, waiting for transfers between devices, across_z(): return lax.ppermute(value, 'patch', [(z, (z + step) % 4) for z in range(4)])  17.9 us
    ppermute x9, starting transfers between devices, turn(): return lax.ppermute(value, 'visit', pairs)  16.4 us
    pallas_call x2, Pallas kernels, build_frame(): pl.pallas_call(functools.partial(frame_kernel, far, sources), in_specs=[p...  15.5 us
    pallas_call x1, Pallas kernels, match_tiles(): pl.pallas_call(match_kernel, grid=(4,), in_specs=[pl.BlockSpec(memory_spa...  11.4 us
    unnamed x12, local copies, waits for them, and re-layouts  5.9 us
    ppermute x3, starting transfers between devices, across_z(): return lax.ppermute(value, 'patch', [(z, (z + step) % 4) for z in range(4)])  4.4 us
  transfers between devices with their start and end apart: 16, of which 9 were waited for; matrix products, arithmetic and copies ran while one was open for 2% of the time, Pallas kernels for 12%

profile of v3, /device:TPU:1, one launch (start us, length us, event | category | flops | bytes accessed | tf_op | source)
XLA Modules:
  0.0 134.1 jit_solution(13288624556369171929)
XLA Ops:
  0.6 1.6 %copy-done = bf16[1,4,512,512]{3,2,1,0:T(8,128)(2,1)S(1)} copy-done((bf16[1,4,512,512]{3,2,1,0:T(8,128)(2,1)S(1)}, bf16[1,4,512,512]{3,2,1,0:T(8,128)(2,1)}, u32[]{:S(2)}) %copy-start) | copy-done | bytes 2097176
  2.2 1.6 %copy-done.1 = bf16[1,4,512,512]{3,2,1,0:T(8,128)(2,1)S(1)} copy-done((bf16[1,4,512,512]{3,2,1,0:T(8,128)(2,1)S(1)}, bf16[1,4,512,512]{3,2,1,0:T(8,128)(2,1)}, u32[]{:S(2)}) %copy-start.1) | copy-done | bytes 2097176
  3.8 0.7 copy-done.2
  6.5 11.4 %shard_map.77 = (bf16[2,2,528,512]{3,2,1,0:T(8,128)(2,1)S(1)}, bf16[2,528,512]{2,1,0:T(8,128)(2,1)S(1)}, bf16[2,528,512]{2,1,0:T(8,128)(2,1)S(1)}, bf16[2,2,528,...) custom-call(s32[2,4]{1,0:T(2,128)S(1)} %bitcast.23, ...), custom_call_target="tpu_custom_call" | custom-call | flops 6442450944 | bytes 12582912 | tf_op jit(solution)/shard_map/pallas_call | solution.py:171
  18.0 1.5 %collective-permute-start = (bf16[2,2,528,512]{3,2,1,0:T(8,128)(2,1)S(1)}, bf16[2,2,528,512]{3,2,1,0:T(8,128)(2,1)S(1)}, u32[]{:S(2)}, u32[]{:S(2)}) collective-permute-start(bf16[2,2,528,512]{3,2,1,0:T(8,128)(2,1)S(1)} %get-tuple-element.21), channel_id=1, source_target_pairs={{0,4},{4,0},{8,12},{12,8},{16,20},{20,16},{24,28},{28,24},{32,36},... | collective-permute-start | bytes 6488072 | tf_op jit(solution)/shard_map/ppermute | solution.py:46
  19.5 1.7 %collective-permute-start.1 = (bf16[2,528,512]{2,1,0:T(8,128)(2,1)S(1)}, bf16[2,528,512]{2,1,0:T(8,128)(2,1)S(1)}, u32[]{:S(2)}, u32[]{:S(2)}) collective-permute-start(bf16[2,528,512]{2,1,0:T(8,128)(2,1)S(1)} %get-tuple-element.22), channel_id=1, source_target_pairs={{0,1},{1,2},{2,3},{3,0},{4,5},{5,6},{6,7},{7,4},{8,9},{9,10},{10,1... | collective-permute-start | bytes 3244040 | tf_op jit(solution)/shard_map/ppermute | solution.py:41
  21.2 1.9 %collective-permute-start.2 = (bf16[2,528,512]{2,1,0:T(8,128)(2,1)S(1)}, bf16[2,528,512]{2,1,0:T(8,128)(2,1)S(1)}, u32[]{:S(2)}, u32[]{:S(2)}) collective-permute-start(bf16[2,528,512]{2,1,0:T(8,128)(2,1)S(1)} %get-tuple-element.23), channel_id=1, source_target_pairs={{0,5},{1,6},{2,7},{3,4},{4,1},{5,2},{6,3},{7,0},{8,13},{9,14},{10,... | collective-permute-start | bytes 3244040 | tf_op jit(solution)/shard_map/ppermute | solution.py:56
  23.1 1.0 collective-permute-start.3
  24.1 1.3 collective-permute-start.4
  25.4 4.9 %shard_map.79 = (bf16[384,1536]{1,0:T(8,128)(2,1)S(1)}, bf16[384,1536]{1,0:T(8,128)(2,1)S(1)}, bf16[384,1536]{1,0:T(8,128)(2,1)S(1)}, bf16[384,1536]{1,0:T(8,128)(2,1)S(1)}) custom-call(bf16[2,2,528,512]{3,2,1,0:T(8,128)(2,1)S(1)} %get-tuple-element.20.refs_0_, bf16[2,2,528,512]{3,2,1,0:T(8,128)(2,1)S(1)} %collective-permute-done.refs_1_), custom_call_target="tpu_custom_call" | custom-call | flops 2147483648 | bytes 7340032 | tf_op jit(solution)/shard_map/pallas_call | solution.py:268
  30.4 3.0 %collective-permute-start.10 = (bf16[384,1536]{1,0:T(8,128)(2,1)S(1)}, bf16[384,1536]{1,0:T(8,128)(2,1)S(1)}, u32[]{:S(2)}, u32[]{:S(2)}) collective-permute-start(bf16[384,1536]{1,0:T(8,128)(2,1)S(1)} %get-tuple-element.33), channel_id=1, source_target_pairs={{0,16},{4,68},{8,24},{12,76},{16,0},{20,84},{24,8},{28,92},{32,48}... | collective-permute-start | bytes 3538952 | tf_op jit(solution)/shard_map/ppermute | solution.py:37
  33.4 14.1 %collective-permute-done.1.refs_2_ = bf16[2,528,512]{2,1,0:T(8,128)(2,1)S(1)} collective-permute-done((bf16[2,528,512]{2,1,0:T(8,128)(2,1)S(1)}, bf16[2,528,512]{2,1,0:T(8,128)(2,1)S(1)}, u32[]{:S(2)}, u32[]{:S(2)}) %collective-permute-start.1) | collective-permute-done | bytes 1081376 | tf_op jit(solution)/shard_map/ppermute | solution.py:41
  47.5 2.7 %collective-permute-start.9 = (bf16[384,1536]{1,0:T(8,128)(2,1)S(1)}, bf16[384,1536]{1,0:T(8,128)(2,1)}, u32[]{:S(2)}, u32[]{:S(2)}) collective-permute-start(bf16[384,1536]{1,0:T(8,128)(2,1)S(1)} %get-tuple-element.32), channel_id=1, source_target_pairs={{0,24},{4,100},{8,0},{12,108},{16,8},{20,116},{24,16},{28,124},{32... | collective-permute-start | bytes 3538952 | tf_op jit(solution)/shard_map/ppermute | solution.py:37
  50.2 20.4 %collective-permute-done.2.refs_3_ = bf16[2,528,512]{2,1,0:T(8,128)(2,1)S(1)} collective-permute-done((bf16[2,528,512]{2,1,0:T(8,128)(2,1)S(1)}, bf16[2,528,512]{2,1,0:T(8,128)(2,1)S(1)}, u32[]{:S(2)}, u32[]{:S(2)}) %collective-permute-start.2) | collective-permute-done | bytes 1081376 | tf_op jit(solution)/shard_map/ppermute | solution.py:56
  70.7 1.3 collective-permute-start.8
  72.0 10.5 %shard_map.78 = (bf16[384,1536]{1,0:T(8,128)(2,1)S(1)}, bf16[384,1536]{1,0:T(8,128)(2,1)S(1)}, bf16[384,1536]{1,0:T(8,128)(2,1)S(1)}, bf16[384,1536]{1,0:T(8,128)(2,1)S(1)}) custom-call(bf16[2,2,528,512]{3,2,1,0:T(8,128)(2,1)S(1)} %get-tuple-element.20.refs_0_, bf16[2,2,528,512]{3,2,1,0:T(8,128)(2,1)S(1)} %collective-permute-done.refs_1_, ...), custom_call_target="tpu_custom_call" | custom-call | flops 6442450944 | bytes 11534336 | tf_op jit(solution)/shard_map/pallas_call | solution.py:268
  82.5 1.4 %collective-permute-start.5 = (bf16[384,1536]{1,0:T(8,128)(2,1)S(1)}, bf16[384,1536]{1,0:T(8,128)(2,1)S(1)}, u32[]{:S(2)}, u32[]{:S(2)}) collective-permute-start(bf16[384,1536]{1,0:T(8,128)(2,1)S(1)} %get-tuple-element.27), channel_id=1, source_target_pairs={{0,8},{4,36},{8,16},{12,44},{16,24},{20,52},{24,0},{28,60},{32,40}... | collective-permute-start | bytes 3538952 | tf_op jit(solution)/shard_map/ppermute | solution.py:37
  83.9 1.4 %collective-permute-start.6 = (bf16[384,1536]{1,0:T(8,128)(2,1)S(1)}, bf16[384,1536]{1,0:T(8,128)(2,1)S(1)}, u32[]{:S(2)}, u32[]{:S(2)}) collective-permute-start(bf16[384,1536]{1,0:T(8,128)(2,1)S(1)} %get-tuple-element.28), channel_id=1, source_target_pairs={{0,24},{4,100},{8,0},{12,108},{16,8},{20,116},{24,16},{28,124},{32... | collective-permute-start | bytes 3538952 | tf_op jit(solution)/shard_map/ppermute | solution.py:37
  85.2 1.6 %collective-permute-start.7 = (bf16[384,1536]{1,0:T(8,128)(2,1)S(1)}, bf16[384,1536]{1,0:T(8,128)(2,1)S(1)}, u32[]{:S(2)}, u32[]{:S(2)}) collective-permute-start(bf16[384,1536]{1,0:T(8,128)(2,1)S(1)} %get-tuple-element.29), channel_id=1, source_target_pairs={{0,16},{4,68},{8,24},{12,76},{16,0},{20,84},{24,8},{28,92},{32,48}... | collective-permute-start | bytes 3538952 | tf_op jit(solution)/shard_map/ppermute | solution.py:37
  87.4 2.2 %add_convert_fusion = bf16[384,1536]{1,0:T(8,128)(2,1)S(1)} fusion(bf16[384,1536]{1,0:T(8,128)(2,1)S(1)} %collective-permute-done.10, bf16[384,1536]{1,0:T(8,128)(2,1)} %collective-permute-done.9, bf16[384,1536]{1,0:T(8,128)(2,1)} %collective-permute-done.8, bf16[384,1536]{1,0:T(8,128)(2,1)S(1)} %get-tuple-element.30), kind=kLoop, calls=%fused_computation | loop fusion | flops 4718592 | bytes 5898240 | tf_op jit(solution)/shard_map/convert_element_type | solution.py:327
  89.6 1.6 %collective-permute-start.11 = (bf16[384,1536]{1,0:T(8,128)(2,1)S(1)}, bf16[384,1536]{1,0:T(8,128)(2,1)S(1)}, u32[]{:S(2)}, u32[]{:S(2)}) collective-permute-start(bf16[384,1536]{1,0:T(8,128)(2,1)S(1)} %add_convert_fusion), channel_id=1, source_target_pairs={{0,2},{1,3},{2,0},{3,1},{4,6},{5,7},{6,4},{7,5},{8,10},{9,11},{10,... | collective-permute-start | bytes 3538952 | tf_op jit(solution)/shard_map/ppermute | solution.py:41
  91.3 8.7 %collective-permute-done.5.refs_1_ = bf16[384,1536]{1,0:T(8,128)(2,1)S(1)} collective-permute-done((bf16[384,1536]{1,0:T(8,128)(2,1)S(1)}, bf16[384,1536]{1,0:T(8,128)(2,1)S(1)}, u32[]{:S(2)}, u32[]{:S(2)}) %collective-permute-start.5) | collective-permute-done | bytes 1179680 | tf_op jit(solution)/shard_map/ppermute | solution.py:37
  99.9 13.8 %collective-permute-done.7.refs_3_ = bf16[384,1536]{1,0:T(8,128)(2,1)S(1)} collective-permute-done((bf16[384,1536]{1,0:T(8,128)(2,1)S(1)}, bf16[384,1536]{1,0:T(8,128)(2,1)S(1)}, u32[]{:S(2)}, u32[]{:S(2)}) %collective-permute-start.7) | collective-permute-done | bytes 1179680 | tf_op jit(solution)/shard_map/ppermute | solution.py:37
  113.8 3.7 %collective-permute-done.11.refs_4_ = bf16[384,1536]{1,0:T(8,128)(2,1)S(1)} collective-permute-done((bf16[384,1536]{1,0:T(8,128)(2,1)S(1)}, bf16[384,1536]{1,0:T(8,128)(2,1)S(1)}, u32[]{:S(2)}, u32[]{:S(2)}) %collective-permute-start.11) | collective-permute-done | bytes 1179680 | tf_op jit(solution)/shard_map/ppermute | solution.py:41
  117.5 0.7 shard_map.80
  118.2 3.5 %collective-permute-start.14 = (bf16[96,1536]{1,0:T(8,128)(2,1)S(1)}, bf16[96,1536]{1,0:T(8,128)(2,1)S(1)}, u32[]{:S(2)}, u32[]{:S(2)}) collective-permute-start(bf16[96,1536]{1,0:T(8,128)(2,1)S(1)} %get-tuple-element.37), channel_id=1, source_target_pairs={{0,64},{4,20},{8,72},{12,28},{16,80},{20,4},{24,88},{28,12},{32,96... | collective-permute-start | bytes 884744 | tf_op jit(solution)/shard_map/ppermute | solution.py:37
  121.7 0.9 collective-permute-start.13
  123.2 2.9 %collective-permute-done.14 = bf16[96,1536]{1,0:T(8,128)(2,1)S(1)} collective-permute-done((bf16[96,1536]{1,0:T(8,128)(2,1)S(1)}, bf16[96,1536]{1,0:T(8,128)(2,1)S(1)}, u32[]{:S(2)}, u32[]{:S(2)}) %collective-permute-start.14) | collective-permute-done | bytes 294944 | tf_op jit(solution)/shard_map/ppermute | solution.py:37
  126.1 3.5 %collective-permute-done.13 = bf16[96,1536]{1,0:T(8,128)(2,1)S(1)} collective-permute-done((bf16[96,1536]{1,0:T(8,128)(2,1)S(1)}, bf16[96,1536]{1,0:T(8,128)(2,1)S(1)}, u32[]{:S(2)}, u32[]{:S(2)}) %collective-permute-start.13) | collective-permute-done | bytes 294944 | tf_op jit(solution)/shard_map/ppermute | solution.py:37
  129.9 2.2 %collective-permute-start.15 = (f32[48,1536]{1,0:T(8,128)S(1)}, f32[48,1536]{1,0:T(8,128)S(1)}, u32[]{:S(2)}, u32[]{:S(2)}) collective-permute-start(f32[48,1536]{1,0:T(8,128)S(1)} %slice.9), channel_id=1, source_target_pairs={{0,4},{4,0},{8,12},{12,8},{16,20},{20,16},{24,28},{28,24},{32,36},... | collective-permute-start | bytes 884744 | tf_op jit(solution)/shard_map/ppermute | solution.py:46
  132.0 1.2 collective-permute-done.15
  133.2 0.9 fusion
  (20 shorter events, 3.4 us)
Async XLA Ops:
  0.6 1.6 %copy-start = (bf16[1,4,512,512]{3,2,1,0:T(8,128)(2,1)S(1)}, bf16[1,4,512,512]{3,2,1,0:T(8,128)(2,1)}, u32[]{:S(2)}) copy-start(bf16[1,4,512,512]{3,2,1,0:T(8,128)(2,1)} %param.6) | copy-start | bytes 6291460
  2.2 1.6 %copy-start.1 = (bf16[1,4,512,512]{3,2,1,0:T(8,128)(2,1)S(1)}, bf16[1,4,512,512]{3,2,1,0:T(8,128)(2,1)}, u32[]{:S(2)}) copy-start(bf16[1,4,512,512]{3,2,1,0:T(8,128)(2,1)} %param.7) | copy-start | bytes 6291460
  3.8 0.7 copy-start.2
  4.5 0.7 copy-start.3
  5.2 0.7 copy-start.4
  5.9 0.7 copy-start.5
  18.0 7.4 %collective-permute-start = (bf16[2,2,528,512]{3,2,1,0:T(8,128)(2,1)S(1)}, bf16[2,2,528,512]{3,2,1,0:T(8,128)(2,1)S(1)}, u32[]{:S(2)}, u32[]{:S(2)}) collective-permute-start(bf16[2,2,528,512]{3,2,1,0:T(8,128)(2,1)S(1)} %get-tuple-element.21), channel_id=1, source_target_pairs={{0,4},{4,0},{8,12},{12,8},{16,20},{20,16},{24,28},{28,24},{32,36},... | collective-permute-start | bytes 6488072 | tf_op jit(solution)/shard_map/ppermute | solution.py:46
  19.5 28.0 %collective-permute-start.1 = (bf16[2,528,512]{2,1,0:T(8,128)(2,1)S(1)}, bf16[2,528,512]{2,1,0:T(8,128)(2,1)S(1)}, u32[]{:S(2)}, u32[]{:S(2)}) collective-permute-start(bf16[2,528,512]{2,1,0:T(8,128)(2,1)S(1)} %get-tuple-element.22), channel_id=1, source_target_pairs={{0,1},{1,2},{2,3},{3,0},{4,5},{5,6},{6,7},{7,4},{8,9},{9,10},{10,1... | collective-permute-start | bytes 3244040 | tf_op jit(solution)/shard_map/ppermute | solution.py:41
  21.2 49.4 %collective-permute-start.2 = (bf16[2,528,512]{2,1,0:T(8,128)(2,1)S(1)}, bf16[2,528,512]{2,1,0:T(8,128)(2,1)S(1)}, u32[]{:S(2)}, u32[]{:S(2)}) collective-permute-start(bf16[2,528,512]{2,1,0:T(8,128)(2,1)S(1)} %get-tuple-element.23), channel_id=1, source_target_pairs={{0,5},{1,6},{2,7},{3,4},{4,1},{5,2},{6,3},{7,0},{8,13},{9,14},{10,... | collective-permute-start | bytes 3244040 | tf_op jit(solution)/shard_map/ppermute | solution.py:56
  23.1 48.9 %collective-permute-start.3 = (bf16[2,528,512]{2,1,0:T(8,128)(2,1)S(1)}, bf16[2,528,512]{2,1,0:T(8,128)(2,1)S(1)}, u32[]{:S(2)}, u32[]{:S(2)}) collective-permute-start(bf16[2,528,512]{2,1,0:T(8,128)(2,1)S(1)} %get-tuple-element.24), channel_id=1, source_target_pairs={{0,3},{1,0},{2,1},{3,2},{4,7},{5,4},{6,5},{7,6},{8,11},{9,8},{10,9... | collective-permute-start | bytes 3244040 | tf_op jit(solution)/shard_map/ppermute | solution.py:41
  24.1 47.8 %collective-permute-start.4 = (bf16[2,528,512]{2,1,0:T(8,128)(2,1)S(1)}, bf16[2,528,512]{2,1,0:T(8,128)(2,1)S(1)}, u32[]{:S(2)}, u32[]{:S(2)}) collective-permute-start(bf16[2,528,512]{2,1,0:T(8,128)(2,1)S(1)} %get-tuple-element.25), channel_id=1, source_target_pairs={{0,7},{1,4},{2,5},{3,6},{4,3},{5,0},{6,1},{7,2},{8,15},{9,12},{10,... | collective-permute-start | bytes 3244040 | tf_op jit(solution)/shard_map/ppermute | solution.py:56
  30.4 54.9 %collective-permute-start.10 = (bf16[384,1536]{1,0:T(8,128)(2,1)S(1)}, bf16[384,1536]{1,0:T(8,128)(2,1)S(1)}, u32[]{:S(2)}, u32[]{:S(2)}) collective-permute-start(bf16[384,1536]{1,0:T(8,128)(2,1)S(1)} %get-tuple-element.33), channel_id=1, source_target_pairs={{0,16},{4,68},{8,24},{12,76},{16,0},{20,84},{24,8},{28,92},{32,48}... | collective-permute-start | bytes 3538952 | tf_op jit(solution)/shard_map/ppermute | solution.py:37
  47.5 39.4 %collective-permute-start.9 = (bf16[384,1536]{1,0:T(8,128)(2,1)S(1)}, bf16[384,1536]{1,0:T(8,128)(2,1)}, u32[]{:S(2)}, u32[]{:S(2)}) collective-permute-start(bf16[384,1536]{1,0:T(8,128)(2,1)S(1)} %get-tuple-element.32), channel_id=1, source_target_pairs={{0,24},{4,100},{8,0},{12,108},{16,8},{20,116},{24,16},{28,124},{32... | collective-permute-start | bytes 3538952 | tf_op jit(solution)/shard_map/ppermute | solution.py:37
  70.7 16.7 %collective-permute-start.8 = (bf16[384,1536]{1,0:T(8,128)(2,1)S(1)}, bf16[384,1536]{1,0:T(8,128)(2,1)}, u32[]{:S(2)}, u32[]{:S(2)}) collective-permute-start(bf16[384,1536]{1,0:T(8,128)(2,1)S(1)} %get-tuple-element.31), channel_id=1, source_target_pairs={{0,8},{4,36},{8,16},{12,44},{16,24},{20,52},{24,0},{28,60},{32,40}... | collective-permute-start | bytes 3538952 | tf_op jit(solution)/shard_map/ppermute | solution.py:37
  82.5 17.4 %collective-permute-start.5 = (bf16[384,1536]{1,0:T(8,128)(2,1)S(1)}, bf16[384,1536]{1,0:T(8,128)(2,1)S(1)}, u32[]{:S(2)}, u32[]{:S(2)}) collective-permute-start(bf16[384,1536]{1,0:T(8,128)(2,1)S(1)} %get-tuple-element.27), channel_id=1, source_target_pairs={{0,8},{4,36},{8,16},{12,44},{16,24},{20,52},{24,0},{28,60},{32,40}... | collective-permute-start | bytes 3538952 | tf_op jit(solution)/shard_map/ppermute | solution.py:37
  83.9 16.1 %collective-permute-start.6 = (bf16[384,1536]{1,0:T(8,128)(2,1)S(1)}, bf16[384,1536]{1,0:T(8,128)(2,1)S(1)}, u32[]{:S(2)}, u32[]{:S(2)}) collective-permute-start(bf16[384,1536]{1,0:T(8,128)(2,1)S(1)} %get-tuple-element.28), channel_id=1, source_target_pairs={{0,24},{4,100},{8,0},{12,108},{16,8},{20,116},{24,16},{28,124},{32... | collective-permute-start | bytes 3538952 | tf_op jit(solution)/shard_map/ppermute | solution.py:37
  85.2 28.5 %collective-permute-start.7 = (bf16[384,1536]{1,0:T(8,128)(2,1)S(1)}, bf16[384,1536]{1,0:T(8,128)(2,1)S(1)}, u32[]{:S(2)}, u32[]{:S(2)}) collective-permute-start(bf16[384,1536]{1,0:T(8,128)(2,1)S(1)} %get-tuple-element.29), channel_id=1, source_target_pairs={{0,16},{4,68},{8,24},{12,76},{16,0},{20,84},{24,8},{28,92},{32,48}... | collective-permute-start | bytes 3538952 | tf_op jit(solution)/shard_map/ppermute | solution.py:37
  89.6 27.9 %collective-permute-start.11 = (bf16[384,1536]{1,0:T(8,128)(2,1)S(1)}, bf16[384,1536]{1,0:T(8,128)(2,1)S(1)}, u32[]{:S(2)}, u32[]{:S(2)}) collective-permute-start(bf16[384,1536]{1,0:T(8,128)(2,1)S(1)} %add_convert_fusion), channel_id=1, source_target_pairs={{0,2},{1,3},{2,0},{3,1},{4,6},{5,7},{6,4},{7,5},{8,10},{9,11},{10,... | collective-permute-start | bytes 3538952 | tf_op jit(solution)/shard_map/ppermute | solution.py:41
  118.2 7.9 %collective-permute-start.14 = (bf16[96,1536]{1,0:T(8,128)(2,1)S(1)}, bf16[96,1536]{1,0:T(8,128)(2,1)S(1)}, u32[]{:S(2)}, u32[]{:S(2)}) collective-permute-start(bf16[96,1536]{1,0:T(8,128)(2,1)S(1)} %get-tuple-element.37), channel_id=1, source_target_pairs={{0,64},{4,20},{8,72},{12,28},{16,80},{20,4},{24,88},{28,12},{32,96... | collective-permute-start | bytes 884744 | tf_op jit(solution)/shard_map/ppermute | solution.py:37
  121.7 7.9 %collective-permute-start.13 = (bf16[96,1536]{1,0:T(8,128)(2,1)S(1)}, bf16[96,1536]{1,0:T(8,128)(2,1)S(1)}, u32[]{:S(2)}, u32[]{:S(2)}) collective-permute-start(bf16[96,1536]{1,0:T(8,128)(2,1)S(1)} %get-tuple-element.36), channel_id=1, source_target_pairs={{0,96},{4,28},{8,104},{12,4},{16,112},{20,12},{24,120},{28,20},{32... | collective-permute-start | bytes 884744 | tf_op jit(solution)/shard_map/ppermute | solution.py:37
  122.6 7.1 %collective-permute-start.12 = (bf16[96,1536]{1,0:T(8,128)(2,1)S(1)}, bf16[96,1536]{1,0:T(8,128)(2,1)S(1)}, u32[]{:S(2)}, u32[]{:S(2)}) collective-permute-start(bf16[96,1536]{1,0:T(8,128)(2,1)S(1)} %get-tuple-element.35), channel_id=1, source_target_pairs={{0,32},{4,12},{8,40},{12,20},{16,48},{20,28},{24,56},{28,4},{32,64... | collective-permute-start | bytes 884744 | tf_op jit(solution)/shard_map/ppermute | solution.py:37
  129.9 3.4 %collective-permute-start.15 = (f32[48,1536]{1,0:T(8,128)S(1)}, f32[48,1536]{1,0:T(8,128)S(1)}, u32[]{:S(2)}, u32[]{:S(2)}) collective-permute-start(f32[48,1536]{1,0:T(8,128)S(1)} %slice.9), channel_id=1, source_target_pairs={{0,4},{4,0},{8,12},{12,8},{16,20},{20,16},{24,28},{28,24},{32,36},... | collective-permute-start | bytes 884744 | tf_op jit(solution)/shard_map/ppermute | solution.py:46

commit v4 on v3

--- a/solution.py
+++ b/solution.py
@@ -196,58 +196,56 @@
             pltpu.SemaphoreType.DMA((4, 2)),
             pltpu.SemaphoreType.DMA((4, 2)),
         ],
-        compiler_params=pltpu.CompilerParams(vmem_limit_bytes=40 << 20),
+        compiler_params=pltpu.CompilerParams(vmem_limit_bytes=62 << 20),
         cost_estimate=pl.CostEstimate(flops=6 << 30, bytes_accessed=12 << 20, transcendentals=0),
     )(patches, corners, taps, coeffs, images, variances)
 
 
 def frame_kernel(far, sources, *refs):
-    stacks, outs, (frame, held, packed, sems, out_sems) = refs[:sources], refs[sources : sources + 4], refs[sources + 4 :]
+    stacks, outs, frame = refs[:sources], refs[-5:-1], refs[-1]
     y, x, core, z = position()
     patch = lax.rem(z + 2 * far, 4).astype(F32)
-
-    for number in range(2 * sources):
-        source, slot = number // 2, number % 2
-        stack = stacks[source].at[far, slot] if source < 2 else stacks[source].at[slot]
-        pltpu.make_async_copy(stack, held.at[number], sems.at[number]).start()
     frame[...] = jnp.zeros_like(frame)
-    apart = lax.broadcasted_iota(jnp.int32, (2 * LANES, LANES), 1) - lax.broadcasted_iota(
-        jnp.int32, (2 * LANES, LANES), 0
-    )
-    inner = lax.broadcasted_iota(jnp.int32, (TILE // ROWS + 1, ROWS, LANES), 1)
-    nothing = jnp.zeros((1, ROWS, LANES), F32)
-
-    def add(number, carry):
-        pltpu.make_async_copy(stacks[0].at[far, 0], held.at[number], sems.at[number]).wait()
+    inner = lax.broadcasted_iota(jnp.int32, (1, ROWS, LANES), 1)
+    lane = lax.broadcasted_iota(jnp.int32, (1, ROWS, LANES), 2)
+    groups = TILE // ROWS
+
+    def add(tile):
         named, tops, lefts = (
-            held[number, TILE : TILE + 16, part * LANES : (part + 1) * LANES].astype(F32)[0:1] for part in range(3)
+            tile[TILE : TILE + 16, part * LANES : (part + 1) * LANES].astype(F32)[0:1] for part in range(3)
         )
         top = jnp.sum(jnp.where(named == patch, tops, 0.0)).astype(jnp.int32)
         left = jnp.sum(jnp.where(named == patch, lefts, 0.0)).astype(jnp.int32)
         first = jnp.minimum(lax.div(left, LANES) * LANES, PATCH_PIX - TILE - LANES)
+        shift = left - first
         group, lead = lax.div(top, ROWS), lax.rem(top, ROWS)
-        shift = jnp.where(apart == left - first - LANES, F32(1.0), F32(0.0)).astype(BF16)
+        before = jnp.zeros((groups, ROWS, LANES), F32)
         for block in range(5):
-            low, high = max(block - 1, 0) * LANES, min(block + 1, 4) * LANES
-            moved = jnp.dot(
-                held[number, 0:TILE, low:high],
-                shift[LANES * (block == 0) : 2 * LANES - LANES * (block == 4)],
-                preferred_element_type=F32,
-            )
-            turned = pltpu.roll(moved.reshape(TILE // ROWS, ROWS, LANES), lead, axis=1)
-            lower = jnp.concatenate([turned, nothing], axis=0)
-            upper = jnp.concatenate([nothing, turned], axis=0)
+            turned = jnp.zeros((groups, ROWS, LANES), F32)
+            if block < 4:
+                part = tile[0:TILE, block * LANES : (block + 1) * LANES].astype(F32)
+                turned = pltpu.roll(part, shift, axis=1).reshape(groups, ROWS, LANES)
+                turned = pltpu.roll(turned, lead, axis=1)
+            moved = jnp.where(lane >= shift, turned, before)
+            before = turned
+            nothing = jnp.zeros((1, ROWS, LANES), F32)
+            lower = jnp.concatenate([moved, nothing], axis=0)
+            upper = jnp.concatenate([nothing, moved], axis=0)
             where = (
-                pl.ds(group, TILE // ROWS + 1),
+                pl.ds(group, groups + 1),
                 slice(None),
                 pl.ds(pl.multiple_of(first + block * LANES, LANES), LANES),
             )
             frame[where] += jnp.where(inner >= lead, lower, upper)
-        return carry
-
-    lax.fori_loop(0, 2 * sources, add, 0)
-
-    copies = []
+
+    for source, stack in enumerate(stacks):
+
+        def both(slot, carry, stack=stack, source=source):
+            add(stack.at[far, slot] if source < 2 else stack.at[slot])
+            return carry
+
+        lax.fori_loop(0, 2, both, 0)
+
     for out in range(4):
         for part in range(4):
             dx, dy = jnp.where(core == 0, out, part), jnp.where(core == 0, part, out)
@@ -255,31 +253,30 @@
                 row = 8 * STRIP * lax.rem(y + dy, 4) + 2 * STRIP * lax.rem(x + dx, 4) + STRIP * lax.rem(core + dc, 2)
                 strip = frame[pl.ds(lax.div(row, ROWS), STRIP // ROWS)]
                 at = (2 * part + dc) * STRIP
-                packed[out, at : at + STRIP, :] = strip.reshape(STRIP, PATCH_PIX).astype(BF16)
-        copies.append(pltpu.make_async_copy(packed.at[out], outs[out], out_sems.at[out]))
-        copies[-1].start()
-    for copy in copies:
-        copy.wait()
-
-
-def build_frame(far, stacks):
+                outs[out][at : at + STRIP, :] = strip.reshape(STRIP, PATCH_PIX).astype(BF16)
+
+
+def build_frame(far, stacks, after=()):
     sources = len(stacks)
     out = jax.ShapeDtypeStruct((SLAB, PATCH_PIX), BF16)
     return pl.pallas_call(
         functools.partial(frame_kernel, far, sources),
-        in_specs=[pl.BlockSpec(memory_space=pl.ANY)] * sources,
-        out_specs=[pl.BlockSpec(memory_space=pl.ANY)] * 4,
+        in_specs=[pl.BlockSpec(memory_space=pltpu.VMEM)] * sources + [pl.BlockSpec(memory_space=pl.ANY)] * len(after),
         out_shape=[out] * 4,
-        scratch_shapes=[
-            pltpu.VMEM((PATCH_PIX // ROWS + 1, ROWS, PATCH_PIX), F32),
-            pltpu.VMEM((2 * sources, TILE + 16, TILE), BF16),
-            pltpu.VMEM((4, SLAB, PATCH_PIX), BF16),
-            pltpu.SemaphoreType.DMA((2 * sources,)),
-            pltpu.SemaphoreType.DMA((4,)),
-        ],
+        scratch_shapes=[pltpu.VMEM((PATCH_PIX // ROWS + 1, ROWS, PATCH_PIX), F32)],
         compiler_params=pltpu.CompilerParams(vmem_limit_bytes=40 << 20),
         cost_estimate=pl.CostEstimate(flops=sources << 30, bytes_accessed=(5 + sources) << 20, transcendentals=0),
-    )(*stacks)
+    )(*stacks, *after)
+
+
+def tie(value, *after):
+    return pl.pallas_call(
+        lambda *refs: None,
+        in_specs=[pl.BlockSpec(memory_space=pl.ANY)] * (1 + len(after)),
+        out_specs=pl.BlockSpec(memory_space=pl.ANY),
+        out_shape=jax.ShapeDtypeStruct(value.shape, value.dtype),
+        input_output_aliases={0: 0},
+    )(value, *after)
 
 
 def sum_kernel(count, *refs):
@@ -321,11 +318,13 @@
         variances[0],
     )
     swapped = across_core(swaps)
-    arrived = [across_z(plus, 1), across_both(swap_plus, 1), across_z(minus, 3), across_both(swap_minus, 3)]
-
+    below, above = across_z(plus, 1), across_z(minus, 3)
     opposite = build_frame(1, [stays, swapped])
-    passed = across_z(add_up(spread(opposite, False)).astype(BF16), 2)
-    own = build_frame(0, [stays, swapped] + arrived)
+    summed = add_up(spread(opposite, False)).astype(BF16)
+    passed = across_z(summed, 2)
+    below_too = across_both(tie(swap_plus, below, opposite[0]), 1)
+    above_too = across_both(tie(swap_minus, above, opposite[0]), 3)
+    own = build_frame(0, [stays, swapped, below, below_too, above, above_too], [summed])
     pieces = sum_slabs(spread(own, False) + [passed])
     rows = add_up(spread(pieces, True))
     keep, got = rows[:STRIP], across_core(rows[STRIP:])

time: 134 us -> 129 us (0.963)
  waiting for transfers between devices: 69 us -> 66.2 us
  Pallas kernels: 27.6 us -> 25 us
    ppermute x9, waiting for transfers between devices: 29.5 us -> 40 us  [turn(): return lax.ppermute(value, 'visit', pairs)]
    ppermute x2, waiting for transfers between devices: 20.4 us -> 11.8 us  [across_both(): return lax.ppermute(value, ('visit', 'patch'), pairs)]
    ppermute x3, waiting for transfers between devices: 17.9 us -> 13.1 us  [across_z(): return lax.ppermute(value, 'patch', [(z, (z + step) % 4) for z in range(4)])]
    pallas_call x2, Pallas kernels: 15.5 us -> 11.5 us  [build_frame(): pl.pallas_call(functools.partial(frame_kernel, far, sources), in_specs=[p...]
    ppermute x9, starting transfers between devices: 16.4 us -> 14.6 us  [turn(): return lax.ppermute(value, 'visit', pairs)]
    ppermute x3, starting transfers between devices: 4.4 us -> 6.03 us  [across_z(): return lax.ppermute(value, 'patch', [(z, (z + step) % 4) for z in range(4)])]
    unnamed x12 -> x20, local copies, waits for them, and re-layouts: 5.9 us -> 7.09 us
  transfers between devices with their start and end apart: 16 -> 16, of which waited for: 9 -> 11; matrix products, arithmetic and copies ran while one was open for 2% -> 2% of each run, Pallas kernels for 12% -> 4%
where the time goes in v4:
time: 129 us
  waiting for transfers between devices  66.2 us (51%)
  starting transfers between devices  26.6 us (21%)
  Pallas kernels  25 us (19%)
  local copies, waits for them, and re-layouts  7.11 us (6%)
  other arithmetic  3.56 us (3%)
    ppermute x9, waiting for transfers between devices, turn(): return lax.ppermute(value, 'visit', pairs)  40 us
    ppermute x9, starting transfers between devices, turn(): return lax.ppermute(value, 'visit', pairs)  14.6 us
    ppermute x3, waiting for transfers between devices, across_z(): return lax.ppermute(value, 'patch', [(z, (z + step) % 4) for z in range(4)])  13.1 us
    pallas_call x1, Pallas kernels, match_tiles(): pl.pallas_call(match_kernel, grid=(4,), in_specs=[pl.BlockSpec(memory_spa...  12.7 us
    ppermute x2, waiting for transfers between devices, across_both(): return lax.ppermute(value, ('visit', 'patch'), pairs)  11.8 us
    pallas_call x2, Pallas kernels, build_frame(): pl.pallas_call(functools.partial(frame_kernel, far, sources), in_specs=[p...  11.5 us
    unnamed x20, local copies, waits for them, and re-layouts  7.09 us
    ppermute x3, starting transfers between devices, across_z(): return lax.ppermute(value, 'patch', [(z, (z + step) % 4) for z in range(4)])  6.03 us
  transfers between devices with their start and end apart: 16, of which 11 were waited for; matrix products, arithmetic and copies ran while one was open for 2% of the time, Pallas kernels for 4%

profile of v4, /device:TPU:1, one launch (start us, length us, event | category | flops | bytes accessed | tf_op | source)
XLA Modules:
  0.0 129.2 jit_solution(2623894012957623146)
XLA Ops:
  0.6 12.7 %shard_map.77 = (bf16[2,2,528,512]{3,2,1,0:T(8,128)(2,1)}, bf16[2,528,512]{2,1,0:T(8,128)(2,1)}, bf16[2,528,512]{2,1,0:T(8,128)(2,1)}, bf16[2,2,528,512]{3,2,1,0...) custom-call(s32[2,4]{1,0:T(2,128)} %bitcast.23, s32[2,2,4]{2,1,0:T(2,128)} %bitcast.21, ...), custom_call_target="tpu_custom_call" | custom-call | flops 6442450944 | bytes 12582912 | tf_op jit(solution)/shard_map/pallas_call | solution.py:171
  13.4 1.5 %collective-permute-start = (bf16[2,2,528,512]{3,2,1,0:T(8,128)(2,1)}, bf16[2,2,528,512]{3,2,1,0:T(8,128)(2,1)S(1)}, u32[]{:S(2)}, u32[]{:S(2)}) collective-permute-start(bf16[2,2,528,512]{3,2,1,0:T(8,128)(2,1)} %get-tuple-element.21), channel_id=1, source_target_pairs={{0,4},{4,0},{8,12},{12,8},{16,20},{20,16},{24,28},{28,24},{32,36},... | collective-permute-start | bytes 6488072 | tf_op jit(solution)/shard_map/ppermute | solution.py:46
  14.8 1.8 %collective-permute-start.1 = (bf16[2,528,512]{2,1,0:T(8,128)(2,1)}, bf16[2,528,512]{2,1,0:T(8,128)(2,1)S(1)}, u32[]{:S(2)}, u32[]{:S(2)}) collective-permute-start(bf16[2,528,512]{2,1,0:T(8,128)(2,1)} %get-tuple-element.22), channel_id=1, source_target_pairs={{0,1},{1,2},{2,3},{3,0},{4,5},{5,6},{6,7},{7,4},{8,9},{9,10},{10,1... | collective-permute-start | bytes 3244040 | tf_op jit(solution)/shard_map/ppermute | solution.py:41
  16.7 2.1 %collective-permute-start.3 = (bf16[2,528,512]{2,1,0:T(8,128)(2,1)}, bf16[2,528,512]{2,1,0:T(8,128)(2,1)S(1)}, u32[]{:S(2)}, u32[]{:S(2)}) collective-permute-start(bf16[2,528,512]{2,1,0:T(8,128)(2,1)} %get-tuple-element.25), channel_id=1, source_target_pairs={{0,3},{1,0},{2,1},{3,2},{4,7},{5,4},{6,5},{7,6},{8,11},{9,8},{10,9... | collective-permute-start | bytes 3244040 | tf_op jit(solution)/shard_map/ppermute | solution.py:41
  18.9 2.4 %copy-done.8 = bf16[2,2,528,512]{3,2,1,0:T(8,128)(2,1)S(1)} copy-done((bf16[2,2,528,512]{3,2,1,0:T(8,128)(2,1)S(1)}, bf16[2,2,528,512]{3,2,1,0:T(8,128)(2,1)}, u32[]{:S(2)}) %copy-start.8) | copy-done | bytes 2162712
  21.3 4.7 %shard_map.78 = (bf16[384,1536]{1,0:T(8,128)(2,1)S(1)}, bf16[384,1536]{1,0:T(8,128)(2,1)}, bf16[384,1536]{1,0:T(8,128)(2,1)}, bf16[384,1536]{1,0:T(8,128)(2,1)}) custom-call(bf16[2,2,528,512]{3,2,1,0:T(8,128)(2,1)S(1)} %copy-done.8, bf16[2,2,528,512]{3,2,1,0:T(8,128)(2,1)S(1)} %collective-permute-done.refs_1_), custom_call_target="tpu_custom_call" | custom-call | flops 2147483648 | bytes 7340032 | tf_op jit(solution)/shard_map/pallas_call | solution.py:262
  26.0 1.1 copy-done
  27.1 3.1 %collective-permute-start.7 = (bf16[384,1536]{1,0:T(8,128)(2,1)}, bf16[384,1536]{1,0:T(8,128)(2,1)}, u32[]{:S(2)}, u32[]{:S(2)}) collective-permute-start(bf16[384,1536]{1,0:T(8,128)(2,1)} %get-tuple-element.29), channel_id=1, source_target_pairs={{0,16},{4,68},{8,24},{12,76},{16,0},{20,84},{24,8},{28,92},{32,48}... | collective-permute-start | bytes 3538952 | tf_op jit(solution)/shard_map/ppermute | solution.py:37
  31.7 11.6 %collective-permute-done.1.refs_1_.refs_2_ = bf16[2,528,512]{2,1,0:T(8,128)(2,1)S(1)} collective-permute-done((bf16[2,528,512]{2,1,0:T(8,128)(2,1)}, bf16[2,528,512]{2,1,0:T(8,128)(2,1)S(1)}, u32[]{:S(2)}, u32[]{:S(2)}) %collective-permute-start.1) | collective-permute-done | bytes 1081376 | tf_op jit(solution)/shard_map/ppermute | solution.py:41
  43.3 1.0 copy-done.2
  44.2 1.0 copy-done.4
  45.2 3.0 %collective-permute-start.4 = (bf16[2,528,512]{2,1,0:T(8,128)(2,1)}, bf16[2,528,512]{2,1,0:T(8,128)(2,1)S(1)}, u32[]{:S(2)}, u32[]{:S(2)}) collective-permute-start(bf16[2,528,512]{2,1,0:T(8,128)(2,1)} %shard_map.80), channel_id=1, source_target_pairs={{0,7},{1,4},{2,5},{3,6},{4,3},{5,0},{6,1},{7,2},{8,15},{9,12},{10,... | collective-permute-start | bytes 3244040 | tf_op jit(solution)/shard_map/ppermute | solution.py:56
  48.3 9.2 %collective-permute-done.6 = bf16[384,1536]{1,0:T(8,128)(2,1)} collective-permute-done((bf16[384,1536]{1,0:T(8,128)(2,1)}, bf16[384,1536]{1,0:T(8,128)(2,1)}, u32[]{:S(2)}, u32[]{:S(2)}) %collective-permute-start.6) | collective-permute-done | bytes 1179680 | tf_op jit(solution)/shard_map/ppermute | solution.py:37
  57.5 2.6 %add_convert_fusion.refs_6_ = bf16[384,1536]{1,0:T(8,128)(2,1)S(1)} fusion(bf16[384,1536]{1,0:T(8,128)(2,1)} %collective-permute-done.7, bf16[384,1536]{1,0:T(8,128)(2,1)} %collective-permute-done.6, bf16[384,1536]{1,0:T(8,128)(2,1)} %collective-permute-done.5, bf16[384,1536]{1,0:T(8,128)(2,1)S(1)} %copy-done.1), kind=kLoop, calls=%fused_computation | loop fusion | flops 4718592 | bytes 5898240 | tf_op jit(solution)/shard_map/convert_element_type | solution.py:323
  60.1 11.8 %collective-permute-done.2.refs_3_ = bf16[2,528,512]{2,1,0:T(8,128)(2,1)S(1)} collective-permute-done((bf16[2,528,512]{2,1,0:T(8,128)(2,1)}, bf16[2,528,512]{2,1,0:T(8,128)(2,1)S(1)}, u32[]{:S(2)}, u32[]{:S(2)}) %collective-permute-start.2) | collective-permute-done | bytes 1081376 | tf_op jit(solution)/shard_map/ppermute | solution.py:56
  71.9 1.6 %copy-done.9 = bf16[2,2,528,512]{3,2,1,0:T(8,128)(2,1)S(1)} copy-done((bf16[2,2,528,512]{3,2,1,0:T(8,128)(2,1)S(1)}, bf16[2,2,528,512]{3,2,1,0:T(8,128)(2,1)}, u32[]{:S(2)}) %copy-start.9) | copy-done | bytes 2162712
  73.5 6.8 %shard_map.81 = (bf16[384,1536]{1,0:T(8,128)(2,1)S(1)}, bf16[384,1536]{1,0:T(8,128)(2,1)S(1)}, bf16[384,1536]{1,0:T(8,128)(2,1)S(1)}, bf16[384,1536]{1,0:T(8,128)(2,1)S(1)}) custom-call(bf16[2,2,528,512]{3,2,1,0:T(8,128)(2,1)S(1)} %copy-done.9, bf16[2,2,528,512]{3,2,1,0:T(8,128)(2,1)S(1)} %copy-done.7, bf16[2,528,512]{2,1,0:T(8,128)(2,1)S(1)} %copy-done.3, ...), custom_call_target="tpu_custom_call" | custom-call | flops 6442450944 | bytes 11534336 | tf_op jit(solution)/shard_map/pallas_call | solution.py:262
  80.3 1.4 %collective-permute-start.8 = (bf16[384,1536]{1,0:T(8,128)(2,1)S(1)}, bf16[384,1536]{1,0:T(8,128)(2,1)S(1)}, u32[]{:S(2)}, u32[]{:S(2)}) collective-permute-start(bf16[384,1536]{1,0:T(8,128)(2,1)S(1)} %get-tuple-element.31), channel_id=1, source_target_pairs={{0,8},{4,36},{8,16},{12,44},{16,24},{20,52},{24,0},{28,60},{32,40}... | collective-permute-start | bytes 3538952 | tf_op jit(solution)/shard_map/ppermute | solution.py:37
  81.7 1.5 %collective-permute-start.9 = (bf16[384,1536]{1,0:T(8,128)(2,1)S(1)}, bf16[384,1536]{1,0:T(8,128)(2,1)S(1)}, u32[]{:S(2)}, u32[]{:S(2)}) collective-permute-start(bf16[384,1536]{1,0:T(8,128)(2,1)S(1)} %get-tuple-element.32), channel_id=1, source_target_pairs={{0,24},{4,100},{8,0},{12,108},{16,8},{20,116},{24,16},{28,124},{32... | collective-permute-start | bytes 3538952 | tf_op jit(solution)/shard_map/ppermute | solution.py:37
  83.2 1.6 %collective-permute-start.10 = (bf16[384,1536]{1,0:T(8,128)(2,1)S(1)}, bf16[384,1536]{1,0:T(8,128)(2,1)S(1)}, u32[]{:S(2)}, u32[]{:S(2)}) collective-permute-start(bf16[384,1536]{1,0:T(8,128)(2,1)S(1)} %get-tuple-element.33), channel_id=1, source_target_pairs={{0,16},{4,68},{8,24},{12,76},{16,0},{20,84},{24,8},{28,92},{32,48}... | collective-permute-start | bytes 3538952 | tf_op jit(solution)/shard_map/ppermute | solution.py:37
  84.8 2.1 %collective-permute-start.11 = (bf16[384,1536]{1,0:T(8,128)(2,1)S(1)}, bf16[384,1536]{1,0:T(8,128)(2,1)S(1)}, u32[]{:S(2)}, u32[]{:S(2)}) collective-permute-start(bf16[384,1536]{1,0:T(8,128)(2,1)S(1)} %add_convert_fusion.refs_6_), channel_id=1, source_target_pairs={{0,2},{1,3},{2,0},{3,1},{4,6},{5,7},{6,4},{7,5},{8,10},{9,11},{10,... | collective-permute-start | bytes 3538952 | tf_op jit(solution)/shard_map/ppermute | solution.py:41
  86.9 10.2 %collective-permute-done.8.refs_1_ = bf16[384,1536]{1,0:T(8,128)(2,1)S(1)} collective-permute-done((bf16[384,1536]{1,0:T(8,128)(2,1)S(1)}, bf16[384,1536]{1,0:T(8,128)(2,1)S(1)}, u32[]{:S(2)}, u32[]{:S(2)}) %collective-permute-start.8) | collective-permute-done | bytes 1179680 | tf_op jit(solution)/shard_map/ppermute | solution.py:37
  97.0 12.0 %collective-permute-done.9.refs_2_ = bf16[384,1536]{1,0:T(8,128)(2,1)S(1)} collective-permute-done((bf16[384,1536]{1,0:T(8,128)(2,1)S(1)}, bf16[384,1536]{1,0:T(8,128)(2,1)S(1)}, u32[]{:S(2)}, u32[]{:S(2)}) %collective-permute-start.9) | collective-permute-done | bytes 1179680 | tf_op jit(solution)/shard_map/ppermute | solution.py:37
  109.0 1.8 %collective-permute-done.10.refs_3_ = bf16[384,1536]{1,0:T(8,128)(2,1)S(1)} collective-permute-done((bf16[384,1536]{1,0:T(8,128)(2,1)S(1)}, bf16[384,1536]{1,0:T(8,128)(2,1)S(1)}, u32[]{:S(2)}, u32[]{:S(2)}) %collective-permute-start.10) | collective-permute-done | bytes 1179680 | tf_op jit(solution)/shard_map/ppermute | solution.py:37
  110.8 1.5 %collective-permute-done.11.refs_4_ = bf16[384,1536]{1,0:T(8,128)(2,1)S(1)} collective-permute-done((bf16[384,1536]{1,0:T(8,128)(2,1)S(1)}, bf16[384,1536]{1,0:T(8,128)(2,1)S(1)}, u32[]{:S(2)}, u32[]{:S(2)}) %collective-permute-start.11) | collective-permute-done | bytes 1179680 | tf_op jit(solution)/shard_map/ppermute | solution.py:41
  113.1 4.2 %collective-permute-start.14 = (bf16[96,1536]{1,0:T(8,128)(2,1)S(1)}, bf16[96,1536]{1,0:T(8,128)(2,1)S(1)}, u32[]{:S(2)}, u32[]{:S(2)}) collective-permute-start(bf16[96,1536]{1,0:T(8,128)(2,1)S(1)} %get-tuple-element.37), channel_id=1, source_target_pairs={{0,64},{4,20},{8,72},{12,28},{16,80},{20,4},{24,88},{28,12},{32,96... | collective-permute-start | bytes 884744 | tf_op jit(solution)/shard_map/ppermute | solution.py:37
  117.8 0.9 collective-permute-start.12
  118.7 2.9 %collective-permute-done.14 = bf16[96,1536]{1,0:T(8,128)(2,1)S(1)} collective-permute-done((bf16[96,1536]{1,0:T(8,128)(2,1)S(1)}, bf16[96,1536]{1,0:T(8,128)(2,1)S(1)}, u32[]{:S(2)}, u32[]{:S(2)}) %collective-permute-start.14) | collective-permute-done | bytes 294944 | tf_op jit(solution)/shard_map/ppermute | solution.py:37
  121.7 3.9 %collective-permute-done.13 = bf16[96,1536]{1,0:T(8,128)(2,1)S(1)} collective-permute-done((bf16[96,1536]{1,0:T(8,128)(2,1)S(1)}, bf16[96,1536]{1,0:T(8,128)(2,1)S(1)}, u32[]{:S(2)}, u32[]{:S(2)}) %collective-permute-start.13) | collective-permute-done | bytes 294944 | tf_op jit(solution)/shard_map/ppermute | solution.py:37
  125.7 1.4 %collective-permute-start.15 = (f32[48,1536]{1,0:T(8,128)S(1)}, f32[48,1536]{1,0:T(8,128)S(1)}, u32[]{:S(2)}, u32[]{:S(2)}) collective-permute-start(f32[48,1536]{1,0:T(8,128)S(1)} %slice.9), channel_id=1, source_target_pairs={{0,4},{4,0},{8,12},{12,8},{16,20},{20,16},{24,28},{28,24},{32,36},... | collective-permute-start | bytes 884744 | tf_op jit(solution)/shard_map/ppermute | solution.py:46
  127.1 1.2 collective-permute-done.15
  128.3 0.9 fusion
  (30 shorter events, 3.1 us)
Async XLA Ops:
  13.4 5.6 %collective-permute-start = (bf16[2,2,528,512]{3,2,1,0:T(8,128)(2,1)}, bf16[2,2,528,512]{3,2,1,0:T(8,128)(2,1)S(1)}, u32[]{:S(2)}, u32[]{:S(2)}) collective-permute-start(bf16[2,2,528,512]{3,2,1,0:T(8,128)(2,1)} %get-tuple-element.21), channel_id=1, source_target_pairs={{0,4},{4,0},{8,12},{12,8},{16,20},{20,16},{24,28},{28,24},{32,36},... | collective-permute-start | bytes 6488072 | tf_op jit(solution)/shard_map/ppermute | solution.py:46
  14.8 28.4 %collective-permute-start.1 = (bf16[2,528,512]{2,1,0:T(8,128)(2,1)}, bf16[2,528,512]{2,1,0:T(8,128)(2,1)S(1)}, u32[]{:S(2)}, u32[]{:S(2)}) collective-permute-start(bf16[2,528,512]{2,1,0:T(8,128)(2,1)} %get-tuple-element.22), channel_id=1, source_target_pairs={{0,1},{1,2},{2,3},{3,0},{4,5},{5,6},{6,7},{7,4},{8,9},{9,10},{10,1... | collective-permute-start | bytes 3244040 | tf_op jit(solution)/shard_map/ppermute | solution.py:41
  16.7 27.6 %collective-permute-start.3 = (bf16[2,528,512]{2,1,0:T(8,128)(2,1)}, bf16[2,528,512]{2,1,0:T(8,128)(2,1)S(1)}, u32[]{:S(2)}, u32[]{:S(2)}) collective-permute-start(bf16[2,528,512]{2,1,0:T(8,128)(2,1)} %get-tuple-element.25), channel_id=1, source_target_pairs={{0,3},{1,0},{2,1},{3,2},{4,7},{5,4},{6,5},{7,6},{8,11},{9,8},{10,9... | collective-permute-start | bytes 3244040 | tf_op jit(solution)/shard_map/ppermute | solution.py:41
  18.9 7.1 %copy-start.6 = (bf16[2,2,528,512]{3,2,1,0:T(8,128)(2,1)}, bf16[2,2,528,512]{3,2,1,0:T(8,128)(2,1)S(1)}, u32[]{:S(2)}) copy-start(bf16[2,2,528,512]{3,2,1,0:T(8,128)(2,1)S(1)} %collective-permute-done.refs_1_) | copy-start | bytes 6488068
  18.9 2.4 %copy-start.8 = (bf16[2,2,528,512]{3,2,1,0:T(8,128)(2,1)S(1)}, bf16[2,2,528,512]{3,2,1,0:T(8,128)(2,1)}, u32[]{:S(2)}) copy-start(bf16[2,2,528,512]{3,2,1,0:T(8,128)(2,1)} %get-tuple-element.20.refs_0_) | copy-start | bytes 6488068
  26.0 1.1 copy-start
  27.1 21.1 %collective-permute-start.7 = (bf16[384,1536]{1,0:T(8,128)(2,1)}, bf16[384,1536]{1,0:T(8,128)(2,1)}, u32[]{:S(2)}, u32[]{:S(2)}) collective-permute-start(bf16[384,1536]{1,0:T(8,128)(2,1)} %get-tuple-element.29), channel_id=1, source_target_pairs={{0,16},{4,68},{8,24},{12,76},{16,0},{20,84},{24,8},{28,92},{32,48}... | collective-permute-start | bytes 3538952 | tf_op jit(solution)/shard_map/ppermute | solution.py:37
  30.2 27.3 %collective-permute-start.6 = (bf16[384,1536]{1,0:T(8,128)(2,1)}, bf16[384,1536]{1,0:T(8,128)(2,1)}, u32[]{:S(2)}, u32[]{:S(2)}) collective-permute-start(bf16[384,1536]{1,0:T(8,128)(2,1)} %get-tuple-element.28), channel_id=1, source_target_pairs={{0,24},{4,100},{8,0},{12,108},{16,8},{20,116},{24,16},{28,124},{32... | collective-permute-start | bytes 3538952 | tf_op jit(solution)/shard_map/ppermute | solution.py:37
  30.9 26.6 %collective-permute-start.5 = (bf16[384,1536]{1,0:T(8,128)(2,1)}, bf16[384,1536]{1,0:T(8,128)(2,1)}, u32[]{:S(2)}, u32[]{:S(2)}) collective-permute-start(bf16[384,1536]{1,0:T(8,128)(2,1)} %get-tuple-element.27), channel_id=1, source_target_pairs={{0,8},{4,36},{8,16},{12,44},{16,24},{20,52},{24,0},{28,60},{32,40}... | collective-permute-start | bytes 3538952 | tf_op jit(solution)/shard_map/ppermute | solution.py:37
  43.3 1.0 copy-start.2
  44.2 27.6 %collective-permute-start.2 = (bf16[2,528,512]{2,1,0:T(8,128)(2,1)}, bf16[2,528,512]{2,1,0:T(8,128)(2,1)S(1)}, u32[]{:S(2)}, u32[]{:S(2)}) collective-permute-start(bf16[2,528,512]{2,1,0:T(8,128)(2,1)} %shard_map.79), channel_id=1, source_target_pairs={{0,5},{1,6},{2,7},{3,4},{4,1},{5,2},{6,3},{7,0},{8,13},{9,14},{10,... | collective-permute-start | bytes 3244040 | tf_op jit(solution)/shard_map/ppermute | solution.py:56
  44.2 1.0 copy-start.4
  45.2 12.3 %copy-start.1 = (bf16[384,1536]{1,0:T(8,128)(2,1)S(1)}, bf16[384,1536]{1,0:T(8,128)(2,1)}, u32[]{:S(2)}) copy-start(bf16[384,1536]{1,0:T(8,128)(2,1)} %copy-done) | copy-start | bytes 3538948
  45.2 26.6 %copy-start.3 = (bf16[2,528,512]{2,1,0:T(8,128)(2,1)S(1)}, bf16[2,528,512]{2,1,0:T(8,128)(2,1)}, u32[]{:S(2)}) copy-start(bf16[2,528,512]{2,1,0:T(8,128)(2,1)} %copy-done.2) | copy-start | bytes 3244036
  45.2 26.6 %copy-start.5 = (bf16[2,528,512]{2,1,0:T(8,128)(2,1)S(1)}, bf16[2,528,512]{2,1,0:T(8,128)(2,1)}, u32[]{:S(2)}) copy-start(bf16[2,528,512]{2,1,0:T(8,128)(2,1)} %copy-done.4) | copy-start | bytes 3244036
  45.2 26.6 %copy-start.7 = (bf16[2,2,528,512]{3,2,1,0:T(8,128)(2,1)S(1)}, bf16[2,2,528,512]{3,2,1,0:T(8,128)(2,1)}, u32[]{:S(2)}) copy-start(bf16[2,2,528,512]{3,2,1,0:T(8,128)(2,1)} %copy-done.6) | copy-start | bytes 6488068
  45.2 26.6 %collective-permute-start.4 = (bf16[2,528,512]{2,1,0:T(8,128)(2,1)}, bf16[2,528,512]{2,1,0:T(8,128)(2,1)S(1)}, u32[]{:S(2)}, u32[]{:S(2)}) collective-permute-start(bf16[2,528,512]{2,1,0:T(8,128)(2,1)} %shard_map.80), channel_id=1, source_target_pairs={{0,7},{1,4},{2,5},{3,6},{4,3},{5,0},{6,1},{7,2},{8,15},{9,12},{10,... | collective-permute-start | bytes 3244040 | tf_op jit(solution)/shard_map/ppermute | solution.py:56
  71.9 1.6 %copy-start.9 = (bf16[2,2,528,512]{3,2,1,0:T(8,128)(2,1)S(1)}, bf16[2,2,528,512]{3,2,1,0:T(8,128)(2,1)}, u32[]{:S(2)}) copy-start(bf16[2,2,528,512]{3,2,1,0:T(8,128)(2,1)} %get-tuple-element.20.refs_0_) | copy-start | bytes 6488068
  80.3 16.7 %collective-permute-start.8 = (bf16[384,1536]{1,0:T(8,128)(2,1)S(1)}, bf16[384,1536]{1,0:T(8,128)(2,1)S(1)}, u32[]{:S(2)}, u32[]{:S(2)}) collective-permute-start(bf16[384,1536]{1,0:T(8,128)(2,1)S(1)} %get-tuple-element.31), channel_id=1, source_target_pairs={{0,8},{4,36},{8,16},{12,44},{16,24},{20,52},{24,0},{28,60},{32,40}... | collective-permute-start | bytes 3538952 | tf_op jit(solution)/shard_map/ppermute | solution.py:37
  81.7 27.3 %collective-permute-start.9 = (bf16[384,1536]{1,0:T(8,128)(2,1)S(1)}, bf16[384,1536]{1,0:T(8,128)(2,1)S(1)}, u32[]{:S(2)}, u32[]{:S(2)}) collective-permute-start(bf16[384,1536]{1,0:T(8,128)(2,1)S(1)} %get-tuple-element.32), channel_id=1, source_target_pairs={{0,24},{4,100},{8,0},{12,108},{16,8},{20,116},{24,16},{28,124},{32... | collective-permute-start | bytes 3538952 | tf_op jit(solution)/shard_map/ppermute | solution.py:37
  83.2 27.6 %collective-permute-start.10 = (bf16[384,1536]{1,0:T(8,128)(2,1)S(1)}, bf16[384,1536]{1,0:T(8,128)(2,1)S(1)}, u32[]{:S(2)}, u32[]{:S(2)}) collective-permute-start(bf16[384,1536]{1,0:T(8,128)(2,1)S(1)} %get-tuple-element.33), channel_id=1, source_target_pairs={{0,16},{4,68},{8,24},{12,76},{16,0},{20,84},{24,8},{28,92},{32,48}... | collective-permute-start | bytes 3538952 | tf_op jit(solution)/shard_map/ppermute | solution.py:37
  84.8 27.6 %collective-permute-start.11 = (bf16[384,1536]{1,0:T(8,128)(2,1)S(1)}, bf16[384,1536]{1,0:T(8,128)(2,1)S(1)}, u32[]{:S(2)}, u32[]{:S(2)}) collective-permute-start(bf16[384,1536]{1,0:T(8,128)(2,1)S(1)} %add_convert_fusion.refs_6_), channel_id=1, source_target_pairs={{0,2},{1,3},{2,0},{3,1},{4,6},{5,7},{6,4},{7,5},{8,10},{9,11},{10,... | collective-permute-start | bytes 3538952 | tf_op jit(solution)/shard_map/ppermute | solution.py:41
  113.1 8.6 %collective-permute-start.14 = (bf16[96,1536]{1,0:T(8,128)(2,1)S(1)}, bf16[96,1536]{1,0:T(8,128)(2,1)S(1)}, u32[]{:S(2)}, u32[]{:S(2)}) collective-permute-start(bf16[96,1536]{1,0:T(8,128)(2,1)S(1)} %get-tuple-element.37), channel_id=1, source_target_pairs={{0,64},{4,20},{8,72},{12,28},{16,80},{20,4},{24,88},{28,12},{32,96... | collective-permute-start | bytes 884744 | tf_op jit(solution)/shard_map/ppermute | solution.py:37
  117.3 8.3 %collective-permute-start.13 = (bf16[96,1536]{1,0:T(8,128)(2,1)S(1)}, bf16[96,1536]{1,0:T(8,128)(2,1)S(1)}, u32[]{:S(2)}, u32[]{:S(2)}) collective-permute-start(bf16[96,1536]{1,0:T(8,128)(2,1)S(1)} %get-tuple-element.36), channel_id=1, source_target_pairs={{0,96},{4,28},{8,104},{12,4},{16,112},{20,12},{24,120},{28,20},{32... | collective-permute-start | bytes 884744 | tf_op jit(solution)/shard_map/ppermute | solution.py:37
  117.8 7.7 %collective-permute-start.12 = (bf16[96,1536]{1,0:T(8,128)(2,1)S(1)}, bf16[96,1536]{1,0:T(8,128)(2,1)S(1)}, u32[]{:S(2)}, u32[]{:S(2)}) collective-permute-start(bf16[96,1536]{1,0:T(8,128)(2,1)S(1)} %get-tuple-element.35), channel_id=1, source_target_pairs={{0,32},{4,12},{8,40},{12,20},{16,48},{20,28},{24,56},{28,4},{32,64... | collective-permute-start | bytes 884744 | tf_op jit(solution)/shard_map/ppermute | solution.py:37
  125.7 2.6 %collective-permute-start.15 = (f32[48,1536]{1,0:T(8,128)S(1)}, f32[48,1536]{1,0:T(8,128)S(1)}, u32[]{:S(2)}, u32[]{:S(2)}) collective-permute-start(f32[48,1536]{1,0:T(8,128)S(1)} %slice.9), channel_id=1, source_target_pairs={{0,4},{4,0},{8,12},{12,8},{16,20},{20,16},{24,28},{28,24},{32,36},... | collective-permute-start | bytes 884744 | tf_op jit(solution)/shard_map/ppermute | solution.py:46

commit v5 on v4

--- a/solution.py
+++ b/solution.py
@@ -70,10 +70,18 @@
 
 
 def match_kernel(
-    patches_in, corners_in, taps_in, coeffs_in, image, variance, stays, plus, minus, swaps, swap_plus, swap_minus,
-    patches, corners, taps, coeffs, across, down, lanes, factors, numer, weight, in_sems, sems, wsems,
+    patches_in, corners_in, taps_in, coeffs_in, images_in, variances_in, stays, plus, minus, swaps, swap_plus, swap_minus,
+    patches, corners, taps, coeffs, images, variances, across, down, lanes, factors, numer, weight,
+    in_sems, tile_sems, sems, wsems,
 ):
     tile = pl.program_id(0)
+    loads = [
+        [
+            pltpu.make_async_copy(images_in.at[index], images.at[index], tile_sems.at[0, index]),
+            pltpu.make_async_copy(variances_in.at[index], variances.at[index], tile_sems.at[1, index]),
+        ]
+        for index in (0, 1, 2, 3, tile)
+    ]
     _, _, core, z = position()
 
     @pl.when(tile == 0)
@@ -82,6 +90,9 @@
         copies = [pltpu.make_async_copy(a, b, in_sems.at[k]) for k, (a, b) in enumerate(small)]
         for copy in copies:
             copy.start()
+        for pair in loads[:4]:
+            for copy in pair:
+                copy.start()
         for copy in copies:
             copy.wait()
         lanes[...] = jnp.zeros_like(lanes)
@@ -111,13 +122,15 @@
     columns = lax.broadcasted_iota(jnp.int32, (1, TILE), 1).astype(F32)
     rows = (rows - (TILE - 1) / 2.0) / (TILE / 2.0)
     columns = (columns - (TILE - 1) / 2.0) / (TILE / 2.0)
+    for copy in loads[4]:
+        copy.wait()
     total = jnp.zeros((TILE, TILE), F32)
     for basis in range(BASES):
-        middle = jnp.dot(image[0], across[basis], preferred_element_type=F32).astype(BF16)
+        middle = jnp.dot(images[tile], across[basis], preferred_element_type=F32).astype(BF16)
         smoothed = jnp.dot(down[basis], middle, preferred_element_type=F32)
         c0, c1, c2 = (factors[basis, pl.ds(tile, 1), k : k + 1] for k in range(3))
         total += ((c0 + c1 * columns) + c2 * rows) * smoothed
-    inverse = 1.0 / variance[0].astype(F32)
+    inverse = 1.0 / variances[tile].astype(F32)
     numer[tile, 0:TILE] = (inverse * total).astype(BF16)
     weight[tile, 0:TILE] = inverse.astype(BF16)
     named, tops, lefts = [], [], []
@@ -171,14 +184,7 @@
     return pl.pallas_call(
         match_kernel,
         grid=(4,),
-        in_specs=[
-            pl.BlockSpec(memory_space=pl.ANY),
-            pl.BlockSpec(memory_space=pl.ANY),
-            pl.BlockSpec(memory_space=pl.ANY),
-            pl.BlockSpec(memory_space=pl.ANY),
-            pl.BlockSpec((1, TILE, TILE), lambda t: (t, 0, 0)),
-            pl.BlockSpec((1, TILE, TILE), lambda t: (t, 0, 0)),
-        ],
+        in_specs=[pl.BlockSpec(memory_space=pltpu.HBM)] * 6,
         out_specs=[pl.BlockSpec(memory_space=pl.ANY)] * 6,
         out_shape=[quad, pair, pair, quad, pair, pair],
         scratch_shapes=[
@@ -186,6 +192,8 @@
             pltpu.SMEM((2, 2, 4), jnp.int32),
             pltpu.VMEM((BASES, 2, TAPS), BF16),
             pltpu.VMEM((BASES, 4, 3), BF16),
+            pltpu.VMEM((4, TILE, TILE), BF16),
+            pltpu.VMEM((4, TILE, TILE), BF16),
             pltpu.VMEM((BASES, TILE, TILE), BF16),
             pltpu.VMEM((BASES, TILE, TILE), BF16),
             pltpu.VMEM((8, 3 * LANES), F32),
@@ -193,19 +201,36 @@
             pltpu.VMEM((4, TILE + 16, TILE), BF16),
             pltpu.VMEM((4, TILE + 16, TILE), BF16),
             pltpu.SemaphoreType.DMA((4,)),
+            pltpu.SemaphoreType.DMA((2, 4)),
             pltpu.SemaphoreType.DMA((4, 2)),
             pltpu.SemaphoreType.DMA((4, 2)),
         ],
-        compiler_params=pltpu.CompilerParams(vmem_limit_bytes=62 << 20),
+        compiler_params=pltpu.CompilerParams(vmem_limit_bytes=60 << 20),
         cost_estimate=pl.CostEstimate(flops=6 << 30, bytes_accessed=12 << 20, transcendentals=0),
     )(patches, corners, taps, coeffs, images, variances)
 
 
-def frame_kernel(far, sources, *refs):
-    stacks, outs, frame = refs[:sources], refs[-5:-1], refs[-1]
-    y, x, core, z = position()
-    patch = lax.rem(z + 2 * far, 4).astype(F32)
+def start_kernel(*refs):
+    stacks, frame = refs[:-1], refs[-1]
     frame[...] = jnp.zeros_like(frame)
+    add_tiles(0, stacks, frame)
+
+
+def finish_kernel(count, *refs):
+    stacks, outs, frame = refs[1 : 1 + count], refs[-5:-1], refs[-1]
+    add_tiles(0, stacks, frame)
+    pack(frame, outs)
+
+
+def opposite_kernel(*refs):
+    stacks, outs, frame = refs[:-5], refs[-5:-1], refs[-1]
+    frame[...] = jnp.zeros_like(frame)
+    add_tiles(1, stacks, frame)
+    pack(frame, outs)
+
+
+def add_tiles(far, stacks, frame):
+    patch = lax.rem(lax.axis_index("patch") + 2 * far, 4).astype(F32)
     inner = lax.broadcasted_iota(jnp.int32, (1, ROWS, LANES), 1)
     lane = lax.broadcasted_iota(jnp.int32, (1, ROWS, LANES), 2)
     groups = TILE // ROWS
@@ -238,14 +263,17 @@
             )
             frame[where] += jnp.where(inner >= lead, lower, upper)
 
-    for source, stack in enumerate(stacks):
-
-        def both(slot, carry, stack=stack, source=source):
-            add(stack.at[far, slot] if source < 2 else stack.at[slot])
+    for stack in stacks:
+
+        def both(slot, carry, stack=stack):
+            add(stack.at[far, slot] if len(stack.shape) == 4 else stack.at[slot])
             return carry
 
         lax.fori_loop(0, 2, both, 0)
 
+
+def pack(frame, outs):
+    y, x, core, _ = position()
     for out in range(4):
         for part in range(4):
             dx, dy = jnp.where(core == 0, out, part), jnp.where(core == 0, part, out)
@@ -256,27 +284,34 @@
                 outs[out][at : at + STRIP, :] = strip.reshape(STRIP, PATCH_PIX).astype(BF16)
 
 
-def build_frame(far, stacks, after=()):
-    sources = len(stacks)
-    out = jax.ShapeDtypeStruct((SLAB, PATCH_PIX), BF16)
+SLABS = [jax.ShapeDtypeStruct((SLAB, PATCH_PIX), BF16)] * 4
+FRAME = (PATCH_PIX // ROWS + 1, ROWS, PATCH_PIX)
+
+
+def frame_options(tiles):
+    cost = pl.CostEstimate(flops=tiles << 29, bytes_accessed=(5 + tiles) << 20, transcendentals=0)
+    return dict(compiler_params=pltpu.CompilerParams(vmem_limit_bytes=36 << 20), cost_estimate=cost)
+
+
+def opposite_frame(stacks):
     return pl.pallas_call(
-        functools.partial(frame_kernel, far, sources),
-        in_specs=[pl.BlockSpec(memory_space=pltpu.VMEM)] * sources + [pl.BlockSpec(memory_space=pl.ANY)] * len(after),
-        out_shape=[out] * 4,
-        scratch_shapes=[pltpu.VMEM((PATCH_PIX // ROWS + 1, ROWS, PATCH_PIX), F32)],
-        compiler_params=pltpu.CompilerParams(vmem_limit_bytes=40 << 20),
-        cost_estimate=pl.CostEstimate(flops=sources << 30, bytes_accessed=(5 + sources) << 20, transcendentals=0),
-    )(*stacks, *after)
-
-
-def tie(value, *after):
+        opposite_kernel, out_shape=SLABS, scratch_shapes=[pltpu.VMEM(FRAME, F32)], **frame_options(4)
+    )(*stacks)
+
+
+def start_frame(stacks):
+    return pl.pallas_call(start_kernel, out_shape=jax.ShapeDtypeStruct(FRAME, F32), **frame_options(8))(*stacks)
+
+
+def finish_frame(frame, stacks, after):
+    spaces = [pltpu.VMEM] * (1 + len(stacks)) + [pl.ANY]
     return pl.pallas_call(
-        lambda *refs: None,
-        in_specs=[pl.BlockSpec(memory_space=pl.ANY)] * (1 + len(after)),
-        out_specs=pl.BlockSpec(memory_space=pl.ANY),
-        out_shape=jax.ShapeDtypeStruct(value.shape, value.dtype),
-        input_output_aliases={0: 0},
-    )(value, *after)
+        functools.partial(finish_kernel, len(stacks)),
+        in_specs=[pl.BlockSpec(memory_space=space) for space in spaces],
+        out_shape=SLABS + [jax.ShapeDtypeStruct(FRAME, F32)],
+        input_output_aliases={0: 4},
+        **frame_options(4),
+    )(frame, *stacks, after)[:4]
 
 
 def sum_kernel(count, *refs):
@@ -319,12 +354,13 @@
     )
     swapped = across_core(swaps)
     below, above = across_z(plus, 1), across_z(minus, 3)
-    opposite = build_frame(1, [stays, swapped])
+    opposite = opposite_frame([stays, swapped])
     summed = add_up(spread(opposite, False)).astype(BF16)
     passed = across_z(summed, 2)
-    below_too = across_both(tie(swap_plus, below, opposite[0]), 1)
-    above_too = across_both(tie(swap_minus, above, opposite[0]), 3)
-    own = build_frame(0, [stays, swapped, below, below_too, above, above_too], [summed])
+    below_too = across_both(lax.optimization_barrier((swap_plus, below, opposite[0]))[0], 1)
+    above_too = across_both(lax.optimization_barrier((swap_minus, above, opposite[0]))[0], 3)
+    begun = start_frame([stays, swapped, below, above])
+    own = finish_frame(begun, [below_too, above_too], summed)
     pieces = sum_slabs(spread(own, False) + [passed])
     rows = add_up(spread(pieces, True))
     keep, got = rows[:STRIP], across_core(rows[STRIP:])

time: 129 us -> 126 us (0.977)
  waiting for transfers between devices: 66.2 us -> 73 us
  local copies, waits for them, and re-layouts: 7.11 us -> 1.63 us
  other arithmetic: 3.56 us -> 1.58 us
  Pallas kernels: 25 us -> 23.7 us
    ppermute x2, waiting for transfers between devices: 11.8 us -> 18.3 us  [across_both(): return lax.ppermute(value, ('visit', 'patch'), pairs)]
    unnamed x20 -> x4, local copies, waits for them, and re-layouts: 7.09 us -> 1.61 us
    ppermute x3, waiting for transfers between devices: 13.1 us -> 17.9 us  [across_z(): return lax.ppermute(value, 'patch', [(z, (z + step) % 4) for z in range(4)])]
    ppermute x9, waiting for transfers between devices: 40 us -> 35.3 us  [turn(): return lax.ppermute(value, 'visit', pairs)]
    ppermute x3, starting transfers between devices: 6.03 us -> 3.86 us  [across_z(): return lax.ppermute(value, 'patch', [(z, (z + step) % 4) for z in range(4)])]
    convert_element_type x1, other arithmetic: 2.56 us -> 0.58 us  [body(): summed = add_up(spread(opposite, False)).astype(BF16)]
    pallas_call x4 -> x3, Pallas kernels: 11.5 us -> 9.87 us  [the longest x1 4.46 us: start_frame(): pl.pallas_call(start_kernel, out_shape=jax.ShapeDtypeStruct(FRAME, F32),...]
  transfers between devices with their start and end apart: 16 -> 16, of which waited for: 11 -> 14; matrix products, arithmetic and copies ran while one was open for 2% -> 0% of each run, Pallas kernels for 4% -> 6%
where the time goes in v5:
time: 126 us
  waiting for transfers between devices  73 us (58%)
  starting transfers between devices  25.4 us (20%)
  Pallas kernels  23.7 us (19%)
  local copies, waits for them, and re-layouts  1.63 us (1%)
  other arithmetic  1.58 us (1%)
    ppermute x9, waiting for transfers between devices, turn(): return lax.ppermute(value, 'visit', pairs)  35.3 us
    ppermute x2, waiting for transfers between devices, across_both(): return lax.ppermute(value, ('visit', 'patch'), pairs)  18.3 us
    ppermute x3, waiting for transfers between devices, across_z(): return lax.ppermute(value, 'patch', [(z, (z + step) % 4) for z in range(4)])  17.9 us
    ppermute x9, starting transfers between devices, turn(): return lax.ppermute(value, 'visit', pairs)  13.6 us
    pallas_call x1, Pallas kernels, match_tiles(): pl.pallas_call(match_kernel, grid=(4,), in_specs=[pl.BlockSpec(memory_spa...  13.1 us
    pallas_call x1, Pallas kernels, start_frame(): pl.pallas_call(start_kernel, out_shape=jax.ShapeDtypeStruct(FRAME, F32),...  4.46 us
    ppermute x2, starting transfers between devices, across_both(): return lax.ppermute(value, ('visit', 'patch'), pairs)  4.05 us
    ppermute x2, starting transfers between devices, across_core(): return lax.ppermute(value, 'visit', pairs)  3.9 us
  transfers between devices with their start and end apart: 16, of which 14 were waited for; matrix products, arithmetic and copies ran while one was open for 0% of the time, Pallas kernels for 6%

profile of v5, /device:TPU:1, one launch (start us, length us, event | category | flops | bytes accessed | tf_op | source)
XLA Modules:
  0.0 126.0 jit_solution(16996993116074289480)
XLA Ops:
  0.6 13.1 %shard_map.77 = (bf16[2,2,528,512]{3,2,1,0:T(8,128)(2,1)}, bf16[2,528,512]{2,1,0:T(8,128)(2,1)}, bf16[2,528,512]{2,1,0:T(8,128)(2,1)}, bf16[2,2,528,512]{3,2,1,0...) custom-call(s32[2,4]{1,0:T(2,128)} %bitcast.23, s32[2,2,4]{2,1,0:T(2,128)} %bitcast.21, ...), custom_call_target="tpu_custom_call" | custom-call | flops 6442450944 | bytes 12582912 | tf_op jit(solution)/shard_map/pallas_call | solution.py:184
  13.8 1.5 %collective-permute-start = (bf16[2,2,528,512]{3,2,1,0:T(8,128)(2,1)}, bf16[2,2,528,512]{3,2,1,0:T(8,128)(2,1)S(1)}, u32[]{:S(2)}, u32[]{:S(2)}) collective-permute-start(bf16[2,2,528,512]{3,2,1,0:T(8,128)(2,1)} %get-tuple-element.23), channel_id=1, source_target_pairs={{0,4},{4,0},{8,12},{12,8},{16,20},{20,16},{24,28},{28,24},{32,36},... | collective-permute-start | bytes 6488072 | tf_op jit(solution)/shard_map/ppermute | solution.py:46
  15.2 3.9 %collective-permute-start.2 = (bf16[2,528,512]{2,1,0:T(8,128)(2,1)}, bf16[2,528,512]{2,1,0:T(8,128)(2,1)S(1)}, u32[]{:S(2)}, u32[]{:S(2)}) collective-permute-start(bf16[2,528,512]{2,1,0:T(8,128)(2,1)} %get-tuple-element.25), channel_id=1, source_target_pairs={{0,3},{1,0},{2,1},{3,2},{4,7},{5,4},{6,5},{7,6},{8,11},{9,8},{10,9... | collective-permute-start | bytes 3244040 | tf_op jit(solution)/shard_map/ppermute | solution.py:41
  19.3 1.6 %copy-done = bf16[2,2,528,512]{3,2,1,0:T(8,128)(2,1)S(1)} copy-done((bf16[2,2,528,512]{3,2,1,0:T(8,128)(2,1)S(1)}, bf16[2,2,528,512]{3,2,1,0:T(8,128)(2,1)}, u32[]{:S(2)}) %copy-start) | copy-done | bytes 2162712
  20.9 3.0 %shard_map.79 = (bf16[384,1536]{1,0:T(8,128)(2,1)S(1)}, bf16[384,1536]{1,0:T(8,128)(2,1)S(1)}, bf16[384,1536]{1,0:T(8,128)(2,1)S(1)}, bf16[384,1536]{1,0:T(8,128)(2,1)S(1)}) custom-call(bf16[2,2,528,512]{3,2,1,0:T(8,128)(2,1)S(1)} %copy-done, bf16[2,2,528,512]{3,2,1,0:T(8,128)(2,1)S(1)} %collective-permute-done.refs_1_), custom_call_target="tpu_custom_call" | custom-call | flops 2147483648 | bytes 9437184 | tf_op jit(solution)/shard_map/pallas_call | solution.py:297
  23.9 1.4 %collective-permute-start.5 = (bf16[384,1536]{1,0:T(8,128)(2,1)S(1)}, bf16[384,1536]{1,0:T(8,128)(2,1)S(1)}, u32[]{:S(2)}, u32[]{:S(2)}) collective-permute-start(bf16[384,1536]{1,0:T(8,128)(2,1)S(1)} %get-tuple-element.31), channel_id=1, source_target_pairs={{0,8},{4,36},{8,16},{12,44},{16,24},{20,52},{24,0},{28,60},{32,40}... | collective-permute-start | bytes 3538952 | tf_op jit(solution)/shard_map/ppermute | solution.py:37
  25.4 1.6 %collective-permute-start.6 = (bf16[384,1536]{1,0:T(8,128)(2,1)S(1)}, bf16[384,1536]{1,0:T(8,128)(2,1)S(1)}, u32[]{:S(2)}, u32[]{:S(2)}) collective-permute-start(bf16[384,1536]{1,0:T(8,128)(2,1)S(1)} %get-tuple-element.32), channel_id=1, source_target_pairs={{0,24},{4,100},{8,0},{12,108},{16,8},{20,116},{24,16},{28,124},{32... | collective-permute-start | bytes 3538952 | tf_op jit(solution)/shard_map/ppermute | solution.py:37
  27.0 1.5 %collective-permute-start.7 = (bf16[384,1536]{1,0:T(8,128)(2,1)S(1)}, bf16[384,1536]{1,0:T(8,128)(2,1)S(1)}, u32[]{:S(2)}, u32[]{:S(2)}) collective-permute-start(bf16[384,1536]{1,0:T(8,128)(2,1)S(1)} %get-tuple-element.33), channel_id=1, source_target_pairs={{0,16},{4,68},{8,24},{12,76},{16,0},{20,84},{24,8},{28,92},{32,48}... | collective-permute-start | bytes 3538952 | tf_op jit(solution)/shard_map/ppermute | solution.py:37
  28.5 14.1 %collective-permute-done.2.refs_3_ = bf16[2,528,512]{2,1,0:T(8,128)(2,1)S(1)} collective-permute-done((bf16[2,528,512]{2,1,0:T(8,128)(2,1)}, bf16[2,528,512]{2,1,0:T(8,128)(2,1)S(1)}, u32[]{:S(2)}, u32[]{:S(2)}) %collective-permute-start.2) | collective-permute-done | bytes 1081376 | tf_op jit(solution)/shard_map/ppermute | solution.py:41
  42.6 4.1 %collective-permute-start.4 = (bf16[2,528,512]{2,1,0:T(8,128)(2,1)}, bf16[2,528,512]{2,1,0:T(8,128)(2,1)S(1)}, u32[]{:S(2)}, u32[]{:S(2)}) collective-permute-start(bf16[2,528,512]{2,1,0:T(8,128)(2,1)} %get-tuple-element.30), channel_id=1, source_target_pairs={{0,7},{1,4},{2,5},{3,6},{4,3},{5,0},{6,1},{7,2},{8,15},{9,12},{10,... | collective-permute-start | bytes 3244040 | tf_op jit(solution)/shard_map/ppermute | solution.py:56
  46.7 4.5 %shard_map.78.refs_0_ = f32[193,8,1536]{2,1,0:T(8,128)S(1)} custom-call(bf16[2,2,528,512]{3,2,1,0:T(8,128)(2,1)S(1)} %copy-done, bf16[2,2,528,512]{3,2,1,0:T(8,128)(2,1)S(1)} %collective-permute-done.refs_1_, bf16[2,528,512]{2,1,0:T(8,128)(2,1)S(1)} %collective-permute-done.1.refs_2_, bf16[2,528,512]{2,1,0:T(8,128)(2,1)S(1)} %collective-permute-done.2.refs_3_), custom_call_target="tpu_custom_call" | custom-call | flops 4294967296 | bytes 13631488 | tf_op jit(solution)/shard_map/pallas_call | solution.py:303
  51.1 1.6 %collective-permute-done.6 = bf16[384,1536]{1,0:T(8,128)(2,1)S(1)} collective-permute-done((bf16[384,1536]{1,0:T(8,128)(2,1)S(1)}, bf16[384,1536]{1,0:T(8,128)(2,1)S(1)}, u32[]{:S(2)}, u32[]{:S(2)}) %collective-permute-start.6) | collective-permute-done | bytes 1179680 | tf_op jit(solution)/shard_map/ppermute | solution.py:37
  52.7 1.8 %collective-permute-done.7 = bf16[384,1536]{1,0:T(8,128)(2,1)S(1)} collective-permute-done((bf16[384,1536]{1,0:T(8,128)(2,1)S(1)}, bf16[384,1536]{1,0:T(8,128)(2,1)S(1)}, u32[]{:S(2)}, u32[]{:S(2)}) %collective-permute-start.7) | collective-permute-done | bytes 1179680 | tf_op jit(solution)/shard_map/ppermute | solution.py:37
  54.6 0.6 add_convert_fusion.refs_3_
  55.2 15.3 %collective-permute-done.4.refs_2_ = bf16[2,528,512]{2,1,0:T(8,128)(2,1)S(1)} collective-permute-done((bf16[2,528,512]{2,1,0:T(8,128)(2,1)}, bf16[2,528,512]{2,1,0:T(8,128)(2,1)S(1)}, u32[]{:S(2)}, u32[]{:S(2)}) %collective-permute-start.4) | collective-permute-done | bytes 1081376 | tf_op jit(solution)/shard_map/ppermute | solution.py:56
  70.5 3.0 %collective-permute-done.3.refs_1_ = bf16[2,528,512]{2,1,0:T(8,128)(2,1)S(1)} collective-permute-done((bf16[2,528,512]{2,1,0:T(8,128)(2,1)S(1)}, bf16[2,528,512]{2,1,0:T(8,128)(2,1)S(1)}, u32[]{:S(2)}, u32[]{:S(2)}) %collective-permute-start.3) | collective-permute-done | bytes 1081376 | tf_op jit(solution)/shard_map/ppermute | solution.py:56
  73.5 2.4 %shard_map.80 = (bf16[384,1536]{1,0:T(8,128)(2,1)S(1)}, bf16[384,1536]{1,0:T(8,128)(2,1)S(1)}, bf16[384,1536]{1,0:T(8,128)(2,1)S(1)}, bf16[384,1536]{1,0:T(8,128)(2,1)S(1)}, f32[193,8,1536]{2,1,0:T(8,128)S(1)}) custom-call(f32[193,8,1536]{2,1,0:T(8,128)S(1)} %shard_map.78.refs_0_, ...), custom_call_target="tpu_custom_call", output_to_operand_aliasing={{4}: (0, {})} | custom-call | flops 2147483648 | bytes 9437184 | tf_op jit(solution)/shard_map/pallas_call | solution.py:308
  75.9 3.0 %collective-permute-start.10 = (bf16[384,1536]{1,0:T(8,128)(2,1)S(1)}, bf16[384,1536]{1,0:T(8,128)(2,1)S(1)}, u32[]{:S(2)}, u32[]{:S(2)}) collective-permute-start(bf16[384,1536]{1,0:T(8,128)(2,1)S(1)} %get-tuple-element.37), channel_id=1, source_target_pairs={{0,16},{4,68},{8,24},{12,76},{16,0},{20,84},{24,8},{28,92},{32,48}... | collective-permute-start | bytes 3538952 | tf_op jit(solution)/shard_map/ppermute | solution.py:37
  78.8 0.5 collective-permute-start.8
  79.3 2.2 %collective-permute-start.9 = (bf16[384,1536]{1,0:T(8,128)(2,1)S(1)}, bf16[384,1536]{1,0:T(8,128)(2,1)S(1)}, u32[]{:S(2)}, u32[]{:S(2)}) collective-permute-start(bf16[384,1536]{1,0:T(8,128)(2,1)S(1)} %get-tuple-element.36), channel_id=1, source_target_pairs={{0,24},{4,100},{8,0},{12,108},{16,8},{20,116},{24,16},{28,124},{32... | collective-permute-start | bytes 3538952 | tf_op jit(solution)/shard_map/ppermute | solution.py:37
  81.5 11.3 %collective-permute-done.10.refs_3_ = bf16[384,1536]{1,0:T(8,128)(2,1)S(1)} collective-permute-done((bf16[384,1536]{1,0:T(8,128)(2,1)S(1)}, bf16[384,1536]{1,0:T(8,128)(2,1)S(1)}, u32[]{:S(2)}, u32[]{:S(2)}) %collective-permute-start.10) | collective-permute-done | bytes 1179680 | tf_op jit(solution)/shard_map/ppermute | solution.py:37
  92.8 12.6 %collective-permute-done.8.refs_1_ = bf16[384,1536]{1,0:T(8,128)(2,1)S(1)} collective-permute-done((bf16[384,1536]{1,0:T(8,128)(2,1)S(1)}, bf16[384,1536]{1,0:T(8,128)(2,1)S(1)}, u32[]{:S(2)}, u32[]{:S(2)}) %collective-permute-start.8) | collective-permute-done | bytes 1179680 | tf_op jit(solution)/shard_map/ppermute | solution.py:37
  105.9 3.8 %collective-permute-done.11.refs_4_ = bf16[384,1536]{1,0:T(8,128)(2,1)S(1)} collective-permute-done((bf16[384,1536]{1,0:T(8,128)(2,1)S(1)}, bf16[384,1536]{1,0:T(8,128)(2,1)S(1)}, u32[]{:S(2)}, u32[]{:S(2)}) %collective-permute-start.11) | collective-permute-done | bytes 1179680 | tf_op jit(solution)/shard_map/ppermute | solution.py:41
  109.6 0.7 shard_map.81
  110.4 1.5 %collective-permute-start.12 = (bf16[96,1536]{1,0:T(8,128)(2,1)S(1)}, bf16[96,1536]{1,0:T(8,128)(2,1)S(1)}, u32[]{:S(2)}, u32[]{:S(2)}) collective-permute-start(bf16[96,1536]{1,0:T(8,128)(2,1)S(1)} %get-tuple-element.39), channel_id=1, source_target_pairs={{0,32},{4,12},{8,40},{12,20},{16,48},{20,28},{24,56},{28,4},{32,64... | collective-permute-start | bytes 884744 | tf_op jit(solution)/shard_map/ppermute | solution.py:37
  111.9 1.2 collective-permute-start.13
  113.1 0.7 collective-permute-start.14
  113.8 3.7 %collective-permute-done.12 = bf16[96,1536]{1,0:T(8,128)(2,1)S(1)} collective-permute-done((bf16[96,1536]{1,0:T(8,128)(2,1)S(1)}, bf16[96,1536]{1,0:T(8,128)(2,1)S(1)}, u32[]{:S(2)}, u32[]{:S(2)}) %collective-permute-start.12) | collective-permute-done | bytes 294944 | tf_op jit(solution)/shard_map/ppermute | solution.py:37
  117.8 3.5 %collective-permute-done.14 = bf16[96,1536]{1,0:T(8,128)(2,1)S(1)} collective-permute-done((bf16[96,1536]{1,0:T(8,128)(2,1)S(1)}, bf16[96,1536]{1,0:T(8,128)(2,1)S(1)}, u32[]{:S(2)}, u32[]{:S(2)}) %collective-permute-start.14) | collective-permute-done | bytes 294944 | tf_op jit(solution)/shard_map/ppermute | solution.py:37
  121.5 2.4 %collective-permute-start.15 = (f32[48,1536]{1,0:T(8,128)S(1)}, f32[48,1536]{1,0:T(8,128)S(1)}, u32[]{:S(2)}, u32[]{:S(2)}) collective-permute-start(f32[48,1536]{1,0:T(8,128)S(1)} %slice.9), channel_id=1, source_target_pairs={{0,4},{4,0},{8,12},{12,8},{16,20},{20,16},{24,28},{28,24},{32,36},... | collective-permute-start | bytes 884744 | tf_op jit(solution)/shard_map/ppermute | solution.py:46
  123.9 1.2 collective-permute-done.15
  125.1 0.9 fusion
  (13 shorter events, 1.1 us)
Async XLA Ops:
  13.8 5.6 %collective-permute-start = (bf16[2,2,528,512]{3,2,1,0:T(8,128)(2,1)}, bf16[2,2,528,512]{3,2,1,0:T(8,128)(2,1)S(1)}, u32[]{:S(2)}, u32[]{:S(2)}) collective-permute-start(bf16[2,2,528,512]{3,2,1,0:T(8,128)(2,1)} %get-tuple-element.23), channel_id=1, source_target_pairs={{0,4},{4,0},{8,12},{12,8},{16,20},{20,16},{24,28},{28,24},{32,36},... | collective-permute-start | bytes 6488072 | tf_op jit(solution)/shard_map/ppermute | solution.py:46
  15.2 27.4 %collective-permute-start.2 = (bf16[2,528,512]{2,1,0:T(8,128)(2,1)}, bf16[2,528,512]{2,1,0:T(8,128)(2,1)S(1)}, u32[]{:S(2)}, u32[]{:S(2)}) collective-permute-start(bf16[2,528,512]{2,1,0:T(8,128)(2,1)} %get-tuple-element.25), channel_id=1, source_target_pairs={{0,3},{1,0},{2,1},{3,2},{4,7},{5,4},{6,5},{7,6},{8,11},{9,8},{10,9... | collective-permute-start | bytes 3244040 | tf_op jit(solution)/shard_map/ppermute | solution.py:41
  19.1 27.6 %collective-permute-start.1 = (bf16[2,528,512]{2,1,0:T(8,128)(2,1)}, bf16[2,528,512]{2,1,0:T(8,128)(2,1)S(1)}, u32[]{:S(2)}, u32[]{:S(2)}) collective-permute-start(bf16[2,528,512]{2,1,0:T(8,128)(2,1)} %get-tuple-element.24), channel_id=1, source_target_pairs={{0,1},{1,2},{2,3},{3,0},{4,5},{5,6},{6,7},{7,4},{8,9},{9,10},{10,1... | collective-permute-start | bytes 3244040 | tf_op jit(solution)/shard_map/ppermute | solution.py:41
  19.3 1.6 %copy-start = (bf16[2,2,528,512]{3,2,1,0:T(8,128)(2,1)S(1)}, bf16[2,2,528,512]{3,2,1,0:T(8,128)(2,1)}, u32[]{:S(2)}) copy-start(bf16[2,2,528,512]{3,2,1,0:T(8,128)(2,1)} %get-tuple-element.22.refs_0_) | copy-start | bytes 6488068
  20.9 25.7 %copy-start.1 = (bf16[2,528,512]{2,1,0:T(8,128)(2,1)S(1)}, bf16[2,528,512]{2,1,0:T(8,128)(2,1)}, u32[]{:S(2)}) copy-start(bf16[2,528,512]{2,1,0:T(8,128)(2,1)} %get-tuple-element.28) | copy-start | bytes 3244036
  23.9 27.2 %collective-permute-start.5 = (bf16[384,1536]{1,0:T(8,128)(2,1)S(1)}, bf16[384,1536]{1,0:T(8,128)(2,1)S(1)}, u32[]{:S(2)}, u32[]{:S(2)}) collective-permute-start(bf16[384,1536]{1,0:T(8,128)(2,1)S(1)} %get-tuple-element.31), channel_id=1, source_target_pairs={{0,8},{4,36},{8,16},{12,44},{16,24},{20,52},{24,0},{28,60},{32,40}... | collective-permute-start | bytes 3538952 | tf_op jit(solution)/shard_map/ppermute | solution.py:37
  25.4 27.4 %collective-permute-start.6 = (bf16[384,1536]{1,0:T(8,128)(2,1)S(1)}, bf16[384,1536]{1,0:T(8,128)(2,1)S(1)}, u32[]{:S(2)}, u32[]{:S(2)}) collective-permute-start(bf16[384,1536]{1,0:T(8,128)(2,1)S(1)} %get-tuple-element.32), channel_id=1, source_target_pairs={{0,24},{4,100},{8,0},{12,108},{16,8},{20,116},{24,16},{28,124},{32... | collective-permute-start | bytes 3538952 | tf_op jit(solution)/shard_map/ppermute | solution.py:37
  27.0 27.6 %collective-permute-start.7 = (bf16[384,1536]{1,0:T(8,128)(2,1)S(1)}, bf16[384,1536]{1,0:T(8,128)(2,1)S(1)}, u32[]{:S(2)}, u32[]{:S(2)}) collective-permute-start(bf16[384,1536]{1,0:T(8,128)(2,1)S(1)} %get-tuple-element.33), channel_id=1, source_target_pairs={{0,16},{4,68},{8,24},{12,76},{16,0},{20,84},{24,8},{28,92},{32,48}... | collective-permute-start | bytes 3538952 | tf_op jit(solution)/shard_map/ppermute | solution.py:37
  42.6 27.9 %collective-permute-start.4 = (bf16[2,528,512]{2,1,0:T(8,128)(2,1)}, bf16[2,528,512]{2,1,0:T(8,128)(2,1)S(1)}, u32[]{:S(2)}, u32[]{:S(2)}) collective-permute-start(bf16[2,528,512]{2,1,0:T(8,128)(2,1)} %get-tuple-element.30), channel_id=1, source_target_pairs={{0,7},{1,4},{2,5},{3,6},{4,3},{5,0},{6,1},{7,2},{8,15},{9,12},{10,... | collective-permute-start | bytes 3244040 | tf_op jit(solution)/shard_map/ppermute | solution.py:56
  46.7 26.8 %collective-permute-start.3 = (bf16[2,528,512]{2,1,0:T(8,128)(2,1)S(1)}, bf16[2,528,512]{2,1,0:T(8,128)(2,1)S(1)}, u32[]{:S(2)}, u32[]{:S(2)}) collective-permute-start(bf16[2,528,512]{2,1,0:T(8,128)(2,1)S(1)} %copy-done.1), channel_id=1, source_target_pairs={{0,5},{1,6},{2,7},{3,4},{4,1},{5,2},{6,3},{7,0},{8,13},{9,14},{10,... | collective-permute-start | bytes 3244040 | tf_op jit(solution)/shard_map/ppermute | solution.py:56
  75.9 17.0 %collective-permute-start.10 = (bf16[384,1536]{1,0:T(8,128)(2,1)S(1)}, bf16[384,1536]{1,0:T(8,128)(2,1)S(1)}, u32[]{:S(2)}, u32[]{:S(2)}) collective-permute-start(bf16[384,1536]{1,0:T(8,128)(2,1)S(1)} %get-tuple-element.37), channel_id=1, source_target_pairs={{0,16},{4,68},{8,24},{12,76},{16,0},{20,84},{24,8},{28,92},{32,48}... | collective-permute-start | bytes 3538952 | tf_op jit(solution)/shard_map/ppermute | solution.py:37
  78.8 26.6 %collective-permute-start.8 = (bf16[384,1536]{1,0:T(8,128)(2,1)S(1)}, bf16[384,1536]{1,0:T(8,128)(2,1)S(1)}, u32[]{:S(2)}, u32[]{:S(2)}) collective-permute-start(bf16[384,1536]{1,0:T(8,128)(2,1)S(1)} %get-tuple-element.35), channel_id=1, source_target_pairs={{0,8},{4,36},{8,16},{12,44},{16,24},{20,52},{24,0},{28,60},{32,40}... | collective-permute-start | bytes 3538952 | tf_op jit(solution)/shard_map/ppermute | solution.py:37
  79.3 26.6 %collective-permute-start.9 = (bf16[384,1536]{1,0:T(8,128)(2,1)S(1)}, bf16[384,1536]{1,0:T(8,128)(2,1)S(1)}, u32[]{:S(2)}, u32[]{:S(2)}) collective-permute-start(bf16[384,1536]{1,0:T(8,128)(2,1)S(1)} %get-tuple-element.36), channel_id=1, source_target_pairs={{0,24},{4,100},{8,0},{12,108},{16,8},{20,116},{24,16},{28,124},{32... | collective-permute-start | bytes 3538952 | tf_op jit(solution)/shard_map/ppermute | solution.py:37
  81.5 28.1 %collective-permute-start.11 = (bf16[384,1536]{1,0:T(8,128)(2,1)S(1)}, bf16[384,1536]{1,0:T(8,128)(2,1)S(1)}, u32[]{:S(2)}, u32[]{:S(2)}) collective-permute-start(bf16[384,1536]{1,0:T(8,128)(2,1)S(1)} %add_convert_fusion.refs_3_), channel_id=1, source_target_pairs={{0,2},{1,3},{2,0},{3,1},{4,6},{5,7},{6,4},{7,5},{8,10},{9,11},{10,... | collective-permute-start | bytes 3538952 | tf_op jit(solution)/shard_map/ppermute | solution.py:41
  110.4 7.1 %collective-permute-start.12 = (bf16[96,1536]{1,0:T(8,128)(2,1)S(1)}, bf16[96,1536]{1,0:T(8,128)(2,1)S(1)}, u32[]{:S(2)}, u32[]{:S(2)}) collective-permute-start(bf16[96,1536]{1,0:T(8,128)(2,1)S(1)} %get-tuple-element.39), channel_id=1, source_target_pairs={{0,32},{4,12},{8,40},{12,20},{16,48},{20,28},{24,56},{28,4},{32,64... | collective-permute-start | bytes 884744 | tf_op jit(solution)/shard_map/ppermute | solution.py:37
  111.9 5.9 %collective-permute-start.13 = (bf16[96,1536]{1,0:T(8,128)(2,1)S(1)}, bf16[96,1536]{1,0:T(8,128)(2,1)S(1)}, u32[]{:S(2)}, u32[]{:S(2)}) collective-permute-start(bf16[96,1536]{1,0:T(8,128)(2,1)S(1)} %get-tuple-element.40), channel_id=1, source_target_pairs={{0,96},{4,28},{8,104},{12,4},{16,112},{20,12},{24,120},{28,20},{32... | collective-permute-start | bytes 884744 | tf_op jit(solution)/shard_map/ppermute | solution.py:37
  113.1 8.2 %collective-permute-start.14 = (bf16[96,1536]{1,0:T(8,128)(2,1)S(1)}, bf16[96,1536]{1,0:T(8,128)(2,1)S(1)}, u32[]{:S(2)}, u32[]{:S(2)}) collective-permute-start(bf16[96,1536]{1,0:T(8,128)(2,1)S(1)} %get-tuple-element.41), channel_id=1, source_target_pairs={{0,64},{4,20},{8,72},{12,28},{16,80},{20,4},{24,88},{28,12},{32,96... | collective-permute-start | bytes 884744 | tf_op jit(solution)/shard_map/ppermute | solution.py:37
  121.5 3.6 %collective-permute-start.15 = (f32[48,1536]{1,0:T(8,128)S(1)}, f32[48,1536]{1,0:T(8,128)S(1)}, u32[]{:S(2)}, u32[]{:S(2)}) collective-permute-start(f32[48,1536]{1,0:T(8,128)S(1)} %slice.9), channel_id=1, source_target_pairs={{0,4},{4,0},{8,12},{12,8},{16,20},{20,16},{24,28},{28,24},{32,36},... | collective-permute-start | bytes 884744 | tf_op jit(solution)/shard_map/ppermute | solution.py:46

commit v6 on v5

--- a/solution.py
+++ b/solution.py
@@ -355,14 +355,14 @@
     swapped = across_core(swaps)
     below, above = across_z(plus, 1), across_z(minus, 3)
     opposite = opposite_frame([stays, swapped])
-    summed = add_up(spread(opposite, False)).astype(BF16)
+    summed = add_up(spread(sum_slabs(spread(opposite, False)), True)).astype(BF16)
     passed = across_z(summed, 2)
     below_too = across_both(lax.optimization_barrier((swap_plus, below, opposite[0]))[0], 1)
     above_too = across_both(lax.optimization_barrier((swap_minus, above, opposite[0]))[0], 3)
     begun = start_frame([stays, swapped, below, above])
     own = finish_frame(begun, [below_too, above_too], summed)
-    pieces = sum_slabs(spread(own, False) + [passed])
-    rows = add_up(spread(pieces, True))
+    pieces = sum_slabs(spread(own, False))
+    rows = add_up(spread(pieces, True) + [passed])
     keep, got = rows[:STRIP], across_core(rows[STRIP:])
     numer = jnp.where(core == 0, keep, got)
     weight = jnp.where(core == 0, got, keep)

time: 126 us -> 124 us (0.984)
  waiting for transfers between devices: 73 us -> 65.3 us
  starting transfers between devices: 25.4 us -> 29.8 us
  Pallas kernels: 23.7 us -> 25.4 us
    ppermute x2, waiting for transfers between devices: 18.3 us -> 7.79 us  [across_both(): return lax.ppermute(value, ('visit', 'patch'), pairs)]
    ppermute x9 -> x12, waiting for transfers between devices: 35.3 us -> 41.9 us  [turn(): return lax.ppermute(value, 'visit', pairs)]
    ppermute x9 -> x12, starting transfers between devices: 13.6 us -> 18.2 us  [turn(): return lax.ppermute(value, 'visit', pairs)]
    ppermute x3, waiting for transfers between devices: 17.9 us -> 14.1 us  [across_z(): return lax.ppermute(value, 'patch', [(z, (z + step) % 4) for z in range(4)])]
  transfers between devices with their start and end apart: 16 -> 19, of which waited for: 14 -> 14; matrix products, arithmetic and copies ran while one was open for 0% -> 0% of each run, Pallas kernels for 6% -> 7%
where the time goes in v6:
time: 124 us
  waiting for transfers between devices  65.3 us (53%)
  starting transfers between devices  29.8 us (24%)
  Pallas kernels  25.4 us (20%)
  local copies, waits for them, and re-layouts  1.63 us (1%)
    ppermute x12, waiting for transfers between devices, turn(): return lax.ppermute(value, 'visit', pairs)  41.9 us
    ppermute x12, starting transfers between devices, turn(): return lax.ppermute(value, 'visit', pairs)  18.2 us
    ppermute x3, waiting for transfers between devices, across_z(): return lax.ppermute(value, 'patch', [(z, (z + step) % 4) for z in range(4)])  14.1 us
    pallas_call x1, Pallas kernels, match_tiles(): pl.pallas_call(match_kernel, grid=(4,), in_specs=[pl.BlockSpec(memory_spa...  13.1 us
    ppermute x2, waiting for transfers between devices, across_both(): return lax.ppermute(value, ('visit', 'patch'), pairs)  7.79 us
    pallas_call x1, Pallas kernels, start_frame(): pl.pallas_call(start_kernel, out_shape=jax.ShapeDtypeStruct(FRAME, F32),...  4.46 us
    ppermute x2, starting transfers between devices, across_both(): return lax.ppermute(value, ('visit', 'patch'), pairs)  4.05 us
    ppermute x3, starting transfers between devices, across_z(): return lax.ppermute(value, 'patch', [(z, (z + step) % 4) for z in range(4)])  3.86 us
  transfers between devices with their start and end apart: 19, of which 14 were waited for; matrix products, arithmetic and copies ran while one was open for 0% of the time, Pallas kernels for 7%

profile of v6, /device:TPU:1, one launch (start us, length us, event | category | flops | bytes accessed | tf_op | source)
XLA Modules:
  0.0 124.0 jit_solution(1655143334634125954)
XLA Ops:
  0.6 13.1 %shard_map.77 = (bf16[2,2,528,512]{3,2,1,0:T(8,128)(2,1)}, bf16[2,528,512]{2,1,0:T(8,128)(2,1)}, bf16[2,528,512]{2,1,0:T(8,128)(2,1)}, bf16[2,2,528,512]{3,2,1,0...) custom-call(s32[2,4]{1,0:T(2,128)} %bitcast.23, s32[2,2,4]{2,1,0:T(2,128)} %bitcast.21, ...), custom_call_target="tpu_custom_call" | custom-call | flops 6442450944 | bytes 12582912 | tf_op jit(solution)/shard_map/pallas_call | solution.py:184
  13.8 1.5 %collective-permute-start = (bf16[2,2,528,512]{3,2,1,0:T(8,128)(2,1)}, bf16[2,2,528,512]{3,2,1,0:T(8,128)(2,1)S(1)}, u32[]{:S(2)}, u32[]{:S(2)}) collective-permute-start(bf16[2,2,528,512]{3,2,1,0:T(8,128)(2,1)} %get-tuple-element.27), channel_id=1, source_target_pairs={{0,4},{4,0},{8,12},{12,8},{16,20},{20,16},{24,28},{28,24},{32,36},... | collective-permute-start | bytes 6488072 | tf_op jit(solution)/shard_map/ppermute | solution.py:46
  15.3 3.9 %collective-permute-start.2 = (bf16[2,528,512]{2,1,0:T(8,128)(2,1)}, bf16[2,528,512]{2,1,0:T(8,128)(2,1)S(1)}, u32[]{:S(2)}, u32[]{:S(2)}) collective-permute-start(bf16[2,528,512]{2,1,0:T(8,128)(2,1)} %get-tuple-element.29), channel_id=1, source_target_pairs={{0,3},{1,0},{2,1},{3,2},{4,7},{5,4},{6,5},{7,6},{8,11},{9,8},{10,9... | collective-permute-start | bytes 3244040 | tf_op jit(solution)/shard_map/ppermute | solution.py:41
  19.4 1.6 %copy-done = bf16[2,2,528,512]{3,2,1,0:T(8,128)(2,1)S(1)} copy-done((bf16[2,2,528,512]{3,2,1,0:T(8,128)(2,1)S(1)}, bf16[2,2,528,512]{3,2,1,0:T(8,128)(2,1)}, u32[]{:S(2)}) %copy-start) | copy-done | bytes 2162712
  21.0 3.0 %shard_map.79 = (bf16[384,1536]{1,0:T(8,128)(2,1)S(1)}, bf16[384,1536]{1,0:T(8,128)(2,1)S(1)}, bf16[384,1536]{1,0:T(8,128)(2,1)S(1)}, bf16[384,1536]{1,0:T(8,128)(2,1)S(1)}) custom-call(bf16[2,2,528,512]{3,2,1,0:T(8,128)(2,1)S(1)} %copy-done, bf16[2,2,528,512]{3,2,1,0:T(8,128)(2,1)S(1)} %collective-permute-done.refs_1_), custom_call_target="tpu_custom_call" | custom-call | flops 2147483648 | bytes 9437184 | tf_op jit(solution)/shard_map/pallas_call | solution.py:297
  24.0 1.4 %collective-permute-start.5 = (bf16[384,1536]{1,0:T(8,128)(2,1)S(1)}, bf16[384,1536]{1,0:T(8,128)(2,1)S(1)}, u32[]{:S(2)}, u32[]{:S(2)}) collective-permute-start(bf16[384,1536]{1,0:T(8,128)(2,1)S(1)} %get-tuple-element.35), channel_id=1, source_target_pairs={{0,8},{4,36},{8,16},{12,44},{16,24},{20,52},{24,0},{28,60},{32,40}... | collective-permute-start | bytes 3538952 | tf_op jit(solution)/shard_map/ppermute | solution.py:37
  25.4 1.5 %collective-permute-start.6 = (bf16[384,1536]{1,0:T(8,128)(2,1)S(1)}, bf16[384,1536]{1,0:T(8,128)(2,1)S(1)}, u32[]{:S(2)}, u32[]{:S(2)}) collective-permute-start(bf16[384,1536]{1,0:T(8,128)(2,1)S(1)} %get-tuple-element.36), channel_id=1, source_target_pairs={{0,24},{4,100},{8,0},{12,108},{16,8},{20,116},{24,16},{28,124},{32... | collective-permute-start | bytes 3538952 | tf_op jit(solution)/shard_map/ppermute | solution.py:37
  26.9 1.6 %collective-permute-start.7 = (bf16[384,1536]{1,0:T(8,128)(2,1)S(1)}, bf16[384,1536]{1,0:T(8,128)(2,1)S(1)}, u32[]{:S(2)}, u32[]{:S(2)}) collective-permute-start(bf16[384,1536]{1,0:T(8,128)(2,1)S(1)} %get-tuple-element.37), channel_id=1, source_target_pairs={{0,16},{4,68},{8,24},{12,76},{16,0},{20,84},{24,8},{28,92},{32,48}... | collective-permute-start | bytes 3538952 | tf_op jit(solution)/shard_map/ppermute | solution.py:37
  28.5 14.1 %collective-permute-done.2.refs_3_ = bf16[2,528,512]{2,1,0:T(8,128)(2,1)S(1)} collective-permute-done((bf16[2,528,512]{2,1,0:T(8,128)(2,1)}, bf16[2,528,512]{2,1,0:T(8,128)(2,1)S(1)}, u32[]{:S(2)}, u32[]{:S(2)}) %collective-permute-start.2) | collective-permute-done | bytes 1081376 | tf_op jit(solution)/shard_map/ppermute | solution.py:41
  42.6 4.1 %collective-permute-start.4 = (bf16[2,528,512]{2,1,0:T(8,128)(2,1)}, bf16[2,528,512]{2,1,0:T(8,128)(2,1)S(1)}, u32[]{:S(2)}, u32[]{:S(2)}) collective-permute-start(bf16[2,528,512]{2,1,0:T(8,128)(2,1)} %get-tuple-element.34), channel_id=1, source_target_pairs={{0,7},{1,4},{2,5},{3,6},{4,3},{5,0},{6,1},{7,2},{8,15},{9,12},{10,... | collective-permute-start | bytes 3244040 | tf_op jit(solution)/shard_map/ppermute | solution.py:56
  46.7 6.0 %collective-permute-done.6.refs_2_ = bf16[384,1536]{1,0:T(8,128)(2,1)S(1)} collective-permute-done((bf16[384,1536]{1,0:T(8,128)(2,1)S(1)}, bf16[384,1536]{1,0:T(8,128)(2,1)S(1)}, u32[]{:S(2)}, u32[]{:S(2)}) %collective-permute-start.6) | collective-permute-done | bytes 1179680 | tf_op jit(solution)/shard_map/ppermute | solution.py:37
  52.7 1.8 %collective-permute-done.7.refs_3_ = bf16[384,1536]{1,0:T(8,128)(2,1)S(1)} collective-permute-done((bf16[384,1536]{1,0:T(8,128)(2,1)S(1)}, bf16[384,1536]{1,0:T(8,128)(2,1)S(1)}, u32[]{:S(2)}, u32[]{:S(2)}) %collective-permute-start.7) | collective-permute-done | bytes 1179680 | tf_op jit(solution)/shard_map/ppermute | solution.py:37
  55.1 2.5 %collective-permute-start.10 = (bf16[96,1536]{1,0:T(8,128)(2,1)S(1)}, bf16[96,1536]{1,0:T(8,128)(2,1)S(1)}, u32[]{:S(2)}, u32[]{:S(2)}) collective-permute-start(bf16[96,1536]{1,0:T(8,128)(2,1)S(1)} %get-tuple-element.41), channel_id=1, source_target_pairs={{0,64},{4,20},{8,72},{12,28},{16,80},{20,4},{24,88},{28,12},{32,96... | collective-permute-start | bytes 884744 | tf_op jit(solution)/shard_map/ppermute | solution.py:37
  58.1 2.2 %collective-permute-start.9 = (bf16[96,1536]{1,0:T(8,128)(2,1)S(1)}, bf16[96,1536]{1,0:T(8,128)(2,1)S(1)}, u32[]{:S(2)}, u32[]{:S(2)}) collective-permute-start(bf16[96,1536]{1,0:T(8,128)(2,1)S(1)} %get-tuple-element.40), channel_id=1, source_target_pairs={{0,96},{4,28},{8,104},{12,4},{16,112},{20,12},{24,120},{28,20},{32... | collective-permute-start | bytes 884744 | tf_op jit(solution)/shard_map/ppermute | solution.py:37
  60.4 4.5 %shard_map.78.refs_0_ = f32[193,8,1536]{2,1,0:T(8,128)S(1)} custom-call(bf16[2,2,528,512]{3,2,1,0:T(8,128)(2,1)S(1)} %copy-done.1, bf16[2,2,528,512]{3,2,1,0:T(8,128)(2,1)S(1)} %collective-permute-done.refs_1_, bf16[2,528,512]{2,1,0:T(8,128)(2,1)S(1)} %collective-permute-done.1.refs_2_, bf16[2,528,512]{2,1,0:T(8,128)(2,1)S(1)} %collective-permute-done.2.refs_3_), custom_call_target="tpu_custom_call" | custom-call | flops 4294967296 | bytes 13631488 | tf_op jit(solution)/shard_map/pallas_call | solution.py:303
  64.8 1.0 collective-permute-done.8
  66.0 4.5 %collective-permute-done.4.refs_2_ = bf16[2,528,512]{2,1,0:T(8,128)(2,1)S(1)} collective-permute-done((bf16[2,528,512]{2,1,0:T(8,128)(2,1)}, bf16[2,528,512]{2,1,0:T(8,128)(2,1)S(1)}, u32[]{:S(2)}, u32[]{:S(2)}) %collective-permute-start.4) | collective-permute-done | bytes 1081376 | tf_op jit(solution)/shard_map/ppermute | solution.py:56
  70.5 3.3 %collective-permute-done.3.refs_1_ = bf16[2,528,512]{2,1,0:T(8,128)(2,1)} collective-permute-done((bf16[2,528,512]{2,1,0:T(8,128)(2,1)}, bf16[2,528,512]{2,1,0:T(8,128)(2,1)}, u32[]{:S(2)}, u32[]{:S(2)}) %collective-permute-start.3) | collective-permute-done | bytes 1081376 | tf_op jit(solution)/shard_map/ppermute | solution.py:56
  73.8 3.6 %shard_map.81 = (bf16[384,1536]{1,0:T(8,128)(2,1)S(1)}, bf16[384,1536]{1,0:T(8,128)(2,1)S(1)}, bf16[384,1536]{1,0:T(8,128)(2,1)S(1)}, bf16[384,1536]{1,0:T(8,128)(2,1)S(1)}, f32[193,8,1536]{2,1,0:T(8,128)S(1)}) custom-call(f32[193,8,1536]{2,1,0:T(8,128)S(1)} %shard_map.78.refs_0_, ...), custom_call_target="tpu_custom_call", output_to_operand_aliasing={{4}: (0, {})} | custom-call | flops 2147483648 | bytes 9437184 | tf_op jit(solution)/shard_map/pallas_call | solution.py:308
  77.5 1.4 %collective-permute-start.11 = (bf16[384,1536]{1,0:T(8,128)(2,1)S(1)}, bf16[384,1536]{1,0:T(8,128)(2,1)S(1)}, u32[]{:S(2)}, u32[]{:S(2)}) collective-permute-start(bf16[384,1536]{1,0:T(8,128)(2,1)S(1)} %get-tuple-element.43), channel_id=1, source_target_pairs={{0,8},{4,36},{8,16},{12,44},{16,24},{20,52},{24,0},{28,60},{32,40}... | collective-permute-start | bytes 3538952 | tf_op jit(solution)/shard_map/ppermute | solution.py:37
  78.8 1.5 %collective-permute-start.12 = (bf16[384,1536]{1,0:T(8,128)(2,1)S(1)}, bf16[384,1536]{1,0:T(8,128)(2,1)S(1)}, u32[]{:S(2)}, u32[]{:S(2)}) collective-permute-start(bf16[384,1536]{1,0:T(8,128)(2,1)S(1)} %get-tuple-element.44), channel_id=1, source_target_pairs={{0,24},{4,100},{8,0},{12,108},{16,8},{20,116},{24,16},{28,124},{32... | collective-permute-start | bytes 3538952 | tf_op jit(solution)/shard_map/ppermute | solution.py:37
  80.3 1.6 %collective-permute-start.13 = (bf16[384,1536]{1,0:T(8,128)(2,1)S(1)}, bf16[384,1536]{1,0:T(8,128)(2,1)S(1)}, u32[]{:S(2)}, u32[]{:S(2)}) collective-permute-start(bf16[384,1536]{1,0:T(8,128)(2,1)S(1)} %get-tuple-element.45), channel_id=1, source_target_pairs={{0,16},{4,68},{8,24},{12,76},{16,0},{20,84},{24,8},{28,92},{32,48}... | collective-permute-start | bytes 3538952 | tf_op jit(solution)/shard_map/ppermute | solution.py:37
  81.9 12.2 %collective-permute-done.11.refs_1_ = bf16[384,1536]{1,0:T(8,128)(2,1)S(1)} collective-permute-done((bf16[384,1536]{1,0:T(8,128)(2,1)S(1)}, bf16[384,1536]{1,0:T(8,128)(2,1)S(1)}, u32[]{:S(2)}, u32[]{:S(2)}) %collective-permute-start.11) | collective-permute-done | bytes 1179680 | tf_op jit(solution)/shard_map/ppermute | solution.py:37
  94.1 12.0 %collective-permute-done.12.refs_2_ = bf16[384,1536]{1,0:T(8,128)(2,1)S(1)} collective-permute-done((bf16[384,1536]{1,0:T(8,128)(2,1)S(1)}, bf16[384,1536]{1,0:T(8,128)(2,1)S(1)}, u32[]{:S(2)}, u32[]{:S(2)}) %collective-permute-start.12) | collective-permute-done | bytes 1179680 | tf_op jit(solution)/shard_map/ppermute | solution.py:37
  106.1 1.8 %collective-permute-done.13.refs_3_ = bf16[384,1536]{1,0:T(8,128)(2,1)S(1)} collective-permute-done((bf16[384,1536]{1,0:T(8,128)(2,1)S(1)}, bf16[384,1536]{1,0:T(8,128)(2,1)S(1)}, u32[]{:S(2)}, u32[]{:S(2)}) %collective-permute-start.13) | collective-permute-done | bytes 1179680 | tf_op jit(solution)/shard_map/ppermute | solution.py:37
  109.5 1.8 %collective-permute-start.15 = (bf16[96,1536]{1,0:T(8,128)(2,1)S(1)}, bf16[96,1536]{1,0:T(8,128)(2,1)S(1)}, u32[]{:S(2)}, u32[]{:S(2)}) collective-permute-start(bf16[96,1536]{1,0:T(8,128)(2,1)S(1)} %get-tuple-element.48), channel_id=1, source_target_pairs={{0,96},{4,28},{8,104},{12,4},{16,112},{20,12},{24,120},{28,20},{32... | collective-permute-start | bytes 884744 | tf_op jit(solution)/shard_map/ppermute | solution.py:37
  111.3 1.2 %collective-permute-start.16 = (bf16[96,1536]{1,0:T(8,128)(2,1)S(1)}, bf16[96,1536]{1,0:T(8,128)(2,1)S(1)}, u32[]{:S(2)}, u32[]{:S(2)}) collective-permute-start(bf16[96,1536]{1,0:T(8,128)(2,1)S(1)} %get-tuple-element.49), channel_id=1, source_target_pairs={{0,64},{4,20},{8,72},{12,28},{16,80},{20,4},{24,88},{28,12},{32,96... | collective-permute-start | bytes 884744 | tf_op jit(solution)/shard_map/ppermute | solution.py:37
  112.5 3.1 %collective-permute-done.14 = bf16[96,1536]{1,0:T(8,128)(2,1)S(1)} collective-permute-done((bf16[96,1536]{1,0:T(8,128)(2,1)S(1)}, bf16[96,1536]{1,0:T(8,128)(2,1)S(1)}, u32[]{:S(2)}, u32[]{:S(2)}) %collective-permute-start.14) | collective-permute-done | bytes 294944 | tf_op jit(solution)/shard_map/ppermute | solution.py:37
  115.7 2.4 %collective-permute-done.15 = bf16[96,1536]{1,0:T(8,128)(2,1)S(1)} collective-permute-done((bf16[96,1536]{1,0:T(8,128)(2,1)S(1)}, bf16[96,1536]{1,0:T(8,128)(2,1)S(1)}, u32[]{:S(2)}, u32[]{:S(2)}) %collective-permute-start.15) | collective-permute-done | bytes 294944 | tf_op jit(solution)/shard_map/ppermute | solution.py:37
  118.1 1.4 %collective-permute-done.16 = bf16[96,1536]{1,0:T(8,128)(2,1)S(1)} collective-permute-done((bf16[96,1536]{1,0:T(8,128)(2,1)S(1)}, bf16[96,1536]{1,0:T(8,128)(2,1)S(1)}, u32[]{:S(2)}, u32[]{:S(2)}) %collective-permute-start.16) | collective-permute-done | bytes 294944 | tf_op jit(solution)/shard_map/ppermute | solution.py:37
  119.7 2.2 %collective-permute-start.18 = (f32[48,1536]{1,0:T(8,128)S(1)}, f32[48,1536]{1,0:T(8,128)S(1)}, u32[]{:S(2)}, u32[]{:S(2)}) collective-permute-start(f32[48,1536]{1,0:T(8,128)S(1)} %slice.9), channel_id=1, source_target_pairs={{0,4},{4,0},{8,12},{12,8},{16,20},{20,16},{24,28},{28,24},{32,36},... | collective-permute-start | bytes 884744 | tf_op jit(solution)/shard_map/ppermute | solution.py:46
  122.0 1.2 collective-permute-done.18
  (20 shorter events, 4.0 us)
Async XLA Ops:
  13.8 5.6 %collective-permute-start = (bf16[2,2,528,512]{3,2,1,0:T(8,128)(2,1)}, bf16[2,2,528,512]{3,2,1,0:T(8,128)(2,1)S(1)}, u32[]{:S(2)}, u32[]{:S(2)}) collective-permute-start(bf16[2,2,528,512]{3,2,1,0:T(8,128)(2,1)} %get-tuple-element.27), channel_id=1, source_target_pairs={{0,4},{4,0},{8,12},{12,8},{16,20},{20,16},{24,28},{28,24},{32,36},... | collective-permute-start | bytes 6488072 | tf_op jit(solution)/shard_map/ppermute | solution.py:46
  15.3 27.4 %collective-permute-start.2 = (bf16[2,528,512]{2,1,0:T(8,128)(2,1)}, bf16[2,528,512]{2,1,0:T(8,128)(2,1)S(1)}, u32[]{:S(2)}, u32[]{:S(2)}) collective-permute-start(bf16[2,528,512]{2,1,0:T(8,128)(2,1)} %get-tuple-element.29), channel_id=1, source_target_pairs={{0,3},{1,0},{2,1},{3,2},{4,7},{5,4},{6,5},{7,6},{8,11},{9,8},{10,9... | collective-permute-start | bytes 3244040 | tf_op jit(solution)/shard_map/ppermute | solution.py:41
  19.1 27.6 %collective-permute-start.1 = (bf16[2,528,512]{2,1,0:T(8,128)(2,1)}, bf16[2,528,512]{2,1,0:T(8,128)(2,1)S(1)}, u32[]{:S(2)}, u32[]{:S(2)}) collective-permute-start(bf16[2,528,512]{2,1,0:T(8,128)(2,1)} %get-tuple-element.28), channel_id=1, source_target_pairs={{0,1},{1,2},{2,3},{3,0},{4,5},{5,6},{6,7},{7,4},{8,9},{9,10},{10,1... | collective-permute-start | bytes 3244040 | tf_op jit(solution)/shard_map/ppermute | solution.py:41
  19.3 1.6 %copy-start = (bf16[2,2,528,512]{3,2,1,0:T(8,128)(2,1)S(1)}, bf16[2,2,528,512]{3,2,1,0:T(8,128)(2,1)}, u32[]{:S(2)}) copy-start(bf16[2,2,528,512]{3,2,1,0:T(8,128)(2,1)} %get-tuple-element.26.refs_0_) | copy-start | bytes 6488068
  24.0 22.7 %collective-permute-start.5 = (bf16[384,1536]{1,0:T(8,128)(2,1)S(1)}, bf16[384,1536]{1,0:T(8,128)(2,1)S(1)}, u32[]{:S(2)}, u32[]{:S(2)}) collective-permute-start(bf16[384,1536]{1,0:T(8,128)(2,1)S(1)} %get-tuple-element.35), channel_id=1, source_target_pairs={{0,8},{4,36},{8,16},{12,44},{16,24},{20,52},{24,0},{28,60},{32,40}... | collective-permute-start | bytes 3538952 | tf_op jit(solution)/shard_map/ppermute | solution.py:37
  25.4 27.3 %collective-permute-start.6 = (bf16[384,1536]{1,0:T(8,128)(2,1)S(1)}, bf16[384,1536]{1,0:T(8,128)(2,1)S(1)}, u32[]{:S(2)}, u32[]{:S(2)}) collective-permute-start(bf16[384,1536]{1,0:T(8,128)(2,1)S(1)} %get-tuple-element.36), channel_id=1, source_target_pairs={{0,24},{4,100},{8,0},{12,108},{16,8},{20,116},{24,16},{28,124},{32... | collective-permute-start | bytes 3538952 | tf_op jit(solution)/shard_map/ppermute | solution.py:37
  26.9 27.6 %collective-permute-start.7 = (bf16[384,1536]{1,0:T(8,128)(2,1)S(1)}, bf16[384,1536]{1,0:T(8,128)(2,1)S(1)}, u32[]{:S(2)}, u32[]{:S(2)}) collective-permute-start(bf16[384,1536]{1,0:T(8,128)(2,1)S(1)} %get-tuple-element.37), channel_id=1, source_target_pairs={{0,16},{4,68},{8,24},{12,76},{16,0},{20,84},{24,8},{28,92},{32,48}... | collective-permute-start | bytes 3538952 | tf_op jit(solution)/shard_map/ppermute | solution.py:37
  42.6 27.9 %collective-permute-start.4 = (bf16[2,528,512]{2,1,0:T(8,128)(2,1)}, bf16[2,528,512]{2,1,0:T(8,128)(2,1)S(1)}, u32[]{:S(2)}, u32[]{:S(2)}) collective-permute-start(bf16[2,528,512]{2,1,0:T(8,128)(2,1)} %get-tuple-element.34), channel_id=1, source_target_pairs={{0,7},{1,4},{2,5},{3,6},{4,3},{5,0},{6,1},{7,2},{8,15},{9,12},{10,... | collective-permute-start | bytes 3244040 | tf_op jit(solution)/shard_map/ppermute | solution.py:56
  46.7 13.7 %copy-start.1 = (bf16[2,2,528,512]{3,2,1,0:T(8,128)(2,1)S(1)}, bf16[2,2,528,512]{3,2,1,0:T(8,128)(2,1)}, u32[]{:S(2)}) copy-start(bf16[2,2,528,512]{3,2,1,0:T(8,128)(2,1)} %get-tuple-element.26.refs_0_) | copy-start | bytes 6488068
  46.7 27.1 %collective-permute-start.3 = (bf16[2,528,512]{2,1,0:T(8,128)(2,1)}, bf16[2,528,512]{2,1,0:T(8,128)(2,1)}, u32[]{:S(2)}, u32[]{:S(2)}) collective-permute-start(bf16[2,528,512]{2,1,0:T(8,128)(2,1)} %get-tuple-element.32), channel_id=1, source_target_pairs={{0,5},{1,6},{2,7},{3,4},{4,1},{5,2},{6,3},{7,0},{8,13},{9,14},{10,... | collective-permute-start | bytes 3244040 | tf_op jit(solution)/shard_map/ppermute | solution.py:56
  55.1 9.7 %collective-permute-start.10 = (bf16[96,1536]{1,0:T(8,128)(2,1)S(1)}, bf16[96,1536]{1,0:T(8,128)(2,1)S(1)}, u32[]{:S(2)}, u32[]{:S(2)}) collective-permute-start(bf16[96,1536]{1,0:T(8,128)(2,1)S(1)} %get-tuple-element.41), channel_id=1, source_target_pairs={{0,64},{4,20},{8,72},{12,28},{16,80},{20,4},{24,88},{28,12},{32,96... | collective-permute-start | bytes 884744 | tf_op jit(solution)/shard_map/ppermute | solution.py:37
  57.7 8.2 %collective-permute-start.8 = (bf16[96,1536]{1,0:T(8,128)(2,1)S(1)}, bf16[96,1536]{1,0:T(8,128)(2,1)S(1)}, u32[]{:S(2)}, u32[]{:S(2)}) collective-permute-start(bf16[96,1536]{1,0:T(8,128)(2,1)S(1)} %get-tuple-element.39), channel_id=1, source_target_pairs={{0,32},{4,12},{8,40},{12,20},{16,48},{20,28},{24,56},{28,4},{32,64... | collective-permute-start | bytes 884744 | tf_op jit(solution)/shard_map/ppermute | solution.py:37
  58.1 7.7 %collective-permute-start.9 = (bf16[96,1536]{1,0:T(8,128)(2,1)S(1)}, bf16[96,1536]{1,0:T(8,128)(2,1)S(1)}, u32[]{:S(2)}, u32[]{:S(2)}) collective-permute-start(bf16[96,1536]{1,0:T(8,128)(2,1)S(1)} %get-tuple-element.40), channel_id=1, source_target_pairs={{0,96},{4,28},{8,104},{12,4},{16,112},{20,12},{24,120},{28,20},{32... | collective-permute-start | bytes 884744 | tf_op jit(solution)/shard_map/ppermute | solution.py:37
  77.5 16.7 %collective-permute-start.11 = (bf16[384,1536]{1,0:T(8,128)(2,1)S(1)}, bf16[384,1536]{1,0:T(8,128)(2,1)S(1)}, u32[]{:S(2)}, u32[]{:S(2)}) collective-permute-start(bf16[384,1536]{1,0:T(8,128)(2,1)S(1)} %get-tuple-element.43), channel_id=1, source_target_pairs={{0,8},{4,36},{8,16},{12,44},{16,24},{20,52},{24,0},{28,60},{32,40}... | collective-permute-start | bytes 3538952 | tf_op jit(solution)/shard_map/ppermute | solution.py:37
  78.8 27.3 %collective-permute-start.12 = (bf16[384,1536]{1,0:T(8,128)(2,1)S(1)}, bf16[384,1536]{1,0:T(8,128)(2,1)S(1)}, u32[]{:S(2)}, u32[]{:S(2)}) collective-permute-start(bf16[384,1536]{1,0:T(8,128)(2,1)S(1)} %get-tuple-element.44), channel_id=1, source_target_pairs={{0,24},{4,100},{8,0},{12,108},{16,8},{20,116},{24,16},{28,124},{32... | collective-permute-start | bytes 3538952 | tf_op jit(solution)/shard_map/ppermute | solution.py:37
  80.3 27.6 %collective-permute-start.13 = (bf16[384,1536]{1,0:T(8,128)(2,1)S(1)}, bf16[384,1536]{1,0:T(8,128)(2,1)S(1)}, u32[]{:S(2)}, u32[]{:S(2)}) collective-permute-start(bf16[384,1536]{1,0:T(8,128)(2,1)S(1)} %get-tuple-element.45), channel_id=1, source_target_pairs={{0,16},{4,68},{8,24},{12,76},{16,0},{20,84},{24,8},{28,92},{32,48}... | collective-permute-start | bytes 3538952 | tf_op jit(solution)/shard_map/ppermute | solution.py:37
  81.9 30.6 %collective-permute-start.17 = (bf16[96,1536]{1,0:T(8,128)(2,1)S(1)}, bf16[96,1536]{1,0:T(8,128)(2,1)S(1)}, u32[]{:S(2)}, u32[]{:S(2)}) collective-permute-start(bf16[96,1536]{1,0:T(8,128)(2,1)S(1)} %add_convert_fusion.refs_3_), channel_id=1, source_target_pairs={{0,2},{1,3},{2,0},{3,1},{4,6},{5,7},{6,4},{7,5},{8,10},{9,11},{10,... | collective-permute-start | bytes 884744 | tf_op jit(solution)/shard_map/ppermute | solution.py:41
  108.5 7.1 %collective-permute-start.14 = (bf16[96,1536]{1,0:T(8,128)(2,1)S(1)}, bf16[96,1536]{1,0:T(8,128)(2,1)S(1)}, u32[]{:S(2)}, u32[]{:S(2)}) collective-permute-start(bf16[96,1536]{1,0:T(8,128)(2,1)S(1)} %get-tuple-element.47), channel_id=1, source_target_pairs={{0,32},{4,12},{8,40},{12,20},{16,48},{20,28},{24,56},{28,4},{32,64... | collective-permute-start | bytes 884744 | tf_op jit(solution)/shard_map/ppermute | solution.py:37
  109.5 8.6 %collective-permute-start.15 = (bf16[96,1536]{1,0:T(8,128)(2,1)S(1)}, bf16[96,1536]{1,0:T(8,128)(2,1)S(1)}, u32[]{:S(2)}, u32[]{:S(2)}) collective-permute-start(bf16[96,1536]{1,0:T(8,128)(2,1)S(1)} %get-tuple-element.48), channel_id=1, source_target_pairs={{0,96},{4,28},{8,104},{12,4},{16,112},{20,12},{24,120},{28,20},{32... | collective-permute-start | bytes 884744 | tf_op jit(solution)/shard_map/ppermute | solution.py:37
  111.3 8.3 %collective-permute-start.16 = (bf16[96,1536]{1,0:T(8,128)(2,1)S(1)}, bf16[96,1536]{1,0:T(8,128)(2,1)S(1)}, u32[]{:S(2)}, u32[]{:S(2)}) collective-permute-start(bf16[96,1536]{1,0:T(8,128)(2,1)S(1)} %get-tuple-element.49), channel_id=1, source_target_pairs={{0,64},{4,20},{8,72},{12,28},{16,80},{20,4},{24,88},{28,12},{32,96... | collective-permute-start | bytes 884744 | tf_op jit(solution)/shard_map/ppermute | solution.py:37
  119.7 3.4 %collective-permute-start.18 = (f32[48,1536]{1,0:T(8,128)S(1)}, f32[48,1536]{1,0:T(8,128)S(1)}, u32[]{:S(2)}, u32[]{:S(2)}) collective-permute-start(f32[48,1536]{1,0:T(8,128)S(1)} %slice.9), channel_id=1, source_target_pairs={{0,4},{4,0},{8,12},{12,8},{16,20},{20,16},{24,28},{28,24},{32,36},... | collective-permute-start | bytes 884744 | tf_op jit(solution)/shard_map/ppermute | solution.py:46

commit v7 on v6

--- a/solution.py
+++ b/solution.py
@@ -15,6 +15,7 @@
 LANES = 128
 ROWS = 8
 SLAB = 384
+WINDOWS = ((0, 0), (1, 64), (1, 192), (2, 256))
 BF16 = jnp.bfloat16
 F32 = jnp.float32
 
@@ -104,19 +105,19 @@
             for axis in range(2):
                 row = jnp.broadcast_to(lanes[2 * basis + axis : 2 * basis + axis + 1, :], (LANES, 3 * LANES))
                 band = pltpu.roll(row, LANES - TAPS // 2, axis=1, stride=1, stride_axis=0)
-                if axis == 1:
-                    band = band.T
-                band = band.astype(BF16)
-                table = across if axis == 1 else down
-                table[basis] = jnp.zeros((TILE, TILE), BF16)
+                if axis == 0:
+                    centred = pltpu.roll(row, LANES // 2 - TAPS // 2, axis=1, stride=1, stride_axis=0)
+                    down[basis, 0] = band[:, LANES:].astype(BF16)
+                    down[basis, 1] = centred[:, : 2 * LANES].astype(BF16)
+                    down[basis, 2] = band[:, : 2 * LANES].astype(BF16)
+                    continue
+                band = band.T.astype(BF16)
+                across[basis] = jnp.zeros((TILE, TILE), BF16)
                 for block in range(TILE // LANES):
                     first = (block - 1) * LANES
                     low, high = max(first, 0), min(first + 3 * LANES, TILE)
                     span = slice(block * LANES, (block + 1) * LANES)
-                    if axis == 1:
-                        table[basis, low:high, span] = band[low - first : high - first, :]
-                    else:
-                        table[basis, span, low:high] = band[:, low - first : high - first]
+                    across[basis, low:high, span] = band[low - first : high - first, :]
 
     rows = lax.broadcasted_iota(jnp.int32, (TILE, 1), 0).astype(F32)
     columns = lax.broadcasted_iota(jnp.int32, (1, TILE), 1).astype(F32)
@@ -127,7 +128,13 @@
     total = jnp.zeros((TILE, TILE), F32)
     for basis in range(BASES):
         middle = jnp.dot(images[tile], across[basis], preferred_element_type=F32).astype(BF16)
-        smoothed = jnp.dot(down[basis], middle, preferred_element_type=F32)
+        smoothed = jnp.concatenate(
+            [
+                jnp.dot(down[basis, kind], middle[first : first + 2 * LANES], preferred_element_type=F32)
+                for kind, first in WINDOWS
+            ],
+            axis=0,
+        )
         c0, c1, c2 = (factors[basis, pl.ds(tile, 1), k : k + 1] for k in range(3))
         total += ((c0 + c1 * columns) + c2 * rows) * smoothed
     inverse = 1.0 / variances[tile].astype(F32)
@@ -195,7 +202,7 @@
             pltpu.VMEM((4, TILE, TILE), BF16),
             pltpu.VMEM((4, TILE, TILE), BF16),
             pltpu.VMEM((BASES, TILE, TILE), BF16),
-            pltpu.VMEM((BASES, TILE, TILE), BF16),
+            pltpu.VMEM((BASES, 3, LANES, 2 * LANES), BF16),
             pltpu.VMEM((8, 3 * LANES), F32),
             pltpu.VMEM((BASES, 8, LANES), F32),
             pltpu.VMEM((4, TILE + 16, TILE), BF16),
@@ -288,19 +295,19 @@
 FRAME = (PATCH_PIX // ROWS + 1, ROWS, PATCH_PIX)
 
 
-def frame_options(tiles):
+def frame_options(tiles, grant):
     cost = pl.CostEstimate(flops=tiles << 29, bytes_accessed=(5 + tiles) << 20, transcendentals=0)
-    return dict(compiler_params=pltpu.CompilerParams(vmem_limit_bytes=36 << 20), cost_estimate=cost)
+    return dict(compiler_params=pltpu.CompilerParams(vmem_limit_bytes=grant << 20), cost_estimate=cost)
 
 
 def opposite_frame(stacks):
     return pl.pallas_call(
-        opposite_kernel, out_shape=SLABS, scratch_shapes=[pltpu.VMEM(FRAME, F32)], **frame_options(4)
+        opposite_kernel, out_shape=SLABS, scratch_shapes=[pltpu.VMEM(FRAME, F32)], **frame_options(4, 22)
     )(*stacks)
 
 
 def start_frame(stacks):
-    return pl.pallas_call(start_kernel, out_shape=jax.ShapeDtypeStruct(FRAME, F32), **frame_options(8))(*stacks)
+    return pl.pallas_call(start_kernel, out_shape=jax.ShapeDtypeStruct(FRAME, F32), **frame_options(8, 20))(*stacks)
 
 
 def finish_frame(frame, stacks, after):
@@ -310,7 +317,7 @@
         in_specs=[pl.BlockSpec(memory_space=space) for space in spaces],
         out_shape=SLABS + [jax.ShapeDtypeStruct(FRAME, F32)],
         input_output_aliases={0: 4},
-        **frame_options(4),
+        **frame_options(4, 30),
     )(frame, *stacks, after)[:4]
 
 
@@ -329,7 +336,7 @@
     return pl.pallas_call(
         functools.partial(sum_kernel, count),
         out_shape=[out] * 4,
-        compiler_params=pltpu.CompilerParams(vmem_limit_bytes=40 << 20),
+        compiler_params=pltpu.CompilerParams(vmem_limit_bytes=12 << 20),
         cost_estimate=pl.CostEstimate(flops=3 << 20, bytes_accessed=(count + 1) << 20, transcendentals=0),
     )(*slabs)
 

time: 124 us -> 121 us (0.976)
  Pallas kernels: 25.4 us -> 22.6 us
    pallas_call x1, Pallas kernels: 13.1 us -> 11.6 us  [match_tiles(): pl.pallas_call(match_kernel, grid=(4,), in_specs=[pl.BlockSpec(memory_spa...]
where the time goes in v7:
time: 121 us
  waiting for transfers between devices  64.9 us (54%)
  starting transfers between devices  29.8 us (25%)
  Pallas kernels  22.6 us (19%)
  local copies, waits for them, and re-layouts  1.64 us (1%)
    ppermute x12, waiting for transfers between devices, turn(): return lax.ppermute(value, 'visit', pairs)  41.7 us
    ppermute x12, starting transfers between devices, turn(): return lax.ppermute(value, 'visit', pairs)  18.1 us
    ppermute x3, waiting for transfers between devices, across_z(): return lax.ppermute(value, 'patch', [(z, (z + step) % 4) for z in range(4)])  14.2 us
    pallas_call x1, Pallas kernels, match_tiles(): pl.pallas_call(match_kernel, grid=(4,), in_specs=[pl.BlockSpec(memory_spa...  11.6 us
    ppermute x2, waiting for transfers between devices, across_both(): return lax.ppermute(value, ('visit', 'patch'), pairs)  7.58 us
    pallas_call x1, Pallas kernels, start_frame(): pl.pallas_call(start_kernel, out_shape=jax.ShapeDtypeStruct(FRAME, F32),...  4.46 us
    ppermute x2, starting transfers between devices, across_both(): return lax.ppermute(value, ('visit', 'patch'), pairs)  4.12 us
    ppermute x3, starting transfers between devices, across_z(): return lax.ppermute(value, 'patch', [(z, (z + step) % 4) for z in range(4)])  3.86 us
  transfers between devices with their start and end apart: 19, of which 14 were waited for; matrix products, arithmetic and copies ran while one was open for 0% of the time, Pallas kernels for 7%

profile of v7, /device:TPU:1, one launch (start us, length us, event | category | flops | bytes accessed | tf_op | source)
XLA Modules:
  0.0 120.9 jit_solution(9514392625060339656)
XLA Ops:
  0.6 11.6 %shard_map.77 = (bf16[2,2,528,512]{3,2,1,0:T(8,128)(2,1)}, bf16[2,528,512]{2,1,0:T(8,128)(2,1)}, bf16[2,528,512]{2,1,0:T(8,128)(2,1)}, bf16[2,2,528,512]{3,2,1,0...) custom-call(s32[2,4]{1,0:T(2,128)} %bitcast.23, s32[2,2,4]{2,1,0:T(2,128)} %bitcast.21, ...), custom_call_target="tpu_custom_call" | custom-call | flops 6442450944 | bytes 12582912 | tf_op jit(solution)/shard_map/pallas_call | solution.py:191
  12.2 1.5 %collective-permute-start = (bf16[2,2,528,512]{3,2,1,0:T(8,128)(2,1)}, bf16[2,2,528,512]{3,2,1,0:T(8,128)(2,1)S(1)}, u32[]{:S(2)}, u32[]{:S(2)}) collective-permute-start(bf16[2,2,528,512]{3,2,1,0:T(8,128)(2,1)} %get-tuple-element.27), channel_id=1, source_target_pairs={{0,4},{4,0},{8,12},{12,8},{16,20},{20,16},{24,28},{28,24},{32,36},... | collective-permute-start | bytes 6488072 | tf_op jit(solution)/shard_map/ppermute | solution.py:47
  13.7 3.9 %collective-permute-start.2 = (bf16[2,528,512]{2,1,0:T(8,128)(2,1)}, bf16[2,528,512]{2,1,0:T(8,128)(2,1)S(1)}, u32[]{:S(2)}, u32[]{:S(2)}) collective-permute-start(bf16[2,528,512]{2,1,0:T(8,128)(2,1)} %get-tuple-element.29), channel_id=1, source_target_pairs={{0,3},{1,0},{2,1},{3,2},{4,7},{5,4},{6,5},{7,6},{8,11},{9,8},{10,9... | collective-permute-start | bytes 3244040 | tf_op jit(solution)/shard_map/ppermute | solution.py:42
  17.8 1.6 %copy-done = bf16[2,2,528,512]{3,2,1,0:T(8,128)(2,1)S(1)} copy-done((bf16[2,2,528,512]{3,2,1,0:T(8,128)(2,1)S(1)}, bf16[2,2,528,512]{3,2,1,0:T(8,128)(2,1)}, u32[]{:S(2)}) %copy-start) | copy-done | bytes 2162712
  19.4 3.0 %shard_map.79 = (bf16[384,1536]{1,0:T(8,128)(2,1)S(1)}, bf16[384,1536]{1,0:T(8,128)(2,1)S(1)}, bf16[384,1536]{1,0:T(8,128)(2,1)S(1)}, bf16[384,1536]{1,0:T(8,128)(2,1)S(1)}) custom-call(bf16[2,2,528,512]{3,2,1,0:T(8,128)(2,1)S(1)} %copy-done, bf16[2,2,528,512]{3,2,1,0:T(8,128)(2,1)S(1)} %collective-permute-done.refs_1_), custom_call_target="tpu_custom_call" | custom-call | flops 2147483648 | bytes 9437184 | tf_op jit(solution)/shard_map/pallas_call | solution.py:304
  22.4 1.5 %collective-permute-start.5 = (bf16[384,1536]{1,0:T(8,128)(2,1)S(1)}, bf16[384,1536]{1,0:T(8,128)(2,1)S(1)}, u32[]{:S(2)}, u32[]{:S(2)}) collective-permute-start(bf16[384,1536]{1,0:T(8,128)(2,1)S(1)} %get-tuple-element.35), channel_id=1, source_target_pairs={{0,8},{4,36},{8,16},{12,44},{16,24},{20,52},{24,0},{28,60},{32,40}... | collective-permute-start | bytes 3538952 | tf_op jit(solution)/shard_map/ppermute | solution.py:38
  23.9 1.5 %collective-permute-start.6 = (bf16[384,1536]{1,0:T(8,128)(2,1)S(1)}, bf16[384,1536]{1,0:T(8,128)(2,1)S(1)}, u32[]{:S(2)}, u32[]{:S(2)}) collective-permute-start(bf16[384,1536]{1,0:T(8,128)(2,1)S(1)} %get-tuple-element.36), channel_id=1, source_target_pairs={{0,24},{4,100},{8,0},{12,108},{16,8},{20,116},{24,16},{28,124},{32... | collective-permute-start | bytes 3538952 | tf_op jit(solution)/shard_map/ppermute | solution.py:38
  25.4 1.5 %collective-permute-start.7 = (bf16[384,1536]{1,0:T(8,128)(2,1)S(1)}, bf16[384,1536]{1,0:T(8,128)(2,1)S(1)}, u32[]{:S(2)}, u32[]{:S(2)}) collective-permute-start(bf16[384,1536]{1,0:T(8,128)(2,1)S(1)} %get-tuple-element.37), channel_id=1, source_target_pairs={{0,16},{4,68},{8,24},{12,76},{16,0},{20,84},{24,8},{28,92},{32,48}... | collective-permute-start | bytes 3538952 | tf_op jit(solution)/shard_map/ppermute | solution.py:38
  26.9 14.2 %collective-permute-done.2.refs_3_ = bf16[2,528,512]{2,1,0:T(8,128)(2,1)S(1)} collective-permute-done((bf16[2,528,512]{2,1,0:T(8,128)(2,1)}, bf16[2,528,512]{2,1,0:T(8,128)(2,1)S(1)}, u32[]{:S(2)}, u32[]{:S(2)}) %collective-permute-start.2) | collective-permute-done | bytes 1081376 | tf_op jit(solution)/shard_map/ppermute | solution.py:42
  41.1 4.1 %collective-permute-start.4 = (bf16[2,528,512]{2,1,0:T(8,128)(2,1)S(1)}, bf16[2,528,512]{2,1,0:T(8,128)(2,1)S(1)}, u32[]{:S(2)}, u32[]{:S(2)}) collective-permute-start(bf16[2,528,512]{2,1,0:T(8,128)(2,1)S(1)} %copy-done.3), channel_id=1, source_target_pairs={{0,7},{1,4},{2,5},{3,6},{4,3},{5,0},{6,1},{7,2},{8,15},{9,12},{10,... | collective-permute-start | bytes 3244040 | tf_op jit(solution)/shard_map/ppermute | solution.py:57
  45.2 5.9 %collective-permute-done.6.refs_2_ = bf16[384,1536]{1,0:T(8,128)(2,1)S(1)} collective-permute-done((bf16[384,1536]{1,0:T(8,128)(2,1)S(1)}, bf16[384,1536]{1,0:T(8,128)(2,1)S(1)}, u32[]{:S(2)}, u32[]{:S(2)}) %collective-permute-start.6) | collective-permute-done | bytes 1179680 | tf_op jit(solution)/shard_map/ppermute | solution.py:38
  51.2 1.8 %collective-permute-done.7.refs_3_ = bf16[384,1536]{1,0:T(8,128)(2,1)S(1)} collective-permute-done((bf16[384,1536]{1,0:T(8,128)(2,1)S(1)}, bf16[384,1536]{1,0:T(8,128)(2,1)S(1)}, u32[]{:S(2)}, u32[]{:S(2)}) %collective-permute-start.7) | collective-permute-done | bytes 1179680 | tf_op jit(solution)/shard_map/ppermute | solution.py:38
  53.6 2.5 %collective-permute-start.10 = (bf16[96,1536]{1,0:T(8,128)(2,1)S(1)}, bf16[96,1536]{1,0:T(8,128)(2,1)S(1)}, u32[]{:S(2)}, u32[]{:S(2)}) collective-permute-start(bf16[96,1536]{1,0:T(8,128)(2,1)S(1)} %get-tuple-element.41), channel_id=1, source_target_pairs={{0,64},{4,20},{8,72},{12,28},{16,80},{20,4},{24,88},{28,12},{32,96... | collective-permute-start | bytes 884744 | tf_op jit(solution)/shard_map/ppermute | solution.py:38
  56.5 2.3 %collective-permute-start.9 = (bf16[96,1536]{1,0:T(8,128)(2,1)S(1)}, bf16[96,1536]{1,0:T(8,128)(2,1)S(1)}, u32[]{:S(2)}, u32[]{:S(2)}) collective-permute-start(bf16[96,1536]{1,0:T(8,128)(2,1)S(1)} %get-tuple-element.40), channel_id=1, source_target_pairs={{0,96},{4,28},{8,104},{12,4},{16,112},{20,12},{24,120},{28,20},{32... | collective-permute-start | bytes 884744 | tf_op jit(solution)/shard_map/ppermute | solution.py:38
  58.8 4.5 %shard_map.78.refs_0_ = f32[193,8,1536]{2,1,0:T(8,128)S(1)} custom-call(bf16[2,2,528,512]{3,2,1,0:T(8,128)(2,1)S(1)} %copy-done.1, bf16[2,2,528,512]{3,2,1,0:T(8,128)(2,1)S(1)} %collective-permute-done.refs_1_, bf16[2,528,512]{2,1,0:T(8,128)(2,1)S(1)} %collective-permute-done.1.refs_2_, bf16[2,528,512]{2,1,0:T(8,128)(2,1)S(1)} %collective-permute-done.2.refs_3_), custom_call_target="tpu_custom_call" | custom-call | flops 4294967296 | bytes 13631488 | tf_op jit(solution)/shard_map/pallas_call | solution.py:310
  63.3 0.9 collective-permute-done.8
  64.4 4.3 %collective-permute-done.4.refs_2_ = bf16[2,528,512]{2,1,0:T(8,128)(2,1)S(1)} collective-permute-done((bf16[2,528,512]{2,1,0:T(8,128)(2,1)S(1)}, bf16[2,528,512]{2,1,0:T(8,128)(2,1)S(1)}, u32[]{:S(2)}, u32[]{:S(2)}) %collective-permute-start.4) | collective-permute-done | bytes 1081376 | tf_op jit(solution)/shard_map/ppermute | solution.py:57
  68.7 3.3 %collective-permute-done.3.refs_1_ = bf16[2,528,512]{2,1,0:T(8,128)(2,1)S(1)} collective-permute-done((bf16[2,528,512]{2,1,0:T(8,128)(2,1)S(1)}, bf16[2,528,512]{2,1,0:T(8,128)(2,1)S(1)}, u32[]{:S(2)}, u32[]{:S(2)}) %collective-permute-start.3) | collective-permute-done | bytes 1081376 | tf_op jit(solution)/shard_map/ppermute | solution.py:57
  71.9 2.4 %shard_map.81 = (bf16[384,1536]{1,0:T(8,128)(2,1)S(1)}, bf16[384,1536]{1,0:T(8,128)(2,1)S(1)}, bf16[384,1536]{1,0:T(8,128)(2,1)S(1)}, bf16[384,1536]{1,0:T(8,128)(2,1)S(1)}, f32[193,8,1536]{2,1,0:T(8,128)S(1)}) custom-call(f32[193,8,1536]{2,1,0:T(8,128)S(1)} %shard_map.78.refs_0_, ...), custom_call_target="tpu_custom_call", output_to_operand_aliasing={{4}: (0, {})} | custom-call | flops 2147483648 | bytes 9437184 | tf_op jit(solution)/shard_map/pallas_call | solution.py:315
  74.4 1.4 %collective-permute-start.11 = (bf16[384,1536]{1,0:T(8,128)(2,1)S(1)}, bf16[384,1536]{1,0:T(8,128)(2,1)S(1)}, u32[]{:S(2)}, u32[]{:S(2)}) collective-permute-start(bf16[384,1536]{1,0:T(8,128)(2,1)S(1)} %get-tuple-element.43), channel_id=1, source_target_pairs={{0,8},{4,36},{8,16},{12,44},{16,24},{20,52},{24,0},{28,60},{32,40}... | collective-permute-start | bytes 3538952 | tf_op jit(solution)/shard_map/ppermute | solution.py:38
  75.7 1.5 %collective-permute-start.12 = (bf16[384,1536]{1,0:T(8,128)(2,1)S(1)}, bf16[384,1536]{1,0:T(8,128)(2,1)S(1)}, u32[]{:S(2)}, u32[]{:S(2)}) collective-permute-start(bf16[384,1536]{1,0:T(8,128)(2,1)S(1)} %get-tuple-element.44), channel_id=1, source_target_pairs={{0,24},{4,100},{8,0},{12,108},{16,8},{20,116},{24,16},{28,124},{32... | collective-permute-start | bytes 3538952 | tf_op jit(solution)/shard_map/ppermute | solution.py:38
  77.2 1.6 %collective-permute-start.13 = (bf16[384,1536]{1,0:T(8,128)(2,1)S(1)}, bf16[384,1536]{1,0:T(8,128)(2,1)S(1)}, u32[]{:S(2)}, u32[]{:S(2)}) collective-permute-start(bf16[384,1536]{1,0:T(8,128)(2,1)S(1)} %get-tuple-element.45), channel_id=1, source_target_pairs={{0,16},{4,68},{8,24},{12,76},{16,0},{20,84},{24,8},{28,92},{32,48}... | collective-permute-start | bytes 3538952 | tf_op jit(solution)/shard_map/ppermute | solution.py:38
  78.8 12.2 %collective-permute-done.11.refs_1_ = bf16[384,1536]{1,0:T(8,128)(2,1)S(1)} collective-permute-done((bf16[384,1536]{1,0:T(8,128)(2,1)S(1)}, bf16[384,1536]{1,0:T(8,128)(2,1)S(1)}, u32[]{:S(2)}, u32[]{:S(2)}) %collective-permute-start.11) | collective-permute-done | bytes 1179680 | tf_op jit(solution)/shard_map/ppermute | solution.py:38
  91.1 13.8 %collective-permute-done.13.refs_3_ = bf16[384,1536]{1,0:T(8,128)(2,1)S(1)} collective-permute-done((bf16[384,1536]{1,0:T(8,128)(2,1)S(1)}, bf16[384,1536]{1,0:T(8,128)(2,1)S(1)}, u32[]{:S(2)}, u32[]{:S(2)}) %collective-permute-start.13) | collective-permute-done | bytes 1179680 | tf_op jit(solution)/shard_map/ppermute | solution.py:38
  105.4 1.0 collective-permute-start.14
  106.4 1.7 %collective-permute-start.15 = (bf16[96,1536]{1,0:T(8,128)(2,1)S(1)}, bf16[96,1536]{1,0:T(8,128)(2,1)S(1)}, u32[]{:S(2)}, u32[]{:S(2)}) collective-permute-start(bf16[96,1536]{1,0:T(8,128)(2,1)S(1)} %get-tuple-element.48), channel_id=1, source_target_pairs={{0,96},{4,28},{8,104},{12,4},{16,112},{20,12},{24,120},{28,20},{32... | collective-permute-start | bytes 884744 | tf_op jit(solution)/shard_map/ppermute | solution.py:38
  108.2 1.3 %collective-permute-start.16 = (bf16[96,1536]{1,0:T(8,128)(2,1)S(1)}, bf16[96,1536]{1,0:T(8,128)(2,1)S(1)}, u32[]{:S(2)}, u32[]{:S(2)}) collective-permute-start(bf16[96,1536]{1,0:T(8,128)(2,1)S(1)} %get-tuple-element.49), channel_id=1, source_target_pairs={{0,64},{4,20},{8,72},{12,28},{16,80},{20,4},{24,88},{28,12},{32,96... | collective-permute-start | bytes 884744 | tf_op jit(solution)/shard_map/ppermute | solution.py:38
  109.4 3.1 %collective-permute-done.14 = bf16[96,1536]{1,0:T(8,128)(2,1)S(1)} collective-permute-done((bf16[96,1536]{1,0:T(8,128)(2,1)S(1)}, bf16[96,1536]{1,0:T(8,128)(2,1)S(1)}, u32[]{:S(2)}, u32[]{:S(2)}) %collective-permute-start.14) | collective-permute-done | bytes 294944 | tf_op jit(solution)/shard_map/ppermute | solution.py:38
  112.6 2.4 %collective-permute-done.15 = bf16[96,1536]{1,0:T(8,128)(2,1)S(1)} collective-permute-done((bf16[96,1536]{1,0:T(8,128)(2,1)S(1)}, bf16[96,1536]{1,0:T(8,128)(2,1)S(1)}, u32[]{:S(2)}, u32[]{:S(2)}) %collective-permute-start.15) | collective-permute-done | bytes 294944 | tf_op jit(solution)/shard_map/ppermute | solution.py:38
  115.0 1.4 %collective-permute-done.16 = bf16[96,1536]{1,0:T(8,128)(2,1)S(1)} collective-permute-done((bf16[96,1536]{1,0:T(8,128)(2,1)S(1)}, bf16[96,1536]{1,0:T(8,128)(2,1)S(1)}, u32[]{:S(2)}, u32[]{:S(2)}) %collective-permute-start.16) | collective-permute-done | bytes 294944 | tf_op jit(solution)/shard_map/ppermute | solution.py:38
  116.6 2.2 %collective-permute-start.18 = (f32[48,1536]{1,0:T(8,128)S(1)}, f32[48,1536]{1,0:T(8,128)S(1)}, u32[]{:S(2)}, u32[]{:S(2)}) collective-permute-start(f32[48,1536]{1,0:T(8,128)S(1)} %slice.9), channel_id=1, source_target_pairs={{0,4},{4,0},{8,12},{12,8},{16,20},{20,16},{24,28},{28,24},{32,36},... | collective-permute-start | bytes 884744 | tf_op jit(solution)/shard_map/ppermute | solution.py:47
  118.8 1.2 %collective-permute-done.18 = f32[48,1536]{1,0:T(8,128)S(1)} collective-permute-done((f32[48,1536]{1,0:T(8,128)S(1)}, f32[48,1536]{1,0:T(8,128)S(1)}, u32[]{:S(2)}, u32[]{:S(2)}) %collective-permute-start.18) | collective-permute-done | bytes 294944 | tf_op jit(solution)/shard_map/ppermute | solution.py:47
  (24 shorter events, 3.2 us)
Async XLA Ops:
  12.2 5.6 %collective-permute-start = (bf16[2,2,528,512]{3,2,1,0:T(8,128)(2,1)}, bf16[2,2,528,512]{3,2,1,0:T(8,128)(2,1)S(1)}, u32[]{:S(2)}, u32[]{:S(2)}) collective-permute-start(bf16[2,2,528,512]{3,2,1,0:T(8,128)(2,1)} %get-tuple-element.27), channel_id=1, source_target_pairs={{0,4},{4,0},{8,12},{12,8},{16,20},{20,16},{24,28},{28,24},{32,36},... | collective-permute-start | bytes 6488072 | tf_op jit(solution)/shard_map/ppermute | solution.py:47
  13.7 27.4 %collective-permute-start.2 = (bf16[2,528,512]{2,1,0:T(8,128)(2,1)}, bf16[2,528,512]{2,1,0:T(8,128)(2,1)S(1)}, u32[]{:S(2)}, u32[]{:S(2)}) collective-permute-start(bf16[2,528,512]{2,1,0:T(8,128)(2,1)} %get-tuple-element.29), channel_id=1, source_target_pairs={{0,3},{1,0},{2,1},{3,2},{4,7},{5,4},{6,5},{7,6},{8,11},{9,8},{10,9... | collective-permute-start | bytes 3244040 | tf_op jit(solution)/shard_map/ppermute | solution.py:42
  17.6 27.6 %collective-permute-start.1 = (bf16[2,528,512]{2,1,0:T(8,128)(2,1)}, bf16[2,528,512]{2,1,0:T(8,128)(2,1)S(1)}, u32[]{:S(2)}, u32[]{:S(2)}) collective-permute-start(bf16[2,528,512]{2,1,0:T(8,128)(2,1)} %get-tuple-element.28), channel_id=1, source_target_pairs={{0,1},{1,2},{2,3},{3,0},{4,5},{5,6},{6,7},{7,4},{8,9},{9,10},{10,1... | collective-permute-start | bytes 3244040 | tf_op jit(solution)/shard_map/ppermute | solution.py:42
  17.8 1.6 %copy-start = (bf16[2,2,528,512]{3,2,1,0:T(8,128)(2,1)S(1)}, bf16[2,2,528,512]{3,2,1,0:T(8,128)(2,1)}, u32[]{:S(2)}) copy-start(bf16[2,2,528,512]{3,2,1,0:T(8,128)(2,1)} %get-tuple-element.26.refs_0_) | copy-start | bytes 6488068
  19.4 21.7 %copy-start.3 = (bf16[2,528,512]{2,1,0:T(8,128)(2,1)S(1)}, bf16[2,528,512]{2,1,0:T(8,128)(2,1)}, u32[]{:S(2)}) copy-start(bf16[2,528,512]{2,1,0:T(8,128)(2,1)} %get-tuple-element.34) | copy-start | bytes 3244036
  19.4 25.7 %copy-start.2 = (bf16[2,528,512]{2,1,0:T(8,128)(2,1)S(1)}, bf16[2,528,512]{2,1,0:T(8,128)(2,1)}, u32[]{:S(2)}) copy-start(bf16[2,528,512]{2,1,0:T(8,128)(2,1)} %get-tuple-element.32) | copy-start | bytes 3244036
  22.4 22.8 %collective-permute-start.5 = (bf16[384,1536]{1,0:T(8,128)(2,1)S(1)}, bf16[384,1536]{1,0:T(8,128)(2,1)S(1)}, u32[]{:S(2)}, u32[]{:S(2)}) collective-permute-start(bf16[384,1536]{1,0:T(8,128)(2,1)S(1)} %get-tuple-element.35), channel_id=1, source_target_pairs={{0,8},{4,36},{8,16},{12,44},{16,24},{20,52},{24,0},{28,60},{32,40}... | collective-permute-start | bytes 3538952 | tf_op jit(solution)/shard_map/ppermute | solution.py:38
  23.9 27.3 %collective-permute-start.6 = (bf16[384,1536]{1,0:T(8,128)(2,1)S(1)}, bf16[384,1536]{1,0:T(8,128)(2,1)S(1)}, u32[]{:S(2)}, u32[]{:S(2)}) collective-permute-start(bf16[384,1536]{1,0:T(8,128)(2,1)S(1)} %get-tuple-element.36), channel_id=1, source_target_pairs={{0,24},{4,100},{8,0},{12,108},{16,8},{20,116},{24,16},{28,124},{32... | collective-permute-start | bytes 3538952 | tf_op jit(solution)/shard_map/ppermute | solution.py:38
  25.4 27.6 %collective-permute-start.7 = (bf16[384,1536]{1,0:T(8,128)(2,1)S(1)}, bf16[384,1536]{1,0:T(8,128)(2,1)S(1)}, u32[]{:S(2)}, u32[]{:S(2)}) collective-permute-start(bf16[384,1536]{1,0:T(8,128)(2,1)S(1)} %get-tuple-element.37), channel_id=1, source_target_pairs={{0,16},{4,68},{8,24},{12,76},{16,0},{20,84},{24,8},{28,92},{32,48}... | collective-permute-start | bytes 3538952 | tf_op jit(solution)/shard_map/ppermute | solution.py:38
  41.1 27.6 %collective-permute-start.4 = (bf16[2,528,512]{2,1,0:T(8,128)(2,1)S(1)}, bf16[2,528,512]{2,1,0:T(8,128)(2,1)S(1)}, u32[]{:S(2)}, u32[]{:S(2)}) collective-permute-start(bf16[2,528,512]{2,1,0:T(8,128)(2,1)S(1)} %copy-done.3), channel_id=1, source_target_pairs={{0,7},{1,4},{2,5},{3,6},{4,3},{5,0},{6,1},{7,2},{8,15},{9,12},{10,... | collective-permute-start | bytes 3244040 | tf_op jit(solution)/shard_map/ppermute | solution.py:57
  45.2 13.7 %copy-start.1 = (bf16[2,2,528,512]{3,2,1,0:T(8,128)(2,1)S(1)}, bf16[2,2,528,512]{3,2,1,0:T(8,128)(2,1)}, u32[]{:S(2)}) copy-start(bf16[2,2,528,512]{3,2,1,0:T(8,128)(2,1)} %get-tuple-element.26.refs_0_) | copy-start | bytes 6488068
  45.2 26.8 %collective-permute-start.3 = (bf16[2,528,512]{2,1,0:T(8,128)(2,1)S(1)}, bf16[2,528,512]{2,1,0:T(8,128)(2,1)S(1)}, u32[]{:S(2)}, u32[]{:S(2)}) collective-permute-start(bf16[2,528,512]{2,1,0:T(8,128)(2,1)S(1)} %copy-done.2), channel_id=1, source_target_pairs={{0,5},{1,6},{2,7},{3,4},{4,1},{5,2},{6,3},{7,0},{8,13},{9,14},{10,... | collective-permute-start | bytes 3244040 | tf_op jit(solution)/shard_map/ppermute | solution.py:57
  53.6 9.7 %collective-permute-start.10 = (bf16[96,1536]{1,0:T(8,128)(2,1)S(1)}, bf16[96,1536]{1,0:T(8,128)(2,1)S(1)}, u32[]{:S(2)}, u32[]{:S(2)}) collective-permute-start(bf16[96,1536]{1,0:T(8,128)(2,1)S(1)} %get-tuple-element.41), channel_id=1, source_target_pairs={{0,64},{4,20},{8,72},{12,28},{16,80},{20,4},{24,88},{28,12},{32,96... | collective-permute-start | bytes 884744 | tf_op jit(solution)/shard_map/ppermute | solution.py:38
  56.1 8.1 %collective-permute-start.8 = (bf16[96,1536]{1,0:T(8,128)(2,1)S(1)}, bf16[96,1536]{1,0:T(8,128)(2,1)S(1)}, u32[]{:S(2)}, u32[]{:S(2)}) collective-permute-start(bf16[96,1536]{1,0:T(8,128)(2,1)S(1)} %get-tuple-element.39), channel_id=1, source_target_pairs={{0,32},{4,12},{8,40},{12,20},{16,48},{20,28},{24,56},{28,4},{32,64... | collective-permute-start | bytes 884744 | tf_op jit(solution)/shard_map/ppermute | solution.py:38
  56.5 7.7 %collective-permute-start.9 = (bf16[96,1536]{1,0:T(8,128)(2,1)S(1)}, bf16[96,1536]{1,0:T(8,128)(2,1)S(1)}, u32[]{:S(2)}, u32[]{:S(2)}) collective-permute-start(bf16[96,1536]{1,0:T(8,128)(2,1)S(1)} %get-tuple-element.40), channel_id=1, source_target_pairs={{0,96},{4,28},{8,104},{12,4},{16,112},{20,12},{24,120},{28,20},{32... | collective-permute-start | bytes 884744 | tf_op jit(solution)/shard_map/ppermute | solution.py:38
  74.4 16.7 %collective-permute-start.11 = (bf16[384,1536]{1,0:T(8,128)(2,1)S(1)}, bf16[384,1536]{1,0:T(8,128)(2,1)S(1)}, u32[]{:S(2)}, u32[]{:S(2)}) collective-permute-start(bf16[384,1536]{1,0:T(8,128)(2,1)S(1)} %get-tuple-element.43), channel_id=1, source_target_pairs={{0,8},{4,36},{8,16},{12,44},{16,24},{20,52},{24,0},{28,60},{32,40}... | collective-permute-start | bytes 3538952 | tf_op jit(solution)/shard_map/ppermute | solution.py:38
  75.7 15.3 %collective-permute-start.12 = (bf16[384,1536]{1,0:T(8,128)(2,1)S(1)}, bf16[384,1536]{1,0:T(8,128)(2,1)S(1)}, u32[]{:S(2)}, u32[]{:S(2)}) collective-permute-start(bf16[384,1536]{1,0:T(8,128)(2,1)S(1)} %get-tuple-element.44), channel_id=1, source_target_pairs={{0,24},{4,100},{8,0},{12,108},{16,8},{20,116},{24,16},{28,124},{32... | collective-permute-start | bytes 3538952 | tf_op jit(solution)/shard_map/ppermute | solution.py:38
  77.2 27.6 %collective-permute-start.13 = (bf16[384,1536]{1,0:T(8,128)(2,1)S(1)}, bf16[384,1536]{1,0:T(8,128)(2,1)S(1)}, u32[]{:S(2)}, u32[]{:S(2)}) collective-permute-start(bf16[384,1536]{1,0:T(8,128)(2,1)S(1)} %get-tuple-element.45), channel_id=1, source_target_pairs={{0,16},{4,68},{8,24},{12,76},{16,0},{20,84},{24,8},{28,92},{32,48}... | collective-permute-start | bytes 3538952 | tf_op jit(solution)/shard_map/ppermute | solution.py:38
  78.8 30.7 %collective-permute-start.17 = (bf16[96,1536]{1,0:T(8,128)(2,1)S(1)}, bf16[96,1536]{1,0:T(8,128)(2,1)S(1)}, u32[]{:S(2)}, u32[]{:S(2)}) collective-permute-start(bf16[96,1536]{1,0:T(8,128)(2,1)S(1)} %add_convert_fusion.refs_3_), channel_id=1, source_target_pairs={{0,2},{1,3},{2,0},{3,1},{4,6},{5,7},{6,4},{7,5},{8,10},{9,11},{10,... | collective-permute-start | bytes 884744 | tf_op jit(solution)/shard_map/ppermute | solution.py:42
  105.4 7.1 %collective-permute-start.14 = (bf16[96,1536]{1,0:T(8,128)(2,1)S(1)}, bf16[96,1536]{1,0:T(8,128)(2,1)S(1)}, u32[]{:S(2)}, u32[]{:S(2)}) collective-permute-start(bf16[96,1536]{1,0:T(8,128)(2,1)S(1)} %get-tuple-element.47), channel_id=1, source_target_pairs={{0,32},{4,12},{8,40},{12,20},{16,48},{20,28},{24,56},{28,4},{32,64... | collective-permute-start | bytes 884744 | tf_op jit(solution)/shard_map/ppermute | solution.py:38
  106.4 8.6 %collective-permute-start.15 = (bf16[96,1536]{1,0:T(8,128)(2,1)S(1)}, bf16[96,1536]{1,0:T(8,128)(2,1)S(1)}, u32[]{:S(2)}, u32[]{:S(2)}) collective-permute-start(bf16[96,1536]{1,0:T(8,128)(2,1)S(1)} %get-tuple-element.48), channel_id=1, source_target_pairs={{0,96},{4,28},{8,104},{12,4},{16,112},{20,12},{24,120},{28,20},{32... | collective-permute-start | bytes 884744 | tf_op jit(solution)/shard_map/ppermute | solution.py:38
  108.2 8.3 %collective-permute-start.16 = (bf16[96,1536]{1,0:T(8,128)(2,1)S(1)}, bf16[96,1536]{1,0:T(8,128)(2,1)S(1)}, u32[]{:S(2)}, u32[]{:S(2)}) collective-permute-start(bf16[96,1536]{1,0:T(8,128)(2,1)S(1)} %get-tuple-element.49), channel_id=1, source_target_pairs={{0,64},{4,20},{8,72},{12,28},{16,80},{20,4},{24,88},{28,12},{32,96... | collective-permute-start | bytes 884744 | tf_op jit(solution)/shard_map/ppermute | solution.py:38
  116.6 3.4 %collective-permute-start.18 = (f32[48,1536]{1,0:T(8,128)S(1)}, f32[48,1536]{1,0:T(8,128)S(1)}, u32[]{:S(2)}, u32[]{:S(2)}) collective-permute-start(f32[48,1536]{1,0:T(8,128)S(1)} %slice.9), channel_id=1, source_target_pairs={{0,4},{4,0},{8,12},{12,8},{16,20},{20,16},{24,28},{28,24},{32,36},... | collective-permute-start | bytes 884744 | tf_op jit(solution)/shard_map/ppermute | solution.py:47

commit v8 on v7

--- a/solution.py
+++ b/solution.py
@@ -224,7 +224,7 @@
 
 
 def finish_kernel(count, *refs):
-    stacks, outs, frame = refs[1 : 1 + count], refs[-5:-1], refs[-1]
+    frame, stacks, outs = refs[0], refs[1 : 1 + count], refs[-5:-1]
     add_tiles(0, stacks, frame)
     pack(frame, outs)
 

time: 121 us -> 121 us (level)
  transfers between devices with their start and end apart: 19 -> 19, of which waited for: 14 -> 13; matrix products, arithmetic and copies ran while one was open for 0% -> 0% of each run, Pallas kernels for 7% -> 7%
where the time goes in v8:
time: 121 us
  waiting for transfers between devices  65 us (54%)
  starting transfers between devices  29.8 us (25%)
  Pallas kernels  22.6 us (19%)
  local copies, waits for them, and re-layouts  1.64 us (1%)
    ppermute x12, waiting for transfers between devices, turn(): return lax.ppermute(value, 'visit', pairs)  41.8 us
    ppermute x12, starting transfers between devices, turn(): return lax.ppermute(value, 'visit', pairs)  18.1 us
    ppermute x3, waiting for transfers between devices, across_z(): return lax.ppermute(value, 'patch', [(z, (z + step) % 4) for z in range(4)])  14.1 us
    pallas_call x1, Pallas kernels, match_tiles(): pl.pallas_call(match_kernel, grid=(4,), in_specs=[pl.BlockSpec(memory_spa...  11.5 us
    ppermute x2, waiting for transfers between devices, across_both(): return lax.ppermute(value, ('visit', 'patch'), pairs)  7.55 us
    pallas_call x1, Pallas kernels, start_frame(): pl.pallas_call(start_kernel, out_shape=jax.ShapeDtypeStruct(FRAME, F32),...  4.46 us
    ppermute x2, starting transfers between devices, across_both(): return lax.ppermute(value, ('visit', 'patch'), pairs)  4.12 us
    ppermute x3, starting transfers between devices, across_z(): return lax.ppermute(value, 'patch', [(z, (z + step) % 4) for z in range(4)])  3.86 us
  transfers between devices with their start and end apart: 19, of which 13 were waited for; matrix products, arithmetic and copies ran while one was open for 0% of the time, Pallas kernels for 7%

profile of v8, /device:TPU:1, one launch (start us, length us, event | category | flops | bytes accessed | tf_op | source)
XLA Modules:
  0.0 120.9 jit_solution(12470326528437032579)
XLA Ops:
  0.6 11.5 %shard_map.77 = (bf16[2,2,528,512]{3,2,1,0:T(8,128)(2,1)}, bf16[2,528,512]{2,1,0:T(8,128)(2,1)}, bf16[2,528,512]{2,1,0:T(8,128)(2,1)}, bf16[2,2,528,512]{3,2,1,0...) custom-call(s32[2,4]{1,0:T(2,128)} %bitcast.23, s32[2,2,4]{2,1,0:T(2,128)} %bitcast.21, ...), custom_call_target="tpu_custom_call" | custom-call | flops 6442450944 | bytes 12582912 | tf_op jit(solution)/shard_map/pallas_call | solution.py:191
  12.2 1.5 %collective-permute-start = (bf16[2,2,528,512]{3,2,1,0:T(8,128)(2,1)}, bf16[2,2,528,512]{3,2,1,0:T(8,128)(2,1)S(1)}, u32[]{:S(2)}, u32[]{:S(2)}) collective-permute-start(bf16[2,2,528,512]{3,2,1,0:T(8,128)(2,1)} %get-tuple-element.27), channel_id=1, source_target_pairs={{0,4},{4,0},{8,12},{12,8},{16,20},{20,16},{24,28},{28,24},{32,36},... | collective-permute-start | bytes 6488072 | tf_op jit(solution)/shard_map/ppermute | solution.py:47
  13.7 3.9 %collective-permute-start.2 = (bf16[2,528,512]{2,1,0:T(8,128)(2,1)}, bf16[2,528,512]{2,1,0:T(8,128)(2,1)S(1)}, u32[]{:S(2)}, u32[]{:S(2)}) collective-permute-start(bf16[2,528,512]{2,1,0:T(8,128)(2,1)} %get-tuple-element.29), channel_id=1, source_target_pairs={{0,3},{1,0},{2,1},{3,2},{4,7},{5,4},{6,5},{7,6},{8,11},{9,8},{10,9... | collective-permute-start | bytes 3244040 | tf_op jit(solution)/shard_map/ppermute | solution.py:42
  17.8 1.6 %copy-done = bf16[2,2,528,512]{3,2,1,0:T(8,128)(2,1)S(1)} copy-done((bf16[2,2,528,512]{3,2,1,0:T(8,128)(2,1)S(1)}, bf16[2,2,528,512]{3,2,1,0:T(8,128)(2,1)}, u32[]{:S(2)}) %copy-start) | copy-done | bytes 2162712
  19.4 3.0 %shard_map.79 = (bf16[384,1536]{1,0:T(8,128)(2,1)S(1)}, bf16[384,1536]{1,0:T(8,128)(2,1)S(1)}, bf16[384,1536]{1,0:T(8,128)(2,1)S(1)}, bf16[384,1536]{1,0:T(8,128)(2,1)S(1)}) custom-call(bf16[2,2,528,512]{3,2,1,0:T(8,128)(2,1)S(1)} %copy-done, bf16[2,2,528,512]{3,2,1,0:T(8,128)(2,1)S(1)} %collective-permute-done.refs_1_), custom_call_target="tpu_custom_call" | custom-call | flops 2147483648 | bytes 9437184 | tf_op jit(solution)/shard_map/pallas_call | solution.py:304
  22.4 1.5 %collective-permute-start.5 = (bf16[384,1536]{1,0:T(8,128)(2,1)S(1)}, bf16[384,1536]{1,0:T(8,128)(2,1)S(1)}, u32[]{:S(2)}, u32[]{:S(2)}) collective-permute-start(bf16[384,1536]{1,0:T(8,128)(2,1)S(1)} %get-tuple-element.35), channel_id=1, source_target_pairs={{0,8},{4,36},{8,16},{12,44},{16,24},{20,52},{24,0},{28,60},{32,40}... | collective-permute-start | bytes 3538952 | tf_op jit(solution)/shard_map/ppermute | solution.py:38
  23.9 1.5 %collective-permute-start.6 = (bf16[384,1536]{1,0:T(8,128)(2,1)S(1)}, bf16[384,1536]{1,0:T(8,128)(2,1)S(1)}, u32[]{:S(2)}, u32[]{:S(2)}) collective-permute-start(bf16[384,1536]{1,0:T(8,128)(2,1)S(1)} %get-tuple-element.36), channel_id=1, source_target_pairs={{0,24},{4,100},{8,0},{12,108},{16,8},{20,116},{24,16},{28,124},{32... | collective-permute-start | bytes 3538952 | tf_op jit(solution)/shard_map/ppermute | solution.py:38
  25.4 1.5 %collective-permute-start.7 = (bf16[384,1536]{1,0:T(8,128)(2,1)S(1)}, bf16[384,1536]{1,0:T(8,128)(2,1)S(1)}, u32[]{:S(2)}, u32[]{:S(2)}) collective-permute-start(bf16[384,1536]{1,0:T(8,128)(2,1)S(1)} %get-tuple-element.37), channel_id=1, source_target_pairs={{0,16},{4,68},{8,24},{12,76},{16,0},{20,84},{24,8},{28,92},{32,48}... | collective-permute-start | bytes 3538952 | tf_op jit(solution)/shard_map/ppermute | solution.py:38
  26.9 14.1 %collective-permute-done.2.refs_3_ = bf16[2,528,512]{2,1,0:T(8,128)(2,1)S(1)} collective-permute-done((bf16[2,528,512]{2,1,0:T(8,128)(2,1)}, bf16[2,528,512]{2,1,0:T(8,128)(2,1)S(1)}, u32[]{:S(2)}, u32[]{:S(2)}) %collective-permute-start.2) | collective-permute-done | bytes 1081376 | tf_op jit(solution)/shard_map/ppermute | solution.py:42
  41.1 4.1 %collective-permute-start.4 = (bf16[2,528,512]{2,1,0:T(8,128)(2,1)S(1)}, bf16[2,528,512]{2,1,0:T(8,128)(2,1)S(1)}, u32[]{:S(2)}, u32[]{:S(2)}) collective-permute-start(bf16[2,528,512]{2,1,0:T(8,128)(2,1)S(1)} %copy-done.3), channel_id=1, source_target_pairs={{0,7},{1,4},{2,5},{3,6},{4,3},{5,0},{6,1},{7,2},{8,15},{9,12},{10,... | collective-permute-start | bytes 3244040 | tf_op jit(solution)/shard_map/ppermute | solution.py:57
  45.2 6.0 %collective-permute-done.6.refs_2_ = bf16[384,1536]{1,0:T(8,128)(2,1)S(1)} collective-permute-done((bf16[384,1536]{1,0:T(8,128)(2,1)S(1)}, bf16[384,1536]{1,0:T(8,128)(2,1)S(1)}, u32[]{:S(2)}, u32[]{:S(2)}) %collective-permute-start.6) | collective-permute-done | bytes 1179680 | tf_op jit(solution)/shard_map/ppermute | solution.py:38
  51.2 1.8 %collective-permute-done.7.refs_3_ = bf16[384,1536]{1,0:T(8,128)(2,1)S(1)} collective-permute-done((bf16[384,1536]{1,0:T(8,128)(2,1)S(1)}, bf16[384,1536]{1,0:T(8,128)(2,1)S(1)}, u32[]{:S(2)}, u32[]{:S(2)}) %collective-permute-start.7) | collective-permute-done | bytes 1179680 | tf_op jit(solution)/shard_map/ppermute | solution.py:38
  53.6 2.5 %collective-permute-start.10 = (bf16[96,1536]{1,0:T(8,128)(2,1)S(1)}, bf16[96,1536]{1,0:T(8,128)(2,1)S(1)}, u32[]{:S(2)}, u32[]{:S(2)}) collective-permute-start(bf16[96,1536]{1,0:T(8,128)(2,1)S(1)} %get-tuple-element.41), channel_id=1, source_target_pairs={{0,64},{4,20},{8,72},{12,28},{16,80},{20,4},{24,88},{28,12},{32,96... | collective-permute-start | bytes 884744 | tf_op jit(solution)/shard_map/ppermute | solution.py:38
  56.6 2.2 %collective-permute-start.9 = (bf16[96,1536]{1,0:T(8,128)(2,1)S(1)}, bf16[96,1536]{1,0:T(8,128)(2,1)S(1)}, u32[]{:S(2)}, u32[]{:S(2)}) collective-permute-start(bf16[96,1536]{1,0:T(8,128)(2,1)S(1)} %get-tuple-element.40), channel_id=1, source_target_pairs={{0,96},{4,28},{8,104},{12,4},{16,112},{20,12},{24,120},{28,20},{32... | collective-permute-start | bytes 884744 | tf_op jit(solution)/shard_map/ppermute | solution.py:38
  58.8 4.5 %shard_map.78.refs_0_ = f32[193,8,1536]{2,1,0:T(8,128)S(1)} custom-call(bf16[2,2,528,512]{3,2,1,0:T(8,128)(2,1)S(1)} %copy-done.1, bf16[2,2,528,512]{3,2,1,0:T(8,128)(2,1)S(1)} %collective-permute-done.refs_1_, bf16[2,528,512]{2,1,0:T(8,128)(2,1)S(1)} %collective-permute-done.1.refs_2_, bf16[2,528,512]{2,1,0:T(8,128)(2,1)S(1)} %collective-permute-done.2.refs_3_), custom_call_target="tpu_custom_call" | custom-call | flops 4294967296 | bytes 13631488 | tf_op jit(solution)/shard_map/pallas_call | solution.py:310
  63.2 1.0 collective-permute-done.8
  64.4 4.3 %collective-permute-done.4.refs_2_ = bf16[2,528,512]{2,1,0:T(8,128)(2,1)S(1)} collective-permute-done((bf16[2,528,512]{2,1,0:T(8,128)(2,1)S(1)}, bf16[2,528,512]{2,1,0:T(8,128)(2,1)S(1)}, u32[]{:S(2)}, u32[]{:S(2)}) %collective-permute-start.4) | collective-permute-done | bytes 1081376 | tf_op jit(solution)/shard_map/ppermute | solution.py:57
  68.7 3.3 %collective-permute-done.3.refs_1_ = bf16[2,528,512]{2,1,0:T(8,128)(2,1)S(1)} collective-permute-done((bf16[2,528,512]{2,1,0:T(8,128)(2,1)S(1)}, bf16[2,528,512]{2,1,0:T(8,128)(2,1)S(1)}, u32[]{:S(2)}, u32[]{:S(2)}) %collective-permute-start.3) | collective-permute-done | bytes 1081376 | tf_op jit(solution)/shard_map/ppermute | solution.py:57
  71.9 2.4 %shard_map.81 = (bf16[384,1536]{1,0:T(8,128)(2,1)S(1)}, bf16[384,1536]{1,0:T(8,128)(2,1)S(1)}, bf16[384,1536]{1,0:T(8,128)(2,1)S(1)}, bf16[384,1536]{1,0:T(8,128)(2,1)S(1)}, f32[193,8,1536]{2,1,0:T(8,128)S(1)}) custom-call(f32[193,8,1536]{2,1,0:T(8,128)S(1)} %shard_map.78.refs_0_, ...), custom_call_target="tpu_custom_call", output_to_operand_aliasing={{4}: (0, {})} | custom-call | flops 2147483648 | bytes 9437184 | tf_op jit(solution)/shard_map/pallas_call | solution.py:315
  74.3 1.4 %collective-permute-start.11 = (bf16[384,1536]{1,0:T(8,128)(2,1)S(1)}, bf16[384,1536]{1,0:T(8,128)(2,1)S(1)}, u32[]{:S(2)}, u32[]{:S(2)}) collective-permute-start(bf16[384,1536]{1,0:T(8,128)(2,1)S(1)} %get-tuple-element.43), channel_id=1, source_target_pairs={{0,8},{4,36},{8,16},{12,44},{16,24},{20,52},{24,0},{28,60},{32,40}... | collective-permute-start | bytes 3538952 | tf_op jit(solution)/shard_map/ppermute | solution.py:38
  75.7 1.5 %collective-permute-start.12 = (bf16[384,1536]{1,0:T(8,128)(2,1)S(1)}, bf16[384,1536]{1,0:T(8,128)(2,1)S(1)}, u32[]{:S(2)}, u32[]{:S(2)}) collective-permute-start(bf16[384,1536]{1,0:T(8,128)(2,1)S(1)} %get-tuple-element.44), channel_id=1, source_target_pairs={{0,24},{4,100},{8,0},{12,108},{16,8},{20,116},{24,16},{28,124},{32... | collective-permute-start | bytes 3538952 | tf_op jit(solution)/shard_map/ppermute | solution.py:38
  77.2 1.6 %collective-permute-start.13 = (bf16[384,1536]{1,0:T(8,128)(2,1)S(1)}, bf16[384,1536]{1,0:T(8,128)(2,1)S(1)}, u32[]{:S(2)}, u32[]{:S(2)}) collective-permute-start(bf16[384,1536]{1,0:T(8,128)(2,1)S(1)} %get-tuple-element.45), channel_id=1, source_target_pairs={{0,16},{4,68},{8,24},{12,76},{16,0},{20,84},{24,8},{28,92},{32,48}... | collective-permute-start | bytes 3538952 | tf_op jit(solution)/shard_map/ppermute | solution.py:38
  78.8 12.2 %collective-permute-done.11.refs_1_ = bf16[384,1536]{1,0:T(8,128)(2,1)S(1)} collective-permute-done((bf16[384,1536]{1,0:T(8,128)(2,1)S(1)}, bf16[384,1536]{1,0:T(8,128)(2,1)S(1)}, u32[]{:S(2)}, u32[]{:S(2)}) %collective-permute-start.11) | collective-permute-done | bytes 1179680 | tf_op jit(solution)/shard_map/ppermute | solution.py:38
  91.1 13.8 %collective-permute-done.13.refs_3_ = bf16[384,1536]{1,0:T(8,128)(2,1)S(1)} collective-permute-done((bf16[384,1536]{1,0:T(8,128)(2,1)S(1)}, bf16[384,1536]{1,0:T(8,128)(2,1)S(1)}, u32[]{:S(2)}, u32[]{:S(2)}) %collective-permute-start.13) | collective-permute-done | bytes 1179680 | tf_op jit(solution)/shard_map/ppermute | solution.py:38
  105.4 1.0 collective-permute-start.14
  106.4 1.8 %collective-permute-start.15 = (bf16[96,1536]{1,0:T(8,128)(2,1)S(1)}, bf16[96,1536]{1,0:T(8,128)(2,1)S(1)}, u32[]{:S(2)}, u32[]{:S(2)}) collective-permute-start(bf16[96,1536]{1,0:T(8,128)(2,1)S(1)} %get-tuple-element.48), channel_id=1, source_target_pairs={{0,96},{4,28},{8,104},{12,4},{16,112},{20,12},{24,120},{28,20},{32... | collective-permute-start | bytes 884744 | tf_op jit(solution)/shard_map/ppermute | solution.py:38
  108.2 1.3 %collective-permute-start.16 = (bf16[96,1536]{1,0:T(8,128)(2,1)S(1)}, bf16[96,1536]{1,0:T(8,128)(2,1)S(1)}, u32[]{:S(2)}, u32[]{:S(2)}) collective-permute-start(bf16[96,1536]{1,0:T(8,128)(2,1)S(1)} %get-tuple-element.49), channel_id=1, source_target_pairs={{0,64},{4,20},{8,72},{12,28},{16,80},{20,4},{24,88},{28,12},{32,96... | collective-permute-start | bytes 884744 | tf_op jit(solution)/shard_map/ppermute | solution.py:38
  109.4 3.1 %collective-permute-done.14 = bf16[96,1536]{1,0:T(8,128)(2,1)S(1)} collective-permute-done((bf16[96,1536]{1,0:T(8,128)(2,1)S(1)}, bf16[96,1536]{1,0:T(8,128)(2,1)S(1)}, u32[]{:S(2)}, u32[]{:S(2)}) %collective-permute-start.14) | collective-permute-done | bytes 294944 | tf_op jit(solution)/shard_map/ppermute | solution.py:38
  112.6 2.4 %collective-permute-done.15 = bf16[96,1536]{1,0:T(8,128)(2,1)S(1)} collective-permute-done((bf16[96,1536]{1,0:T(8,128)(2,1)S(1)}, bf16[96,1536]{1,0:T(8,128)(2,1)S(1)}, u32[]{:S(2)}, u32[]{:S(2)}) %collective-permute-start.15) | collective-permute-done | bytes 294944 | tf_op jit(solution)/shard_map/ppermute | solution.py:38
  115.0 1.4 %collective-permute-done.16 = bf16[96,1536]{1,0:T(8,128)(2,1)S(1)} collective-permute-done((bf16[96,1536]{1,0:T(8,128)(2,1)S(1)}, bf16[96,1536]{1,0:T(8,128)(2,1)S(1)}, u32[]{:S(2)}, u32[]{:S(2)}) %collective-permute-start.16) | collective-permute-done | bytes 294944 | tf_op jit(solution)/shard_map/ppermute | solution.py:38
  116.6 2.2 %collective-permute-start.18 = (f32[48,1536]{1,0:T(8,128)S(1)}, f32[48,1536]{1,0:T(8,128)S(1)}, u32[]{:S(2)}, u32[]{:S(2)}) collective-permute-start(f32[48,1536]{1,0:T(8,128)S(1)} %slice.9), channel_id=1, source_target_pairs={{0,4},{4,0},{8,12},{12,8},{16,20},{20,16},{24,28},{28,24},{32,36},... | collective-permute-start | bytes 884744 | tf_op jit(solution)/shard_map/ppermute | solution.py:47
  118.8 1.2 %collective-permute-done.18 = f32[48,1536]{1,0:T(8,128)S(1)} collective-permute-done((f32[48,1536]{1,0:T(8,128)S(1)}, f32[48,1536]{1,0:T(8,128)S(1)}, u32[]{:S(2)}, u32[]{:S(2)}) %collective-permute-start.18) | collective-permute-done | bytes 294944 | tf_op jit(solution)/shard_map/ppermute | solution.py:47
  (24 shorter events, 3.2 us)
Async XLA Ops:
  12.2 5.6 %collective-permute-start = (bf16[2,2,528,512]{3,2,1,0:T(8,128)(2,1)}, bf16[2,2,528,512]{3,2,1,0:T(8,128)(2,1)S(1)}, u32[]{:S(2)}, u32[]{:S(2)}) collective-permute-start(bf16[2,2,528,512]{3,2,1,0:T(8,128)(2,1)} %get-tuple-element.27), channel_id=1, source_target_pairs={{0,4},{4,0},{8,12},{12,8},{16,20},{20,16},{24,28},{28,24},{32,36},... | collective-permute-start | bytes 6488072 | tf_op jit(solution)/shard_map/ppermute | solution.py:47
  13.7 27.4 %collective-permute-start.2 = (bf16[2,528,512]{2,1,0:T(8,128)(2,1)}, bf16[2,528,512]{2,1,0:T(8,128)(2,1)S(1)}, u32[]{:S(2)}, u32[]{:S(2)}) collective-permute-start(bf16[2,528,512]{2,1,0:T(8,128)(2,1)} %get-tuple-element.29), channel_id=1, source_target_pairs={{0,3},{1,0},{2,1},{3,2},{4,7},{5,4},{6,5},{7,6},{8,11},{9,8},{10,9... | collective-permute-start | bytes 3244040 | tf_op jit(solution)/shard_map/ppermute | solution.py:42
  17.5 27.6 %collective-permute-start.1 = (bf16[2,528,512]{2,1,0:T(8,128)(2,1)}, bf16[2,528,512]{2,1,0:T(8,128)(2,1)S(1)}, u32[]{:S(2)}, u32[]{:S(2)}) collective-permute-start(bf16[2,528,512]{2,1,0:T(8,128)(2,1)} %get-tuple-element.28), channel_id=1, source_target_pairs={{0,1},{1,2},{2,3},{3,0},{4,5},{5,6},{6,7},{7,4},{8,9},{9,10},{10,1... | collective-permute-start | bytes 3244040 | tf_op jit(solution)/shard_map/ppermute | solution.py:42
  17.8 1.6 %copy-start = (bf16[2,2,528,512]{3,2,1,0:T(8,128)(2,1)S(1)}, bf16[2,2,528,512]{3,2,1,0:T(8,128)(2,1)}, u32[]{:S(2)}) copy-start(bf16[2,2,528,512]{3,2,1,0:T(8,128)(2,1)} %get-tuple-element.26.refs_0_) | copy-start | bytes 6488068
  19.4 21.7 %copy-start.3 = (bf16[2,528,512]{2,1,0:T(8,128)(2,1)S(1)}, bf16[2,528,512]{2,1,0:T(8,128)(2,1)}, u32[]{:S(2)}) copy-start(bf16[2,528,512]{2,1,0:T(8,128)(2,1)} %get-tuple-element.34) | copy-start | bytes 3244036
  19.4 25.7 %copy-start.2 = (bf16[2,528,512]{2,1,0:T(8,128)(2,1)S(1)}, bf16[2,528,512]{2,1,0:T(8,128)(2,1)}, u32[]{:S(2)}) copy-start(bf16[2,528,512]{2,1,0:T(8,128)(2,1)} %get-tuple-element.32) | copy-start | bytes 3244036
  22.4 22.8 %collective-permute-start.5 = (bf16[384,1536]{1,0:T(8,128)(2,1)S(1)}, bf16[384,1536]{1,0:T(8,128)(2,1)S(1)}, u32[]{:S(2)}, u32[]{:S(2)}) collective-permute-start(bf16[384,1536]{1,0:T(8,128)(2,1)S(1)} %get-tuple-element.35), channel_id=1, source_target_pairs={{0,8},{4,36},{8,16},{12,44},{16,24},{20,52},{24,0},{28,60},{32,40}... | collective-permute-start | bytes 3538952 | tf_op jit(solution)/shard_map/ppermute | solution.py:38
  23.9 27.3 %collective-permute-start.6 = (bf16[384,1536]{1,0:T(8,128)(2,1)S(1)}, bf16[384,1536]{1,0:T(8,128)(2,1)S(1)}, u32[]{:S(2)}, u32[]{:S(2)}) collective-permute-start(bf16[384,1536]{1,0:T(8,128)(2,1)S(1)} %get-tuple-element.36), channel_id=1, source_target_pairs={{0,24},{4,100},{8,0},{12,108},{16,8},{20,116},{24,16},{28,124},{32... | collective-permute-start | bytes 3538952 | tf_op jit(solution)/shard_map/ppermute | solution.py:38
  25.4 27.6 %collective-permute-start.7 = (bf16[384,1536]{1,0:T(8,128)(2,1)S(1)}, bf16[384,1536]{1,0:T(8,128)(2,1)S(1)}, u32[]{:S(2)}, u32[]{:S(2)}) collective-permute-start(bf16[384,1536]{1,0:T(8,128)(2,1)S(1)} %get-tuple-element.37), channel_id=1, source_target_pairs={{0,16},{4,68},{8,24},{12,76},{16,0},{20,84},{24,8},{28,92},{32,48}... | collective-permute-start | bytes 3538952 | tf_op jit(solution)/shard_map/ppermute | solution.py:38
  41.1 27.6 %collective-permute-start.4 = (bf16[2,528,512]{2,1,0:T(8,128)(2,1)S(1)}, bf16[2,528,512]{2,1,0:T(8,128)(2,1)S(1)}, u32[]{:S(2)}, u32[]{:S(2)}) collective-permute-start(bf16[2,528,512]{2,1,0:T(8,128)(2,1)S(1)} %copy-done.3), channel_id=1, source_target_pairs={{0,7},{1,4},{2,5},{3,6},{4,3},{5,0},{6,1},{7,2},{8,15},{9,12},{10,... | collective-permute-start | bytes 3244040 | tf_op jit(solution)/shard_map/ppermute | solution.py:57
  45.1 13.6 %copy-start.1 = (bf16[2,2,528,512]{3,2,1,0:T(8,128)(2,1)S(1)}, bf16[2,2,528,512]{3,2,1,0:T(8,128)(2,1)}, u32[]{:S(2)}) copy-start(bf16[2,2,528,512]{3,2,1,0:T(8,128)(2,1)} %get-tuple-element.26.refs_0_) | copy-start | bytes 6488068
  45.1 26.8 %collective-permute-start.3 = (bf16[2,528,512]{2,1,0:T(8,128)(2,1)S(1)}, bf16[2,528,512]{2,1,0:T(8,128)(2,1)S(1)}, u32[]{:S(2)}, u32[]{:S(2)}) collective-permute-start(bf16[2,528,512]{2,1,0:T(8,128)(2,1)S(1)} %copy-done.2), channel_id=1, source_target_pairs={{0,5},{1,6},{2,7},{3,4},{4,1},{5,2},{6,3},{7,0},{8,13},{9,14},{10,... | collective-permute-start | bytes 3244040 | tf_op jit(solution)/shard_map/ppermute | solution.py:57
  53.6 9.6 %collective-permute-start.10 = (bf16[96,1536]{1,0:T(8,128)(2,1)S(1)}, bf16[96,1536]{1,0:T(8,128)(2,1)S(1)}, u32[]{:S(2)}, u32[]{:S(2)}) collective-permute-start(bf16[96,1536]{1,0:T(8,128)(2,1)S(1)} %get-tuple-element.41), channel_id=1, source_target_pairs={{0,64},{4,20},{8,72},{12,28},{16,80},{20,4},{24,88},{28,12},{32,96... | collective-permute-start | bytes 884744 | tf_op jit(solution)/shard_map/ppermute | solution.py:38
  56.1 8.1 %collective-permute-start.8 = (bf16[96,1536]{1,0:T(8,128)(2,1)S(1)}, bf16[96,1536]{1,0:T(8,128)(2,1)S(1)}, u32[]{:S(2)}, u32[]{:S(2)}) collective-permute-start(bf16[96,1536]{1,0:T(8,128)(2,1)S(1)} %get-tuple-element.39), channel_id=1, source_target_pairs={{0,32},{4,12},{8,40},{12,20},{16,48},{20,28},{24,56},{28,4},{32,64... | collective-permute-start | bytes 884744 | tf_op jit(solution)/shard_map/ppermute | solution.py:38
  56.6 7.6 %collective-permute-start.9 = (bf16[96,1536]{1,0:T(8,128)(2,1)S(1)}, bf16[96,1536]{1,0:T(8,128)(2,1)S(1)}, u32[]{:S(2)}, u32[]{:S(2)}) collective-permute-start(bf16[96,1536]{1,0:T(8,128)(2,1)S(1)} %get-tuple-element.40), channel_id=1, source_target_pairs={{0,96},{4,28},{8,104},{12,4},{16,112},{20,12},{24,120},{28,20},{32... | collective-permute-start | bytes 884744 | tf_op jit(solution)/shard_map/ppermute | solution.py:38
  74.3 16.7 %collective-permute-start.11 = (bf16[384,1536]{1,0:T(8,128)(2,1)S(1)}, bf16[384,1536]{1,0:T(8,128)(2,1)S(1)}, u32[]{:S(2)}, u32[]{:S(2)}) collective-permute-start(bf16[384,1536]{1,0:T(8,128)(2,1)S(1)} %get-tuple-element.43), channel_id=1, source_target_pairs={{0,8},{4,36},{8,16},{12,44},{16,24},{20,52},{24,0},{28,60},{32,40}... | collective-permute-start | bytes 3538952 | tf_op jit(solution)/shard_map/ppermute | solution.py:38
  75.7 15.3 %collective-permute-start.12 = (bf16[384,1536]{1,0:T(8,128)(2,1)S(1)}, bf16[384,1536]{1,0:T(8,128)(2,1)S(1)}, u32[]{:S(2)}, u32[]{:S(2)}) collective-permute-start(bf16[384,1536]{1,0:T(8,128)(2,1)S(1)} %get-tuple-element.44), channel_id=1, source_target_pairs={{0,24},{4,100},{8,0},{12,108},{16,8},{20,116},{24,16},{28,124},{32... | collective-permute-start | bytes 3538952 | tf_op jit(solution)/shard_map/ppermute | solution.py:38
  77.2 27.6 %collective-permute-start.13 = (bf16[384,1536]{1,0:T(8,128)(2,1)S(1)}, bf16[384,1536]{1,0:T(8,128)(2,1)S(1)}, u32[]{:S(2)}, u32[]{:S(2)}) collective-permute-start(bf16[384,1536]{1,0:T(8,128)(2,1)S(1)} %get-tuple-element.45), channel_id=1, source_target_pairs={{0,16},{4,68},{8,24},{12,76},{16,0},{20,84},{24,8},{28,92},{32,48}... | collective-permute-start | bytes 3538952 | tf_op jit(solution)/shard_map/ppermute | solution.py:38
  78.8 30.6 %collective-permute-start.17 = (bf16[96,1536]{1,0:T(8,128)(2,1)S(1)}, bf16[96,1536]{1,0:T(8,128)(2,1)S(1)}, u32[]{:S(2)}, u32[]{:S(2)}) collective-permute-start(bf16[96,1536]{1,0:T(8,128)(2,1)S(1)} %add_convert_fusion.refs_3_), channel_id=1, source_target_pairs={{0,2},{1,3},{2,0},{3,1},{4,6},{5,7},{6,4},{7,5},{8,10},{9,11},{10,... | collective-permute-start | bytes 884744 | tf_op jit(solution)/shard_map/ppermute | solution.py:42
  105.4 7.1 %collective-permute-start.14 = (bf16[96,1536]{1,0:T(8,128)(2,1)S(1)}, bf16[96,1536]{1,0:T(8,128)(2,1)S(1)}, u32[]{:S(2)}, u32[]{:S(2)}) collective-permute-start(bf16[96,1536]{1,0:T(8,128)(2,1)S(1)} %get-tuple-element.47), channel_id=1, source_target_pairs={{0,32},{4,12},{8,40},{12,20},{16,48},{20,28},{24,56},{28,4},{32,64... | collective-permute-start | bytes 884744 | tf_op jit(solution)/shard_map/ppermute | solution.py:38
  106.4 8.6 %collective-permute-start.15 = (bf16[96,1536]{1,0:T(8,128)(2,1)S(1)}, bf16[96,1536]{1,0:T(8,128)(2,1)S(1)}, u32[]{:S(2)}, u32[]{:S(2)}) collective-permute-start(bf16[96,1536]{1,0:T(8,128)(2,1)S(1)} %get-tuple-element.48), channel_id=1, source_target_pairs={{0,96},{4,28},{8,104},{12,4},{16,112},{20,12},{24,120},{28,20},{32... | collective-permute-start | bytes 884744 | tf_op jit(solution)/shard_map/ppermute | solution.py:38
  108.2 8.3 %collective-permute-start.16 = (bf16[96,1536]{1,0:T(8,128)(2,1)S(1)}, bf16[96,1536]{1,0:T(8,128)(2,1)S(1)}, u32[]{:S(2)}, u32[]{:S(2)}) collective-permute-start(bf16[96,1536]{1,0:T(8,128)(2,1)S(1)} %get-tuple-element.49), channel_id=1, source_target_pairs={{0,64},{4,20},{8,72},{12,28},{16,80},{20,4},{24,88},{28,12},{32,96... | collective-permute-start | bytes 884744 | tf_op jit(solution)/shard_map/ppermute | solution.py:38
  116.6 3.4 %collective-permute-start.18 = (f32[48,1536]{1,0:T(8,128)S(1)}, f32[48,1536]{1,0:T(8,128)S(1)}, u32[]{:S(2)}, u32[]{:S(2)}) collective-permute-start(f32[48,1536]{1,0:T(8,128)S(1)} %slice.9), channel_id=1, source_target_pairs={{0,4},{4,0},{8,12},{12,8},{16,20},{20,16},{24,28},{28,24},{32,36},... | collective-permute-start | bytes 884744 | tf_op jit(solution)/shard_map/ppermute | solution.py:47

commit v9 on v8

--- a/solution.py
+++ b/solution.py
@@ -342,7 +342,7 @@
 
 
 def spread(pieces, second):
-    return [pieces[0]] + [turn(pieces[step], step, second) for step in (1, 3, 2)]
+    return [pieces[0]] + [turn(pieces[step], step, second) for step in (2, 1, 3)]
 
 
 def add_up(pieces):

time: 121 us -> 120 us (level)
  waiting for transfers between devices: 65 us -> 61.9 us
  starting transfers between devices: 29.8 us -> 31.7 us
    ppermute x12, starting transfers between devices: 18.1 us -> 20.3 us  [turn(): return lax.ppermute(value, 'visit', pairs)]
    ppermute x2, waiting for transfers between devices: 7.55 us -> 5.65 us  [across_both(): return lax.ppermute(value, ('visit', 'patch'), pairs)]
    ppermute x3, waiting for transfers between devices: 14.1 us -> 12.9 us  [across_z(): return lax.ppermute(value, 'patch', [(z, (z + step) % 4) for z in range(4)])]
  transfers between devices with their start and end apart: 19 -> 19, of which waited for: 13 -> 16; matrix products, arithmetic and copies ran while one was open for 0% -> 0% of each run, Pallas kernels for 7% -> 7%
where the time goes in v9:
time: 120 us
  waiting for transfers between devices  61.9 us (52%)
  starting transfers between devices  31.7 us (26%)
  Pallas kernels  22.6 us (19%)
  local copies, waits for them, and re-layouts  1.64 us (1%)
    ppermute x12, waiting for transfers between devices, turn(): return lax.ppermute(value, 'visit', pairs)  42 us
    ppermute x12, starting transfers between devices, turn(): return lax.ppermute(value, 'visit', pairs)  20.3 us
    ppermute x3, waiting for transfers between devices, across_z(): return lax.ppermute(value, 'patch', [(z, (z + step) % 4) for z in range(4)])  12.9 us
    pallas_call x1, Pallas kernels, match_tiles(): pl.pallas_call(match_kernel, grid=(4,), in_specs=[pl.BlockSpec(memory_spa...  11.5 us
    ppermute x2, waiting for transfers between devices, across_both(): return lax.ppermute(value, ('visit', 'patch'), pairs)  5.65 us
    pallas_call x1, Pallas kernels, start_frame(): pl.pallas_call(start_kernel, out_shape=jax.ShapeDtypeStruct(FRAME, F32),...  4.46 us
    ppermute x2, starting transfers between devices, across_both(): return lax.ppermute(value, ('visit', 'patch'), pairs)  4.12 us
    ppermute x3, starting transfers between devices, across_z(): return lax.ppermute(value, 'patch', [(z, (z + step) % 4) for z in range(4)])  3.86 us
  transfers between devices with their start and end apart: 19, of which 16 were waited for; matrix products, arithmetic and copies ran while one was open for 0% of the time, Pallas kernels for 7%

profile of v9, /device:TPU:1, one launch (start us, length us, event | category | flops | bytes accessed | tf_op | source)
XLA Modules:
  0.0 119.8 jit_solution(15962731348426693591)
XLA Ops:
  0.6 11.5 %shard_map.77 = (bf16[2,2,528,512]{3,2,1,0:T(8,128)(2,1)}, bf16[2,528,512]{2,1,0:T(8,128)(2,1)}, bf16[2,528,512]{2,1,0:T(8,128)(2,1)}, bf16[2,2,528,512]{3,2,1,0...) custom-call(s32[2,4]{1,0:T(2,128)} %bitcast.23, s32[2,2,4]{2,1,0:T(2,128)} %bitcast.21, ...), custom_call_target="tpu_custom_call" | custom-call | flops 6442450944 | bytes 12582912 | tf_op jit(solution)/shard_map/pallas_call | solution.py:191
  12.2 1.5 %collective-permute-start = (bf16[2,2,528,512]{3,2,1,0:T(8,128)(2,1)}, bf16[2,2,528,512]{3,2,1,0:T(8,128)(2,1)S(1)}, u32[]{:S(2)}, u32[]{:S(2)}) collective-permute-start(bf16[2,2,528,512]{3,2,1,0:T(8,128)(2,1)} %get-tuple-element.27), channel_id=1, source_target_pairs={{0,4},{4,0},{8,12},{12,8},{16,20},{20,16},{24,28},{28,24},{32,36},... | collective-permute-start | bytes 6488072 | tf_op jit(solution)/shard_map/ppermute | solution.py:47
  13.7 3.9 %collective-permute-start.2 = (bf16[2,528,512]{2,1,0:T(8,128)(2,1)}, bf16[2,528,512]{2,1,0:T(8,128)(2,1)S(1)}, u32[]{:S(2)}, u32[]{:S(2)}) collective-permute-start(bf16[2,528,512]{2,1,0:T(8,128)(2,1)} %get-tuple-element.29), channel_id=1, source_target_pairs={{0,3},{1,0},{2,1},{3,2},{4,7},{5,4},{6,5},{7,6},{8,11},{9,8},{10,9... | collective-permute-start | bytes 3244040 | tf_op jit(solution)/shard_map/ppermute | solution.py:42
  17.8 1.6 %copy-done = bf16[2,2,528,512]{3,2,1,0:T(8,128)(2,1)S(1)} copy-done((bf16[2,2,528,512]{3,2,1,0:T(8,128)(2,1)S(1)}, bf16[2,2,528,512]{3,2,1,0:T(8,128)(2,1)}, u32[]{:S(2)}) %copy-start) | copy-done | bytes 2162712
  19.4 3.0 %shard_map.79 = (bf16[384,1536]{1,0:T(8,128)(2,1)S(1)}, bf16[384,1536]{1,0:T(8,128)(2,1)S(1)}, bf16[384,1536]{1,0:T(8,128)(2,1)S(1)}, bf16[384,1536]{1,0:T(8,128)(2,1)S(1)}) custom-call(bf16[2,2,528,512]{3,2,1,0:T(8,128)(2,1)S(1)} %copy-done, bf16[2,2,528,512]{3,2,1,0:T(8,128)(2,1)S(1)} %collective-permute-done.refs_1_), custom_call_target="tpu_custom_call" | custom-call | flops 2147483648 | bytes 9437184 | tf_op jit(solution)/shard_map/pallas_call | solution.py:304
  22.4 3.1 %collective-permute-start.5 = (bf16[384,1536]{1,0:T(8,128)(2,1)S(1)}, bf16[384,1536]{1,0:T(8,128)(2,1)S(1)}, u32[]{:S(2)}, u32[]{:S(2)}) collective-permute-start(bf16[384,1536]{1,0:T(8,128)(2,1)S(1)} %get-tuple-element.35), channel_id=1, source_target_pairs={{0,16},{4,68},{8,24},{12,76},{16,0},{20,84},{24,8},{28,92},{32,48}... | collective-permute-start | bytes 3538952 | tf_op jit(solution)/shard_map/ppermute | solution.py:38
  25.9 2.3 %collective-permute-start.7 = (bf16[384,1536]{1,0:T(8,128)(2,1)S(1)}, bf16[384,1536]{1,0:T(8,128)(2,1)S(1)}, u32[]{:S(2)}, u32[]{:S(2)}) collective-permute-start(bf16[384,1536]{1,0:T(8,128)(2,1)S(1)} %get-tuple-element.37), channel_id=1, source_target_pairs={{0,24},{4,100},{8,0},{12,108},{16,8},{20,116},{24,16},{28,124},{32... | collective-permute-start | bytes 3538952 | tf_op jit(solution)/shard_map/ppermute | solution.py:38
  28.2 12.9 %collective-permute-done.2.refs_3_ = bf16[2,528,512]{2,1,0:T(8,128)(2,1)S(1)} collective-permute-done((bf16[2,528,512]{2,1,0:T(8,128)(2,1)}, bf16[2,528,512]{2,1,0:T(8,128)(2,1)S(1)}, u32[]{:S(2)}, u32[]{:S(2)}) %collective-permute-start.2) | collective-permute-done | bytes 1081376 | tf_op jit(solution)/shard_map/ppermute | solution.py:42
  41.1 4.1 %collective-permute-start.4 = (bf16[2,528,512]{2,1,0:T(8,128)(2,1)S(1)}, bf16[2,528,512]{2,1,0:T(8,128)(2,1)S(1)}, u32[]{:S(2)}, u32[]{:S(2)}) collective-permute-start(bf16[2,528,512]{2,1,0:T(8,128)(2,1)S(1)} %copy-done.3), channel_id=1, source_target_pairs={{0,7},{1,4},{2,5},{3,6},{4,3},{5,0},{6,1},{7,2},{8,15},{9,12},{10,... | collective-permute-start | bytes 3244040 | tf_op jit(solution)/shard_map/ppermute | solution.py:57
  45.2 6.8 %collective-permute-done.6.refs_2_ = bf16[384,1536]{1,0:T(8,128)(2,1)S(1)} collective-permute-done((bf16[384,1536]{1,0:T(8,128)(2,1)S(1)}, bf16[384,1536]{1,0:T(8,128)(2,1)S(1)}, u32[]{:S(2)}, u32[]{:S(2)}) %collective-permute-start.6) | collective-permute-done | bytes 1179680 | tf_op jit(solution)/shard_map/ppermute | solution.py:38
  52.5 0.6 shard_map.80
  53.0 2.6 %collective-permute-start.10 = (bf16[96,1536]{1,0:T(8,128)(2,1)S(1)}, bf16[96,1536]{1,0:T(8,128)(2,1)S(1)}, u32[]{:S(2)}, u32[]{:S(2)}) collective-permute-start(bf16[96,1536]{1,0:T(8,128)(2,1)S(1)} %get-tuple-element.41), channel_id=1, source_target_pairs={{0,96},{4,28},{8,104},{12,4},{16,112},{20,12},{24,120},{28,20},{32... | collective-permute-start | bytes 884744 | tf_op jit(solution)/shard_map/ppermute | solution.py:38
  56.1 0.6 collective-permute-start.9
  56.7 4.5 %shard_map.78.refs_0_ = f32[193,8,1536]{2,1,0:T(8,128)S(1)} custom-call(bf16[2,2,528,512]{3,2,1,0:T(8,128)(2,1)S(1)} %copy-done.1, bf16[2,2,528,512]{3,2,1,0:T(8,128)(2,1)S(1)} %collective-permute-done.refs_1_, bf16[2,528,512]{2,1,0:T(8,128)(2,1)S(1)} %collective-permute-done.1.refs_2_, bf16[2,528,512]{2,1,0:T(8,128)(2,1)S(1)} %collective-permute-done.2.refs_3_), custom_call_target="tpu_custom_call" | custom-call | flops 4294967296 | bytes 13631488 | tf_op jit(solution)/shard_map/pallas_call | solution.py:310
  61.2 1.2 %collective-permute-done.10 = bf16[96,1536]{1,0:T(8,128)(2,1)S(1)} collective-permute-done((bf16[96,1536]{1,0:T(8,128)(2,1)S(1)}, bf16[96,1536]{1,0:T(8,128)(2,1)S(1)}, u32[]{:S(2)}, u32[]{:S(2)}) %collective-permute-start.10) | collective-permute-done | bytes 294944 | tf_op jit(solution)/shard_map/ppermute | solution.py:38
  62.4 0.6 collective-permute-done.8
  63.0 3.1 %collective-permute-done.9 = bf16[96,1536]{1,0:T(8,128)(2,1)S(1)} collective-permute-done((bf16[96,1536]{1,0:T(8,128)(2,1)S(1)}, bf16[96,1536]{1,0:T(8,128)(2,1)S(1)}, u32[]{:S(2)}, u32[]{:S(2)}) %collective-permute-start.9) | collective-permute-done | bytes 294944 | tf_op jit(solution)/shard_map/ppermute | solution.py:38
  66.3 2.4 %collective-permute-done.4.refs_2_ = bf16[2,528,512]{2,1,0:T(8,128)(2,1)S(1)} collective-permute-done((bf16[2,528,512]{2,1,0:T(8,128)(2,1)S(1)}, bf16[2,528,512]{2,1,0:T(8,128)(2,1)S(1)}, u32[]{:S(2)}, u32[]{:S(2)}) %collective-permute-start.4) | collective-permute-done | bytes 1081376 | tf_op jit(solution)/shard_map/ppermute | solution.py:57
  68.7 3.3 %collective-permute-done.3.refs_1_ = bf16[2,528,512]{2,1,0:T(8,128)(2,1)S(1)} collective-permute-done((bf16[2,528,512]{2,1,0:T(8,128)(2,1)S(1)}, bf16[2,528,512]{2,1,0:T(8,128)(2,1)S(1)}, u32[]{:S(2)}, u32[]{:S(2)}) %collective-permute-start.3) | collective-permute-done | bytes 1081376 | tf_op jit(solution)/shard_map/ppermute | solution.py:57
  71.9 2.4 %shard_map.81 = (bf16[384,1536]{1,0:T(8,128)(2,1)S(1)}, bf16[384,1536]{1,0:T(8,128)(2,1)S(1)}, bf16[384,1536]{1,0:T(8,128)(2,1)S(1)}, bf16[384,1536]{1,0:T(8,128)(2,1)S(1)}, f32[193,8,1536]{2,1,0:T(8,128)S(1)}) custom-call(f32[193,8,1536]{2,1,0:T(8,128)S(1)} %shard_map.78.refs_0_, ...), custom_call_target="tpu_custom_call", output_to_operand_aliasing={{4}: (0, {})} | custom-call | flops 2147483648 | bytes 9437184 | tf_op jit(solution)/shard_map/pallas_call | solution.py:315
  74.3 3.0 %collective-permute-start.11 = (bf16[384,1536]{1,0:T(8,128)(2,1)S(1)}, bf16[384,1536]{1,0:T(8,128)(2,1)S(1)}, u32[]{:S(2)}, u32[]{:S(2)}) collective-permute-start(bf16[384,1536]{1,0:T(8,128)(2,1)S(1)} %get-tuple-element.43), channel_id=1, source_target_pairs={{0,16},{4,68},{8,24},{12,76},{16,0},{20,84},{24,8},{28,92},{32,48}... | collective-permute-start | bytes 3538952 | tf_op jit(solution)/shard_map/ppermute | solution.py:38
  77.7 2.3 %collective-permute-start.13 = (bf16[384,1536]{1,0:T(8,128)(2,1)S(1)}, bf16[384,1536]{1,0:T(8,128)(2,1)S(1)}, u32[]{:S(2)}, u32[]{:S(2)}) collective-permute-start(bf16[384,1536]{1,0:T(8,128)(2,1)S(1)} %get-tuple-element.45), channel_id=1, source_target_pairs={{0,24},{4,100},{8,0},{12,108},{16,8},{20,116},{24,16},{28,124},{32... | collective-permute-start | bytes 3538952 | tf_op jit(solution)/shard_map/ppermute | solution.py:38
  80.0 11.3 %collective-permute-done.11.refs_1_ = bf16[384,1536]{1,0:T(8,128)(2,1)S(1)} collective-permute-done((bf16[384,1536]{1,0:T(8,128)(2,1)S(1)}, bf16[384,1536]{1,0:T(8,128)(2,1)S(1)}, u32[]{:S(2)}, u32[]{:S(2)}) %collective-permute-start.11) | collective-permute-done | bytes 1179680 | tf_op jit(solution)/shard_map/ppermute | solution.py:38
  91.3 12.6 %collective-permute-done.12.refs_2_ = bf16[384,1536]{1,0:T(8,128)(2,1)S(1)} collective-permute-done((bf16[384,1536]{1,0:T(8,128)(2,1)S(1)}, bf16[384,1536]{1,0:T(8,128)(2,1)S(1)}, u32[]{:S(2)}, u32[]{:S(2)}) %collective-permute-start.12) | collective-permute-done | bytes 1179680 | tf_op jit(solution)/shard_map/ppermute | solution.py:38
  104.9 2.5 %collective-permute-start.14 = (bf16[96,1536]{1,0:T(8,128)(2,1)S(1)}, bf16[96,1536]{1,0:T(8,128)(2,1)S(1)}, u32[]{:S(2)}, u32[]{:S(2)}) collective-permute-start(bf16[96,1536]{1,0:T(8,128)(2,1)S(1)} %get-tuple-element.47), channel_id=1, source_target_pairs={{0,64},{4,20},{8,72},{12,28},{16,80},{20,4},{24,88},{28,12},{32,96... | collective-permute-start | bytes 884744 | tf_op jit(solution)/shard_map/ppermute | solution.py:38
  107.4 0.6 collective-permute-start.15
  108.0 2.1 %collective-permute-start.16 = (bf16[96,1536]{1,0:T(8,128)(2,1)S(1)}, bf16[96,1536]{1,0:T(8,128)(2,1)S(1)}, u32[]{:S(2)}, u32[]{:S(2)}) collective-permute-start(bf16[96,1536]{1,0:T(8,128)(2,1)S(1)} %get-tuple-element.49), channel_id=1, source_target_pairs={{0,96},{4,28},{8,104},{12,4},{16,112},{20,12},{24,120},{28,20},{32... | collective-permute-start | bytes 884744 | tf_op jit(solution)/shard_map/ppermute | solution.py:38
  110.1 2.2 %collective-permute-done.14 = bf16[96,1536]{1,0:T(8,128)(2,1)S(1)} collective-permute-done((bf16[96,1536]{1,0:T(8,128)(2,1)S(1)}, bf16[96,1536]{1,0:T(8,128)(2,1)S(1)}, u32[]{:S(2)}, u32[]{:S(2)}) %collective-permute-start.14) | collective-permute-done | bytes 294944 | tf_op jit(solution)/shard_map/ppermute | solution.py:38
  112.3 3.2 %collective-permute-done.15 = bf16[96,1536]{1,0:T(8,128)(2,1)S(1)} collective-permute-done((bf16[96,1536]{1,0:T(8,128)(2,1)S(1)}, bf16[96,1536]{1,0:T(8,128)(2,1)S(1)}, u32[]{:S(2)}, u32[]{:S(2)}) %collective-permute-start.15) | collective-permute-done | bytes 294944 | tf_op jit(solution)/shard_map/ppermute | solution.py:38
  115.8 1.9 %collective-permute-start.18 = (f32[48,1536]{1,0:T(8,128)S(1)}, f32[48,1536]{1,0:T(8,128)S(1)}, u32[]{:S(2)}, u32[]{:S(2)}) collective-permute-start(f32[48,1536]{1,0:T(8,128)S(1)} %slice.9), channel_id=1, source_target_pairs={{0,4},{4,0},{8,12},{12,8},{16,20},{20,16},{24,28},{28,24},{32,36},... | collective-permute-start | bytes 884744 | tf_op jit(solution)/shard_map/ppermute | solution.py:47
  117.7 1.2 %collective-permute-done.18 = f32[48,1536]{1,0:T(8,128)S(1)} collective-permute-done((f32[48,1536]{1,0:T(8,128)S(1)}, f32[48,1536]{1,0:T(8,128)S(1)}, u32[]{:S(2)}, u32[]{:S(2)}) %collective-permute-start.18) | collective-permute-done | bytes 294944 | tf_op jit(solution)/shard_map/ppermute | solution.py:47
  118.9 0.9 fusion
  (24 shorter events, 3.5 us)
Async XLA Ops:
  12.2 5.6 %collective-permute-start = (bf16[2,2,528,512]{3,2,1,0:T(8,128)(2,1)}, bf16[2,2,528,512]{3,2,1,0:T(8,128)(2,1)S(1)}, u32[]{:S(2)}, u32[]{:S(2)}) collective-permute-start(bf16[2,2,528,512]{3,2,1,0:T(8,128)(2,1)} %get-tuple-element.27), channel_id=1, source_target_pairs={{0,4},{4,0},{8,12},{12,8},{16,20},{20,16},{24,28},{28,24},{32,36},... | collective-permute-start | bytes 6488072 | tf_op jit(solution)/shard_map/ppermute | solution.py:47
  13.7 27.4 %collective-permute-start.2 = (bf16[2,528,512]{2,1,0:T(8,128)(2,1)}, bf16[2,528,512]{2,1,0:T(8,128)(2,1)S(1)}, u32[]{:S(2)}, u32[]{:S(2)}) collective-permute-start(bf16[2,528,512]{2,1,0:T(8,128)(2,1)} %get-tuple-element.29), channel_id=1, source_target_pairs={{0,3},{1,0},{2,1},{3,2},{4,7},{5,4},{6,5},{7,6},{8,11},{9,8},{10,9... | collective-permute-start | bytes 3244040 | tf_op jit(solution)/shard_map/ppermute | solution.py:42
  17.5 27.6 %collective-permute-start.1 = (bf16[2,528,512]{2,1,0:T(8,128)(2,1)}, bf16[2,528,512]{2,1,0:T(8,128)(2,1)S(1)}, u32[]{:S(2)}, u32[]{:S(2)}) collective-permute-start(bf16[2,528,512]{2,1,0:T(8,128)(2,1)} %get-tuple-element.28), channel_id=1, source_target_pairs={{0,1},{1,2},{2,3},{3,0},{4,5},{5,6},{6,7},{7,4},{8,9},{9,10},{10,1... | collective-permute-start | bytes 3244040 | tf_op jit(solution)/shard_map/ppermute | solution.py:42
  17.8 1.6 %copy-start = (bf16[2,2,528,512]{3,2,1,0:T(8,128)(2,1)S(1)}, bf16[2,2,528,512]{3,2,1,0:T(8,128)(2,1)}, u32[]{:S(2)}) copy-start(bf16[2,2,528,512]{3,2,1,0:T(8,128)(2,1)} %get-tuple-element.26.refs_0_) | copy-start | bytes 6488068
  19.4 21.7 %copy-start.3 = (bf16[2,528,512]{2,1,0:T(8,128)(2,1)S(1)}, bf16[2,528,512]{2,1,0:T(8,128)(2,1)}, u32[]{:S(2)}) copy-start(bf16[2,528,512]{2,1,0:T(8,128)(2,1)} %get-tuple-element.34) | copy-start | bytes 3244036
  19.4 25.7 %copy-start.2 = (bf16[2,528,512]{2,1,0:T(8,128)(2,1)S(1)}, bf16[2,528,512]{2,1,0:T(8,128)(2,1)}, u32[]{:S(2)}) copy-start(bf16[2,528,512]{2,1,0:T(8,128)(2,1)} %get-tuple-element.32) | copy-start | bytes 3244036
  22.4 22.8 %collective-permute-start.5 = (bf16[384,1536]{1,0:T(8,128)(2,1)S(1)}, bf16[384,1536]{1,0:T(8,128)(2,1)S(1)}, u32[]{:S(2)}, u32[]{:S(2)}) collective-permute-start(bf16[384,1536]{1,0:T(8,128)(2,1)S(1)} %get-tuple-element.35), channel_id=1, source_target_pairs={{0,16},{4,68},{8,24},{12,76},{16,0},{20,84},{24,8},{28,92},{32,48}... | collective-permute-start | bytes 3538952 | tf_op jit(solution)/shard_map/ppermute | solution.py:38
  25.5 26.5 %collective-permute-start.6 = (bf16[384,1536]{1,0:T(8,128)(2,1)S(1)}, bf16[384,1536]{1,0:T(8,128)(2,1)S(1)}, u32[]{:S(2)}, u32[]{:S(2)}) collective-permute-start(bf16[384,1536]{1,0:T(8,128)(2,1)S(1)} %get-tuple-element.36), channel_id=1, source_target_pairs={{0,8},{4,36},{8,16},{12,44},{16,24},{20,52},{24,0},{28,60},{32,40}... | collective-permute-start | bytes 3538952 | tf_op jit(solution)/shard_map/ppermute | solution.py:38
  25.9 26.6 %collective-permute-start.7 = (bf16[384,1536]{1,0:T(8,128)(2,1)S(1)}, bf16[384,1536]{1,0:T(8,128)(2,1)S(1)}, u32[]{:S(2)}, u32[]{:S(2)}) collective-permute-start(bf16[384,1536]{1,0:T(8,128)(2,1)S(1)} %get-tuple-element.37), channel_id=1, source_target_pairs={{0,24},{4,100},{8,0},{12,108},{16,8},{20,116},{24,16},{28,124},{32... | collective-permute-start | bytes 3538952 | tf_op jit(solution)/shard_map/ppermute | solution.py:38
  41.1 27.6 %collective-permute-start.4 = (bf16[2,528,512]{2,1,0:T(8,128)(2,1)S(1)}, bf16[2,528,512]{2,1,0:T(8,128)(2,1)S(1)}, u32[]{:S(2)}, u32[]{:S(2)}) collective-permute-start(bf16[2,528,512]{2,1,0:T(8,128)(2,1)S(1)} %copy-done.3), channel_id=1, source_target_pairs={{0,7},{1,4},{2,5},{3,6},{4,3},{5,0},{6,1},{7,2},{8,15},{9,12},{10,... | collective-permute-start | bytes 3244040 | tf_op jit(solution)/shard_map/ppermute | solution.py:57
  45.1 11.6 %copy-start.1 = (bf16[2,2,528,512]{3,2,1,0:T(8,128)(2,1)S(1)}, bf16[2,2,528,512]{3,2,1,0:T(8,128)(2,1)}, u32[]{:S(2)}) copy-start(bf16[2,2,528,512]{3,2,1,0:T(8,128)(2,1)} %get-tuple-element.26.refs_0_) | copy-start | bytes 6488068
  45.1 26.8 %collective-permute-start.3 = (bf16[2,528,512]{2,1,0:T(8,128)(2,1)S(1)}, bf16[2,528,512]{2,1,0:T(8,128)(2,1)S(1)}, u32[]{:S(2)}, u32[]{:S(2)}) collective-permute-start(bf16[2,528,512]{2,1,0:T(8,128)(2,1)S(1)} %copy-done.2), channel_id=1, source_target_pairs={{0,5},{1,6},{2,7},{3,4},{4,1},{5,2},{6,3},{7,0},{8,13},{9,14},{10,... | collective-permute-start | bytes 3244040 | tf_op jit(solution)/shard_map/ppermute | solution.py:57
  53.0 9.4 %collective-permute-start.10 = (bf16[96,1536]{1,0:T(8,128)(2,1)S(1)}, bf16[96,1536]{1,0:T(8,128)(2,1)S(1)}, u32[]{:S(2)}, u32[]{:S(2)}) collective-permute-start(bf16[96,1536]{1,0:T(8,128)(2,1)S(1)} %get-tuple-element.41), channel_id=1, source_target_pairs={{0,96},{4,28},{8,104},{12,4},{16,112},{20,12},{24,120},{28,20},{32... | collective-permute-start | bytes 884744 | tf_op jit(solution)/shard_map/ppermute | solution.py:38
  55.6 7.4 %collective-permute-start.8 = (bf16[96,1536]{1,0:T(8,128)(2,1)S(1)}, bf16[96,1536]{1,0:T(8,128)(2,1)S(1)}, u32[]{:S(2)}, u32[]{:S(2)}) collective-permute-start(bf16[96,1536]{1,0:T(8,128)(2,1)S(1)} %get-tuple-element.39), channel_id=1, source_target_pairs={{0,64},{4,20},{8,72},{12,28},{16,80},{20,4},{24,88},{28,12},{32,96... | collective-permute-start | bytes 884744 | tf_op jit(solution)/shard_map/ppermute | solution.py:38
  56.1 10.0 %collective-permute-start.9 = (bf16[96,1536]{1,0:T(8,128)(2,1)S(1)}, bf16[96,1536]{1,0:T(8,128)(2,1)S(1)}, u32[]{:S(2)}, u32[]{:S(2)}) collective-permute-start(bf16[96,1536]{1,0:T(8,128)(2,1)S(1)} %get-tuple-element.40), channel_id=1, source_target_pairs={{0,32},{4,12},{8,40},{12,20},{16,48},{20,28},{24,56},{28,4},{32,64... | collective-permute-start | bytes 884744 | tf_op jit(solution)/shard_map/ppermute | solution.py:38
  74.3 17.0 %collective-permute-start.11 = (bf16[384,1536]{1,0:T(8,128)(2,1)S(1)}, bf16[384,1536]{1,0:T(8,128)(2,1)S(1)}, u32[]{:S(2)}, u32[]{:S(2)}) collective-permute-start(bf16[384,1536]{1,0:T(8,128)(2,1)S(1)} %get-tuple-element.43), channel_id=1, source_target_pairs={{0,16},{4,68},{8,24},{12,76},{16,0},{20,84},{24,8},{28,92},{32,48}... | collective-permute-start | bytes 3538952 | tf_op jit(solution)/shard_map/ppermute | solution.py:38
  77.4 26.6 %collective-permute-start.12 = (bf16[384,1536]{1,0:T(8,128)(2,1)S(1)}, bf16[384,1536]{1,0:T(8,128)(2,1)S(1)}, u32[]{:S(2)}, u32[]{:S(2)}) collective-permute-start(bf16[384,1536]{1,0:T(8,128)(2,1)S(1)} %get-tuple-element.44), channel_id=1, source_target_pairs={{0,8},{4,36},{8,16},{12,44},{16,24},{20,52},{24,0},{28,60},{32,40}... | collective-permute-start | bytes 3538952 | tf_op jit(solution)/shard_map/ppermute | solution.py:38
  77.7 26.6 %collective-permute-start.13 = (bf16[384,1536]{1,0:T(8,128)(2,1)S(1)}, bf16[384,1536]{1,0:T(8,128)(2,1)S(1)}, u32[]{:S(2)}, u32[]{:S(2)}) collective-permute-start(bf16[384,1536]{1,0:T(8,128)(2,1)S(1)} %get-tuple-element.45), channel_id=1, source_target_pairs={{0,24},{4,100},{8,0},{12,108},{16,8},{20,116},{24,16},{28,124},{32... | collective-permute-start | bytes 3538952 | tf_op jit(solution)/shard_map/ppermute | solution.py:38
  80.0 30.1 %collective-permute-start.17 = (bf16[96,1536]{1,0:T(8,128)(2,1)S(1)}, bf16[96,1536]{1,0:T(8,128)(2,1)S(1)}, u32[]{:S(2)}, u32[]{:S(2)}) collective-permute-start(bf16[96,1536]{1,0:T(8,128)(2,1)S(1)} %add_convert_fusion.refs_3_), channel_id=1, source_target_pairs={{0,2},{1,3},{2,0},{3,1},{4,6},{5,7},{6,4},{7,5},{8,10},{9,11},{10,... | collective-permute-start | bytes 884744 | tf_op jit(solution)/shard_map/ppermute | solution.py:42
  104.9 7.5 %collective-permute-start.14 = (bf16[96,1536]{1,0:T(8,128)(2,1)S(1)}, bf16[96,1536]{1,0:T(8,128)(2,1)S(1)}, u32[]{:S(2)}, u32[]{:S(2)}) collective-permute-start(bf16[96,1536]{1,0:T(8,128)(2,1)S(1)} %get-tuple-element.47), channel_id=1, source_target_pairs={{0,64},{4,20},{8,72},{12,28},{16,80},{20,4},{24,88},{28,12},{32,96... | collective-permute-start | bytes 884744 | tf_op jit(solution)/shard_map/ppermute | solution.py:38
  107.4 8.1 %collective-permute-start.15 = (bf16[96,1536]{1,0:T(8,128)(2,1)S(1)}, bf16[96,1536]{1,0:T(8,128)(2,1)S(1)}, u32[]{:S(2)}, u32[]{:S(2)}) collective-permute-start(bf16[96,1536]{1,0:T(8,128)(2,1)S(1)} %get-tuple-element.48), channel_id=1, source_target_pairs={{0,32},{4,12},{8,40},{12,20},{16,48},{20,28},{24,56},{28,4},{32,64... | collective-permute-start | bytes 884744 | tf_op jit(solution)/shard_map/ppermute | solution.py:38
  108.0 7.6 %collective-permute-start.16 = (bf16[96,1536]{1,0:T(8,128)(2,1)S(1)}, bf16[96,1536]{1,0:T(8,128)(2,1)S(1)}, u32[]{:S(2)}, u32[]{:S(2)}) collective-permute-start(bf16[96,1536]{1,0:T(8,128)(2,1)S(1)} %get-tuple-element.49), channel_id=1, source_target_pairs={{0,96},{4,28},{8,104},{12,4},{16,112},{20,12},{24,120},{28,20},{32... | collective-permute-start | bytes 884744 | tf_op jit(solution)/shard_map/ppermute | solution.py:38
  115.8 3.1 %collective-permute-start.18 = (f32[48,1536]{1,0:T(8,128)S(1)}, f32[48,1536]{1,0:T(8,128)S(1)}, u32[]{:S(2)}, u32[]{:S(2)}) collective-permute-start(f32[48,1536]{1,0:T(8,128)S(1)} %slice.9), channel_id=1, source_target_pairs={{0,4},{4,0},{8,12},{12,8},{16,20},{20,16},{24,28},{28,24},{32,36},... | collective-permute-start | bytes 884744 | tf_op jit(solution)/shard_map/ppermute | solution.py:47

commit v10 on v9

--- a/solution.py
+++ b/solution.py
@@ -112,12 +112,12 @@
                     down[basis, 2] = band[:, : 2 * LANES].astype(BF16)
                     continue
                 band = band.T.astype(BF16)
-                across[basis] = jnp.zeros((TILE, TILE), BF16)
+                across[:, basis * TILE : (basis + 1) * TILE] = jnp.zeros((TILE, TILE), BF16)
                 for block in range(TILE // LANES):
                     first = (block - 1) * LANES
                     low, high = max(first, 0), min(first + 3 * LANES, TILE)
-                    span = slice(block * LANES, (block + 1) * LANES)
-                    across[basis, low:high, span] = band[low - first : high - first, :]
+                    at = basis * TILE + block * LANES
+                    across[low:high, at : at + LANES] = band[low - first : high - first, :]
 
     rows = lax.broadcasted_iota(jnp.int32, (TILE, 1), 0).astype(F32)
     columns = lax.broadcasted_iota(jnp.int32, (1, TILE), 1).astype(F32)
@@ -125,9 +125,10 @@
     columns = (columns - (TILE - 1) / 2.0) / (TILE / 2.0)
     for copy in loads[4]:
         copy.wait()
+    middles = jnp.dot(images[tile], across[...], preferred_element_type=F32).astype(BF16)
     total = jnp.zeros((TILE, TILE), F32)
     for basis in range(BASES):
-        middle = jnp.dot(images[tile], across[basis], preferred_element_type=F32).astype(BF16)
+        middle = middles[:, basis * TILE : (basis + 1) * TILE]
         smoothed = jnp.concatenate(
             [
                 jnp.dot(down[basis, kind], middle[first : first + 2 * LANES], preferred_element_type=F32)
@@ -201,7 +202,7 @@
             pltpu.VMEM((BASES, 4, 3), BF16),
             pltpu.VMEM((4, TILE, TILE), BF16),
             pltpu.VMEM((4, TILE, TILE), BF16),
-            pltpu.VMEM((BASES, TILE, TILE), BF16),
+            pltpu.VMEM((TILE, BASES * TILE), BF16),
             pltpu.VMEM((BASES, 3, LANES, 2 * LANES), BF16),
             pltpu.VMEM((8, 3 * LANES), F32),
             pltpu.VMEM((BASES, 8, LANES), F32),

time: 120 us -> 120 us (level)
  no operation moved by 1% of the time
where the time goes in v10:
time: 120 us; the launch traced here: 119 us
  waiting for transfers between devices  62 us (52%)
  starting transfers between devices  31.6 us (26%)
  Pallas kernels  22.2 us (18%)
  local copies, waits for them, and re-layouts  1.64 us (1%)
    ppermute x12, waiting for transfers between devices, turn(): return lax.ppermute(value, 'visit', pairs)  41.9 us
    ppermute x12, starting transfers between devices, turn(): return lax.ppermute(value, 'visit', pairs)  20.3 us
    ppermute x3, waiting for transfers between devices, across_z(): return lax.ppermute(value, 'patch', [(z, (z + step) % 4) for z in range(4)])  12.9 us
    pallas_call x1, Pallas kernels, match_tiles(): pl.pallas_call(match_kernel, grid=(4,), in_specs=[pl.BlockSpec(memory_spa...  11.2 us
    ppermute x2, waiting for transfers between devices, across_both(): return lax.ppermute(value, ('visit', 'patch'), pairs)  5.7 us
    pallas_call x1, Pallas kernels, start_frame(): pl.pallas_call(start_kernel, out_shape=jax.ShapeDtypeStruct(FRAME, F32),...  4.46 us
    ppermute x2, starting transfers between devices, across_both(): return lax.ppermute(value, ('visit', 'patch'), pairs)  4.12 us
    ppermute x3, starting transfers between devices, across_z(): return lax.ppermute(value, 'patch', [(z, (z + step) % 4) for z in range(4)])  3.87 us
  transfers between devices with their start and end apart: 19, of which 16 were waited for; matrix products, arithmetic and copies ran while one was open for 0% of the time, Pallas kernels for 7%

profile of v10, /device:TPU:1, one launch (start us, length us, event | category | flops | bytes accessed | tf_op | source)
XLA Modules:
  0.0 119.4 jit_solution(11816645501057317900)
XLA Ops:
  0.6 11.2 %shard_map.77 = (bf16[2,2,528,512]{3,2,1,0:T(8,128)(2,1)}, bf16[2,528,512]{2,1,0:T(8,128)(2,1)}, bf16[2,528,512]{2,1,0:T(8,128)(2,1)}, bf16[2,2,528,512]{3,2,1,0...) custom-call(s32[2,4]{1,0:T(2,128)} %bitcast.23, s32[2,2,4]{2,1,0:T(2,128)} %bitcast.21, ...), custom_call_target="tpu_custom_call" | custom-call | flops 6442450944 | bytes 12582912 | tf_op jit(solution)/shard_map/pallas_call | solution.py:192
  11.8 1.5 %collective-permute-start = (bf16[2,2,528,512]{3,2,1,0:T(8,128)(2,1)}, bf16[2,2,528,512]{3,2,1,0:T(8,128)(2,1)S(1)}, u32[]{:S(2)}, u32[]{:S(2)}) collective-permute-start(bf16[2,2,528,512]{3,2,1,0:T(8,128)(2,1)} %get-tuple-element.27), channel_id=1, source_target_pairs={{0,4},{4,0},{8,12},{12,8},{16,20},{20,16},{24,28},{28,24},{32,36},... | collective-permute-start | bytes 6488072 | tf_op jit(solution)/shard_map/ppermute | solution.py:47
  13.3 3.9 %collective-permute-start.2 = (bf16[2,528,512]{2,1,0:T(8,128)(2,1)}, bf16[2,528,512]{2,1,0:T(8,128)(2,1)S(1)}, u32[]{:S(2)}, u32[]{:S(2)}) collective-permute-start(bf16[2,528,512]{2,1,0:T(8,128)(2,1)} %get-tuple-element.29), channel_id=1, source_target_pairs={{0,3},{1,0},{2,1},{3,2},{4,7},{5,4},{6,5},{7,6},{8,11},{9,8},{10,9... | collective-permute-start | bytes 3244040 | tf_op jit(solution)/shard_map/ppermute | solution.py:42
  17.4 1.6 %copy-done = bf16[2,2,528,512]{3,2,1,0:T(8,128)(2,1)S(1)} copy-done((bf16[2,2,528,512]{3,2,1,0:T(8,128)(2,1)S(1)}, bf16[2,2,528,512]{3,2,1,0:T(8,128)(2,1)}, u32[]{:S(2)}) %copy-start) | copy-done | bytes 2162712
  19.0 3.0 %shard_map.79 = (bf16[384,1536]{1,0:T(8,128)(2,1)S(1)}, bf16[384,1536]{1,0:T(8,128)(2,1)S(1)}, bf16[384,1536]{1,0:T(8,128)(2,1)S(1)}, bf16[384,1536]{1,0:T(8,128)(2,1)S(1)}) custom-call(bf16[2,2,528,512]{3,2,1,0:T(8,128)(2,1)S(1)} %copy-done, bf16[2,2,528,512]{3,2,1,0:T(8,128)(2,1)S(1)} %collective-permute-done.refs_1_), custom_call_target="tpu_custom_call" | custom-call | flops 2147483648 | bytes 9437184 | tf_op jit(solution)/shard_map/pallas_call | solution.py:305
  22.1 3.1 %collective-permute-start.5 = (bf16[384,1536]{1,0:T(8,128)(2,1)S(1)}, bf16[384,1536]{1,0:T(8,128)(2,1)S(1)}, u32[]{:S(2)}, u32[]{:S(2)}) collective-permute-start(bf16[384,1536]{1,0:T(8,128)(2,1)S(1)} %get-tuple-element.35), channel_id=1, source_target_pairs={{0,16},{4,68},{8,24},{12,76},{16,0},{20,84},{24,8},{28,92},{32,48}... | collective-permute-start | bytes 3538952 | tf_op jit(solution)/shard_map/ppermute | solution.py:38
  25.5 2.3 %collective-permute-start.7 = (bf16[384,1536]{1,0:T(8,128)(2,1)S(1)}, bf16[384,1536]{1,0:T(8,128)(2,1)S(1)}, u32[]{:S(2)}, u32[]{:S(2)}) collective-permute-start(bf16[384,1536]{1,0:T(8,128)(2,1)S(1)} %get-tuple-element.37), channel_id=1, source_target_pairs={{0,24},{4,100},{8,0},{12,108},{16,8},{20,116},{24,16},{28,124},{32... | collective-permute-start | bytes 3538952 | tf_op jit(solution)/shard_map/ppermute | solution.py:38
  27.8 12.9 %collective-permute-done.2.refs_3_ = bf16[2,528,512]{2,1,0:T(8,128)(2,1)S(1)} collective-permute-done((bf16[2,528,512]{2,1,0:T(8,128)(2,1)}, bf16[2,528,512]{2,1,0:T(8,128)(2,1)S(1)}, u32[]{:S(2)}, u32[]{:S(2)}) %collective-permute-start.2) | collective-permute-done | bytes 1081376 | tf_op jit(solution)/shard_map/ppermute | solution.py:42
  40.7 4.1 %collective-permute-start.4 = (bf16[2,528,512]{2,1,0:T(8,128)(2,1)S(1)}, bf16[2,528,512]{2,1,0:T(8,128)(2,1)S(1)}, u32[]{:S(2)}, u32[]{:S(2)}) collective-permute-start(bf16[2,528,512]{2,1,0:T(8,128)(2,1)S(1)} %copy-done.3), channel_id=1, source_target_pairs={{0,7},{1,4},{2,5},{3,6},{4,3},{5,0},{6,1},{7,2},{8,15},{9,12},{10,... | collective-permute-start | bytes 3244040 | tf_op jit(solution)/shard_map/ppermute | solution.py:57
  44.9 6.8 %collective-permute-done.6.refs_2_ = bf16[384,1536]{1,0:T(8,128)(2,1)S(1)} collective-permute-done((bf16[384,1536]{1,0:T(8,128)(2,1)S(1)}, bf16[384,1536]{1,0:T(8,128)(2,1)S(1)}, u32[]{:S(2)}, u32[]{:S(2)}) %collective-permute-start.6) | collective-permute-done | bytes 1179680 | tf_op jit(solution)/shard_map/ppermute | solution.py:38
  52.1 0.6 shard_map.80
  52.7 2.5 %collective-permute-start.10 = (bf16[96,1536]{1,0:T(8,128)(2,1)S(1)}, bf16[96,1536]{1,0:T(8,128)(2,1)S(1)}, u32[]{:S(2)}, u32[]{:S(2)}) collective-permute-start(bf16[96,1536]{1,0:T(8,128)(2,1)S(1)} %get-tuple-element.41), channel_id=1, source_target_pairs={{0,96},{4,28},{8,104},{12,4},{16,112},{20,12},{24,120},{28,20},{32... | collective-permute-start | bytes 884744 | tf_op jit(solution)/shard_map/ppermute | solution.py:38
  55.8 0.6 collective-permute-start.9
  56.4 4.5 %shard_map.78.refs_0_ = f32[193,8,1536]{2,1,0:T(8,128)S(1)} custom-call(bf16[2,2,528,512]{3,2,1,0:T(8,128)(2,1)S(1)} %copy-done.1, bf16[2,2,528,512]{3,2,1,0:T(8,128)(2,1)S(1)} %collective-permute-done.refs_1_, bf16[2,528,512]{2,1,0:T(8,128)(2,1)S(1)} %collective-permute-done.1.refs_2_, bf16[2,528,512]{2,1,0:T(8,128)(2,1)S(1)} %collective-permute-done.2.refs_3_), custom_call_target="tpu_custom_call" | custom-call | flops 4294967296 | bytes 13631488 | tf_op jit(solution)/shard_map/pallas_call | solution.py:311
  60.8 1.2 %collective-permute-done.10 = bf16[96,1536]{1,0:T(8,128)(2,1)S(1)} collective-permute-done((bf16[96,1536]{1,0:T(8,128)(2,1)S(1)}, bf16[96,1536]{1,0:T(8,128)(2,1)S(1)}, u32[]{:S(2)}, u32[]{:S(2)}) %collective-permute-start.10) | collective-permute-done | bytes 294944 | tf_op jit(solution)/shard_map/ppermute | solution.py:38
  62.0 0.6 collective-permute-done.8
  62.6 3.1 %collective-permute-done.9 = bf16[96,1536]{1,0:T(8,128)(2,1)S(1)} collective-permute-done((bf16[96,1536]{1,0:T(8,128)(2,1)S(1)}, bf16[96,1536]{1,0:T(8,128)(2,1)S(1)}, u32[]{:S(2)}, u32[]{:S(2)}) %collective-permute-start.9) | collective-permute-done | bytes 294944 | tf_op jit(solution)/shard_map/ppermute | solution.py:38
  65.9 2.5 %collective-permute-done.4.refs_2_ = bf16[2,528,512]{2,1,0:T(8,128)(2,1)S(1)} collective-permute-done((bf16[2,528,512]{2,1,0:T(8,128)(2,1)S(1)}, bf16[2,528,512]{2,1,0:T(8,128)(2,1)S(1)}, u32[]{:S(2)}, u32[]{:S(2)}) %collective-permute-start.4) | collective-permute-done | bytes 1081376 | tf_op jit(solution)/shard_map/ppermute | solution.py:57
  68.3 3.3 %collective-permute-done.3.refs_1_ = bf16[2,528,512]{2,1,0:T(8,128)(2,1)S(1)} collective-permute-done((bf16[2,528,512]{2,1,0:T(8,128)(2,1)S(1)}, bf16[2,528,512]{2,1,0:T(8,128)(2,1)S(1)}, u32[]{:S(2)}, u32[]{:S(2)}) %collective-permute-start.3) | collective-permute-done | bytes 1081376 | tf_op jit(solution)/shard_map/ppermute | solution.py:57
  71.6 2.4 %shard_map.81 = (bf16[384,1536]{1,0:T(8,128)(2,1)S(1)}, bf16[384,1536]{1,0:T(8,128)(2,1)S(1)}, bf16[384,1536]{1,0:T(8,128)(2,1)S(1)}, bf16[384,1536]{1,0:T(8,128)(2,1)S(1)}, f32[193,8,1536]{2,1,0:T(8,128)S(1)}) custom-call(f32[193,8,1536]{2,1,0:T(8,128)S(1)} %shard_map.78.refs_0_, ...), custom_call_target="tpu_custom_call", output_to_operand_aliasing={{4}: (0, {})} | custom-call | flops 2147483648 | bytes 9437184 | tf_op jit(solution)/shard_map/pallas_call | solution.py:316
  74.0 3.0 %collective-permute-start.11 = (bf16[384,1536]{1,0:T(8,128)(2,1)S(1)}, bf16[384,1536]{1,0:T(8,128)(2,1)S(1)}, u32[]{:S(2)}, u32[]{:S(2)}) collective-permute-start(bf16[384,1536]{1,0:T(8,128)(2,1)S(1)} %get-tuple-element.43), channel_id=1, source_target_pairs={{0,16},{4,68},{8,24},{12,76},{16,0},{20,84},{24,8},{28,92},{32,48}... | collective-permute-start | bytes 3538952 | tf_op jit(solution)/shard_map/ppermute | solution.py:38
  77.4 2.3 %collective-permute-start.13 = (bf16[384,1536]{1,0:T(8,128)(2,1)S(1)}, bf16[384,1536]{1,0:T(8,128)(2,1)S(1)}, u32[]{:S(2)}, u32[]{:S(2)}) collective-permute-start(bf16[384,1536]{1,0:T(8,128)(2,1)S(1)} %get-tuple-element.45), channel_id=1, source_target_pairs={{0,24},{4,100},{8,0},{12,108},{16,8},{20,116},{24,16},{28,124},{32... | collective-permute-start | bytes 3538952 | tf_op jit(solution)/shard_map/ppermute | solution.py:38
  79.7 11.3 %collective-permute-done.11.refs_1_ = bf16[384,1536]{1,0:T(8,128)(2,1)S(1)} collective-permute-done((bf16[384,1536]{1,0:T(8,128)(2,1)S(1)}, bf16[384,1536]{1,0:T(8,128)(2,1)S(1)}, u32[]{:S(2)}, u32[]{:S(2)}) %collective-permute-start.11) | collective-permute-done | bytes 1179680 | tf_op jit(solution)/shard_map/ppermute | solution.py:38
  91.0 12.6 %collective-permute-done.12.refs_2_ = bf16[384,1536]{1,0:T(8,128)(2,1)S(1)} collective-permute-done((bf16[384,1536]{1,0:T(8,128)(2,1)S(1)}, bf16[384,1536]{1,0:T(8,128)(2,1)S(1)}, u32[]{:S(2)}, u32[]{:S(2)}) %collective-permute-start.12) | collective-permute-done | bytes 1179680 | tf_op jit(solution)/shard_map/ppermute | solution.py:38
  104.5 2.5 %collective-permute-start.14 = (bf16[96,1536]{1,0:T(8,128)(2,1)S(1)}, bf16[96,1536]{1,0:T(8,128)(2,1)S(1)}, u32[]{:S(2)}, u32[]{:S(2)}) collective-permute-start(bf16[96,1536]{1,0:T(8,128)(2,1)S(1)} %get-tuple-element.47), channel_id=1, source_target_pairs={{0,64},{4,20},{8,72},{12,28},{16,80},{20,4},{24,88},{28,12},{32,96... | collective-permute-start | bytes 884744 | tf_op jit(solution)/shard_map/ppermute | solution.py:38
  107.0 0.6 collective-permute-start.15
  107.7 2.1 %collective-permute-start.16 = (bf16[96,1536]{1,0:T(8,128)(2,1)S(1)}, bf16[96,1536]{1,0:T(8,128)(2,1)S(1)}, u32[]{:S(2)}, u32[]{:S(2)}) collective-permute-start(bf16[96,1536]{1,0:T(8,128)(2,1)S(1)} %get-tuple-element.49), channel_id=1, source_target_pairs={{0,96},{4,28},{8,104},{12,4},{16,112},{20,12},{24,120},{28,20},{32... | collective-permute-start | bytes 884744 | tf_op jit(solution)/shard_map/ppermute | solution.py:38
  109.7 2.3 %collective-permute-done.14 = bf16[96,1536]{1,0:T(8,128)(2,1)S(1)} collective-permute-done((bf16[96,1536]{1,0:T(8,128)(2,1)S(1)}, bf16[96,1536]{1,0:T(8,128)(2,1)S(1)}, u32[]{:S(2)}, u32[]{:S(2)}) %collective-permute-start.14) | collective-permute-done | bytes 294944 | tf_op jit(solution)/shard_map/ppermute | solution.py:38
  112.0 3.2 %collective-permute-done.15 = bf16[96,1536]{1,0:T(8,128)(2,1)S(1)} collective-permute-done((bf16[96,1536]{1,0:T(8,128)(2,1)S(1)}, bf16[96,1536]{1,0:T(8,128)(2,1)S(1)}, u32[]{:S(2)}, u32[]{:S(2)}) %collective-permute-start.15) | collective-permute-done | bytes 294944 | tf_op jit(solution)/shard_map/ppermute | solution.py:38
  115.4 1.9 %collective-permute-start.18 = (f32[48,1536]{1,0:T(8,128)S(1)}, f32[48,1536]{1,0:T(8,128)S(1)}, u32[]{:S(2)}, u32[]{:S(2)}) collective-permute-start(f32[48,1536]{1,0:T(8,128)S(1)} %slice.9), channel_id=1, source_target_pairs={{0,4},{4,0},{8,12},{12,8},{16,20},{20,16},{24,28},{28,24},{32,36},... | collective-permute-start | bytes 884744 | tf_op jit(solution)/shard_map/ppermute | solution.py:47
  117.3 1.2 %collective-permute-done.18 = f32[48,1536]{1,0:T(8,128)S(1)} collective-permute-done((f32[48,1536]{1,0:T(8,128)S(1)}, f32[48,1536]{1,0:T(8,128)S(1)}, u32[]{:S(2)}, u32[]{:S(2)}) %collective-permute-start.18) | collective-permute-done | bytes 294944 | tf_op jit(solution)/shard_map/ppermute | solution.py:47
  118.5 0.9 fusion
  (24 shorter events, 3.5 us)
Async XLA Ops:
  11.8 5.6 %collective-permute-start = (bf16[2,2,528,512]{3,2,1,0:T(8,128)(2,1)}, bf16[2,2,528,512]{3,2,1,0:T(8,128)(2,1)S(1)}, u32[]{:S(2)}, u32[]{:S(2)}) collective-permute-start(bf16[2,2,528,512]{3,2,1,0:T(8,128)(2,1)} %get-tuple-element.27), channel_id=1, source_target_pairs={{0,4},{4,0},{8,12},{12,8},{16,20},{20,16},{24,28},{28,24},{32,36},... | collective-permute-start | bytes 6488072 | tf_op jit(solution)/shard_map/ppermute | solution.py:47
  13.3 27.4 %collective-permute-start.2 = (bf16[2,528,512]{2,1,0:T(8,128)(2,1)}, bf16[2,528,512]{2,1,0:T(8,128)(2,1)S(1)}, u32[]{:S(2)}, u32[]{:S(2)}) collective-permute-start(bf16[2,528,512]{2,1,0:T(8,128)(2,1)} %get-tuple-element.29), channel_id=1, source_target_pairs={{0,3},{1,0},{2,1},{3,2},{4,7},{5,4},{6,5},{7,6},{8,11},{9,8},{10,9... | collective-permute-start | bytes 3244040 | tf_op jit(solution)/shard_map/ppermute | solution.py:42
  17.2 27.6 %collective-permute-start.1 = (bf16[2,528,512]{2,1,0:T(8,128)(2,1)}, bf16[2,528,512]{2,1,0:T(8,128)(2,1)S(1)}, u32[]{:S(2)}, u32[]{:S(2)}) collective-permute-start(bf16[2,528,512]{2,1,0:T(8,128)(2,1)} %get-tuple-element.28), channel_id=1, source_target_pairs={{0,1},{1,2},{2,3},{3,0},{4,5},{5,6},{6,7},{7,4},{8,9},{9,10},{10,1... | collective-permute-start | bytes 3244040 | tf_op jit(solution)/shard_map/ppermute | solution.py:42
  17.4 1.6 %copy-start = (bf16[2,2,528,512]{3,2,1,0:T(8,128)(2,1)S(1)}, bf16[2,2,528,512]{3,2,1,0:T(8,128)(2,1)}, u32[]{:S(2)}) copy-start(bf16[2,2,528,512]{3,2,1,0:T(8,128)(2,1)} %get-tuple-element.26.refs_0_) | copy-start | bytes 6488068
  19.0 21.7 %copy-start.3 = (bf16[2,528,512]{2,1,0:T(8,128)(2,1)S(1)}, bf16[2,528,512]{2,1,0:T(8,128)(2,1)}, u32[]{:S(2)}) copy-start(bf16[2,528,512]{2,1,0:T(8,128)(2,1)} %get-tuple-element.34) | copy-start | bytes 3244036
  19.0 25.8 %copy-start.2 = (bf16[2,528,512]{2,1,0:T(8,128)(2,1)S(1)}, bf16[2,528,512]{2,1,0:T(8,128)(2,1)}, u32[]{:S(2)}) copy-start(bf16[2,528,512]{2,1,0:T(8,128)(2,1)} %get-tuple-element.32) | copy-start | bytes 3244036
  22.1 22.8 %collective-permute-start.5 = (bf16[384,1536]{1,0:T(8,128)(2,1)S(1)}, bf16[384,1536]{1,0:T(8,128)(2,1)S(1)}, u32[]{:S(2)}, u32[]{:S(2)}) collective-permute-start(bf16[384,1536]{1,0:T(8,128)(2,1)S(1)} %get-tuple-element.35), channel_id=1, source_target_pairs={{0,16},{4,68},{8,24},{12,76},{16,0},{20,84},{24,8},{28,92},{32,48}... | collective-permute-start | bytes 3538952 | tf_op jit(solution)/shard_map/ppermute | solution.py:38
  25.1 26.5 %collective-permute-start.6 = (bf16[384,1536]{1,0:T(8,128)(2,1)S(1)}, bf16[384,1536]{1,0:T(8,128)(2,1)S(1)}, u32[]{:S(2)}, u32[]{:S(2)}) collective-permute-start(bf16[384,1536]{1,0:T(8,128)(2,1)S(1)} %get-tuple-element.36), channel_id=1, source_target_pairs={{0,8},{4,36},{8,16},{12,44},{16,24},{20,52},{24,0},{28,60},{32,40}... | collective-permute-start | bytes 3538952 | tf_op jit(solution)/shard_map/ppermute | solution.py:38
  25.5 26.6 %collective-permute-start.7 = (bf16[384,1536]{1,0:T(8,128)(2,1)S(1)}, bf16[384,1536]{1,0:T(8,128)(2,1)S(1)}, u32[]{:S(2)}, u32[]{:S(2)}) collective-permute-start(bf16[384,1536]{1,0:T(8,128)(2,1)S(1)} %get-tuple-element.37), channel_id=1, source_target_pairs={{0,24},{4,100},{8,0},{12,108},{16,8},{20,116},{24,16},{28,124},{32... | collective-permute-start | bytes 3538952 | tf_op jit(solution)/shard_map/ppermute | solution.py:38
  40.7 27.6 %collective-permute-start.4 = (bf16[2,528,512]{2,1,0:T(8,128)(2,1)S(1)}, bf16[2,528,512]{2,1,0:T(8,128)(2,1)S(1)}, u32[]{:S(2)}, u32[]{:S(2)}) collective-permute-start(bf16[2,528,512]{2,1,0:T(8,128)(2,1)S(1)} %copy-done.3), channel_id=1, source_target_pairs={{0,7},{1,4},{2,5},{3,6},{4,3},{5,0},{6,1},{7,2},{8,15},{9,12},{10,... | collective-permute-start | bytes 3244040 | tf_op jit(solution)/shard_map/ppermute | solution.py:57
  44.8 11.6 %copy-start.1 = (bf16[2,2,528,512]{3,2,1,0:T(8,128)(2,1)S(1)}, bf16[2,2,528,512]{3,2,1,0:T(8,128)(2,1)}, u32[]{:S(2)}) copy-start(bf16[2,2,528,512]{3,2,1,0:T(8,128)(2,1)} %get-tuple-element.26.refs_0_) | copy-start | bytes 6488068
  44.8 26.8 %collective-permute-start.3 = (bf16[2,528,512]{2,1,0:T(8,128)(2,1)S(1)}, bf16[2,528,512]{2,1,0:T(8,128)(2,1)S(1)}, u32[]{:S(2)}, u32[]{:S(2)}) collective-permute-start(bf16[2,528,512]{2,1,0:T(8,128)(2,1)S(1)} %copy-done.2), channel_id=1, source_target_pairs={{0,5},{1,6},{2,7},{3,4},{4,1},{5,2},{6,3},{7,0},{8,13},{9,14},{10,... | collective-permute-start | bytes 3244040 | tf_op jit(solution)/shard_map/ppermute | solution.py:57
  52.7 9.3 %collective-permute-start.10 = (bf16[96,1536]{1,0:T(8,128)(2,1)S(1)}, bf16[96,1536]{1,0:T(8,128)(2,1)S(1)}, u32[]{:S(2)}, u32[]{:S(2)}) collective-permute-start(bf16[96,1536]{1,0:T(8,128)(2,1)S(1)} %get-tuple-element.41), channel_id=1, source_target_pairs={{0,96},{4,28},{8,104},{12,4},{16,112},{20,12},{24,120},{28,20},{32... | collective-permute-start | bytes 884744 | tf_op jit(solution)/shard_map/ppermute | solution.py:38
  55.2 7.4 %collective-permute-start.8 = (bf16[96,1536]{1,0:T(8,128)(2,1)S(1)}, bf16[96,1536]{1,0:T(8,128)(2,1)S(1)}, u32[]{:S(2)}, u32[]{:S(2)}) collective-permute-start(bf16[96,1536]{1,0:T(8,128)(2,1)S(1)} %get-tuple-element.39), channel_id=1, source_target_pairs={{0,64},{4,20},{8,72},{12,28},{16,80},{20,4},{24,88},{28,12},{32,96... | collective-permute-start | bytes 884744 | tf_op jit(solution)/shard_map/ppermute | solution.py:38
  55.8 10.0 %collective-permute-start.9 = (bf16[96,1536]{1,0:T(8,128)(2,1)S(1)}, bf16[96,1536]{1,0:T(8,128)(2,1)S(1)}, u32[]{:S(2)}, u32[]{:S(2)}) collective-permute-start(bf16[96,1536]{1,0:T(8,128)(2,1)S(1)} %get-tuple-element.40), channel_id=1, source_target_pairs={{0,32},{4,12},{8,40},{12,20},{16,48},{20,28},{24,56},{28,4},{32,64... | collective-permute-start | bytes 884744 | tf_op jit(solution)/shard_map/ppermute | solution.py:38
  74.0 17.0 %collective-permute-start.11 = (bf16[384,1536]{1,0:T(8,128)(2,1)S(1)}, bf16[384,1536]{1,0:T(8,128)(2,1)S(1)}, u32[]{:S(2)}, u32[]{:S(2)}) collective-permute-start(bf16[384,1536]{1,0:T(8,128)(2,1)S(1)} %get-tuple-element.43), channel_id=1, source_target_pairs={{0,16},{4,68},{8,24},{12,76},{16,0},{20,84},{24,8},{28,92},{32,48}... | collective-permute-start | bytes 3538952 | tf_op jit(solution)/shard_map/ppermute | solution.py:38
  77.0 26.6 %collective-permute-start.12 = (bf16[384,1536]{1,0:T(8,128)(2,1)S(1)}, bf16[384,1536]{1,0:T(8,128)(2,1)S(1)}, u32[]{:S(2)}, u32[]{:S(2)}) collective-permute-start(bf16[384,1536]{1,0:T(8,128)(2,1)S(1)} %get-tuple-element.44), channel_id=1, source_target_pairs={{0,8},{4,36},{8,16},{12,44},{16,24},{20,52},{24,0},{28,60},{32,40}... | collective-permute-start | bytes 3538952 | tf_op jit(solution)/shard_map/ppermute | solution.py:38
  77.4 26.6 %collective-permute-start.13 = (bf16[384,1536]{1,0:T(8,128)(2,1)S(1)}, bf16[384,1536]{1,0:T(8,128)(2,1)S(1)}, u32[]{:S(2)}, u32[]{:S(2)}) collective-permute-start(bf16[384,1536]{1,0:T(8,128)(2,1)S(1)} %get-tuple-element.45), channel_id=1, source_target_pairs={{0,24},{4,100},{8,0},{12,108},{16,8},{20,116},{24,16},{28,124},{32... | collective-permute-start | bytes 3538952 | tf_op jit(solution)/shard_map/ppermute | solution.py:38
  79.7 30.0 %collective-permute-start.17 = (bf16[96,1536]{1,0:T(8,128)(2,1)S(1)}, bf16[96,1536]{1,0:T(8,128)(2,1)S(1)}, u32[]{:S(2)}, u32[]{:S(2)}) collective-permute-start(bf16[96,1536]{1,0:T(8,128)(2,1)S(1)} %add_convert_fusion.refs_3_), channel_id=1, source_target_pairs={{0,2},{1,3},{2,0},{3,1},{4,6},{5,7},{6,4},{7,5},{8,10},{9,11},{10,... | collective-permute-start | bytes 884744 | tf_op jit(solution)/shard_map/ppermute | solution.py:42
  104.5 7.5 %collective-permute-start.14 = (bf16[96,1536]{1,0:T(8,128)(2,1)S(1)}, bf16[96,1536]{1,0:T(8,128)(2,1)S(1)}, u32[]{:S(2)}, u32[]{:S(2)}) collective-permute-start(bf16[96,1536]{1,0:T(8,128)(2,1)S(1)} %get-tuple-element.47), channel_id=1, source_target_pairs={{0,64},{4,20},{8,72},{12,28},{16,80},{20,4},{24,88},{28,12},{32,96... | collective-permute-start | bytes 884744 | tf_op jit(solution)/shard_map/ppermute | solution.py:38
  107.0 8.1 %collective-permute-start.15 = (bf16[96,1536]{1,0:T(8,128)(2,1)S(1)}, bf16[96,1536]{1,0:T(8,128)(2,1)S(1)}, u32[]{:S(2)}, u32[]{:S(2)}) collective-permute-start(bf16[96,1536]{1,0:T(8,128)(2,1)S(1)} %get-tuple-element.48), channel_id=1, source_target_pairs={{0,32},{4,12},{8,40},{12,20},{16,48},{20,28},{24,56},{28,4},{32,64... | collective-permute-start | bytes 884744 | tf_op jit(solution)/shard_map/ppermute | solution.py:38
  107.7 7.6 %collective-permute-start.16 = (bf16[96,1536]{1,0:T(8,128)(2,1)S(1)}, bf16[96,1536]{1,0:T(8,128)(2,1)S(1)}, u32[]{:S(2)}, u32[]{:S(2)}) collective-permute-start(bf16[96,1536]{1,0:T(8,128)(2,1)S(1)} %get-tuple-element.49), channel_id=1, source_target_pairs={{0,96},{4,28},{8,104},{12,4},{16,112},{20,12},{24,120},{28,20},{32... | collective-permute-start | bytes 884744 | tf_op jit(solution)/shard_map/ppermute | solution.py:38
  115.4 3.1 %collective-permute-start.18 = (f32[48,1536]{1,0:T(8,128)S(1)}, f32[48,1536]{1,0:T(8,128)S(1)}, u32[]{:S(2)}, u32[]{:S(2)}) collective-permute-start(f32[48,1536]{1,0:T(8,128)S(1)} %slice.9), channel_id=1, source_target_pairs={{0,4},{4,0},{8,12},{12,8},{16,20},{20,16},{24,28},{28,24},{32,36},... | collective-permute-start | bytes 884744 | tf_op jit(solution)/shard_map/ppermute | solution.py:47
